TPU v7x, 128 devices: a whole 4x4x4 slice. The times are simulated.
128 devices in a mesh: clus: 4 (over x), split: 32 (over z, y, core).
Axes of the slice: x: 4, y: 4, z: 4, core: 2. Of those that a mesh axis runs over, the one named last changes fastest.
Arguments:
- embeddings: float32 [16384, 4096], P(('clus', 'split'))
- cluster_ids: int32 [16384], P(('clus', 'split')), may hold values from 0 to 63, as said below
Outputs:
- best_similarity: float32 [16384], P(('clus', 'split'))
Inputs may be any that keep to these rules, and one draw needn't show every extreme that they name: `cluster_ids`: the documents of one device's shard hold at most 64 cluster ids with any one residue modulo 4, and every shard has a residue reached exactly 64 times. Some clusters hold a single document.
All inputs are finite; a program needn't handle non-finite values.
Results may differ from a plain program's by a relative error of at most 0.0003.
Values may be sent and summed in bfloat16 or wider, within the bound.
No kernel may reach another device: no remote copies, remote signals or barrier semaphores. Data moves between devices by JAX's collectives and lax.ppermute only.
A program may use at most 192 MiB of HBM per device.

v0:
```python
import jax
import jax.numpy as jnp
from jax import lax
from jax.sharding import PartitionSpec as P


def masked_scores(left, left_ids, right, right_ids, left_start):
    scores = lax.dot_general(
        left, right, (((1,), (1,)), ((), ())), preferred_element_type=jnp.float32
    )
    left_at = left_start + jnp.arange(left.shape[0], dtype=jnp.int32)
    right_at = jnp.arange(right.shape[0], dtype=jnp.int32)
    mask = (
        (left_ids[:, None] == right_ids[None, :])
        & (left_ids[:, None] >= 0)
        & (left_at[:, None] != right_at[None, :])
    )
    return jnp.where(mask, scores, -1.0)


def normalise_rows(values):
    squares = jnp.sum(values * values, axis=1, keepdims=True)
    return (values * lax.rsqrt(squares + 1e-06)).astype(jnp.bfloat16)


def on_device(embeddings, cluster_ids):
    rows = embeddings.shape[0]
    groups = lax.axis_size("clus")
    cap = 2 * rows // groups
    slots = groups * cap
    owner_of = cluster_ids % groups
    onehot = (owner_of[:, None] == jnp.arange(groups, dtype=jnp.int32)[None, :]).astype(jnp.int32)
    before = jnp.cumsum(onehot, axis=0) - onehot
    rank = jnp.sum(before * onehot, axis=1)
    place = owner_of * cap + rank
    picked = place[None, :] == jnp.arange(slots, dtype=jnp.int32)[:, None]
    filled = jnp.any(picked, axis=1)
    source = jnp.sum(jnp.where(picked, jnp.arange(rows, dtype=jnp.int32)[None, :], 0), axis=1)
    out_labels = jnp.where(filled, cluster_ids[source], -1)
    local_unit = normalise_rows(embeddings)
    outgoing_unit = jnp.where(filled[:, None], local_unit[source], jnp.zeros((), jnp.bfloat16))
    unit, labels = (
        lax.all_to_all(outgoing_unit, "clus", split_axis=0, concat_axis=0, tiled=True),
        lax.all_to_all(out_labels, "clus", split_axis=0, concat_axis=0, tiled=True),
    )
    own_start = lax.axis_index("split") * slots
    floor_values = jnp.full((slots,), -1.0, jnp.float32)
    scores = masked_scores(
        unit,
        labels,
        lax.all_gather(unit, "split", axis=0, tiled=True),
        lax.all_gather(labels, "split", axis=0, tiled=True),
        own_start,
    )
    best = jnp.maximum(floor_values, jnp.max(scores, axis=1))
    returned_max = lax.all_to_all(best, "clus", split_axis=0, concat_axis=0, tiled=True)
    return returned_max[place]


def solution(mesh):
    in_specs = (P(("clus", "split"), None), P(("clus", "split")))
    out_specs = P(("clus", "split"))
    return jax.shard_map(
        on_device, mesh=mesh, in_specs=in_specs, out_specs=out_specs, check_vma=False
    )
```

profile of v0, /device:TPU:1, one launch (start us, length us, event | category | flops | bytes accessed | tf_op | source)
XLA Modules:
  0.0 294.8 jit_solution(16780526485380917887)
XLA Ops:
  6.5 0.0 copy-start.1
  6.5 0.0 all-gather.3.cloned.1.call-start
  6.5 0.8 and_select_fusion
  7.4 0.1 fusion.3
  7.4 0.2 reduce_window_sum.11
  7.6 0.2 select_reduce_fusion.1
  7.8 0.7 compare_select_fusion.1
  8.5 0.1 select_reduce_fusion
  8.6 0.1 fusion.2
  8.7 1.8 multiply_reduce_fusion
  10.6 0.0 copy-done.1
  10.6 0.2 multiply_convert_fusion
  10.8 0.1 broadcast_in_dim.57
  10.9 1.8 gather_fusion.1
  12.7 0.2 broadcast_select_fusion
  12.9 30.2 %all_to_all.24 = bf16[4,64,4096]{2,1,0:T(8,128)(2,1)} all-to-all(bf16[4,64,4096]{2,1,0:T(8,128)(2,1)S(1)} %broadcast_select_fusion), channel_id=1, replica_groups=mesh['clus'=4,'split'=32] {'clus'}, dimensions={0} | all-to-all | bytes 4194304 | tf_op jit(solution)/shard_map/all_to_all | solution.py:43
  43.1 0.0 copy-start
  43.1 0.0 copy-start.2
  43.1 0.0 all-gather.3.cloned.1.call-update
  43.1 0.6 copy-done
  43.8 1.9 gather_fusion
  45.6 0.7 select_n.52
  46.3 3.2 %all-to-all-start = ((s32[4,64,1]{1,2,0:T(1,128)}), s32[4,64,1]{1,2,0:T(1,128)S(1)}, u32[]{:S(2)}, u32[]{:S(2)}) async-start(s32[4,64,1]{1,2,0:T(1,128)} %bitcast.2), calls=%async_computation | async-start | bytes 4096 | tf_op jit(solution)/shard_map/all_to_all | solution.py:44
  49.6 4.1 %all-to-all-done = s32[4,64,1]{1,2,0:T(1,128)S(1)} async-done(((s32[4,64,1]{1,2,0:T(1,128)}), s32[4,64,1]{1,2,0:T(1,128)S(1)}, u32[]{:S(2)}, u32[]{:S(2)}) %all-to-all-start) | async-done | bytes 1056 | tf_op jit(solution)/shard_map/all_to_all | solution.py:44
  53.6 0.5 broadcast.98
  54.1 0.7 reduce.8
  54.8 0.1 eq.49
  54.9 0.1 reshape.103
  55.0 28.3 %all-gather = s32[32,1,256]{2,1,0:T(1,128)S(1)} all-gather(s32[1,1,256]{2,1,0:T(1,128)S(1)} %reshape.103), channel_id=1, replica_groups=mesh['clus'=4,'split'=32] {'split'}, dimensions={0}, use_global_device_ids=true | all-gather | bytes 33792 | tf_op jit(solution)/shard_map/all_gather | solution.py:52
  83.3 163.4 %all-gather.3.cloned.1.call-done = bf16[8192,4096]{1,0:T(8,128)(2,1)} async-done(((bf16[256,4096]{1,0:T(8,128)(2,1)}), bf16[8192,4096]{1,0:T(8,128)(2,1)}) %all-gather.3.cloned.1.call-update) | async-done | bytes 67108880 | tf_op jit(solution)/shard_map/all_gather | solution.py:51
  246.8 0.0 copy-done.2
  246.8 29.4 %fusion.1 = f32[256]{0:T(256)S(1)} fusion(bf16[256,4096]{1,0:T(8,128)(2,1)S(1)} %bitcast.14, bf16[8192,4096]{1,0:T(8,128)(2,1)} %all-gather.3.cloned.1.call-done, s32[256]{0:T(256)S(1)} %iota_add_fusion, pred[256]{0:T(512)(128)(4,1)S(1)} %broadcast_compare_fusion, s32[8192]{0:T(1024)S(1)} %bitcast.15, s32[256]{0:T(256)S(1)} %eq.49), kind=kOutput, calls=%fused_computation.9 | convolution fusion | flops 17192452096 | bytes 69242112 | tf_op jit(solution)/shard_map/dot_general | solution.py:8
  276.1 0.7 max_broadcast_in_dim.14
  276.8 4.0 %all-to-all-start.2 = ((f32[4,64,1]{1,2,0:T(1,128)}), f32[4,64,1]{1,2,0:T(1,128)S(1)}, u32[]{:S(2)}, u32[]{:S(2)}) async-start(f32[4,64,1]{1,2,0:T(1,128)} %bitcast.6), calls=%async_computation.2 | async-start | bytes 4096 | tf_op jit(solution)/shard_map/all_to_all | solution.py:56
  280.8 4.1 %all-to-all-done.2 = f32[4,64,1]{1,2,0:T(1,128)S(1)} async-done(((f32[4,64,1]{1,2,0:T(1,128)}), f32[4,64,1]{1,2,0:T(1,128)S(1)}, u32[]{:S(2)}, u32[]{:S(2)}) %all-to-all-start.2) | async-done | bytes 1056 | tf_op jit(solution)/shard_map/all_to_all | solution.py:56
  284.9 0.5 broadcast.99
  285.4 0.7 reduce.9
  286.1 0.1 all_to_all.20
  286.1 1.8 gather_fusion.2
  (8 shorter events, 0.0 us)
Async XLA Ops:
  6.5 4.0 %copy-start.1 = (f32[128,4096]{1,0:T(8,128)S(1)}, f32[128,4096]{1,0:T(8,128)}, u32[]{:S(2)}) copy-start(f32[128,4096]{1,0:T(8,128)} %param.2) | copy-start | bytes 6291460
  6.5 240.2 %all-gather.3.cloned.1.call-start = ((), (), s32[]{:S(2)}) async-start(), calls=%async_computation.3 | async-start | bytes 69206016 | tf_op jit(solution)/shard_map/all_gather | solution.py:51
  43.1 0.7 copy-start
  43.1 203.6 %copy-start.2 = (bf16[4,64,4096]{2,1,0:T(8,128)(2,1)S(1)}, bf16[4,64,4096]{2,1,0:T(8,128)(2,1)}, u32[]{:S(2)}) copy-start(bf16[4,64,4096]{2,1,0:T(8,128)(2,1)} %all_to_all.24) | copy-start | bytes 6291460
  46.3 7.3 %all-to-all-start = ((s32[4,64,1]{1,2,0:T(1,128)}), s32[4,64,1]{1,2,0:T(1,128)S(1)}, u32[]{:S(2)}, u32[]{:S(2)}) async-start(s32[4,64,1]{1,2,0:T(1,128)} %bitcast.2), calls=%async_computation | async-start | bytes 4096 | tf_op jit(solution)/shard_map/all_to_all | solution.py:44
  276.8 8.1 %all-to-all-start.2 = ((f32[4,64,1]{1,2,0:T(1,128)}), f32[4,64,1]{1,2,0:T(1,128)S(1)}, u32[]{:S(2)}, u32[]{:S(2)}) async-start(f32[4,64,1]{1,2,0:T(1,128)} %bitcast.6), calls=%async_computation.2 | async-start | bytes 4096 | tf_op jit(solution)/shard_map/all_to_all | solution.py:56
Sparse Core Ops, SparseCore 0:
  43.3 203.4 all-gather.2
where the time goes:
time: 295 us
  waiting for transfers between devices  172 us (58%)
  blocking collectives  58.5 us (20%)
  matrix products  29.4 us (10%)
  between operations  13.5 us (5%)
  local copies, waits for them, and re-layouts  8.82 us (3%)
  starting transfers between devices  7.19 us (2%)
  other arithmetic  5.77 us (2%)
    all_gather x1, waiting for transfers between devices, on_device(): lax.all_gather(unit, 'split', axis=0, tiled=True)  163 us
    all_to_all x1, blocking collectives, on_device(): lax.all_to_all(outgoing_unit, 'clus', split_axis=0, concat_axis=0, tiled=...  30.2 us
    dot_general x1, matrix products, masked_scores(): lax.dot_general(left, right, (((1,), (1,)), ((), ())), preferred_element_...  29.4 us
    all_gather x1, blocking collectives, on_device(): lax.all_gather(labels, 'split', axis=0, tiled=True)  28.3 us
  transfers between devices with their start and end apart: 3, of which 3 were waited for; matrix products, arithmetic and copies ran while one was open for 1% of the time, Pallas kernels for 0%

commit v1 on v0

v1 whole, which is shorter than its diff:
```python
import functools

import jax
import jax.numpy as jnp
from jax import lax
from jax.experimental import pallas as pl
from jax.experimental.pallas import tpu as pltpu
from jax.sharding import Mesh, PartitionSpec as P

ROWS = 128
SLICES = 8
WIDTH = 512
LABEL_ROWS = 16
BINS = 16
BLOCK = 128
SLOTS = BLOCK - 1
CAPS = (704, 512, 320, 256)
STARTS = (0, 704, 1216, 1536)
SORTED = 1792
HALF = 64
CHUNK = 9 * HALF
PARTIAL = 4 * CHUNK
VMEM_LIMIT = 56 * 1024 * 1024
f32, bf16, i32 = jnp.float32, jnp.bfloat16, jnp.int32
WHOLE = pl.BlockSpec(memory_space=pltpu.VMEM)
SCALARS = pl.BlockSpec(memory_space=pltpu.SMEM)


def params():
    return pltpu.CompilerParams(vmem_limit_bytes=VMEM_LIMIT)


def iota(shape, dim):
    return lax.broadcasted_iota(i32, shape, dim)


def dot_last(a, b):
    return lax.dot_general(a, b, (((1,), (1,)), ((), ())), preferred_element_type=f32)


def dot(a, b):
    return lax.dot_general(a, b, (((1,), (0,)), ((), ())), preferred_element_type=f32)


def as_bf16(mask):
    return jnp.where(mask, 1.0, 0.0).astype(bf16)


def bin_of(labels):
    return ((labels >> 2) + 4 * (labels & 3)) & (BINS - 1)


def unit_kernel(x_ref, ids_ref, out_ref):
    x = x_ref[...]
    squares = jnp.sum(x * x, axis=1, keepdims=True)
    unit = (x * lax.rsqrt(squares + 1e-06)).astype(bf16)
    ids = jnp.concatenate([ids_ref[...].astype(f32), jnp.zeros((1, WIDTH - ROWS), f32)], axis=1)
    ids = jnp.broadcast_to(ids, (LABEL_ROWS, WIDTH)).astype(bf16)
    for j in range(SLICES):
        out_ref[j, :ROWS, :] = unit[:, j * WIDTH:(j + 1) * WIDTH]
        out_ref[j, ROWS:, :] = ids


def pack_kernel(x_ref, out_ref, code_ref):
    labels = jnp.max(x_ref[:, ROWS:, :ROWS].astype(f32), axis=1).astype(i32)
    bins = bin_of(labels)
    member = jnp.concatenate([jnp.where(bins == b, 1.0, 0.0) for b in range(BINS)], axis=0)
    member16 = member.astype(bf16)
    row, col = iota((BLOCK, BLOCK), 0), iota((BLOCK, BLOCK), 1)
    along = dot(member16, as_bf16(row < col))
    earlier = dot(as_bf16(((row >> 3) == (col >> 3)) & (col < row)), member16)
    ranks = member * (along + jnp.sum(earlier, axis=1, keepdims=True))
    rank = sum(ranks[8 * b:8 * b + 8] for b in range(BINS)).astype(i32)
    code = jnp.where(rank < SLOTS, bins * BLOCK + rank, -1)
    code_ref[...] = code
    docs = SLICES * ROWS
    flat = lambda v: jnp.concatenate([v[i:i + 1] for i in range(SLICES)], axis=1)
    code_row, label_row = flat(code), flat(labels)
    x = x_ref[:, :ROWS, :].reshape(docs, WIDTH)
    counts = dot_last(jnp.ones((8, docs), bf16), as_bf16(iota((BLOCK, docs), 0) == label_row))[:1]
    high = jnp.floor(counts * (1.0 / 32.0))
    low = counts - 32.0 * high
    plus_one = jnp.broadcast_to((label_row + 1).astype(f32), (8, docs)).astype(bf16)
    is_last = iota((BLOCK, WIDTH), 0) == SLOTS
    group = 4
    for start in range(0, BINS, group):
        onehot = as_bf16(iota((group * BLOCK, docs), 0) + start * BLOCK == code_row)
        packed = dot(onehot, x)
        names = dot_last(plus_one, onehot)[:1]
        for b in range(group):
            extra = jnp.concatenate(
                [names[:, b * BLOCK:(b + 1) * BLOCK], low, high, jnp.zeros((1, BLOCK), f32)], axis=1
            )
            out_ref[start + b] = jnp.where(is_last, extra, packed[b * BLOCK:(b + 1) * BLOCK]).astype(bf16)


def sort_kernel(where_ref, x_ref, out_ref, pos_ref, meta_ref):
    mine = where_ref[0] * 4 + where_ref[1]
    tail = x_ref[:, BLOCK - 16:, :3 * BLOCK].astype(f32)
    tail = jnp.max(jnp.where(iota(tail.shape, 1) == 15, tail, 0.0), axis=1)
    labels = tail[:, :BLOCK].astype(i32) - 1
    low, high = tail[:, BLOCK:2 * BLOCK].astype(bf16), tail[:, 2 * BLOCK:].astype(bf16)
    row, col = iota((BLOCK, BLOCK), 0), iota((BLOCK, BLOCK), 1)
    in_bin = (bin_of(row) == col) & (row < 4 * BINS)
    sizes, total = [], 0.0
    for r in range(4):
        pick = as_bf16(in_bin & ((row & 3) == r))
        counts = dot(low, pick) + 32.0 * dot(high, pick)
        total = total + counts
        sizes.append(jnp.sum(counts, axis=0, keepdims=True))
    a, b = jnp.maximum(sizes[0], sizes[1]), jnp.minimum(sizes[0], sizes[1])
    c, d = jnp.maximum(sizes[2], sizes[3]), jnp.minimum(sizes[2], sizes[3])
    first, e = jnp.maximum(a, c), jnp.minimum(a, c)
    g, fourth = jnp.maximum(b, d), jnp.minimum(b, d)
    ordered = (first, jnp.maximum(e, g), jnp.minimum(e, g), fourth)
    over = jnp.max(jnp.where(total > SLOTS, 1.0, 0.0), axis=0, keepdims=True)
    for size, cap in zip(ordered, CAPS):
        over = jnp.maximum(over, jnp.where(size > cap, 1.0, 0.0))
    over = jnp.max(over, axis=1, keepdims=True)
    here = iota((1, BLOCK), 1) == mine
    own = lambda v: jnp.sum(jnp.where(here, v, 0.0), axis=1, keepdims=True)
    wide = lambda v: jnp.broadcast_to(v, (1, BLOCK))
    meta_ref[...] = jnp.concatenate([wide(own(v)) for v in ordered] + [wide(over)] * 4, axis=0)

    n = [own(v) for v in sizes]
    valid = (labels >= 0) & (iota(labels.shape, 1) < SLOTS)
    upper = as_bf16(row < col)
    lower = as_bf16(iota((BINS, BINS), 1) < iota((BINS, BINS), 0))
    pos = jnp.full(labels.shape, -1.0, f32)
    for r in range(4):
        place = sum(
            jnp.where((n[q] > n[r]) | ((n[q] == n[r]) & (q < r)), 1.0, 0.0) for q in range(4) if q != r
        )
        start = jnp.where(
            place < 0.5, float(STARTS[0]),
            jnp.where(place < 1.5, float(STARTS[1]), jnp.where(place < 2.5, float(STARTS[2]), float(STARTS[3]))),
        )
        member = valid & ((labels & 3) == r)
        member16 = as_bf16(member)
        rank = dot(member16, upper) + jnp.sum(dot(lower, member16), axis=1, keepdims=True)
        pos = jnp.where(member, start + rank, pos)
    pos = pos.astype(i32)
    pos_ref[...] = pos
    x = x_ref[...].reshape(BINS * BLOCK, WIDTH)
    pos_row = jnp.concatenate([pos[i:i + 1] for i in range(BINS)], axis=1)
    step = SORTED // 4
    for i in range(4):
        onehot = as_bf16(iota((step, BINS * BLOCK), 0) + i * step == pos_row)
        out_ref[i * step:(i + 1) * step, :] = dot(onehot, x).astype(bf16)


def column_blocks(core):
    for q in ((0,) if core == 0 else (1, 2, 3)):
        for first in range(0, CAPS[q], BLOCK):
            yield q, first


def gram_kernel(where_ref, a_ref, b_ref, meta_ref, out0, out1, out2, out3, part_ref):
    y, c = where_ref[2], where_ref[3]
    for core in range(2):
        @pl.when(c == core)
        def _():
            at = 0
            for q, first in column_blocks(core):
                rows = CAPS[q] - first
                left = pl.ds(STARTS[q] + first, rows)
                right = pl.ds(STARTS[q] + first, BLOCK)
                score = dot_last(a_ref[left, :], a_ref[right, :]) + dot_last(b_ref[left, :], b_ref[right, :])
                size = meta_ref[q:q + 1, :].astype(i32)
                i, j = iota(score.shape, 0), iota(score.shape, 1)
                keep = (i + first < size) & (j + first < size) & (i != j)
                score = jnp.where(keep, score, -4.0)
                done = 0
                while done < rows:
                    chunk, offset = divmod(at + done, CHUNK)
                    take = min(rows - done, CHUNK - offset)
                    part_ref[chunk, offset:offset + take, :] = score[done:done + take]
                    done += take
                at += rows
            while at < PARTIAL:
                chunk, offset = divmod(at, CHUNK)
                part_ref[chunk, offset:offset + HALF, :] = jnp.full((HALF, BLOCK), -4.0, f32)
                at += HALF
    for shift, out in enumerate((out0, out1, out2, out3)):
        out[...] = part_ref[lax.rem(y + shift, 4)]


def tables():
    rows, cols = [], []
    for core in range(2):
        have = []
        for q, first in column_blocks(core):
            for r in range(first, CAPS[q], HALF):
                have.append((STARTS[q] + r, STARTS[q] + first))
        have += [(SORTED, SORTED)] * (36 - len(have))
        rows += [h[0] for h in have]
        cols += [h[1] for h in have]
    return rows, cols


def max_kernel(where_ref, rows_ref, cols_ref, p0, p1, p2, p3, pos_ref, out_ref, best_ref):
    y, c = where_ref[2], where_ref[3]
    done = p0[...] + p1[...] + p2[...] + p3[...]
    best_ref[...] = jnp.full(best_ref.shape, -1.0, f32)
    eye = iota((BLOCK, BLOCK), 0) == iota((BLOCK, BLOCK), 1)
    for t in range(CHUNK // HALF):
        block = done[t * HALF:(t + 1) * HALF]
        index = c * 36 + y * 9 + t
        at = pl.ds(pl.multiple_of(rows_ref[index], HALF), HALF)
        best_ref[at, :] = jnp.maximum(best_ref[at, :], jnp.max(block, axis=1, keepdims=True))
        column = jnp.max(block, axis=0, keepdims=True)
        column = jnp.max(jnp.where(eye, column, -1.0), axis=1, keepdims=True)
        at = pl.ds(pl.multiple_of(cols_ref[index], HALF), BLOCK)
        best_ref[at, :] = jnp.maximum(best_ref[at, :], column)
    best = best_ref[:SORTED, :]
    index = iota((SORTED, BLOCK), 0)
    for s in range(BINS):
        out_ref[s:s + 1, :] = jnp.max(jnp.where(index == pos_ref[s:s + 1, :], best, -1.0), axis=0, keepdims=True)


def pick_kernel(where_ref, v_ref, code_ref, out_ref):
    line = where_ref[2] * 2 + where_ref[3]
    values = jnp.max(v_ref[...].reshape(BINS, 8, BLOCK), axis=1)
    eye = iota((BLOCK, BLOCK), 0) == iota((BLOCK, BLOCK), 1)
    code = jnp.max(jnp.where(iota((8, ROWS), 0) == line, code_ref[...], -1), axis=0, keepdims=True)
    code = jnp.max(jnp.where(eye, code.astype(f32), -1.0), axis=1, keepdims=True).astype(i32)
    slot = iota((ROWS, BLOCK), 1)
    best = jnp.full((ROWS, BLOCK), -1.0, f32)
    for b in range(BINS):
        best = jnp.maximum(best, jnp.where(slot + b * BLOCK == code, values[b:b + 1], -1.0))
    best = jnp.max(best, axis=1, keepdims=True)
    out_ref[...] = jnp.max(jnp.where(eye, best, -1.0), axis=0, keepdims=True)


def masked_scores(left, left_ids, right, right_ids, left_start):
    scores = dot_last(left, right)
    left_at = left_start + jnp.arange(left.shape[0], dtype=i32)
    right_at = jnp.arange(right.shape[0], dtype=i32)
    mask = (
        (left_ids[:, None] == right_ids[None, :])
        & (left_ids[:, None] >= 0)
        & (left_at[:, None] != right_at[None, :])
    )
    return jnp.where(mask, scores, -1.0)


def gather_groups(embeddings, cluster_ids):
    split = ("z", "y", "c")
    rows = embeddings.shape[0]
    groups = lax.axis_size("x")
    cap = 2 * rows // groups
    slots = groups * cap
    owner_of = cluster_ids % groups
    onehot = (owner_of[:, None] == jnp.arange(groups, dtype=i32)[None, :]).astype(i32)
    before = jnp.cumsum(onehot, axis=0) - onehot
    rank = jnp.sum(before * onehot, axis=1)
    place = owner_of * cap + rank
    picked = place[None, :] == jnp.arange(slots, dtype=i32)[:, None]
    filled = jnp.any(picked, axis=1)
    source = jnp.sum(jnp.where(picked, jnp.arange(rows, dtype=i32)[None, :], 0), axis=1)
    out_labels = jnp.where(filled, cluster_ids[source], -1)
    squares = jnp.sum(embeddings * embeddings, axis=1, keepdims=True)
    local_unit = (embeddings * lax.rsqrt(squares + 1e-06)).astype(bf16)
    outgoing_unit = jnp.where(filled[:, None], local_unit[source], jnp.zeros((), bf16))
    unit = lax.all_to_all(outgoing_unit, "x", split_axis=0, concat_axis=0, tiled=True)
    labels = lax.all_to_all(out_labels, "x", split_axis=0, concat_axis=0, tiled=True)
    scores = masked_scores(
        unit,
        labels,
        lax.all_gather(unit, split, axis=0, tiled=True),
        lax.all_gather(labels, split, axis=0, tiled=True),
        lax.axis_index(split) * slots,
    )
    best = jnp.maximum(-1.0, jnp.max(scores, axis=1))
    returned = lax.all_to_all(best, "x", split_axis=0, concat_axis=0, tiled=True)
    return returned[place]


def on_device(embeddings, cluster_ids):
    where = jnp.stack([lax.axis_index(a) for a in ("x", "z", "y", "c")]).astype(i32)
    shape = jax.ShapeDtypeStruct
    cut = pl.pallas_call(
        unit_kernel,
        out_shape=shape((SLICES, ROWS + LABEL_ROWS, WIDTH), bf16),
        in_specs=[WHOLE, WHOLE], out_specs=WHOLE, compiler_params=params(), name="unit",
    )(embeddings, cluster_ids.reshape(1, ROWS))
    cut = lax.all_to_all(cut, ("y", "c"), 0, 0, tiled=True)
    packed, code = pl.pallas_call(
        pack_kernel,
        out_shape=(shape((BINS, BLOCK, WIDTH), bf16), shape((SLICES, ROWS), i32)),
        in_specs=[WHOLE], out_specs=(WHOLE, WHOLE), compiler_params=params(), name="pack",
    )(cut)
    packed = lax.all_to_all(packed, ("x", "z"), 0, 0, tiled=True)
    ordered, pos, meta = pl.pallas_call(
        sort_kernel,
        out_shape=(shape((SORTED, WIDTH), bf16), shape((BINS, BLOCK), i32), shape((8, BLOCK), f32)),
        in_specs=[SCALARS, WHOLE], out_specs=(WHOLE, WHOLE, WHOLE), compiler_params=params(), name="sort",
    )(where, packed)

    def within_bins(embeddings, cluster_ids):
        other = lax.ppermute(ordered, "c", [(0, 1), (1, 0)])
        partial = pl.pallas_call(
            gram_kernel,
            out_shape=[shape((CHUNK, BLOCK), f32)] * 4,
            in_specs=[SCALARS, WHOLE, WHOLE, WHOLE], out_specs=[WHOLE] * 4,
            scratch_shapes=[pltpu.VMEM((4, CHUNK, BLOCK), f32)],
            compiler_params=params(), name="gram",
        )(where, ordered, other, meta)
        arrived = [partial[0]] + [
            lax.ppermute(partial[s], "y", [(i, (i + s) % 4) for i in range(4)]) for s in (1, 2, 3)
        ]
        rows, cols = tables()
        best = pl.pallas_call(
            max_kernel,
            out_shape=shape((BINS, BLOCK), f32),
            in_specs=[SCALARS] * 3 + [WHOLE] * 5, out_specs=WHOLE,
            scratch_shapes=[pltpu.VMEM((SORTED + BLOCK, 1), f32)],
            compiler_params=params(), name="maxima",
        )(where, jnp.asarray(rows, i32), jnp.asarray(cols, i32), *arrived, pos)
        sent = jnp.broadcast_to(best[:, None, :], (BINS, 8, BLOCK)).reshape(BINS * 8, 1, BLOCK)
        back = lax.all_to_all(sent, ("x", "z", "y", "c"), 0, 0, tiled=True)
        return pl.pallas_call(
            pick_kernel,
            out_shape=shape((1, ROWS), f32),
            in_specs=[SCALARS, WHOLE, WHOLE], out_specs=WHOLE, compiler_params=params(), name="pick",
        )(where, back.reshape(BINS * 8, BLOCK), code).reshape(ROWS)

    return lax.cond(meta[4, 0] < 0.5, within_bins, gather_groups, embeddings, cluster_ids)


def solution(mesh):
    axes = ("x", "z", "y", "c")
    grid = Mesh(mesh.devices.reshape(4, 4, 4, 2), axes)
    return jax.shard_map(
        on_device, mesh=grid, in_specs=(P(axes, None), P(axes)), out_specs=P(axes), check_vma=False
    )
```

time: 295 us -> 142 us (0.48)
  waiting for transfers between devices: 172 us -> 43.6 us
  matrix products: 29.4 us -> 0 us
  Pallas kernels: 0 us -> 26.1 us
  blocking collectives: 58.5 us -> 38.7 us
  starting transfers between devices: 7.19 us -> 15.1 us
  other arithmetic: 5.77 us -> 0.08 us
  local copies, waits for them, and re-layouts: 8.82 us -> 3.7 us
    all_gather x1 -> x0, waiting for transfers between devices: 163 us -> none  [on_device(): lax.all_gather(unit, 'split', axis=0, tiled=True)]
    dot_general x1 -> x0, matrix products: 29.4 us -> none  [masked_scores(): lax.dot_general(left, right, (((1,), (1,)), ((), ())), preferred_element_...]
    all_gather x1 -> x0, blocking collectives: 28.3 us -> none  [on_device(): lax.all_gather(labels, 'split', axis=0, tiled=True)]
    pallas_call x0 -> x6, Pallas kernels: none -> 26.1 us  [the longest x1 7.1 us: on_device(): pl.pallas_call(sort_kernel, out_shape=(shape((SORTED, WIDTH), bf16), shap...]
    all_to_all x2 -> x1, waiting for transfers between devices: 8.16 us -> 26.4 us  [on_device(): packed = lax.all_to_all(packed, ('x', 'z'), 0, 0, tiled=True)]
    ppermute x0 -> x4, waiting for transfers between devices: none -> 17.2 us  [the longest x3 13.6 us: within_bins(): lax.ppermute(partial[s], 'y', [(i, (i + s) % 4) for i in range(4)])]
    all_to_all x1 -> x2, blocking collectives: 30.2 us -> 38.7 us  [the longest x1 22.7 us: on_device(): cut = lax.all_to_all(cut, ('y', 'c'), 0, 0, tiled=True)]
    ppermute x0 -> x4, starting transfers between devices: none -> 7.43 us  [the longest x1 4.72 us: within_bins(): other = lax.ppermute(ordered, 'c', [(0, 1), (1, 0)])]
  transfers between devices with their start and end apart: 3 -> 5, of which waited for: 3 -> 5; matrix products, arithmetic and copies ran while one was open for 1% -> 0% of each run, Pallas kernels for 0% -> 0%
where the time goes in v1:
time: 142 us
  waiting for transfers between devices  43.6 us (31%)
  blocking collectives  38.7 us (27%)
  Pallas kernels  26.1 us (18%)
  starting transfers between devices  15.1 us (11%)
  between operations  14.1 us (10%)
  local copies, waits for them, and re-layouts  3.7 us (3%)
    all_to_all x1, waiting for transfers between devices, on_device(): packed = lax.all_to_all(packed, ('x', 'z'), 0, 0, tiled=True)  26.4 us
    all_to_all x1, blocking collectives, on_device(): cut = lax.all_to_all(cut, ('y', 'c'), 0, 0, tiled=True)  22.7 us
    all_to_all x1, blocking collectives, within_bins(): back = lax.all_to_all(sent, ('x', 'z', 'y', 'c'), 0, 0, tiled=True)  16 us
    ppermute x3, waiting for transfers between devices, within_bins(): lax.ppermute(partial[s], 'y', [(i, (i + s) % 4) for i in range(4)])  13.6 us
    all_to_all x1, starting transfers between devices, on_device(): packed = lax.all_to_all(packed, ('x', 'z'), 0, 0, tiled=True)  7.65 us
    pallas_call x1, Pallas kernels, on_device(): pl.pallas_call(sort_kernel, out_shape=(shape((SORTED, WIDTH), bf16), shap...  7.1 us
    pallas_call x1, Pallas kernels, on_device(): pl.pallas_call(pack_kernel, out_shape=(shape((BINS, BLOCK, WIDTH), bf16),...  6.19 us
    ppermute x1, starting transfers between devices, within_bins(): other = lax.ppermute(ordered, 'c', [(0, 1), (1, 0)])  4.72 us
  transfers between devices with their start and end apart: 5, of which 5 were waited for; matrix products, arithmetic and copies ran while one was open for 0% of the time, Pallas kernels for 0%

profile of v1, /device:TPU:1, one launch (start us, length us, event | category | flops | bytes accessed | tf_op | source)
XLA Modules:
  0.0 141.6 jit_solution(7795352643623667096)
XLA Ops:
  6.5 3.0 %unit.1 = bf16[8,144,512]{2,1,0:T(8,128)(2,1)} custom-call(f32[128,4096]{1,0:T(8,128)} %x_ref.1, s32[1,128]{1,0:T(1,128)} %bitcast.21), custom_call_target="tpu_custom_call" | custom-call | tf_op jit(solution)/shard_map/unit/pallas_call | solution.py:282
  9.5 22.7 %all_to_all.35.x_ref = bf16[8,144,512]{2,1,0:T(8,128)(2,1)} all-to-all(bf16[8,144,512]{2,1,0:T(8,128)(2,1)} %unit.1), channel_id=1, replica_groups=mesh['x'=4,'z'=4,'y'=4,'c'=2] {'y','c'}, dimensions={0} | all-to-all | bytes 2359296 | tf_op jit(solution)/shard_map/all_to_all | solution.py:287
  32.2 6.2 %pack.1 = (bf16[16,128,512]{2,1,0:T(8,128)(2,1)}, s32[8,128]{1,0:T(8,128)S(1)}) custom-call(bf16[8,144,512]{2,1,0:T(8,128)(2,1)} %all_to_all.35.x_ref), custom_call_target="tpu_custom_call" | custom-call | tf_op jit(solution)/shard_map/pack/pallas_call | solution.py:288
  38.4 7.6 %all-to-all-start.5 = ((bf16[16,128,512]{2,1,0:T(8,128)(2,1)}), bf16[16,128,512]{2,1,0:T(8,128)(2,1)}, u32[]{:S(2)}, u32[]{:S(2)}) async-start(bf16[16,128,512]{2,1,0:T(8,128)(2,1)} %get-tuple-element.44), calls=%async_computation.5 | async-start | bytes 4194304 | tf_op jit(solution)/shard_map/all_to_all | solution.py:293
  46.1 0.0 copy-start
  46.1 0.0 copy-start.1
  46.1 0.1 pad_add_fusion.where_ref
  46.2 26.4 %all-to-all-done.5.x_ref = bf16[16,128,512]{2,1,0:T(8,128)(2,1)} async-done(((bf16[16,128,512]{2,1,0:T(8,128)(2,1)}), bf16[16,128,512]{2,1,0:T(8,128)(2,1)}, u32[]{:S(2)}, u32[]{:S(2)}) %all-to-all-start.5) | async-done | bytes 2097184 | tf_op jit(solution)/shard_map/all_to_all | solution.py:293
  72.6 7.1 %sort.1 = (bf16[1792,512]{1,0:T(8,128)(2,1)}, s32[16,128]{1,0:T(8,128)S(1)}, f32[8,128]{1,0:T(8,128)S(1)}) custom-call(s32[4]{0:T(128)S(1)} %pad_add_fusion.where_ref, bf16[16,128,512]{2,1,0:T(8,128)(2,1)} %all-to-all-done.5.x_ref), custom_call_target="tpu_custom_call" | custom-call | tf_op jit(solution)/shard_map/sort/pallas_call | solution.py:294
  79.7 0.5 slice.3
  80.9 0.0 copy-done
  80.9 0.0 copy-done.1
  80.9 53.4 %conditional.1 = (f32[128]{0:T(128)S(1)}) conditional(s32[]{:T(128)} %bitcast.15, (s32[128]{0:T(128)S(1)}, f32[128,4096]{1,0:T(8,128)S(1)}) %tuple.24, (bf16[1792,512]{1,0:T(8,128)(2,1)}, s32[4]{0:T(128)S(1)}, f32[8,128]{1,0:T(8,128)S(1)}, (), (), /*index=5*/s32[16,128]{1,0:T(8,128)S(1)}, s32[8,128]{1,0:T(8,128)S(1)}) %tuple.12), branch_computations={%region_0.7_spmd, %region_7.8_spmd} | conditional | flops 17195835392 | bytes 303175232 | solution.py:328
  81.1 4.7 %collective-permute-start = (bf16[1792,512]{1,0:T(8,128)(2,1)}, bf16[1792,512]{1,0:T(8,128)(2,1)S(1)}, u32[]{:S(2)}, u32[]{:S(2)}) collective-permute-start(bf16[1792,512]{1,0:T(8,128)(2,1)} %get-tuple-element.31.a_ref), channel_id=1, source_target_pairs={{0,1},{1,0},{2,3},{3,2},{4,5},{5,4},{6,7},{7,6},{8,9},{9,8},{10,11... | collective-permute-start | bytes 5505032 | tf_op jit(solution)/shard_map/cond/branch_1_fun/ppermute | solution.py:301
  85.9 3.6 %collective-permute-done.b_ref = bf16[1792,512]{1,0:T(8,128)(2,1)S(1)} collective-permute-done((bf16[1792,512]{1,0:T(8,128)(2,1)}, bf16[1792,512]{1,0:T(8,128)(2,1)S(1)}, u32[]{:S(2)}, u32[]{:S(2)}) %collective-permute-start) | collective-permute-done | bytes 1835040 | tf_op jit(solution)/shard_map/cond/branch_1_fun/ppermute | solution.py:301
  89.5 0.0 copy-start.3
  89.5 1.3 copy-done.3
  90.7 4.6 %gram.1 = (f32[576,128]{1,0:T(8,128)}, f32[576,128]{1,0:T(8,128)}, f32[576,128]{1,0:T(8,128)}, f32[576,128]{1,0:T(8,128)}) custom-call(s32[4]{0:T(128)S(1)} %get-tuple-element.28.where_ref, bf16[1792,512]{1,0:T(8,128)(2,1)} %get-tuple-element.31.a_ref, bf16[1792,512]{1,0:T(8,128)(2,1)} %copy-done.3, f32[8,128]{1,0:T(8,128)S(1)} %get-tuple-element.32.meta_ref), custom_call_target="tpu_custom_call" | custom-call | tf_op jit(solution)/shard_map/cond/branch_1_fun/gram/pallas_call | solution.py:302
  95.3 0.3 collective-permute-start.1
  95.6 1.8 %collective-permute-start.2 = (f32[576,128]{1,0:T(8,128)}, f32[576,128]{1,0:T(8,128)S(1)}, u32[]{:S(2)}, u32[]{:S(2)}) collective-permute-start(f32[576,128]{1,0:T(8,128)} %get-tuple-element.35), channel_id=1, source_target_pairs={{0,4},{2,6},{4,0},{6,2},{1,5},{3,7},{5,1},{7,3},{8,12},{10,14},{12... | collective-permute-start | bytes 884744 | tf_op jit(solution)/shard_map/cond/branch_1_fun/ppermute | solution.py:310
  97.4 0.6 collective-permute-start.3
  98.0 7.5 %collective-permute-done.1.p1 = f32[576,128]{1,0:T(8,128)S(1)} collective-permute-done((f32[576,128]{1,0:T(8,128)}, f32[576,128]{1,0:T(8,128)S(1)}, u32[]{:S(2)}, u32[]{:S(2)}) %collective-permute-start.1) | collective-permute-done | bytes 294944 | tf_op jit(solution)/shard_map/cond/branch_1_fun/ppermute | solution.py:310
  105.5 0.0 copy-start.4
  105.5 5.1 %collective-permute-done.2.p2 = f32[576,128]{1,0:T(8,128)S(1)} collective-permute-done((f32[576,128]{1,0:T(8,128)}, f32[576,128]{1,0:T(8,128)S(1)}, u32[]{:S(2)}, u32[]{:S(2)}) %collective-permute-start.2) | collective-permute-done | bytes 294944 | tf_op jit(solution)/shard_map/cond/branch_1_fun/ppermute | solution.py:310
  110.7 0.0 copy-start.5
  110.7 0.9 collective-permute-done.3.p3
  111.6 0.0 copy-start.6
  111.6 0.0 copy-done.4
  111.6 0.0 copy-done.5
  111.6 0.7 copy-done.6
  112.3 4.1 %maxima.1 = f32[16,128]{1,0:T(8,128)} custom-call(s32[4]{0:T(128)S(1)} %get-tuple-element.28.where_ref, s32[72]{0:T(128)} %constant.82.clone.1.rows_ref, s32[72]{0:T(128)} %constant.83.clone.1.cols_ref, f32[576,128]{1,0:T(8,128)} %get-tuple-element.33.p0, f32[576,128]{1,0:T(8,128)} %copy-done.4, f32[576,128]{1,0:T(8,128)} %copy-done.5, ...), custom_call_target="tpu_custom_call" | custom-call | tf_op jit(solution)/shard_map/cond/branch_1_fun/maxima/pallas_call | solution.py:313
  116.4 0.7 broadcast_in_dim.52
  117.1 16.0 %all_to_all.34 = f32[128,1,128]{2,1,0:T(1,128)} all-to-all(f32[128,1,128]{2,1,0:T(1,128)S(1)} %bitcast.25), channel_id=1, replica_groups=mesh['x'=4,'z'=4,'y'=4,'c'=2] {'x','z','y','c'}, dimensions={0} | all-to-all | bytes 131072 | tf_op jit(solution)/shard_map/cond/branch_1_fun/all_to_all | solution.py:321
  133.1 1.2 pick.1
  134.3 0.0 copy-start.7
  134.3 0.5 copy-done.7
Async XLA Ops:
  38.4 34.2 %all-to-all-start.5 = ((bf16[16,128,512]{2,1,0:T(8,128)(2,1)}), bf16[16,128,512]{2,1,0:T(8,128)(2,1)}, u32[]{:S(2)}, u32[]{:S(2)}) async-start(bf16[16,128,512]{2,1,0:T(8,128)(2,1)} %get-tuple-element.44), calls=%async_computation.5 | async-start | bytes 4194304 | tf_op jit(solution)/shard_map/all_to_all | solution.py:293
  46.1 34.8 %copy-start = (s32[128]{0:T(128)S(1)}, s32[128]{0:T(128)}, u32[]{:S(2)}) copy-start(s32[128]{0:T(128)} %param.7) | copy-start | bytes 1540
  46.1 34.8 %copy-start.1 = (f32[128,4096]{1,0:T(8,128)S(1)}, f32[128,4096]{1,0:T(8,128)}, u32[]{:S(2)}) copy-start(f32[128,4096]{1,0:T(8,128)} %x_ref.1) | copy-start | bytes 6291460
  81.1 8.3 %collective-permute-start = (bf16[1792,512]{1,0:T(8,128)(2,1)}, bf16[1792,512]{1,0:T(8,128)(2,1)S(1)}, u32[]{:S(2)}, u32[]{:S(2)}) collective-permute-start(bf16[1792,512]{1,0:T(8,128)(2,1)} %get-tuple-element.31.a_ref), channel_id=1, source_target_pairs={{0,1},{1,0},{2,3},{3,2},{4,5},{5,4},{6,7},{7,6},{8,9},{9,8},{10,11... | collective-permute-start | bytes 5505032 | tf_op jit(solution)/shard_map/cond/branch_1_fun/ppermute | solution.py:301
  89.5 1.3 copy-start.3
  95.3 10.2 %collective-permute-start.1 = (f32[576,128]{1,0:T(8,128)}, f32[576,128]{1,0:T(8,128)S(1)}, u32[]{:S(2)}, u32[]{:S(2)}) collective-permute-start(f32[576,128]{1,0:T(8,128)} %get-tuple-element.34), channel_id=1, source_target_pairs={{0,2},{2,4},{4,6},{6,0},{1,3},{3,5},{5,7},{7,1},{8,10},{10,12},{12... | collective-permute-start | bytes 884744 | tf_op jit(solution)/shard_map/cond/branch_1_fun/ppermute | solution.py:310
  95.6 15.1 %collective-permute-start.2 = (f32[576,128]{1,0:T(8,128)}, f32[576,128]{1,0:T(8,128)S(1)}, u32[]{:S(2)}, u32[]{:S(2)}) collective-permute-start(f32[576,128]{1,0:T(8,128)} %get-tuple-element.35), channel_id=1, source_target_pairs={{0,4},{2,6},{4,0},{6,2},{1,5},{3,7},{5,1},{7,3},{8,12},{10,14},{12... | collective-permute-start | bytes 884744 | tf_op jit(solution)/shard_map/cond/branch_1_fun/ppermute | solution.py:310
  97.4 14.2 %collective-permute-start.3 = (f32[576,128]{1,0:T(8,128)}, f32[576,128]{1,0:T(8,128)S(1)}, u32[]{:S(2)}, u32[]{:S(2)}) collective-permute-start(f32[576,128]{1,0:T(8,128)} %get-tuple-element.36), channel_id=1, source_target_pairs={{0,6},{2,0},{4,2},{6,4},{1,7},{3,1},{5,3},{7,5},{8,14},{10,8},{12,... | collective-permute-start | bytes 884744 | tf_op jit(solution)/shard_map/cond/branch_1_fun/ppermute | solution.py:310
  105.5 6.1 %copy-start.4 = (f32[576,128]{1,0:T(8,128)}, f32[576,128]{1,0:T(8,128)S(1)}, u32[]{:S(2)}) copy-start(f32[576,128]{1,0:T(8,128)S(1)} %collective-permute-done.1.p1) | copy-start | bytes 884740 | tf_op jit(solution)/shard_map/cond
  110.7 0.9 copy-start.5
  111.6 0.7 copy-start.6
  134.3 0.5 copy-start.7

commit v2 on v1

--- a/solution.py
+++ b/solution.py
@@ -20,14 +20,13 @@
 HALF = 64
 CHUNK = 9 * HALF
 PARTIAL = 4 * CHUNK
-VMEM_LIMIT = 56 * 1024 * 1024
 f32, bf16, i32 = jnp.float32, jnp.bfloat16, jnp.int32
 WHOLE = pl.BlockSpec(memory_space=pltpu.VMEM)
 SCALARS = pl.BlockSpec(memory_space=pltpu.SMEM)
 
 
-def params():
-    return pltpu.CompilerParams(vmem_limit_bytes=VMEM_LIMIT)
+def params(mib):
+    return pltpu.CompilerParams(vmem_limit_bytes=mib * 1024 * 1024)
 
 
 def iota(shape, dim):
@@ -232,18 +231,6 @@
     out_ref[...] = jnp.max(jnp.where(eye, best, -1.0), axis=0, keepdims=True)
 
 
-def masked_scores(left, left_ids, right, right_ids, left_start):
-    scores = dot_last(left, right)
-    left_at = left_start + jnp.arange(left.shape[0], dtype=i32)
-    right_at = jnp.arange(right.shape[0], dtype=i32)
-    mask = (
-        (left_ids[:, None] == right_ids[None, :])
-        & (left_ids[:, None] >= 0)
-        & (left_at[:, None] != right_at[None, :])
-    )
-    return jnp.where(mask, scores, -1.0)
-
-
 def gather_groups(embeddings, cluster_ids):
     split = ("z", "y", "c")
     rows = embeddings.shape[0]
@@ -264,13 +251,25 @@
     outgoing_unit = jnp.where(filled[:, None], local_unit[source], jnp.zeros((), bf16))
     unit = lax.all_to_all(outgoing_unit, "x", split_axis=0, concat_axis=0, tiled=True)
     labels = lax.all_to_all(out_labels, "x", split_axis=0, concat_axis=0, tiled=True)
-    scores = masked_scores(
-        unit,
-        labels,
-        lax.all_gather(unit, split, axis=0, tiled=True),
-        lax.all_gather(labels, split, axis=0, tiled=True),
-        lax.axis_index(split) * slots,
+    members = lax.axis_size(split)
+
+    def everywhere(v):
+        copies = jnp.broadcast_to(v[None], (members,) + v.shape).reshape((members * slots,) + v.shape[1:])
+        return lax.all_to_all(copies, split, split_axis=0, concat_axis=0, tiled=True)
+
+    def add_slice(i, scores):
+        part = lax.dynamic_slice_in_dim(unit, i * WIDTH, WIDTH, 1)
+        return scores + dot_last(part, everywhere(part))
+
+    scores = lax.fori_loop(0, SLICES, add_slice, jnp.zeros((slots, members * slots), f32))
+    all_labels = everywhere(labels)
+    own = lax.axis_index(split) * slots + jnp.arange(slots, dtype=i32)
+    mask = (
+        (labels[:, None] == all_labels[None, :])
+        & (labels[:, None] >= 0)
+        & (own[:, None] != jnp.arange(members * slots, dtype=i32)[None, :])
     )
+    scores = jnp.where(mask, scores, -1.0)
     best = jnp.maximum(-1.0, jnp.max(scores, axis=1))
     returned = lax.all_to_all(best, "x", split_axis=0, concat_axis=0, tiled=True)
     return returned[place]
@@ -282,19 +281,19 @@
     cut = pl.pallas_call(
         unit_kernel,
         out_shape=shape((SLICES, ROWS + LABEL_ROWS, WIDTH), bf16),
-        in_specs=[WHOLE, WHOLE], out_specs=WHOLE, compiler_params=params(), name="unit",
+        in_specs=[WHOLE, WHOLE], out_specs=WHOLE, compiler_params=params(12), name="unit",
     )(embeddings, cluster_ids.reshape(1, ROWS))
     cut = lax.all_to_all(cut, ("y", "c"), 0, 0, tiled=True)
     packed, code = pl.pallas_call(
         pack_kernel,
         out_shape=(shape((BINS, BLOCK, WIDTH), bf16), shape((SLICES, ROWS), i32)),
-        in_specs=[WHOLE], out_specs=(WHOLE, WHOLE), compiler_params=params(), name="pack",
+        in_specs=[WHOLE], out_specs=(WHOLE, WHOLE), compiler_params=params(24), name="pack",
     )(cut)
     packed = lax.all_to_all(packed, ("x", "z"), 0, 0, tiled=True)
     ordered, pos, meta = pl.pallas_call(
         sort_kernel,
         out_shape=(shape((SORTED, WIDTH), bf16), shape((BINS, BLOCK), i32), shape((8, BLOCK), f32)),
-        in_specs=[SCALARS, WHOLE], out_specs=(WHOLE, WHOLE, WHOLE), compiler_params=params(), name="sort",
+        in_specs=[SCALARS, WHOLE], out_specs=(WHOLE, WHOLE, WHOLE), compiler_params=params(28), name="sort",
     )(where, packed)
 
     def within_bins(embeddings, cluster_ids):
@@ -304,7 +303,7 @@
             out_shape=[shape((CHUNK, BLOCK), f32)] * 4,
             in_specs=[SCALARS, WHOLE, WHOLE, WHOLE], out_specs=[WHOLE] * 4,
             scratch_shapes=[pltpu.VMEM((4, CHUNK, BLOCK), f32)],
-            compiler_params=params(), name="gram",
+            compiler_params=params(20), name="gram",
         )(where, ordered, other, meta)
         arrived = [partial[0]] + [
             lax.ppermute(partial[s], "y", [(i, (i + s) % 4) for i in range(4)]) for s in (1, 2, 3)
@@ -315,14 +314,14 @@
             out_shape=shape((BINS, BLOCK), f32),
             in_specs=[SCALARS] * 3 + [WHOLE] * 5, out_specs=WHOLE,
             scratch_shapes=[pltpu.VMEM((SORTED + BLOCK, 1), f32)],
-            compiler_params=params(), name="maxima",
+            compiler_params=params(12), name="maxima",
         )(where, jnp.asarray(rows, i32), jnp.asarray(cols, i32), *arrived, pos)
         sent = jnp.broadcast_to(best[:, None, :], (BINS, 8, BLOCK)).reshape(BINS * 8, 1, BLOCK)
         back = lax.all_to_all(sent, ("x", "z", "y", "c"), 0, 0, tiled=True)
         return pl.pallas_call(
             pick_kernel,
             out_shape=shape((1, ROWS), f32),
-            in_specs=[SCALARS, WHOLE, WHOLE], out_specs=WHOLE, compiler_params=params(), name="pick",
+            in_specs=[SCALARS, WHOLE, WHOLE], out_specs=WHOLE, compiler_params=params(8), name="pick",
         )(where, back.reshape(BINS * 8, BLOCK), code).reshape(ROWS)
 
     return lax.cond(meta[4, 0] < 0.5, within_bins, gather_groups, embeddings, cluster_ids)

time: 142 us -> 119 us (0.84)
  between operations: 14.1 us -> 0.7 us
  Pallas kernels: 26.1 us -> 18.3 us
    pallas_call x1, Pallas kernels: 6.19 us -> 3.61 us  [on_device(): pl.pallas_call(pack_kernel, out_shape=(shape((BINS, BLOCK, WIDTH), bf16),...]
    cond x8 -> x4, local copies, waits for them, and re-layouts: 1.97 us -> 0.01 us
    pallas_call x1, Pallas kernels: 4.58 us -> 3 us  [within_bins(): pl.pallas_call(gram_kernel, out_shape=[shape((CHUNK, BLOCK), f32)] * 4, i...]
where the time goes in v2:
time: 119 us
  waiting for transfers between devices  43.3 us (36%)
  blocking collectives  38.4 us (32%)
  Pallas kernels  18.3 us (15%)
  starting transfers between devices  15.2 us (13%)
  local copies, waits for them, and re-layouts  2.43 us (2%)
    all_to_all x1, waiting for transfers between devices, on_device(): packed = lax.all_to_all(packed, ('x', 'z'), 0, 0, tiled=True)  26.4 us
    all_to_all x1, blocking collectives, on_device(): cut = lax.all_to_all(cut, ('y', 'c'), 0, 0, tiled=True)  22.4 us
    all_to_all x1, blocking collectives, within_bins(): back = lax.all_to_all(sent, ('x', 'z', 'y', 'c'), 0, 0, tiled=True)  16 us
    ppermute x3, waiting for transfers between devices, within_bins(): lax.ppermute(partial[s], 'y', [(i, (i + s) % 4) for i in range(4)])  13.3 us
    all_to_all x1, starting transfers between devices, on_device(): packed = lax.all_to_all(packed, ('x', 'z'), 0, 0, tiled=True)  7.6 us
    pallas_call x1, Pallas kernels, on_device(): pl.pallas_call(sort_kernel, out_shape=(shape((SORTED, WIDTH), bf16), shap...  6.1 us
    ppermute x1, starting transfers between devices, within_bins(): other = lax.ppermute(ordered, 'c', [(0, 1), (1, 0)])  4.72 us
    ppermute x1, waiting for transfers between devices, within_bins(): other = lax.ppermute(ordered, 'c', [(0, 1), (1, 0)])  3.62 us
  transfers between devices with their start and end apart: 5, of which 5 were waited for; matrix products, arithmetic and copies ran while one was open for 0% of the time, Pallas kernels for 0%

profile of v2, /device:TPU:1, one launch (start us, length us, event | category | flops | bytes accessed | tf_op | source)
XLA Modules:
  0.0 118.7 jit_solution(16778953978303558398)
XLA Ops:
  0.0 1.9 %unit.1 = bf16[8,144,512]{2,1,0:T(8,128)(2,1)S(1)} custom-call(f32[128,4096]{1,0:T(8,128)} %x_ref.1, s32[1,128]{1,0:T(1,128)} %bitcast.28), custom_call_target="tpu_custom_call" | custom-call | tf_op jit(solution)/shard_map/unit/pallas_call | solution.py:281
  1.9 22.4 %all_to_all.56.x_ref = bf16[8,144,512]{2,1,0:T(8,128)(2,1)S(1)} all-to-all(bf16[8,144,512]{2,1,0:T(8,128)(2,1)S(1)} %unit.1), channel_id=1, replica_groups=mesh['x'=4,'z'=4,'y'=4,'c'=2] {'y','c'}, dimensions={0} | all-to-all | bytes 2359296 | tf_op jit(solution)/shard_map/all_to_all | solution.py:286
  24.4 3.6 %pack.1 = (bf16[16,128,512]{2,1,0:T(8,128)(2,1)S(1)}, s32[8,128]{1,0:T(8,128)S(1)}) custom-call(bf16[8,144,512]{2,1,0:T(8,128)(2,1)S(1)} %all_to_all.56.x_ref), custom_call_target="tpu_custom_call" | custom-call | tf_op jit(solution)/shard_map/pack/pallas_call | solution.py:287
  28.0 0.0 copy-start
  28.0 1.4 %copy-done = bf16[16,128,512]{2,1,0:T(8,128)(2,1)} copy-done((bf16[16,128,512]{2,1,0:T(8,128)(2,1)}, bf16[16,128,512]{2,1,0:T(8,128)(2,1)S(1)}, u32[]{:S(2)}) %copy-start) | copy-done | bytes 2097176
  29.4 7.6 %all-to-all-start.7 = ((bf16[16,128,512]{2,1,0:T(8,128)(2,1)}), bf16[16,128,512]{2,1,0:T(8,128)(2,1)S(1)}, u32[]{:S(2)}, u32[]{:S(2)}) async-start(bf16[16,128,512]{2,1,0:T(8,128)(2,1)} %copy-done), calls=%async_computation.7 | async-start | bytes 4194304 | tf_op jit(solution)/shard_map/all_to_all | solution.py:292
  37.0 0.0 copy-start.3
  37.0 0.1 pad_add_fusion.where_ref
  37.1 26.4 %all-to-all-done.7.x_ref = bf16[16,128,512]{2,1,0:T(8,128)(2,1)S(1)} async-done(((bf16[16,128,512]{2,1,0:T(8,128)(2,1)}), bf16[16,128,512]{2,1,0:T(8,128)(2,1)S(1)}, u32[]{:S(2)}, u32[]{:S(2)}) %all-to-all-start.7) | async-done | bytes 2097184 | tf_op jit(solution)/shard_map/all_to_all | solution.py:292
  63.4 6.1 %sort.1 = (bf16[1792,512]{1,0:T(8,128)(2,1)}, s32[16,128]{1,0:T(8,128)S(1)}, f32[8,128]{1,0:T(8,128)S(1)}) custom-call(s32[4]{0:T(128)S(1)} %pad_add_fusion.where_ref, bf16[16,128,512]{2,1,0:T(8,128)(2,1)S(1)} %all-to-all-done.7.x_ref), custom_call_target="tpu_custom_call" | custom-call | tf_op jit(solution)/shard_map/sort/pallas_call | solution.py:293
  69.5 0.5 slice.3
  70.7 0.0 copy-done.3
  70.7 47.4 %conditional.1 = (f32[128]{0:T(128)S(1)}) conditional(s32[]{:T(128)} %bitcast.15, (s32[128]{0:T(128)S(1)}, f32[128,4096]{1,0:T(8,128)}) %tuple.50, (bf16[1792,512]{1,0:T(8,128)(2,1)}, s32[4]{0:T(128)S(1)}, f32[8,128]{1,0:T(8,128)S(1)}, (), (), /*index=5*/s32[16,128]{1,0:T(8,128)S(1)}, s32[8,128]{1,0:T(8,128)S(1)}) %tuple.26), branch_computations={%region_0.9_spmd, %region_9.10_spmd} | conditional | flops 2167645440 | bytes 96702280 | solution.py:327
  71.0 0.0 copy-start.1
  71.0 0.0 copy-start.2
  71.0 4.7 %collective-permute-start = (bf16[1792,512]{1,0:T(8,128)(2,1)}, bf16[1792,512]{1,0:T(8,128)(2,1)S(1)}, u32[]{:S(2)}, u32[]{:S(2)}) collective-permute-start(bf16[1792,512]{1,0:T(8,128)(2,1)} %get-tuple-element.95.a_ref), channel_id=1, source_target_pairs={{0,1},{1,0},{2,3},{3,2},{4,5},{5,4},{6,7},{7,6},{8,9},{9,8},{10,11... | collective-permute-start | bytes 5505032 | tf_op jit(solution)/shard_map/cond/branch_1_fun/ppermute | solution.py:300
  75.7 3.6 %collective-permute-done.b_ref = bf16[1792,512]{1,0:T(8,128)(2,1)S(1)} collective-permute-done((bf16[1792,512]{1,0:T(8,128)(2,1)}, bf16[1792,512]{1,0:T(8,128)(2,1)S(1)}, u32[]{:S(2)}, u32[]{:S(2)}) %collective-permute-start) | collective-permute-done | bytes 1835040 | tf_op jit(solution)/shard_map/cond/branch_1_fun/ppermute | solution.py:300
  79.3 3.0 %gram.1 = (f32[576,128]{1,0:T(8,128)S(1)}, f32[576,128]{1,0:T(8,128)S(1)}, f32[576,128]{1,0:T(8,128)S(1)}, f32[576,128]{1,0:T(8,128)S(1)}) custom-call(s32[4]{0:T(128)S(1)} %get-tuple-element.92.where_ref, bf16[1792,512]{1,0:T(8,128)(2,1)} %get-tuple-element.95.a_ref, bf16[1792,512]{1,0:T(8,128)(2,1)S(1)} %collective-permute-done.b_ref, ...), custom_call_target="tpu_custom_call" | custom-call | tf_op jit(solution)/shard_map/cond/branch_1_fun/gram/pallas_call | solution.py:301
  82.3 0.4 collective-permute-start.1
  82.7 1.8 %collective-permute-start.2 = (f32[576,128]{1,0:T(8,128)S(1)}, f32[576,128]{1,0:T(8,128)S(1)}, u32[]{:S(2)}, u32[]{:S(2)}) collective-permute-start(f32[576,128]{1,0:T(8,128)S(1)} %get-tuple-element.99), channel_id=1, source_target_pairs={{0,4},{2,6},{4,0},{6,2},{1,5},{3,7},{5,1},{7,3},{8,12},{10,14},{12... | collective-permute-start | bytes 884744 | tf_op jit(solution)/shard_map/cond/branch_1_fun/ppermute | solution.py:309
  84.5 0.7 collective-permute-start.3
  85.2 7.2 %collective-permute-done.1.p1 = f32[576,128]{1,0:T(8,128)S(1)} collective-permute-done((f32[576,128]{1,0:T(8,128)S(1)}, f32[576,128]{1,0:T(8,128)S(1)}, u32[]{:S(2)}, u32[]{:S(2)}) %collective-permute-start.1) | collective-permute-done | bytes 294944 | tf_op jit(solution)/shard_map/cond/branch_1_fun/ppermute | solution.py:309
  92.4 5.2 %collective-permute-done.2.p2 = f32[576,128]{1,0:T(8,128)S(1)} collective-permute-done((f32[576,128]{1,0:T(8,128)S(1)}, f32[576,128]{1,0:T(8,128)S(1)}, u32[]{:S(2)}, u32[]{:S(2)}) %collective-permute-start.2) | collective-permute-done | bytes 294944 | tf_op jit(solution)/shard_map/cond/branch_1_fun/ppermute | solution.py:309
  97.6 0.9 collective-permute-done.3.p3
  98.5 0.0 copy-done.1
  98.5 0.0 copy-done.2
  98.5 2.8 %maxima.1 = f32[16,128]{1,0:T(8,128)S(1)} custom-call(s32[4]{0:T(128)S(1)} %get-tuple-element.92.where_ref, s32[72]{0:T(128)S(1)} %copy-done.1, s32[72]{0:T(128)S(1)} %copy-done.2, f32[576,128]{1,0:T(8,128)S(1)} %get-tuple-element.97.p0, f32[576,128]{1,0:T(8,128)S(1)} %collective-permute-done.1.p1, f32[576,128]{1,0:T(8,128)S(1)} %collective-permute-done.2.p2, ...), custom_call_target="tpu_custom_call" | custom-call | tf_op jit(solution)/shard_map/cond/branch_1_fun/maxima/pallas_call | solution.py:312
  101.3 16.0 %all_to_all.55 = f32[128,1,128]{2,1,0:T(1,128)S(1)} all-to-all(f32[128,1,128]{2,1,0:T(1,128)S(1)} %bitcast.31), channel_id=1, replica_groups=mesh['x'=4,'z'=4,'y'=4,'c'=2] {'x','z','y','c'}, dimensions={0} | all-to-all | bytes 131072 | tf_op jit(solution)/shard_map/cond/branch_1_fun/all_to_all | solution.py:320
  117.3 0.8 pick.1
  118.1 0.0 copy-start.5
  118.1 0.5 copy-done.5
  (1 shorter events, 0.0 us)
Async XLA Ops:
  28.0 1.4 %copy-start = (bf16[16,128,512]{2,1,0:T(8,128)(2,1)}, bf16[16,128,512]{2,1,0:T(8,128)(2,1)S(1)}, u32[]{:S(2)}) copy-start(bf16[16,128,512]{2,1,0:T(8,128)(2,1)S(1)} %get-tuple-element.108) | copy-start | bytes 6291460
  29.4 34.1 %all-to-all-start.7 = ((bf16[16,128,512]{2,1,0:T(8,128)(2,1)}), bf16[16,128,512]{2,1,0:T(8,128)(2,1)S(1)}, u32[]{:S(2)}, u32[]{:S(2)}) async-start(bf16[16,128,512]{2,1,0:T(8,128)(2,1)} %copy-done), calls=%async_computation.7 | async-start | bytes 4194304 | tf_op jit(solution)/shard_map/all_to_all | solution.py:292
  37.0 33.8 %copy-start.3 = (s32[128]{0:T(128)S(1)}, s32[128]{0:T(128)}, u32[]{:S(2)}) copy-start(s32[128]{0:T(128)} %param.9) | copy-start | bytes 1540
  71.0 27.5 %copy-start.1 = (s32[72]{0:T(128)S(1)}, s32[72]{0:T(128)}, u32[]{:S(2)}) copy-start(s32[72]{0:T(128)} %constant.111.clone.1.rows_ref) | copy-start | bytes 868 | tf_op jit(solution)/shard_map/cond
  71.0 27.5 %copy-start.2 = (s32[72]{0:T(128)S(1)}, s32[72]{0:T(128)}, u32[]{:S(2)}) copy-start(s32[72]{0:T(128)} %constant.112.clone.1.cols_ref) | copy-start | bytes 868 | tf_op jit(solution)/shard_map/cond
  71.0 8.3 %collective-permute-start = (bf16[1792,512]{1,0:T(8,128)(2,1)}, bf16[1792,512]{1,0:T(8,128)(2,1)S(1)}, u32[]{:S(2)}, u32[]{:S(2)}) collective-permute-start(bf16[1792,512]{1,0:T(8,128)(2,1)} %get-tuple-element.95.a_ref), channel_id=1, source_target_pairs={{0,1},{1,0},{2,3},{3,2},{4,5},{5,4},{6,7},{7,6},{8,9},{9,8},{10,11... | collective-permute-start | bytes 5505032 | tf_op jit(solution)/shard_map/cond/branch_1_fun/ppermute | solution.py:300
  82.3 10.1 %collective-permute-start.1 = (f32[576,128]{1,0:T(8,128)S(1)}, f32[576,128]{1,0:T(8,128)S(1)}, u32[]{:S(2)}, u32[]{:S(2)}) collective-permute-start(f32[576,128]{1,0:T(8,128)S(1)} %get-tuple-element.98), channel_id=1, source_target_pairs={{0,2},{2,4},{4,6},{6,0},{1,3},{3,5},{5,7},{7,1},{8,10},{10,12},{12... | collective-permute-start | bytes 884744 | tf_op jit(solution)/shard_map/cond/branch_1_fun/ppermute | solution.py:309
  82.7 14.9 %collective-permute-start.2 = (f32[576,128]{1,0:T(8,128)S(1)}, f32[576,128]{1,0:T(8,128)S(1)}, u32[]{:S(2)}, u32[]{:S(2)}) collective-permute-start(f32[576,128]{1,0:T(8,128)S(1)} %get-tuple-element.99), channel_id=1, source_target_pairs={{0,4},{2,6},{4,0},{6,2},{1,5},{3,7},{5,1},{7,3},{8,12},{10,14},{12... | collective-permute-start | bytes 884744 | tf_op jit(solution)/shard_map/cond/branch_1_fun/ppermute | solution.py:309
  84.5 14.0 %collective-permute-start.3 = (f32[576,128]{1,0:T(8,128)S(1)}, f32[576,128]{1,0:T(8,128)S(1)}, u32[]{:S(2)}, u32[]{:S(2)}) collective-permute-start(f32[576,128]{1,0:T(8,128)S(1)} %get-tuple-element.100), channel_id=1, source_target_pairs={{0,6},{2,0},{4,2},{6,4},{1,7},{3,1},{5,3},{7,5},{8,14},{10,8},{12,... | collective-permute-start | bytes 884744 | tf_op jit(solution)/shard_map/cond/branch_1_fun/ppermute | solution.py:309
  118.1 0.5 copy-start.5

commit v3 on v2

v3 whole, which is shorter than its diff:
```python
import jax
import jax.numpy as jnp
from jax import lax
from jax.experimental import pallas as pl
from jax.experimental.pallas import tpu as pltpu
from jax.sharding import Mesh, PartitionSpec as P

ROWS = 128
HALF_WIDTH = 2048
WIDTH = 512
LABEL_ROWS = 16
BINS = 16
CHIPS = 64
BLOCK = 40
SLOTS = BLOCK - 1
LANES = 128
CAPS = (704, 512, 320, 256)
STARTS = (0, 704, 1216, 1536)
SORTED = 1792
HALF = 64
CHUNK = 9 * HALF
PARTIAL = 4 * CHUNK
f32, bf16, i32 = jnp.float32, jnp.bfloat16, jnp.int32
WHOLE = pl.BlockSpec(memory_space=pltpu.VMEM)
SCALARS = pl.BlockSpec(memory_space=pltpu.SMEM)


def params(mib):
    return pltpu.CompilerParams(vmem_limit_bytes=mib * 1024 * 1024)


def iota(shape, dim):
    return lax.broadcasted_iota(i32, shape, dim)


def dot_last(a, b):
    return lax.dot_general(a, b, (((1,), (1,)), ((), ())), preferred_element_type=f32)


def dot(a, b):
    return lax.dot_general(a, b, (((1,), (0,)), ((), ())), preferred_element_type=f32)


def as_bf16(mask):
    return jnp.where(mask, 1.0, 0.0).astype(bf16)


def bin_of(labels):
    rank, residue = labels >> 2, labels & 3
    row, col = rank >> 2, rank & 3
    col = jnp.where((row & 1) == 1, 3 - col, col)
    return 4 * col + ((row - residue) & 3)


def unit_kernel(where_ref, x_ref, ids_ref, keep_ref, send_ref):
    c = where_ref[3]
    x = x_ref[...]
    scale = lax.rsqrt(jnp.sum(x * x, axis=1, keepdims=True) + 1e-06)
    ids = jnp.concatenate([ids_ref[...].astype(f32), jnp.zeros((1, HALF_WIDTH - ROWS), f32)], axis=1)
    ids = jnp.broadcast_to(ids, (LABEL_ROWS, HALF_WIDTH)).astype(bf16)
    for half, out_ref in ((c, keep_ref), (1 - c, send_ref)):
        columns = pl.ds(pl.multiple_of(half * HALF_WIDTH, HALF_WIDTH), HALF_WIDTH)
        out_ref[:ROWS, :] = (x_ref[:, columns] * scale).astype(bf16)
        out_ref[ROWS:, :] = ids


def pack_kernel(where_ref, keep_ref, got_ref, out_ref, code_ref):
    first = where_ref[3] == 0
    kept = jnp.max(keep_ref[ROWS:, :ROWS].astype(f32), axis=0, keepdims=True)
    got = jnp.max(got_ref[ROWS:, :ROWS].astype(f32), axis=0, keepdims=True)
    labels = jnp.concatenate([jnp.where(first, kept, got), jnp.where(first, got, kept)], axis=0).astype(i32)
    bins = bin_of(labels)
    member = jnp.concatenate([jnp.where(bins == b, 1.0, 0.0) for b in range(BINS)], axis=0)
    member16 = member.astype(bf16)
    along = dot(member16, as_bf16(iota((ROWS, ROWS), 0) < iota((ROWS, ROWS), 1)))
    row, col = iota((2 * BINS, 2 * BINS), 0), iota((2 * BINS, 2 * BINS), 1)
    earlier = dot(as_bf16(((row >> 1) == (col >> 1)) & (col < row)), member16)
    ranks = member * (along + jnp.sum(earlier, axis=1, keepdims=True))
    rank = sum(ranks[2 * b:2 * b + 2] for b in range(BINS)).astype(i32)
    code = jnp.where(rank < SLOTS, bins * BLOCK + rank, -1)
    code_ref[...] = jnp.concatenate([code] * 4, axis=0)
    docs = 2 * ROWS
    flat = lambda v: jnp.concatenate([v[:1], v[1:]], axis=1)
    rank_row, bin_row, label_row = flat(rank), flat(bins), flat(labels)
    counts = dot_last(jnp.ones((8, docs), bf16), as_bf16(iota((LANES, docs), 0) == label_row))[:1]
    named = jnp.where(iota((BINS, docs), 0) == bin_row, (label_row + 1).astype(f32), 0.0).astype(bf16)
    names = dot_last(named, as_bf16((iota((LANES, docs), 0) == rank_row) & (rank_row < SLOTS)))
    own = jnp.where(first, code[:1], code[1:])
    other = jnp.where(first, code[1:], code[:1])
    onehot = as_bf16(iota((BINS * BLOCK, docs), 0) == jnp.concatenate([own, other], axis=1))
    is_last = iota((BLOCK, WIDTH), 0) == SLOTS
    for y in range(4):
        columns = slice(y * WIDTH, (y + 1) * WIDTH)
        x = jnp.concatenate([keep_ref[:ROWS, columns], got_ref[:ROWS, columns]], axis=0)
        packed = dot(onehot, x)
        for b in range(BINS):
            extra = jnp.concatenate([names[b:b + 1], counts, jnp.zeros((1, 2 * LANES), f32)], axis=1)
            out_ref[4 * b + y] = jnp.where(is_last, extra, packed[b * BLOCK:(b + 1) * BLOCK]).astype(bf16)


def sort_kernel(where_ref, x_ref, out_ref, pos_ref, meta_ref):
    mine = where_ref[0] * 4 + where_ref[1]
    tail = x_ref[:, BLOCK - 8:, :2 * LANES].astype(f32)
    tail = jnp.max(jnp.where(iota(tail.shape, 1) == 7, tail, 0.0), axis=1)
    labels, chip_counts = tail[:, :LANES].astype(i32) - 1, tail[:, LANES:].astype(bf16)
    row, col = iota((LANES, LANES), 0), iota((LANES, LANES), 1)
    in_bin = (bin_of(row) == col) & (row < 4 * BINS)
    sizes, total = [], 0.0
    for r in range(4):
        counts = dot(chip_counts, as_bf16(in_bin & ((row & 3) == r)))
        total = total + counts
        sizes.append(jnp.sum(counts, axis=0, keepdims=True))
    a, b = jnp.maximum(sizes[0], sizes[1]), jnp.minimum(sizes[0], sizes[1])
    c, d = jnp.maximum(sizes[2], sizes[3]), jnp.minimum(sizes[2], sizes[3])
    first, e = jnp.maximum(a, c), jnp.minimum(a, c)
    g, fourth = jnp.maximum(b, d), jnp.minimum(b, d)
    ordered = (first, jnp.maximum(e, g), jnp.minimum(e, g), fourth)
    over = jnp.max(jnp.where(total > SLOTS, 1.0, 0.0), axis=0, keepdims=True)
    for size, cap in zip(ordered, CAPS):
        over = jnp.maximum(over, jnp.where(size > cap, 1.0, 0.0))
    over = jnp.max(over, axis=1, keepdims=True)
    here = iota((1, LANES), 1) == mine
    own = lambda v: jnp.sum(jnp.where(here, v, 0.0), axis=1, keepdims=True)
    wide = lambda v: jnp.broadcast_to(v, (1, LANES))
    meta_ref[...] = jnp.concatenate([wide(own(v)) for v in ordered] + [wide(over)] * 4, axis=0)

    n = [own(v) for v in sizes]
    valid = (labels >= 0) & (iota(labels.shape, 1) < SLOTS)
    upper = as_bf16(row < col)
    lower = as_bf16(iota((CHIPS, CHIPS), 1) < iota((CHIPS, CHIPS), 0))
    pos = jnp.full(labels.shape, -1.0, f32)
    for r in range(4):
        place = sum(
            jnp.where((n[q] > n[r]) | ((n[q] == n[r]) & (q < r)), 1.0, 0.0) for q in range(4) if q != r
        )
        start = jnp.where(
            place < 0.5, float(STARTS[0]),
            jnp.where(place < 1.5, float(STARTS[1]), jnp.where(place < 2.5, float(STARTS[2]), float(STARTS[3]))),
        )
        member = valid & ((labels & 3) == r)
        member16 = as_bf16(member)
        rank = dot(member16, upper) + jnp.sum(dot(lower, member16), axis=1, keepdims=True)
        pos = jnp.where(member, start + rank, pos)
    pos_ref[...] = pos.astype(i32)
    per, groups = 16, CHIPS // 16
    plus = jnp.where(iota(pos.shape, 1) < BLOCK, pos + 1.0, 0.0)
    lined = jnp.zeros((8, per * BLOCK), f32)
    for t in range(per):
        rows = jnp.concatenate([plus[per * g + t:per * g + t + 1] for g in range(groups)] * 2, axis=0)
        rows = jnp.concatenate([rows, jnp.zeros((8, per * BLOCK - LANES), f32)], axis=1)
        lined = lined + (pltpu.roll(rows, t * BLOCK, 1) if t else rows)
    pos_row = jnp.concatenate([lined[g:g + 1] for g in range(groups)], axis=1).astype(i32) - 1
    x = x_ref[...].reshape(CHIPS * BLOCK, WIDTH)
    step = SORTED // 4
    for i in range(4):
        onehot = as_bf16(iota((step, CHIPS * BLOCK), 0) + i * step == pos_row)
        out_ref[i * step:(i + 1) * step, :] = dot(onehot, x).astype(bf16)


def column_blocks(core):
    for q in ((0,) if core == 0 else (1, 2, 3)):
        for first in range(0, CAPS[q], LANES):
            yield q, first


def gram_kernel(where_ref, a_ref, b_ref, meta_ref, out0, out1, out2, out3, part_ref):
    y, c = where_ref[2], where_ref[3]
    for core in range(2):
        @pl.when(c == core)
        def _():
            at = 0
            for q, first in column_blocks(core):
                rows = CAPS[q] - first
                left = pl.ds(STARTS[q] + first, rows)
                right = pl.ds(STARTS[q] + first, LANES)
                score = dot_last(a_ref[left, :], a_ref[right, :]) + dot_last(b_ref[left, :], b_ref[right, :])
                size = meta_ref[q:q + 1, :].astype(i32)
                i, j = iota(score.shape, 0), iota(score.shape, 1)
                keep = (i + first < size) & (j + first < size) & (i != j)
                score = jnp.where(keep, score, -4.0)
                done = 0
                while done < rows:
                    chunk, offset = divmod(at + done, CHUNK)
                    take = min(rows - done, CHUNK - offset)
                    part_ref[chunk, offset:offset + take, :] = score[done:done + take]
                    done += take
                at += rows
            while at < PARTIAL:
                chunk, offset = divmod(at, CHUNK)
                part_ref[chunk, offset:offset + HALF, :] = jnp.full((HALF, LANES), -4.0, f32)
                at += HALF
    for shift, out in enumerate((out0, out1, out2, out3)):
        out[...] = part_ref[lax.rem(y + shift, 4)]


FIRST_ROW = (0, 6, 10, 13)


def tables():
    rows, odd, cols = [], [], []
    for core in range(2):
        have = []
        for q, first in column_blocks(core):
            for r in range(first, CAPS[q], HALF):
                have.append((FIRST_ROW[q] + r // LANES, r // HALF % 2, FIRST_ROW[q] + first // LANES))
        have += [(15, 0, 15)] * (36 - len(have))
        for table, column in ((rows, 0), (odd, 1), (cols, 2)):
            table += [h[column] for h in have]
    return jnp.asarray(rows + odd + cols, i32)


def max_kernel(where_ref, table_ref, p0, p1, p2, p3, pos_ref, out_ref, best_ref):
    y, c = where_ref[2], where_ref[3]
    best_ref[...] = jnp.full(best_ref.shape, -1.0, f32)
    sub, lane = iota((HALF, LANES), 0), iota((HALF, LANES), 1)
    for t in range(CHUNK // HALF):
        at = slice(t * HALF, (t + 1) * HALF)
        block = (p0[at, :] + p1[at, :]) + (p2[at, :] + p3[at, :])
        index = c * 36 + y * 9 + t
        row, odd, col = (table_ref[72 * i + index] for i in range(3))
        along = jnp.max(block, axis=1, keepdims=True)
        along = jnp.max(jnp.where(sub + odd * HALF == lane, along, -1.0), axis=0, keepdims=True)
        best_ref[pl.ds(row, 1), :] = jnp.maximum(best_ref[pl.ds(row, 1), :], along)
        down = jnp.max(block, axis=0, keepdims=True)
        best_ref[pl.ds(col, 1), :] = jnp.maximum(best_ref[pl.ds(col, 1), :], down)
    pos = pos_ref[...]
    pos = jnp.where(pos >= STARTS[1], pos + HALF, pos)
    pos = jnp.where(pos >= STARTS[3] + HALF, pos + HALF, pos)
    row, lane = pos >> 7, pos & (LANES - 1)
    out = jnp.full(pos.shape, -1.0, f32)
    for r in range(15):
        value = jnp.broadcast_to(best_ref[r:r + 1, :], pos.shape)
        value = jnp.take_along_axis(value, lane, axis=1, mode="promise_in_bounds")
        out = jnp.where(row == r, value, out)
    out_ref[...] = out


def pick_kernel(where_ref, v_ref, code_ref, out_ref):
    c = where_ref[3]
    values = jnp.max(v_ref[...].reshape(BINS, 8, LANES), axis=1)
    eye = iota((LANES, LANES), 0) == iota((LANES, LANES), 1)
    code = jnp.max(jnp.where(iota((8, ROWS), 0) == c, code_ref[...], -1), axis=0, keepdims=True)
    code = jnp.max(jnp.where(eye, code.astype(f32), -1.0), axis=1, keepdims=True).astype(i32)
    slot = iota((ROWS, LANES), 1)
    best = jnp.full((ROWS, LANES), -1.0, f32)
    for b in range(BINS):
        best = jnp.where((slot + b * BLOCK == code) & (slot < BLOCK), values[b:b + 1], best)
    best = jnp.max(best, axis=1, keepdims=True)
    out_ref[...] = jnp.max(jnp.where(eye, best, -1.0), axis=0, keepdims=True)


def gather_groups(embeddings, cluster_ids):
    split = ("z", "y", "c")
    rows = embeddings.shape[0]
    groups = lax.axis_size("x")
    cap = 2 * rows // groups
    slots = groups * cap
    owner_of = cluster_ids % groups
    onehot = (owner_of[:, None] == jnp.arange(groups, dtype=i32)[None, :]).astype(i32)
    before = jnp.cumsum(onehot, axis=0) - onehot
    rank = jnp.sum(before * onehot, axis=1)
    place = owner_of * cap + rank
    picked = place[None, :] == jnp.arange(slots, dtype=i32)[:, None]
    filled = jnp.any(picked, axis=1)
    source = jnp.sum(jnp.where(picked, jnp.arange(rows, dtype=i32)[None, :], 0), axis=1)
    out_labels = jnp.where(filled, cluster_ids[source], -1)
    squares = jnp.sum(embeddings * embeddings, axis=1, keepdims=True)
    local_unit = (embeddings * lax.rsqrt(squares + 1e-06)).astype(bf16)
    outgoing_unit = jnp.where(filled[:, None], local_unit[source], jnp.zeros((), bf16))
    unit = lax.all_to_all(outgoing_unit, "x", split_axis=0, concat_axis=0, tiled=True)
    labels = lax.all_to_all(out_labels, "x", split_axis=0, concat_axis=0, tiled=True)
    members = lax.axis_size(split)

    def everywhere(v):
        copies = jnp.broadcast_to(v[None], (members,) + v.shape).reshape((members * slots,) + v.shape[1:])
        return lax.all_to_all(copies, split, split_axis=0, concat_axis=0, tiled=True)

    def add_slice(i, scores):
        part = lax.dynamic_slice_in_dim(unit, i * WIDTH, WIDTH, 1)
        return scores + dot_last(part, everywhere(part))

    scores = lax.fori_loop(0, embeddings.shape[1] // WIDTH, add_slice, jnp.zeros((slots, members * slots), f32))
    all_labels = everywhere(labels)
    own = lax.axis_index(split) * slots + jnp.arange(slots, dtype=i32)
    mask = (
        (labels[:, None] == all_labels[None, :])
        & (labels[:, None] >= 0)
        & (own[:, None] != jnp.arange(members * slots, dtype=i32)[None, :])
    )
    scores = jnp.where(mask, scores, -1.0)
    best = jnp.maximum(-1.0, jnp.max(scores, axis=1))
    returned = lax.all_to_all(best, "x", split_axis=0, concat_axis=0, tiled=True)
    return returned[place]


def on_device(embeddings, cluster_ids):
    where = jnp.stack([lax.axis_index(a) for a in ("x", "z", "y", "c")]).astype(i32)
    shape = jax.ShapeDtypeStruct
    half = shape((ROWS + LABEL_ROWS, HALF_WIDTH), bf16)
    keep, send = pl.pallas_call(
        unit_kernel, out_shape=(half, half),
        in_specs=[SCALARS, WHOLE, WHOLE], out_specs=(WHOLE, WHOLE), compiler_params=params(12), name="unit",
    )(where, embeddings, cluster_ids.reshape(1, ROWS))
    got = lax.ppermute(send, "c", [(0, 1), (1, 0)])
    packed, code = pl.pallas_call(
        pack_kernel,
        out_shape=(shape((CHIPS, BLOCK, WIDTH), bf16), shape((8, ROWS), i32)),
        in_specs=[SCALARS, WHOLE, WHOLE], out_specs=(WHOLE, WHOLE), compiler_params=params(20), name="pack",
    )(where, keep, got)
    packed = lax.all_to_all(packed, ("x", "z", "y"), 0, 0, tiled=True)
    ordered, pos, meta = pl.pallas_call(
        sort_kernel,
        out_shape=(shape((SORTED, WIDTH), bf16), shape((CHIPS, LANES), i32), shape((8, LANES), f32)),
        in_specs=[SCALARS, WHOLE], out_specs=(WHOLE, WHOLE, WHOLE), compiler_params=params(28), name="sort",
    )(where, packed)

    def within_bins(embeddings, cluster_ids):
        other = lax.ppermute(ordered, "c", [(0, 1), (1, 0)])
        partial = pl.pallas_call(
            gram_kernel,
            out_shape=[shape((CHUNK, LANES), f32)] * 4,
            in_specs=[SCALARS, WHOLE, WHOLE, WHOLE], out_specs=[WHOLE] * 4,
            scratch_shapes=[pltpu.VMEM((4, CHUNK, LANES), f32)],
            compiler_params=params(20), name="gram",
        )(where, ordered, other, meta)
        arrived = [partial[0]] + [
            lax.ppermute(partial[s], "y", [(i, (i + s) % 4) for i in range(4)]) for s in (1, 2, 3)
        ]
        best = pl.pallas_call(
            max_kernel,
            out_shape=shape((CHIPS, LANES), f32),
            in_specs=[SCALARS] * 2 + [WHOLE] * 5, out_specs=WHOLE,
            scratch_shapes=[pltpu.VMEM((16, LANES), f32)],
            compiler_params=params(8), name="maxima",
        )(where, tables(), *arrived, pos)
        sent = jnp.broadcast_to(best[:, None, :], (CHIPS, 2, LANES)).reshape(2 * CHIPS, 1, LANES)
        back = lax.all_to_all(sent, ("x", "z", "y", "c"), 0, 0, tiled=True)
        return pl.pallas_call(
            pick_kernel,
            out_shape=shape((1, ROWS), f32),
            in_specs=[SCALARS, WHOLE, WHOLE], out_specs=WHOLE, compiler_params=params(8), name="pick",
        )(where, back.reshape(2 * CHIPS, LANES), code).reshape(ROWS)

    return lax.cond(meta[4, 0] < 0.5, within_bins, gather_groups, embeddings, cluster_ids)


def solution(mesh):
    axes = ("x", "z", "y", "c")
    grid = Mesh(mesh.devices.reshape(4, 4, 4, 2), axes)
    return jax.shard_map(
        on_device, mesh=grid, in_specs=(P(axes, None), P(axes)), out_specs=P(axes), check_vma=False
    )
```

time: 119 us -> 112 us (0.941)
  blocking collectives: 38.4 us -> 21.1 us
  waiting for transfers between devices: 43.3 us -> 52 us
  starting transfers between devices: 15.2 us -> 18.8 us
  Pallas kernels: 18.3 us -> 16 us
    all_to_all x1 -> x0, blocking collectives: 22.4 us -> none  [on_device(): cut = lax.all_to_all(cut, ('y', 'c'), 0, 0, tiled=True)]
    all_to_all x1, waiting for transfers between devices: 26.4 us -> 33.8 us  [on_device(): packed = lax.all_to_all(packed, ('x', 'z', 'y'), 0, 0, tiled=True)]
    all_to_all x1, blocking collectives: 16 us -> 21.1 us  [within_bins(): back = lax.all_to_all(sent, ('x', 'z', 'y', 'c'), 0, 0, tiled=True)]
    pallas_call x4, Pallas kernels: 11.4 us -> 7.72 us  [the longest x1 2.99 us: within_bins(): pl.pallas_call(gram_kernel, out_shape=[shape((CHUNK, LANES), f32)] * 4, i...]
    all_to_all x1, starting transfers between devices: 7.6 us -> 11.2 us  [on_device(): packed = lax.all_to_all(packed, ('x', 'z', 'y'), 0, 0, tiled=True)]
    ppermute x1, starting transfers between devices: 4.72 us -> 2.26 us  [within_bins(): other = lax.ppermute(ordered, 'c', [(0, 1), (1, 0)])]
    ppermute x0 -> x1, waiting for transfers between devices: none -> 1.63 us  [on_device(): got = lax.ppermute(send, 'c', [(0, 1), (1, 0)])]
    ppermute x0 -> x1, starting transfers between devices: none -> 1.5 us  [on_device(): got = lax.ppermute(send, 'c', [(0, 1), (1, 0)])]
  transfers between devices with their start and end apart: 5 -> 6, of which waited for: 5 -> 5; matrix products, arithmetic and copies ran while one was open for 0% -> 0% of each run, Pallas kernels for 0% -> 0%
where the time goes in v3:
time: 112 us; the launch traced here: 111 us
  waiting for transfers between devices  52 us (46%)
  blocking collectives  21.1 us (19%)
  starting transfers between devices  18.8 us (17%)
  Pallas kernels  16 us (14%)
  local copies, waits for them, and re-layouts  2.58 us (2%)
    all_to_all x1, waiting for transfers between devices, on_device(): packed = lax.all_to_all(packed, ('x', 'z', 'y'), 0, 0, tiled=True)  33.8 us
    all_to_all x1, blocking collectives, within_bins(): back = lax.all_to_all(sent, ('x', 'z', 'y', 'c'), 0, 0, tiled=True)  21.1 us
    ppermute x3, waiting for transfers between devices, within_bins(): lax.ppermute(partial[s], 'y', [(i, (i + s) % 4) for i in range(4)])  12.9 us
    all_to_all x1, starting transfers between devices, on_device(): packed = lax.all_to_all(packed, ('x', 'z', 'y'), 0, 0, tiled=True)  11.2 us
    pallas_call x1, Pallas kernels, on_device(): pl.pallas_call(sort_kernel, out_shape=(shape((SORTED, WIDTH), bf16), shap...  7.4 us
    ppermute x3, starting transfers between devices, within_bins(): lax.ppermute(partial[s], 'y', [(i, (i + s) % 4) for i in range(4)])  3.84 us
    ppermute x1, waiting for transfers between devices, within_bins(): other = lax.ppermute(ordered, 'c', [(0, 1), (1, 0)])  3.62 us
    pallas_call x1, Pallas kernels, within_bins(): pl.pallas_call(gram_kernel, out_shape=[shape((CHUNK, LANES), f32)] * 4, i...  2.99 us
  transfers between devices with their start and end apart: 6, of which 5 were waited for; matrix products, arithmetic and copies ran while one was open for 0% of the time, Pallas kernels for 0%

profile of v3, /device:TPU:1, one launch (start us, length us, event | category | flops | bytes accessed | tf_op | source)
XLA Modules:
  0.0 111.5 jit_solution(8373601424467725558)
XLA Ops:
  0.0 0.1 pad_add_fusion.where_ref
  0.1 1.9 %unit.1 = (bf16[144,2048]{1,0:T(8,128)(2,1)S(1)}, bf16[144,2048]{1,0:T(8,128)(2,1)S(1)}) custom-call(s32[4]{0:T(128)S(1)} %pad_add_fusion.where_ref, f32[128,4096]{1,0:T(8,128)} %x_ref.1, s32[1,128]{1,0:T(1,128)} %bitcast.28), custom_call_target="tpu_custom_call" | custom-call | tf_op jit(solution)/shard_map/unit/pallas_call | solution.py:300
  2.0 1.5 %collective-permute-start.4 = (bf16[144,2048]{1,0:T(8,128)(2,1)S(1)}, bf16[144,2048]{1,0:T(8,128)(2,1)S(1)}, u32[]{:S(2)}, u32[]{:S(2)}) collective-permute-start(bf16[144,2048]{1,0:T(8,128)(2,1)S(1)} %get-tuple-element.108), channel_id=1, source_target_pairs={{0,1},{1,0},{2,3},{3,2},{4,5},{5,4},{6,7},{7,6},{8,9},{9,8},{10,11... | collective-permute-start | bytes 1769480 | tf_op jit(solution)/shard_map/ppermute | solution.py:304
  3.5 1.6 %collective-permute-done.4.got_ref = bf16[144,2048]{1,0:T(8,128)(2,1)S(1)} collective-permute-done((bf16[144,2048]{1,0:T(8,128)(2,1)S(1)}, bf16[144,2048]{1,0:T(8,128)(2,1)S(1)}, u32[]{:S(2)}, u32[]{:S(2)}) %collective-permute-start.4) | collective-permute-done | bytes 589856 | tf_op jit(solution)/shard_map/ppermute | solution.py:304
  5.1 1.6 %pack.1 = (bf16[64,40,512]{2,1,0:T(8,128)(2,1)S(1)}, s32[8,128]{1,0:T(8,128)S(1)}) custom-call(s32[4]{0:T(128)S(1)} %pad_add_fusion.where_ref, bf16[144,2048]{1,0:T(8,128)(2,1)S(1)} %get-tuple-element.107.keep_ref, bf16[144,2048]{1,0:T(8,128)(2,1)S(1)} %collective-permute-done.4.got_ref), custom_call_target="tpu_custom_call" | custom-call | tf_op jit(solution)/shard_map/pack/pallas_call | solution.py:305
  6.8 0.0 copy-start
  6.8 1.5 %copy-done = bf16[64,40,512]{2,1,0:T(8,128)(2,1)} copy-done((bf16[64,40,512]{2,1,0:T(8,128)(2,1)}, bf16[64,40,512]{2,1,0:T(8,128)(2,1)S(1)}, u32[]{:S(2)}) %copy-start) | copy-done | bytes 2621464
  8.3 11.2 %all-to-all-start.6 = ((bf16[64,40,512]{2,1,0:T(8,128)(2,1)}), bf16[64,40,512]{2,1,0:T(8,128)(2,1)S(1)}, u32[]{:S(2)}, u32[]{:S(2)}) async-start(bf16[64,40,512]{2,1,0:T(8,128)(2,1)} %copy-done), calls=%async_computation.6 | async-start | bytes 5242880 | tf_op jit(solution)/shard_map/all_to_all | solution.py:310
  19.5 0.0 copy-start.2
  19.5 33.8 %all-to-all-done.6.x_ref = bf16[64,40,512]{2,1,0:T(8,128)(2,1)S(1)} async-done(((bf16[64,40,512]{2,1,0:T(8,128)(2,1)}), bf16[64,40,512]{2,1,0:T(8,128)(2,1)S(1)}, u32[]{:S(2)}, u32[]{:S(2)}) %all-to-all-start.6) | async-done | bytes 2621472 | tf_op jit(solution)/shard_map/all_to_all | solution.py:310
  53.3 7.4 %sort.1 = (bf16[1792,512]{1,0:T(8,128)(2,1)}, s32[64,128]{1,0:T(8,128)S(1)}, f32[8,128]{1,0:T(8,128)S(1)}) custom-call(s32[4]{0:T(128)S(1)} %pad_add_fusion.where_ref, bf16[64,40,512]{2,1,0:T(8,128)(2,1)S(1)} %all-to-all-done.6.x_ref), custom_call_target="tpu_custom_call" | custom-call | tf_op jit(solution)/shard_map/sort/pallas_call | solution.py:311
  60.7 0.5 slice.3
  61.9 0.0 copy-done.2
  61.9 49.0 %conditional.1 = (f32[128]{0:T(128)S(1)}) conditional(s32[]{:T(128)} %bitcast.15, (s32[128]{0:T(128)S(1)}, f32[128,4096]{1,0:T(8,128)}) %tuple.48, (bf16[1792,512]{1,0:T(8,128)(2,1)}, s32[4]{0:T(128)S(1)}, f32[8,128]{1,0:T(8,128)S(1)}, (), s32[64,128]{1,0:T(8,128)S(1)}, /*index=5*/s32[8,128]{1,0:T(8,128)S(1)}) %tuple.26), branch_computations={%region_0.9_spmd, %region_9.10_spmd} | conditional | flops 2167645440 | bytes 96702280 | solution.py:344
  62.2 0.0 copy-start.1
  62.2 2.3 %collective-permute-start = (bf16[1792,512]{1,0:T(8,128)(2,1)}, bf16[1792,512]{1,0:T(8,128)(2,1)S(1)}, u32[]{:S(2)}, u32[]{:S(2)}) collective-permute-start(bf16[1792,512]{1,0:T(8,128)(2,1)} %get-tuple-element.92.a_ref), channel_id=1, source_target_pairs={{0,1},{1,0},{2,3},{3,2},{4,5},{5,4},{6,7},{7,6},{8,9},{9,8},{10,11... | collective-permute-start | bytes 5505032 | tf_op jit(solution)/shard_map/cond/branch_1_fun/ppermute | solution.py:318
  64.4 3.6 %collective-permute-done.b_ref = bf16[1792,512]{1,0:T(8,128)(2,1)S(1)} collective-permute-done((bf16[1792,512]{1,0:T(8,128)(2,1)}, bf16[1792,512]{1,0:T(8,128)(2,1)S(1)}, u32[]{:S(2)}, u32[]{:S(2)}) %collective-permute-start) | collective-permute-done | bytes 1835040 | tf_op jit(solution)/shard_map/cond/branch_1_fun/ppermute | solution.py:318
  68.1 3.0 %gram.1 = (f32[576,128]{1,0:T(8,128)S(1)}, f32[576,128]{1,0:T(8,128)S(1)}, f32[576,128]{1,0:T(8,128)S(1)}, f32[576,128]{1,0:T(8,128)S(1)}) custom-call(s32[4]{0:T(128)S(1)} %get-tuple-element.90.where_ref, bf16[1792,512]{1,0:T(8,128)(2,1)} %get-tuple-element.92.a_ref, bf16[1792,512]{1,0:T(8,128)(2,1)S(1)} %collective-permute-done.b_ref, ...), custom_call_target="tpu_custom_call" | custom-call | tf_op jit(solution)/shard_map/cond/branch_1_fun/gram/pallas_call | solution.py:319
  71.1 1.4 %collective-permute-start.1 = (f32[576,128]{1,0:T(8,128)S(1)}, f32[576,128]{1,0:T(8,128)S(1)}, u32[]{:S(2)}, u32[]{:S(2)}) collective-permute-start(f32[576,128]{1,0:T(8,128)S(1)} %get-tuple-element.95), channel_id=1, source_target_pairs={{0,2},{2,4},{4,6},{6,0},{1,3},{3,5},{5,7},{7,1},{8,10},{10,12},{12... | collective-permute-start | bytes 884744 | tf_op jit(solution)/shard_map/cond/branch_1_fun/ppermute | solution.py:327
  72.4 2.3 %collective-permute-start.2 = (f32[576,128]{1,0:T(8,128)S(1)}, f32[576,128]{1,0:T(8,128)S(1)}, u32[]{:S(2)}, u32[]{:S(2)}) collective-permute-start(f32[576,128]{1,0:T(8,128)S(1)} %get-tuple-element.96), channel_id=1, source_target_pairs={{0,4},{2,6},{4,0},{6,2},{1,5},{3,7},{5,1},{7,3},{8,12},{10,14},{12... | collective-permute-start | bytes 884744 | tf_op jit(solution)/shard_map/cond/branch_1_fun/ppermute | solution.py:327
  74.8 0.1 collective-permute-start.3
  74.9 5.6 %collective-permute-done.1.p1 = f32[576,128]{1,0:T(8,128)S(1)} collective-permute-done((f32[576,128]{1,0:T(8,128)S(1)}, f32[576,128]{1,0:T(8,128)S(1)}, u32[]{:S(2)}, u32[]{:S(2)}) %collective-permute-start.1) | collective-permute-done | bytes 294944 | tf_op jit(solution)/shard_map/cond/branch_1_fun/ppermute | solution.py:327
  80.5 7.3 %collective-permute-done.2.p2 = f32[576,128]{1,0:T(8,128)S(1)} collective-permute-done((f32[576,128]{1,0:T(8,128)S(1)}, f32[576,128]{1,0:T(8,128)S(1)}, u32[]{:S(2)}, u32[]{:S(2)}) %collective-permute-start.2) | collective-permute-done | bytes 294944 | tf_op jit(solution)/shard_map/cond/branch_1_fun/ppermute | solution.py:327
  87.8 0.0 collective-permute-done.3.p3
  87.8 0.0 copy-done.1
  87.8 1.2 %maxima.1 = f32[64,128]{1,0:T(8,128)S(1)} custom-call(s32[4]{0:T(128)S(1)} %get-tuple-element.90.where_ref, s32[216]{0:T(256)S(1)} %copy-done.1, f32[576,128]{1,0:T(8,128)S(1)} %get-tuple-element.94.p0, f32[576,128]{1,0:T(8,128)S(1)} %collective-permute-done.1.p1, f32[576,128]{1,0:T(8,128)S(1)} %collective-permute-done.2.p2, ...), custom_call_target="tpu_custom_call" | custom-call | tf_op jit(solution)/shard_map/cond/branch_1_fun/maxima/pallas_call | solution.py:329
  89.0 21.1 %all_to_all.50 = f32[128,1,128]{2,1,0:T(1,128)S(1)} all-to-all(f32[128,1,128]{2,1,0:T(1,128)S(1)} %bitcast.31), channel_id=1, replica_groups=mesh['x'=4,'z'=4,'y'=4,'c'=2] {'x','z','y','c'}, dimensions={0} | all-to-all | bytes 131072 | tf_op jit(solution)/shard_map/cond/branch_1_fun/all_to_all | solution.py:337
  110.1 0.9 pick.1
  111.0 0.0 copy-start.4
  111.0 0.5 copy-done.4
  (1 shorter events, 0.0 us)
Async XLA Ops:
  2.0 3.1 %collective-permute-start.4 = (bf16[144,2048]{1,0:T(8,128)(2,1)S(1)}, bf16[144,2048]{1,0:T(8,128)(2,1)S(1)}, u32[]{:S(2)}, u32[]{:S(2)}) collective-permute-start(bf16[144,2048]{1,0:T(8,128)(2,1)S(1)} %get-tuple-element.108), channel_id=1, source_target_pairs={{0,1},{1,0},{2,3},{3,2},{4,5},{5,4},{6,7},{7,6},{8,9},{9,8},{10,11... | collective-permute-start | bytes 1769480 | tf_op jit(solution)/shard_map/ppermute | solution.py:304
  6.8 1.5 %copy-start = (bf16[64,40,512]{2,1,0:T(8,128)(2,1)}, bf16[64,40,512]{2,1,0:T(8,128)(2,1)S(1)}, u32[]{:S(2)}) copy-start(bf16[64,40,512]{2,1,0:T(8,128)(2,1)S(1)} %get-tuple-element.109) | copy-start | bytes 7864324
  8.3 45.0 %all-to-all-start.6 = ((bf16[64,40,512]{2,1,0:T(8,128)(2,1)}), bf16[64,40,512]{2,1,0:T(8,128)(2,1)S(1)}, u32[]{:S(2)}, u32[]{:S(2)}) async-start(bf16[64,40,512]{2,1,0:T(8,128)(2,1)} %copy-done), calls=%async_computation.6 | async-start | bytes 5242880 | tf_op jit(solution)/shard_map/all_to_all | solution.py:310
  19.5 42.4 %copy-start.2 = (s32[128]{0:T(128)S(1)}, s32[128]{0:T(128)}, u32[]{:S(2)}) copy-start(s32[128]{0:T(128)} %param.8) | copy-start | bytes 1540
  62.2 25.7 %copy-start.1 = (s32[216]{0:T(256)S(1)}, s32[216]{0:T(256)}, u32[]{:S(2)}) copy-start(s32[216]{0:T(256)} %constant.109.clone.1.table_ref) | copy-start | bytes 2596 | tf_op jit(solution)/shard_map/cond
  62.2 5.9 %collective-permute-start = (bf16[1792,512]{1,0:T(8,128)(2,1)}, bf16[1792,512]{1,0:T(8,128)(2,1)S(1)}, u32[]{:S(2)}, u32[]{:S(2)}) collective-permute-start(bf16[1792,512]{1,0:T(8,128)(2,1)} %get-tuple-element.92.a_ref), channel_id=1, source_target_pairs={{0,1},{1,0},{2,3},{3,2},{4,5},{5,4},{6,7},{7,6},{8,9},{9,8},{10,11... | collective-permute-start | bytes 5505032 | tf_op jit(solution)/shard_map/cond/branch_1_fun/ppermute | solution.py:318
  71.1 9.5 %collective-permute-start.1 = (f32[576,128]{1,0:T(8,128)S(1)}, f32[576,128]{1,0:T(8,128)S(1)}, u32[]{:S(2)}, u32[]{:S(2)}) collective-permute-start(f32[576,128]{1,0:T(8,128)S(1)} %get-tuple-element.95), channel_id=1, source_target_pairs={{0,2},{2,4},{4,6},{6,0},{1,3},{3,5},{5,7},{7,1},{8,10},{10,12},{12... | collective-permute-start | bytes 884744 | tf_op jit(solution)/shard_map/cond/branch_1_fun/ppermute | solution.py:327
  72.4 15.4 %collective-permute-start.2 = (f32[576,128]{1,0:T(8,128)S(1)}, f32[576,128]{1,0:T(8,128)S(1)}, u32[]{:S(2)}, u32[]{:S(2)}) collective-permute-start(f32[576,128]{1,0:T(8,128)S(1)} %get-tuple-element.96), channel_id=1, source_target_pairs={{0,4},{2,6},{4,0},{6,2},{1,5},{3,7},{5,1},{7,3},{8,12},{10,14},{12... | collective-permute-start | bytes 884744 | tf_op jit(solution)/shard_map/cond/branch_1_fun/ppermute | solution.py:327
  74.8 13.0 %collective-permute-start.3 = (f32[576,128]{1,0:T(8,128)S(1)}, f32[576,128]{1,0:T(8,128)S(1)}, u32[]{:S(2)}, u32[]{:S(2)}) collective-permute-start(f32[576,128]{1,0:T(8,128)S(1)} %get-tuple-element.97), channel_id=1, source_target_pairs={{0,6},{2,0},{4,2},{6,4},{1,7},{3,1},{5,3},{7,5},{8,14},{10,8},{12,... | collective-permute-start | bytes 884744 | tf_op jit(solution)/shard_map/cond/branch_1_fun/ppermute | solution.py:327
  111.0 0.5 copy-start.4

commit v4 on v3

--- a/solution.py
+++ b/solution.py
@@ -14,12 +14,23 @@
 BLOCK = 40
 SLOTS = BLOCK - 1
 LANES = 128
-CAPS = (704, 512, 320, 256)
+CAPS = (704, 512, 320, 192)
 STARTS = (0, 704, 1216, 1536)
-SORTED = 1792
 HALF = 64
-CHUNK = 9 * HALF
+COUNT = 7
+CHUNK = COUNT * HALF
 PARTIAL = 4 * CHUNK
+SHARES = (
+    tuple((q, first) for q, first in ((0, 0), (0, 128), (2, 0), (2, 128), (2, 256))),
+    tuple((q, first) for q, first in (
+        (0, 256), (0, 384), (0, 512), (0, 640), (1, 0), (1, 128), (1, 256), (1, 384), (3, 0), (3, 128))),
+)
+BASES = ({0: 0, 2: 704}, {0: -256, 1: 448, 3: 960})
+SHARE_ROWS = 1216
+SEGMENTS = (
+    (0, 256, 0, None), (256, 448, 256, 0), (704, 256, None, 448), (960, 256, None, 704),
+    (1216, 320, 704, None), (1536, 192, None, 960),
+)
 f32, bf16, i32 = jnp.float32, jnp.bfloat16, jnp.int32
 WHOLE = pl.BlockSpec(memory_space=pltpu.VMEM)
 SCALARS = pl.BlockSpec(memory_space=pltpu.SMEM)
@@ -64,7 +75,7 @@
         out_ref[ROWS:, :] = ids
 
 
-def pack_kernel(where_ref, keep_ref, got_ref, out_ref, code_ref):
+def pack_kernel(where_ref, keep_ref, got_ref, out_ref, code_ref, block_ref, sems):
     first = where_ref[3] == 0
     kept = jnp.max(keep_ref[ROWS:, :ROWS].astype(f32), axis=0, keepdims=True)
     got = jnp.max(got_ref[ROWS:, :ROWS].astype(f32), axis=0, keepdims=True)
@@ -95,10 +106,13 @@
         packed = dot(onehot, x)
         for b in range(BINS):
             extra = jnp.concatenate([names[b:b + 1], counts, jnp.zeros((1, 2 * LANES), f32)], axis=1)
-            out_ref[4 * b + y] = jnp.where(is_last, extra, packed[b * BLOCK:(b + 1) * BLOCK]).astype(bf16)
-
-
-def sort_kernel(where_ref, x_ref, out_ref, pos_ref, meta_ref):
+            block_ref[y, b] = jnp.where(is_last, extra, packed[b * BLOCK:(b + 1) * BLOCK]).astype(bf16)
+        pltpu.make_async_copy(block_ref.at[y], out_ref.at[:, y], sems.at[y]).start()
+    for y in range(4):
+        pltpu.make_async_copy(block_ref.at[y], out_ref.at[:, y], sems.at[y]).wait()
+
+
+def sort_kernel(where_ref, x_ref, mine_ref, send_ref, pos_ref, meta_ref):
     mine = where_ref[0] * 4 + where_ref[1]
     tail = x_ref[:, BLOCK - 8:, :2 * LANES].astype(f32)
     tail = jnp.max(jnp.where(iota(tail.shape, 1) == 7, tail, 0.0), axis=1)
@@ -118,11 +132,14 @@
     over = jnp.max(jnp.where(total > SLOTS, 1.0, 0.0), axis=0, keepdims=True)
     for size, cap in zip(ordered, CAPS):
         over = jnp.maximum(over, jnp.where(size > cap, 1.0, 0.0))
+    for share in SHARES:
+        length = sum(jnp.maximum(jnp.floor((ordered[q] + 63.0) * (1 / 64)) - first // HALF, 0.0) for q, first in share)
+        over = jnp.maximum(over, jnp.where(length > 4 * COUNT, 1.0, 0.0))
     over = jnp.max(over, axis=1, keepdims=True)
     here = iota((1, LANES), 1) == mine
     own = lambda v: jnp.sum(jnp.where(here, v, 0.0), axis=1, keepdims=True)
     wide = lambda v: jnp.broadcast_to(v, (1, LANES))
-    meta_ref[...] = jnp.concatenate([wide(own(v)) for v in ordered] + [wide(over)] * 4, axis=0)
+    meta_ref[...] = jnp.concatenate([wide(own(v)) for v in ordered] + [wide(over)] * 4, axis=0).astype(i32)
 
     n = [own(v) for v in sizes]
     valid = (labels >= 0) & (iota(labels.shape, 1) < SLOTS)
@@ -151,75 +168,89 @@
         lined = lined + (pltpu.roll(rows, t * BLOCK, 1) if t else rows)
     pos_row = jnp.concatenate([lined[g:g + 1] for g in range(groups)], axis=1).astype(i32) - 1
     x = x_ref[...].reshape(CHIPS * BLOCK, WIDTH)
-    step = SORTED // 4
-    for i in range(4):
-        onehot = as_bf16(iota((step, CHIPS * BLOCK), 0) + i * step == pos_row)
-        out_ref[i * step:(i + 1) * step, :] = dot(onehot, x).astype(bf16)
-
-
-def column_blocks(core):
-    for q in ((0,) if core == 0 else (1, 2, 3)):
-        for first in range(0, CAPS[q], LANES):
-            yield q, first
-
-
-def gram_kernel(where_ref, a_ref, b_ref, meta_ref, out0, out1, out2, out3, part_ref):
+    core = where_ref[3]
+    for first, rows, *offsets in SEGMENTS:
+        onehot = as_bf16(iota((rows, CHIPS * BLOCK), 0) + first == pos_row)
+        part = dot(onehot, x).astype(bf16)
+        for me in range(2):
+            @pl.when(core == me)
+            def _():
+                for share, at in enumerate(offsets):
+                    if at is not None:
+                        (mine_ref if share == me else send_ref)[at:at + rows, :] = part
+
+
+def blocks_of(core):
+    for q, first in SHARES[core]:
+        at = BASES[core][q] + first
+        yield q, first, pl.ds(at, CAPS[q] - first), pl.ds(at, LANES)
+
+
+RAW_ROWS = max(sum(CAPS[q] - first for q, first in share) for share in SHARES)
+
+
+def own_kernel(where_ref, x_ref, raw_ref):
+    for core in range(2):
+        @pl.when(where_ref[3] == core)
+        def _():
+            at = 0
+            for q, first, left, right in blocks_of(core):
+                rows = CAPS[q] - first
+                raw_ref[at:at + rows, :] = dot_last(x_ref[left, :], x_ref[right, :])
+                at += rows
+
+
+def length_of(size, first):
+    return jnp.maximum(((size + HALF - 1) >> 6) - first // HALF, 0)
+
+
+def gram_kernel(where_ref, meta_ref, x_ref, raw_ref, out0, out1, out2, out3, part_ref):
     y, c = where_ref[2], where_ref[3]
+    part_ref[...] = jnp.full(part_ref.shape, -4.0, f32)
     for core in range(2):
         @pl.when(c == core)
         def _():
-            at = 0
-            for q, first in column_blocks(core):
+            at, to = 0, jnp.zeros((), i32)
+            for q, first, left, right in blocks_of(core):
                 rows = CAPS[q] - first
-                left = pl.ds(STARTS[q] + first, rows)
-                right = pl.ds(STARTS[q] + first, LANES)
-                score = dot_last(a_ref[left, :], a_ref[right, :]) + dot_last(b_ref[left, :], b_ref[right, :])
-                size = meta_ref[q:q + 1, :].astype(i32)
+                score = raw_ref[at:at + rows, :] + dot_last(x_ref[left, :], x_ref[right, :])
+                at += rows
+                size = meta_ref[q, 0]
                 i, j = iota(score.shape, 0), iota(score.shape, 1)
-                keep = (i + first < size) & (j + first < size) & (i != j)
-                score = jnp.where(keep, score, -4.0)
-                done = 0
-                while done < rows:
-                    chunk, offset = divmod(at + done, CHUNK)
-                    take = min(rows - done, CHUNK - offset)
-                    part_ref[chunk, offset:offset + take, :] = score[done:done + take]
-                    done += take
-                at += rows
-            while at < PARTIAL:
-                chunk, offset = divmod(at, CHUNK)
-                part_ref[chunk, offset:offset + HALF, :] = jnp.full((HALF, LANES), -4.0, f32)
-                at += HALF
+                keep = (i < size - first) & (j < size - first) & (i != j)
+                part_ref[pl.ds(pl.multiple_of(to, HALF), rows), :] = jnp.where(keep, score, -4.0)
+                to = jnp.minimum(to + HALF * length_of(size, first), PARTIAL)
     for shift, out in enumerate((out0, out1, out2, out3)):
-        out[...] = part_ref[lax.rem(y + shift, 4)]
+        out[...] = part_ref[pl.ds(pl.multiple_of(lax.rem(y + shift, 4) * CHUNK, HALF), CHUNK), :]
 
 
 FIRST_ROW = (0, 6, 10, 13)
 
 
-def tables():
-    rows, odd, cols = [], [], []
-    for core in range(2):
-        have = []
-        for q, first in column_blocks(core):
-            for r in range(first, CAPS[q], HALF):
-                have.append((FIRST_ROW[q] + r // LANES, r // HALF % 2, FIRST_ROW[q] + first // LANES))
-        have += [(15, 0, 15)] * (36 - len(have))
-        for table, column in ((rows, 0), (odd, 1), (cols, 2)):
-            table += [h[column] for h in have]
-    return jnp.asarray(rows + odd + cols, i32)
-
-
-def max_kernel(where_ref, table_ref, p0, p1, p2, p3, pos_ref, out_ref, best_ref):
+def max_kernel(where_ref, meta_ref, p0, p1, p2, p3, pos_ref, out_ref, best_ref):
     y, c = where_ref[2], where_ref[3]
     best_ref[...] = jnp.full(best_ref.shape, -1.0, f32)
     sub, lane = iota((HALF, LANES), 0), iota((HALF, LANES), 1)
-    for t in range(CHUNK // HALF):
+    blocks = []
+    for core, share in enumerate(SHARES):
+        at = jnp.zeros((), i32)
+        for q, first in share:
+            length = length_of(meta_ref[q, 0], first)
+            col = FIRST_ROW[q] + first // LANES
+            blocks.append((jnp.where((c == core) & (length > 0), at, PARTIAL), col, 2 * col - at))
+            at = at + length
+    for t in range(COUNT):
         at = slice(t * HALF, (t + 1) * HALF)
         block = (p0[at, :] + p1[at, :]) + (p2[at, :] + p3[at, :])
-        index = c * 36 + y * 9 + t
-        row, odd, col = (table_ref[72 * i + index] for i in range(3))
+        index = y * COUNT + t
+        col, shift = jnp.asarray(15, i32), jnp.asarray(0, i32)
+        for start, block_col, block_shift in blocks:
+            inside = index >= start
+            col, shift = jnp.where(inside, block_col, col), jnp.where(inside, block_shift, shift)
+        row = jnp.minimum(jnp.maximum(index + shift, 0), 31)
         along = jnp.max(block, axis=1, keepdims=True)
-        along = jnp.max(jnp.where(sub + odd * HALF == lane, along, -1.0), axis=0, keepdims=True)
+        along = jnp.max(jnp.where(sub + (row & 1) * HALF == lane, along, -1.0), axis=0, keepdims=True)
+        row = row >> 1
         best_ref[pl.ds(row, 1), :] = jnp.maximum(best_ref[pl.ds(row, 1), :], along)
         down = jnp.max(block, axis=0, keepdims=True)
         best_ref[pl.ds(col, 1), :] = jnp.maximum(best_ref[pl.ds(col, 1), :], down)
@@ -304,44 +335,56 @@
     got = lax.ppermute(send, "c", [(0, 1), (1, 0)])
     packed, code = pl.pallas_call(
         pack_kernel,
-        out_shape=(shape((CHIPS, BLOCK, WIDTH), bf16), shape((8, ROWS), i32)),
-        in_specs=[SCALARS, WHOLE, WHOLE], out_specs=(WHOLE, WHOLE), compiler_params=params(20), name="pack",
+        out_shape=(shape((BINS, 4, BLOCK, WIDTH), bf16), shape((8, ROWS), i32)),
+        in_specs=[SCALARS, WHOLE, WHOLE], out_specs=(pl.BlockSpec(memory_space=pltpu.HBM), WHOLE),
+        scratch_shapes=[pltpu.VMEM((4, BINS, BLOCK, WIDTH), bf16), pltpu.SemaphoreType.DMA((4,))],
+        compiler_params=params(20), name="pack",
     )(where, keep, got)
-    packed = lax.all_to_all(packed, ("x", "z", "y"), 0, 0, tiled=True)
-    ordered, pos, meta = pl.pallas_call(
+    packed = lax.all_to_all(packed.reshape(CHIPS, BLOCK, WIDTH), ("x", "z", "y"), 0, 0, tiled=True)
+    mine, send, pos, meta = pl.pallas_call(
         sort_kernel,
-        out_shape=(shape((SORTED, WIDTH), bf16), shape((CHIPS, LANES), i32), shape((8, LANES), f32)),
-        in_specs=[SCALARS, WHOLE], out_specs=(WHOLE, WHOLE, WHOLE), compiler_params=params(28), name="sort",
+        out_shape=(
+            shape((SHARE_ROWS, WIDTH), bf16), shape((SHARE_ROWS, WIDTH), bf16),
+            shape((CHIPS, LANES), i32), shape((8, LANES), i32),
+        ),
+        in_specs=[SCALARS, WHOLE], out_specs=(WHOLE,) * 4, compiler_params=params(28), name="sort",
     )(where, packed)
-
-    def within_bins(embeddings, cluster_ids):
-        other = lax.ppermute(ordered, "c", [(0, 1), (1, 0)])
-        partial = pl.pallas_call(
-            gram_kernel,
-            out_shape=[shape((CHUNK, LANES), f32)] * 4,
-            in_specs=[SCALARS, WHOLE, WHOLE, WHOLE], out_specs=[WHOLE] * 4,
-            scratch_shapes=[pltpu.VMEM((4, CHUNK, LANES), f32)],
-            compiler_params=params(20), name="gram",
-        )(where, ordered, other, meta)
-        arrived = [partial[0]] + [
-            lax.ppermute(partial[s], "y", [(i, (i + s) % 4) for i in range(4)]) for s in (1, 2, 3)
-        ]
-        best = pl.pallas_call(
-            max_kernel,
-            out_shape=shape((CHIPS, LANES), f32),
-            in_specs=[SCALARS] * 2 + [WHOLE] * 5, out_specs=WHOLE,
-            scratch_shapes=[pltpu.VMEM((16, LANES), f32)],
-            compiler_params=params(8), name="maxima",
-        )(where, tables(), *arrived, pos)
-        sent = jnp.broadcast_to(best[:, None, :], (CHIPS, 2, LANES)).reshape(2 * CHIPS, 1, LANES)
-        back = lax.all_to_all(sent, ("x", "z", "y", "c"), 0, 0, tiled=True)
-        return pl.pallas_call(
-            pick_kernel,
-            out_shape=shape((1, ROWS), f32),
-            in_specs=[SCALARS, WHOLE, WHOLE], out_specs=WHOLE, compiler_params=params(8), name="pick",
-        )(where, back.reshape(2 * CHIPS, LANES), code).reshape(ROWS)
-
-    return lax.cond(meta[4, 0] < 0.5, within_bins, gather_groups, embeddings, cluster_ids)
+    other = lax.ppermute(send, "c", [(0, 1), (1, 0)])
+    raw = pl.pallas_call(
+        own_kernel, out_shape=shape((RAW_ROWS, LANES), f32),
+        in_specs=[SCALARS, WHOLE], out_specs=WHOLE, compiler_params=params(12), name="own",
+        cost_estimate=pl.CostEstimate(flops=2 * RAW_ROWS * LANES * WIDTH, bytes_accessed=3 << 20, transcendentals=0),
+    )(where, mine)
+    partial = pl.pallas_call(
+        gram_kernel,
+        out_shape=[shape((CHUNK, LANES), f32)] * 4,
+        in_specs=[SCALARS, SCALARS, WHOLE, WHOLE], out_specs=[WHOLE] * 4,
+        scratch_shapes=[pltpu.VMEM((PARTIAL + CAPS[0], LANES), f32)],
+        compiler_params=params(16), name="gram",
+    )(where, meta, other, raw)
+    arrived = [partial[0]] + [
+        lax.ppermute(partial[s], "y", [(i, (i + s) % 4) for i in range(4)]) for s in (1, 2, 3)
+    ]
+    best = pl.pallas_call(
+        max_kernel,
+        out_shape=shape((CHIPS, LANES), f32),
+        in_specs=[SCALARS] * 2 + [WHOLE] * 5, out_specs=WHOLE,
+        scratch_shapes=[pltpu.VMEM((16, LANES), f32)],
+        compiler_params=params(8), name="maxima",
+    )(where, meta, *arrived, pos)
+    sent = jnp.broadcast_to(best[:, None, :], (CHIPS, 2, LANES)).reshape(2 * CHIPS, 1, LANES)
+    back = lax.all_to_all(sent, ("x", "z", "y", "c"), 0, 0, tiled=True)
+    fitted = pl.pallas_call(
+        pick_kernel,
+        out_shape=shape((1, ROWS), f32),
+        in_specs=[SCALARS, WHOLE, WHOLE], out_specs=WHOLE, compiler_params=params(8), name="pick",
+    )(where, back.reshape(2 * CHIPS, LANES), code).reshape(ROWS)
+    return lax.cond(
+        meta[4, 0] == 0,
+        lambda fitted, embeddings, cluster_ids: fitted,
+        lambda fitted, embeddings, cluster_ids: gather_groups(embeddings, cluster_ids),
+        fitted, embeddings, cluster_ids,
+    )
 
 
 def solution(mesh):

time: 112 us -> 100 us (0.89)
  waiting for transfers between devices: 52 us -> 21.3 us
  blocking collectives: 21.1 us -> 45.5 us
  starting transfers between devices: 18.8 us -> 14 us
    all_to_all x1, waiting for transfers between devices: 33.8 us -> 8.31 us  [on_device(): back = lax.all_to_all(sent, ('x', 'z', 'y', 'c'), 0, 0, tiled=True)]
    all_to_all x1, blocking collectives: 21.1 us -> 45.5 us  [on_device(): lax.all_to_all(packed.reshape(CHIPS, BLOCK, WIDTH), ('x', 'z', 'y'), 0, 0...]
    ppermute x4, waiting for transfers between devices: 16.5 us -> 11.4 us  [the longest x3 10.3 us: on_device(): lax.ppermute(partial[s], 'y', [(i, (i + s) % 4) for i in range(4)])]
    all_to_all x1, starting transfers between devices: 11.2 us -> 7.11 us  [on_device(): back = lax.all_to_all(sent, ('x', 'z', 'y', 'c'), 0, 0, tiled=True)]
    unnamed x6, local copies, waits for them, and re-layouts: 2.03 us -> 0.52 us
    pallas_call x5 -> x6, Pallas kernels: 14.1 us -> 14.5 us  [the longest x1 6.96 us: on_device(): pl.pallas_call(sort_kernel, out_shape=(shape((SHARE_ROWS, WIDTH), bf16),...]
  transfers between devices with their start and end apart: 6 -> 6, of which waited for: 5 -> 5; matrix products, arithmetic and copies ran while one was open for 0% -> 1% of each run, Pallas kernels for 0% -> 1%
where the time goes in v4:
time: 100 us; the launch traced here: 99.8 us
  blocking collectives  45.5 us (46%)
  waiting for transfers between devices  21.3 us (21%)
  Pallas kernels  16.4 us (16%)
  starting transfers between devices  14 us (14%)
  local copies, waits for them, and re-layouts  1.68 us (2%)
    all_to_all x1, blocking collectives, on_device(): lax.all_to_all(packed.reshape(CHIPS, BLOCK, WIDTH), ('x', 'z', 'y'), 0, 0...  45.5 us
    ppermute x3, waiting for transfers between devices, on_device(): lax.ppermute(partial[s], 'y', [(i, (i + s) % 4) for i in range(4)])  10.3 us
    all_to_all x1, waiting for transfers between devices, on_device(): back = lax.all_to_all(sent, ('x', 'z', 'y', 'c'), 0, 0, tiled=True)  8.31 us
    all_to_all x1, starting transfers between devices, on_device(): back = lax.all_to_all(sent, ('x', 'z', 'y', 'c'), 0, 0, tiled=True)  7.11 us
    pallas_call x1, Pallas kernels, on_device(): pl.pallas_call(sort_kernel, out_shape=(shape((SHARE_ROWS, WIDTH), bf16),...  6.96 us
    ppermute x3, starting transfers between devices, on_device(): lax.ppermute(partial[s], 'y', [(i, (i + s) % 4) for i in range(4)])  3.25 us
    pallas_call x1, Pallas kernels, on_device(): pl.pallas_call(pack_kernel, out_shape=(shape((BINS, 4, BLOCK, WIDTH), bf1...  2.39 us
    ppermute x1, starting transfers between devices, on_device(): other = lax.ppermute(send, 'c', [(0, 1), (1, 0)])  2.15 us
  transfers between devices with their start and end apart: 6, of which 5 were waited for; matrix products, arithmetic and copies ran while one was open for 1% of the time, Pallas kernels for 1%

profile of v4, /device:TPU:1, one launch (start us, length us, event | category | flops | bytes accessed | tf_op | source)
XLA Modules:
  0.0 99.8 jit_solution(9525436083300244098)
XLA Ops:
  0.0 0.1 pad_add_fusion.where_ref
  0.1 1.9 %unit.1 = (bf16[144,2048]{1,0:T(8,128)(2,1)S(1)}, bf16[144,2048]{1,0:T(8,128)(2,1)S(1)}) custom-call(s32[4]{0:T(128)S(1)} %pad_add_fusion.where_ref, f32[128,4096]{1,0:T(8,128)} %x_ref.1, s32[1,128]{1,0:T(1,128)} %bitcast.30), custom_call_target="tpu_custom_call" | custom-call | tf_op jit(solution)/shard_map/unit/pallas_call | solution.py:331
  2.0 1.5 %collective-permute-start = (bf16[144,2048]{1,0:T(8,128)(2,1)S(1)}, bf16[144,2048]{1,0:T(8,128)(2,1)S(1)}, u32[]{:S(2)}, u32[]{:S(2)}) collective-permute-start(bf16[144,2048]{1,0:T(8,128)(2,1)S(1)} %get-tuple-element.94), channel_id=1, source_target_pairs={{0,1},{1,0},{2,3},{3,2},{4,5},{5,4},{6,7},{7,6},{8,9},{9,8},{10,11... | collective-permute-start | bytes 1769480 | tf_op jit(solution)/shard_map/ppermute | solution.py:335
  3.5 1.6 %collective-permute-done.got_ref = bf16[144,2048]{1,0:T(8,128)(2,1)S(1)} collective-permute-done((bf16[144,2048]{1,0:T(8,128)(2,1)S(1)}, bf16[144,2048]{1,0:T(8,128)(2,1)S(1)}, u32[]{:S(2)}, u32[]{:S(2)}) %collective-permute-start) | collective-permute-done | bytes 589856 | tf_op jit(solution)/shard_map/ppermute | solution.py:335
  5.1 2.4 %pack.1 = (bf16[16,4,40,512]{3,2,1,0:T(8,128)(2,1)S(1)}, s32[8,128]{1,0:T(8,128)S(1)}) custom-call(s32[4]{0:T(128)S(1)} %pad_add_fusion.where_ref, bf16[144,2048]{1,0:T(8,128)(2,1)S(1)} %get-tuple-element.93.keep_ref, bf16[144,2048]{1,0:T(8,128)(2,1)S(1)} %collective-permute-done.got_ref), custom_call_target="tpu_custom_call" | custom-call | tf_op jit(solution)/shard_map/pack/pallas_call | solution.py:336
  7.5 45.5 %all_to_all.51.x_ref = bf16[64,40,512]{2,1,0:T(8,128)(2,1)S(1)} all-to-all(bf16[64,40,512]{2,1,0:T(8,128)(2,1)S(1)} %bitcast.28), channel_id=1, replica_groups=mesh['x'=4,'z'=4,'y'=4,'c'=2] {'x','z','y'}, dimensions={0} | all-to-all | bytes 5242880 | tf_op jit(solution)/shard_map/all_to_all | solution.py:343
  53.0 7.0 %sort.1 = (bf16[1216,512]{1,0:T(8,128)(2,1)S(1)}, bf16[1216,512]{1,0:T(8,128)(2,1)S(1)}, s32[64,128]{1,0:T(8,128)S(1)}, s32[8,128]{1,0:T(8,128)S(1)}) custom-call(s32[4]{0:T(128)S(1)} %pad_add_fusion.where_ref, bf16[64,40,512]{2,1,0:T(8,128)(2,1)S(1)} %all_to_all.51.x_ref), custom_call_target="tpu_custom_call" | custom-call | tf_op jit(solution)/shard_map/sort/pallas_call | solution.py:344
  60.0 2.1 %collective-permute-start.1 = (bf16[1216,512]{1,0:T(8,128)(2,1)S(1)}, bf16[1216,512]{1,0:T(8,128)(2,1)S(1)}, u32[]{:S(2)}, u32[]{:S(2)}) collective-permute-start(bf16[1216,512]{1,0:T(8,128)(2,1)S(1)} %get-tuple-element.97), channel_id=1, source_target_pairs={{0,1},{1,0},{2,3},{3,2},{4,5},{5,4},{6,7},{7,6},{8,9},{9,8},{10,11... | collective-permute-start | bytes 3735560 | tf_op jit(solution)/shard_map/ppermute | solution.py:352
  62.1 1.4 %own.1.raw_ref = f32[2560,128]{1,0:T(8,128)S(1)} custom-call(s32[4]{0:T(128)S(1)} %pad_add_fusion.where_ref, bf16[1216,512]{1,0:T(8,128)(2,1)S(1)} %get-tuple-element.98.x_ref), custom_call_target="tpu_custom_call" | custom-call | flops 335544320 | bytes 3145728 | tf_op jit(solution)/shard_map/own/pallas_call | solution.py:353
  63.6 0.0 copy-start
  63.6 0.0 copy-start.1
  63.6 1.1 %collective-permute-done.1.x_ref = bf16[1216,512]{1,0:T(8,128)(2,1)S(1)} collective-permute-done((bf16[1216,512]{1,0:T(8,128)(2,1)S(1)}, bf16[1216,512]{1,0:T(8,128)(2,1)S(1)}, u32[]{:S(2)}, u32[]{:S(2)}) %collective-permute-start.1) | collective-permute-done | bytes 1245216 | tf_op jit(solution)/shard_map/ppermute | solution.py:352
  64.7 1.6 %gram.1 = (f32[448,128]{1,0:T(8,128)S(1)}, f32[448,128]{1,0:T(8,128)S(1)}, f32[448,128]{1,0:T(8,128)S(1)}, f32[448,128]{1,0:T(8,128)S(1)}) custom-call(s32[4]{0:T(128)S(1)} %pad_add_fusion.where_ref, s32[8,128]{1,0:T(8,128)S(1)} %get-tuple-element.96.meta_ref, bf16[1216,512]{1,0:T(8,128)(2,1)S(1)} %collective-permute-done.1.x_ref, f32[2560,128]{1,0:T(8,128)S(1)} %own.1.raw_ref), custom_call_target="tpu_custom_call" | custom-call | tf_op jit(solution)/shard_map/gram/pallas_call | solution.py:358
  66.3 0.4 collective-permute-start.2
  66.8 1.5 %collective-permute-start.3 = (f32[448,128]{1,0:T(8,128)S(1)}, f32[448,128]{1,0:T(8,128)S(1)}, u32[]{:S(2)}, u32[]{:S(2)}) collective-permute-start(f32[448,128]{1,0:T(8,128)S(1)} %get-tuple-element.101), channel_id=1, source_target_pairs={{0,4},{2,6},{4,0},{6,2},{1,5},{3,7},{5,1},{7,3},{8,12},{10,14},{12... | collective-permute-start | bytes 688136 | tf_op jit(solution)/shard_map/ppermute | solution.py:366
  68.3 1.3 %collective-permute-start.4 = (f32[448,128]{1,0:T(8,128)S(1)}, f32[448,128]{1,0:T(8,128)S(1)}, u32[]{:S(2)}, u32[]{:S(2)}) collective-permute-start(f32[448,128]{1,0:T(8,128)S(1)} %get-tuple-element.102), channel_id=1, source_target_pairs={{0,6},{2,0},{4,2},{6,4},{1,7},{3,1},{5,3},{7,5},{8,14},{10,8},{12,... | collective-permute-start | bytes 688136 | tf_op jit(solution)/shard_map/ppermute | solution.py:366
  69.6 10.0 %collective-permute-done.2.p1 = f32[448,128]{1,0:T(8,128)S(1)} collective-permute-done((f32[448,128]{1,0:T(8,128)S(1)}, f32[448,128]{1,0:T(8,128)S(1)}, u32[]{:S(2)}, u32[]{:S(2)}) %collective-permute-start.2) | collective-permute-done | bytes 229408 | tf_op jit(solution)/shard_map/ppermute | solution.py:366
  79.6 0.0 collective-permute-done.3.p2
  79.6 0.3 collective-permute-done.4.p3
  79.9 1.2 %maxima.1 = f32[64,128]{1,0:T(8,128)S(1)} custom-call(s32[4]{0:T(128)S(1)} %pad_add_fusion.where_ref, s32[8,128]{1,0:T(8,128)S(1)} %get-tuple-element.96.meta_ref, f32[448,128]{1,0:T(8,128)S(1)} %get-tuple-element.99.p0, f32[448,128]{1,0:T(8,128)S(1)} %collective-permute-done.2.p1, f32[448,128]{1,0:T(8,128)S(1)} %collective-permute-done.3.p2, ...), custom_call_target="tpu_custom_call" | custom-call | tf_op jit(solution)/shard_map/maxima/pallas_call | solution.py:368
  81.1 0.7 broadcast_in_dim.77
  81.8 7.1 %all-to-all-start.6 = ((f32[128,1,128]{2,1,0:T(1,128)}), f32[128,1,128]{2,1,0:T(1,128)S(1)}, u32[]{:S(2)}, u32[]{:S(2)}) async-start(f32[128,1,128]{2,1,0:T(1,128)} %bitcast.15), calls=%async_computation.6 | async-start | bytes 131072 | tf_op jit(solution)/shard_map/all_to_all | solution.py:376
  88.9 0.5 slice.3
  90.1 8.3 %all-to-all-done.6 = f32[128,1,128]{2,1,0:T(1,128)S(1)} async-done(((f32[128,1,128]{2,1,0:T(1,128)}), f32[128,1,128]{2,1,0:T(1,128)S(1)}, u32[]{:S(2)}, u32[]{:S(2)}) %all-to-all-start.6) | async-done | bytes 65568 | tf_op jit(solution)/shard_map/all_to_all | solution.py:376
  98.4 0.9 pick.1
  99.2 0.0 copy-done
  99.2 0.0 copy-done.1
  99.2 0.0 copy-start.2
  99.3 0.5 copy-done.2
  (1 shorter events, 0.0 us)
Async XLA Ops:
  2.0 3.1 %collective-permute-start = (bf16[144,2048]{1,0:T(8,128)(2,1)S(1)}, bf16[144,2048]{1,0:T(8,128)(2,1)S(1)}, u32[]{:S(2)}, u32[]{:S(2)}) collective-permute-start(bf16[144,2048]{1,0:T(8,128)(2,1)S(1)} %get-tuple-element.94), channel_id=1, source_target_pairs={{0,1},{1,0},{2,3},{3,2},{4,5},{5,4},{6,7},{7,6},{8,9},{9,8},{10,11... | collective-permute-start | bytes 1769480 | tf_op jit(solution)/shard_map/ppermute | solution.py:335
  60.0 4.7 %collective-permute-start.1 = (bf16[1216,512]{1,0:T(8,128)(2,1)S(1)}, bf16[1216,512]{1,0:T(8,128)(2,1)S(1)}, u32[]{:S(2)}, u32[]{:S(2)}) collective-permute-start(bf16[1216,512]{1,0:T(8,128)(2,1)S(1)} %get-tuple-element.97), channel_id=1, source_target_pairs={{0,1},{1,0},{2,3},{3,2},{4,5},{5,4},{6,7},{7,6},{8,9},{9,8},{10,11... | collective-permute-start | bytes 3735560 | tf_op jit(solution)/shard_map/ppermute | solution.py:352
  63.6 35.7 %copy-start = (s32[128]{0:T(128)S(1)}, s32[128]{0:T(128)}, u32[]{:S(2)}) copy-start(s32[128]{0:T(128)} %param.7) | copy-start | bytes 1540
  63.6 35.6 %copy-start.1 = (f32[128,4096]{1,0:T(8,128)S(1)}, f32[128,4096]{1,0:T(8,128)}, u32[]{:S(2)}) copy-start(f32[128,4096]{1,0:T(8,128)} %x_ref.1) | copy-start | bytes 6291460
  66.3 13.3 %collective-permute-start.2 = (f32[448,128]{1,0:T(8,128)S(1)}, f32[448,128]{1,0:T(8,128)S(1)}, u32[]{:S(2)}, u32[]{:S(2)}) collective-permute-start(f32[448,128]{1,0:T(8,128)S(1)} %get-tuple-element.100), channel_id=1, source_target_pairs={{0,2},{2,4},{4,6},{6,0},{1,3},{3,5},{5,7},{7,1},{8,10},{10,12},{12... | collective-permute-start | bytes 688136 | tf_op jit(solution)/shard_map/ppermute | solution.py:366
  66.8 12.8 %collective-permute-start.3 = (f32[448,128]{1,0:T(8,128)S(1)}, f32[448,128]{1,0:T(8,128)S(1)}, u32[]{:S(2)}, u32[]{:S(2)}) collective-permute-start(f32[448,128]{1,0:T(8,128)S(1)} %get-tuple-element.101), channel_id=1, source_target_pairs={{0,4},{2,6},{4,0},{6,2},{1,5},{3,7},{5,1},{7,3},{8,12},{10,14},{12... | collective-permute-start | bytes 688136 | tf_op jit(solution)/shard_map/ppermute | solution.py:366
  68.3 11.6 %collective-permute-start.4 = (f32[448,128]{1,0:T(8,128)S(1)}, f32[448,128]{1,0:T(8,128)S(1)}, u32[]{:S(2)}, u32[]{:S(2)}) collective-permute-start(f32[448,128]{1,0:T(8,128)S(1)} %get-tuple-element.102), channel_id=1, source_target_pairs={{0,6},{2,0},{4,2},{6,4},{1,7},{3,1},{5,3},{7,5},{8,14},{10,8},{12,... | collective-permute-start | bytes 688136 | tf_op jit(solution)/shard_map/ppermute | solution.py:366
  81.8 16.6 %all-to-all-start.6 = ((f32[128,1,128]{2,1,0:T(1,128)}), f32[128,1,128]{2,1,0:T(1,128)S(1)}, u32[]{:S(2)}, u32[]{:S(2)}) async-start(f32[128,1,128]{2,1,0:T(1,128)} %bitcast.15), calls=%async_computation.6 | async-start | bytes 131072 | tf_op jit(solution)/shard_map/all_to_all | solution.py:376
  99.2 0.5 copy-start.2

commit v5 on v4

--- a/solution.py
+++ b/solution.py
@@ -63,19 +63,32 @@
     return 4 * col + ((row - residue) & 3)
 
 
-def unit_kernel(where_ref, x_ref, ids_ref, keep_ref, send_ref):
+PIECE = 32
+
+
+def unit_kernel(where_ref, x_ref, ids_ref, keep_ref, send_ref, rows_ref, sems):
     c = where_ref[3]
-    x = x_ref[...]
-    scale = lax.rsqrt(jnp.sum(x * x, axis=1, keepdims=True) + 1e-06)
+    copies = [
+        pltpu.make_async_copy(x_ref.at[pl.ds(at, PIECE)], rows_ref.at[pl.ds(at, PIECE)], sems.at[at // PIECE])
+        for at in range(0, ROWS, PIECE)
+    ]
+    for copy in copies:
+        copy.start()
     ids = jnp.concatenate([ids_ref[...].astype(f32), jnp.zeros((1, HALF_WIDTH - ROWS), f32)], axis=1)
     ids = jnp.broadcast_to(ids, (LABEL_ROWS, HALF_WIDTH)).astype(bf16)
-    for half, out_ref in ((c, keep_ref), (1 - c, send_ref)):
-        columns = pl.ds(pl.multiple_of(half * HALF_WIDTH, HALF_WIDTH), HALF_WIDTH)
-        out_ref[:ROWS, :] = (x_ref[:, columns] * scale).astype(bf16)
-        out_ref[ROWS:, :] = ids
-
-
-def pack_kernel(where_ref, keep_ref, got_ref, out_ref, code_ref, block_ref, sems):
+    keep_ref[ROWS:, :] = ids
+    send_ref[ROWS:, :] = ids
+    for piece, copy in enumerate(copies):
+        at = slice(piece * PIECE, (piece + 1) * PIECE)
+        copy.wait()
+        x = rows_ref[at, :]
+        scale = lax.rsqrt(jnp.sum(x * x, axis=1, keepdims=True) + 1e-06)
+        for half, out_ref in ((c, keep_ref), (1 - c, send_ref)):
+            columns = pl.ds(pl.multiple_of(half * HALF_WIDTH, HALF_WIDTH), HALF_WIDTH)
+            out_ref[at, :] = (rows_ref[at, columns] * scale).astype(bf16)
+
+
+def pack_kernel(where_ref, keep_ref, got_ref, out_ref, code_ref):
     first = where_ref[3] == 0
     kept = jnp.max(keep_ref[ROWS:, :ROWS].astype(f32), axis=0, keepdims=True)
     got = jnp.max(got_ref[ROWS:, :ROWS].astype(f32), axis=0, keepdims=True)
@@ -106,13 +119,10 @@
         packed = dot(onehot, x)
         for b in range(BINS):
             extra = jnp.concatenate([names[b:b + 1], counts, jnp.zeros((1, 2 * LANES), f32)], axis=1)
-            block_ref[y, b] = jnp.where(is_last, extra, packed[b * BLOCK:(b + 1) * BLOCK]).astype(bf16)
-        pltpu.make_async_copy(block_ref.at[y], out_ref.at[:, y], sems.at[y]).start()
-    for y in range(4):
-        pltpu.make_async_copy(block_ref.at[y], out_ref.at[:, y], sems.at[y]).wait()
-
-
-def sort_kernel(where_ref, x_ref, mine_ref, send_ref, pos_ref, meta_ref):
+            out_ref[4 * b + y] = jnp.where(is_last, extra, packed[b * BLOCK:(b + 1) * BLOCK]).astype(bf16)
+
+
+def send_kernel(where_ref, x_ref, send_ref, line_ref, pos_ref, meta_ref):
     mine = where_ref[0] * 4 + where_ref[1]
     tail = x_ref[:, BLOCK - 8:, :2 * LANES].astype(f32)
     tail = jnp.max(jnp.where(iota(tail.shape, 1) == 7, tail, 0.0), axis=1)
@@ -167,17 +177,20 @@
         rows = jnp.concatenate([rows, jnp.zeros((8, per * BLOCK - LANES), f32)], axis=1)
         lined = lined + (pltpu.roll(rows, t * BLOCK, 1) if t else rows)
     pos_row = jnp.concatenate([lined[g:g + 1] for g in range(groups)], axis=1).astype(i32) - 1
+    line_ref[...] = jnp.broadcast_to(pos_row, line_ref.shape)
     x = x_ref[...].reshape(CHIPS * BLOCK, WIDTH)
-    core = where_ref[3]
-    for first, rows, *offsets in SEGMENTS:
-        onehot = as_bf16(iota((rows, CHIPS * BLOCK), 0) + first == pos_row)
-        part = dot(onehot, x).astype(bf16)
-        for me in range(2):
-            @pl.when(core == me)
-            def _():
-                for share, at in enumerate(offsets):
-                    if at is not None:
-                        (mine_ref if share == me else send_ref)[at:at + rows, :] = part
+    for me in range(2):
+        @pl.when(where_ref[3] == me)
+        def _():
+            for segment in SEGMENTS:
+                at = segment[2 + 1 - me]
+                if at is not None:
+                    send_ref[at:at + segment[1], :] = sorted_rows(segment, pos_row, x)
+
+
+def sorted_rows(segment, pos_row, x):
+    onehot = as_bf16(iota((segment[1], CHIPS * BLOCK), 0) + segment[0] == pos_row)
+    return dot(onehot, x).astype(bf16)
 
 
 def blocks_of(core):
@@ -189,14 +202,24 @@
 RAW_ROWS = max(sum(CAPS[q] - first for q, first in share) for share in SHARES)
 
 
-def own_kernel(where_ref, x_ref, raw_ref):
+def own_kernel(where_ref, x_ref, line_ref, send_ref, raw_ref, mine_ref):
+    x = x_ref[...].reshape(CHIPS * BLOCK, WIDTH)
+    pos_row = line_ref[:1, :]
     for core in range(2):
         @pl.when(where_ref[3] == core)
         def _():
+            for segment in SEGMENTS:
+                at, sent = segment[2 + core], segment[2 + 1 - core]
+                if at is not None:
+                    rows = segment[1]
+                    both = sent is not None
+                    mine_ref[at:at + rows, :] = (
+                        send_ref[sent:sent + rows, :] if both else sorted_rows(segment, pos_row, x)
+                    )
             at = 0
             for q, first, left, right in blocks_of(core):
                 rows = CAPS[q] - first
-                raw_ref[at:at + rows, :] = dot_last(x_ref[left, :], x_ref[right, :])
+                raw_ref[at:at + rows, :] = dot_last(mine_ref[left, :], mine_ref[right, :])
                 at += rows
 
 
@@ -263,7 +286,9 @@
         value = jnp.broadcast_to(best_ref[r:r + 1, :], pos.shape)
         value = jnp.take_along_axis(value, lane, axis=1, mode="promise_in_bounds")
         out = jnp.where(row == r, value, out)
-    out_ref[...] = out
+    for s in range(CHIPS):
+        out_ref[2 * s] = out[s:s + 1]
+        out_ref[2 * s + 1] = out[s:s + 1]
 
 
 def pick_kernel(where_ref, v_ref, code_ref, out_ref):
@@ -330,31 +355,34 @@
     half = shape((ROWS + LABEL_ROWS, HALF_WIDTH), bf16)
     keep, send = pl.pallas_call(
         unit_kernel, out_shape=(half, half),
-        in_specs=[SCALARS, WHOLE, WHOLE], out_specs=(WHOLE, WHOLE), compiler_params=params(12), name="unit",
+        in_specs=[SCALARS, pl.BlockSpec(memory_space=pl.ANY), WHOLE], out_specs=(WHOLE, WHOLE),
+        scratch_shapes=[pltpu.VMEM(embeddings.shape, f32), pltpu.SemaphoreType.DMA((ROWS // PIECE,))],
+        compiler_params=params(12), name="unit",
     )(where, embeddings, cluster_ids.reshape(1, ROWS))
     got = lax.ppermute(send, "c", [(0, 1), (1, 0)])
     packed, code = pl.pallas_call(
         pack_kernel,
-        out_shape=(shape((BINS, 4, BLOCK, WIDTH), bf16), shape((8, ROWS), i32)),
-        in_specs=[SCALARS, WHOLE, WHOLE], out_specs=(pl.BlockSpec(memory_space=pltpu.HBM), WHOLE),
-        scratch_shapes=[pltpu.VMEM((4, BINS, BLOCK, WIDTH), bf16), pltpu.SemaphoreType.DMA((4,))],
-        compiler_params=params(20), name="pack",
+        out_shape=(shape((CHIPS, BLOCK, WIDTH), bf16), shape((8, ROWS), i32)),
+        in_specs=[SCALARS, WHOLE, WHOLE], out_specs=(WHOLE, WHOLE), compiler_params=params(20), name="pack",
     )(where, keep, got)
-    packed = lax.all_to_all(packed.reshape(CHIPS, BLOCK, WIDTH), ("x", "z", "y"), 0, 0, tiled=True)
-    mine, send, pos, meta = pl.pallas_call(
-        sort_kernel,
+    packed = lax.all_to_all(packed, ("x", "z", "y"), 0, 0, tiled=True)
+    send, line, pos, meta = pl.pallas_call(
+        send_kernel,
         out_shape=(
-            shape((SHARE_ROWS, WIDTH), bf16), shape((SHARE_ROWS, WIDTH), bf16),
+            shape((SHARE_ROWS, WIDTH), bf16), shape((8, CHIPS * BLOCK), i32),
             shape((CHIPS, LANES), i32), shape((8, LANES), i32),
         ),
-        in_specs=[SCALARS, WHOLE], out_specs=(WHOLE,) * 4, compiler_params=params(28), name="sort",
+        in_specs=[SCALARS, WHOLE], out_specs=(WHOLE,) * 4, compiler_params=params(24), name="sort",
     )(where, packed)
     other = lax.ppermute(send, "c", [(0, 1), (1, 0)])
+    flops = 2 * LANES * WIDTH * (RAW_ROWS + 5 * CHIPS * BLOCK)
     raw = pl.pallas_call(
         own_kernel, out_shape=shape((RAW_ROWS, LANES), f32),
-        in_specs=[SCALARS, WHOLE], out_specs=WHOLE, compiler_params=params(12), name="own",
-        cost_estimate=pl.CostEstimate(flops=2 * RAW_ROWS * LANES * WIDTH, bytes_accessed=3 << 20, transcendentals=0),
-    )(where, mine)
+        in_specs=[SCALARS, WHOLE, WHOLE, WHOLE], out_specs=WHOLE,
+        scratch_shapes=[pltpu.VMEM((SHARE_ROWS, WIDTH), bf16)],
+        compiler_params=params(20), name="own",
+        cost_estimate=pl.CostEstimate(flops=flops, bytes_accessed=8 << 20, transcendentals=0),
+    )(where, packed, line, send)
     partial = pl.pallas_call(
         gram_kernel,
         out_shape=[shape((CHUNK, LANES), f32)] * 4,
@@ -367,13 +395,12 @@
     ]
     best = pl.pallas_call(
         max_kernel,
-        out_shape=shape((CHIPS, LANES), f32),
+        out_shape=shape((2 * CHIPS, 1, LANES), f32),
         in_specs=[SCALARS] * 2 + [WHOLE] * 5, out_specs=WHOLE,
         scratch_shapes=[pltpu.VMEM((16, LANES), f32)],
         compiler_params=params(8), name="maxima",
     )(where, meta, *arrived, pos)
-    sent = jnp.broadcast_to(best[:, None, :], (CHIPS, 2, LANES)).reshape(2 * CHIPS, 1, LANES)
-    back = lax.all_to_all(sent, ("x", "z", "y", "c"), 0, 0, tiled=True)
+    back = lax.all_to_all(best, ("x", "z", "y", "c"), 0, 0, tiled=True)
     fitted = pl.pallas_call(
         pick_kernel,
         out_shape=shape((1, ROWS), f32),

time: 100 us -> 98.3 us (0.983)
    pallas_call x4, Pallas kernels: 12.5 us -> 10.1 us  [the longest x1 4.28 us: on_device(): pl.pallas_call(send_kernel, out_shape=(shape((SHARE_ROWS, WIDTH), bf16),...]
    pallas_call x1, Pallas kernels: 1.44 us -> 3.64 us  [on_device(): pl.pallas_call(own_kernel, out_shape=shape((RAW_ROWS, LANES), f32), in_sp...]
    ppermute x1, waiting for transfers between devices: 1.09 us -> 0.01 us  [on_device(): other = lax.ppermute(send, 'c', [(0, 1), (1, 0)])]
  transfers between devices with their start and end apart: 6 -> 6, of which waited for: 5 -> 4; matrix products, arithmetic and copies ran while one was open for 1% -> 1% of each run, Pallas kernels for 1% -> 4%
where the time goes in v5:
time: 98.3 us; the launch traced here: 98.1 us
  blocking collectives  45.5 us (46%)
  waiting for transfers between devices  21 us (21%)
  Pallas kernels  16.3 us (17%)
  starting transfers between devices  13.5 us (14%)
  local copies, waits for them, and re-layouts  1.03 us (1%)
    all_to_all x1, blocking collectives, on_device(): packed = lax.all_to_all(packed, ('x', 'z', 'y'), 0, 0, tiled=True)  45.5 us
    ppermute x3, waiting for transfers between devices, on_device(): lax.ppermute(partial[s], 'y', [(i, (i + s) % 4) for i in range(4)])  11.1 us
    all_to_all x1, waiting for transfers between devices, on_device(): back = lax.all_to_all(best, ('x', 'z', 'y', 'c'), 0, 0, tiled=True)  8.31 us
    all_to_all x1, starting transfers between devices, on_device(): back = lax.all_to_all(best, ('x', 'z', 'y', 'c'), 0, 0, tiled=True)  6.22 us
    pallas_call x1, Pallas kernels, on_device(): pl.pallas_call(send_kernel, out_shape=(shape((SHARE_ROWS, WIDTH), bf16),...  4.28 us
    pallas_call x1, Pallas kernels, on_device(): pl.pallas_call(own_kernel, out_shape=shape((RAW_ROWS, LANES), f32), in_sp...  3.64 us
    ppermute x3, starting transfers between devices, on_device(): lax.ppermute(partial[s], 'y', [(i, (i + s) % 4) for i in range(4)])  3.25 us
    ppermute x1, starting transfers between devices, on_device(): other = lax.ppermute(send, 'c', [(0, 1), (1, 0)])  2.5 us
  transfers between devices with their start and end apart: 6, of which 4 were waited for; matrix products, arithmetic and copies ran while one was open for 1% of the time, Pallas kernels for 4%

profile of v5, /device:TPU:1, one launch (start us, length us, event | category | flops | bytes accessed | tf_op | source)
XLA Modules:
  0.0 98.1 jit_solution(14692818088631961183)
XLA Ops:
  0.0 0.1 pad_add_fusion.where_ref
  0.1 2.4 %unit.1 = (bf16[144,2048]{1,0:T(8,128)(2,1)S(1)}, bf16[144,2048]{1,0:T(8,128)(2,1)S(1)}) custom-call(s32[4]{0:T(128)S(1)} %pad_add_fusion.where_ref, f32[128,4096]{1,0:T(8,128)} %x_ref.1, s32[1,128]{1,0:T(1,128)} %bitcast.27), custom_call_target="tpu_custom_call" | custom-call | tf_op jit(solution)/shard_map/unit/pallas_call | solution.py:356
  2.4 1.5 %collective-permute-start = (bf16[144,2048]{1,0:T(8,128)(2,1)S(1)}, bf16[144,2048]{1,0:T(8,128)(2,1)S(1)}, u32[]{:S(2)}, u32[]{:S(2)}) collective-permute-start(bf16[144,2048]{1,0:T(8,128)(2,1)S(1)} %get-tuple-element.94), channel_id=1, source_target_pairs={{0,1},{1,0},{2,3},{3,2},{4,5},{5,4},{6,7},{7,6},{8,9},{9,8},{10,11... | collective-permute-start | bytes 1769480 | tf_op jit(solution)/shard_map/ppermute | solution.py:362
  3.9 1.6 %collective-permute-done.got_ref = bf16[144,2048]{1,0:T(8,128)(2,1)S(1)} collective-permute-done((bf16[144,2048]{1,0:T(8,128)(2,1)S(1)}, bf16[144,2048]{1,0:T(8,128)(2,1)S(1)}, u32[]{:S(2)}, u32[]{:S(2)}) %collective-permute-start) | collective-permute-done | bytes 589856 | tf_op jit(solution)/shard_map/ppermute | solution.py:362
  5.6 1.6 %pack.1 = (bf16[64,40,512]{2,1,0:T(8,128)(2,1)S(1)}, s32[8,128]{1,0:T(8,128)S(1)}) custom-call(s32[4]{0:T(128)S(1)} %pad_add_fusion.where_ref, bf16[144,2048]{1,0:T(8,128)(2,1)S(1)} %get-tuple-element.93.keep_ref, bf16[144,2048]{1,0:T(8,128)(2,1)S(1)} %collective-permute-done.got_ref), custom_call_target="tpu_custom_call" | custom-call | tf_op jit(solution)/shard_map/pack/pallas_call | solution.py:363
  7.2 45.5 %all_to_all.51.x_ref = bf16[64,40,512]{2,1,0:T(8,128)(2,1)S(1)} all-to-all(bf16[64,40,512]{2,1,0:T(8,128)(2,1)S(1)} %get-tuple-element.95), channel_id=1, replica_groups=mesh['x'=4,'z'=4,'y'=4,'c'=2] {'x','z','y'}, dimensions={0} | all-to-all | bytes 5242880 | tf_op jit(solution)/shard_map/all_to_all | solution.py:368
  52.7 4.3 %sort.1 = (bf16[1216,512]{1,0:T(8,128)(2,1)S(1)}, s32[8,2560]{1,0:T(8,128)S(1)}, s32[64,128]{1,0:T(8,128)S(1)}, s32[8,128]{1,0:T(8,128)S(1)}) custom-call(s32[4]{0:T(128)S(1)} %pad_add_fusion.where_ref, bf16[64,40,512]{2,1,0:T(8,128)(2,1)S(1)} %all_to_all.51.x_ref), custom_call_target="tpu_custom_call" | custom-call | tf_op jit(solution)/shard_map/sort/pallas_call | solution.py:369
  57.0 2.5 %collective-permute-start.1 = (bf16[1216,512]{1,0:T(8,128)(2,1)S(1)}, bf16[1216,512]{1,0:T(8,128)(2,1)S(1)}, u32[]{:S(2)}, u32[]{:S(2)}) collective-permute-start(bf16[1216,512]{1,0:T(8,128)(2,1)S(1)} %get-tuple-element.97.send_ref), channel_id=1, source_target_pairs={{0,1},{1,0},{2,3},{3,2},{4,5},{5,4},{6,7},{7,6},{8,9},{9,8},{10,11... | collective-permute-start | bytes 3735560 | tf_op jit(solution)/shard_map/ppermute | solution.py:377
  59.5 3.6 %own.1.raw_ref = f32[2560,128]{1,0:T(8,128)S(1)} custom-call(s32[4]{0:T(128)S(1)} %pad_add_fusion.where_ref, bf16[64,40,512]{2,1,0:T(8,128)(2,1)S(1)} %all_to_all.51.x_ref, s32[8,2560]{1,0:T(8,128)S(1)} %get-tuple-element.98.line_ref, bf16[1216,512]{1,0:T(8,128)(2,1)S(1)} %get-tuple-element.97.send_ref), custom_call_target="tpu_custom_call" | custom-call | flops 2013265920 | bytes 8388608 | tf_op jit(solution)/shard_map/own/pallas_call | solution.py:379
  63.1 0.0 copy-start
  63.1 0.0 copy-start.1
  63.2 0.0 collective-permute-done.1.x_ref
  63.2 1.6 %gram.1 = (f32[448,128]{1,0:T(8,128)S(1)}, f32[448,128]{1,0:T(8,128)S(1)}, f32[448,128]{1,0:T(8,128)S(1)}, f32[448,128]{1,0:T(8,128)S(1)}) custom-call(s32[4]{0:T(128)S(1)} %pad_add_fusion.where_ref, s32[8,128]{1,0:T(8,128)S(1)} %get-tuple-element.96.meta_ref, bf16[1216,512]{1,0:T(8,128)(2,1)S(1)} %collective-permute-done.1.x_ref, f32[2560,128]{1,0:T(8,128)S(1)} %own.1.raw_ref), custom_call_target="tpu_custom_call" | custom-call | tf_op jit(solution)/shard_map/gram/pallas_call | solution.py:386
  64.8 0.5 collective-permute-start.2
  65.3 1.5 %collective-permute-start.3 = (f32[448,128]{1,0:T(8,128)S(1)}, f32[448,128]{1,0:T(8,128)S(1)}, u32[]{:S(2)}, u32[]{:S(2)}) collective-permute-start(f32[448,128]{1,0:T(8,128)S(1)} %get-tuple-element.101), channel_id=1, source_target_pairs={{0,4},{2,6},{4,0},{6,2},{1,5},{3,7},{5,1},{7,3},{8,12},{10,14},{12... | collective-permute-start | bytes 688136 | tf_op jit(solution)/shard_map/ppermute | solution.py:394
  66.8 1.3 %collective-permute-start.4 = (f32[448,128]{1,0:T(8,128)S(1)}, f32[448,128]{1,0:T(8,128)S(1)}, u32[]{:S(2)}, u32[]{:S(2)}) collective-permute-start(f32[448,128]{1,0:T(8,128)S(1)} %get-tuple-element.102), channel_id=1, source_target_pairs={{0,6},{2,0},{4,2},{6,4},{1,7},{3,1},{5,3},{7,5},{8,14},{10,8},{12,... | collective-permute-start | bytes 688136 | tf_op jit(solution)/shard_map/ppermute | solution.py:394
  68.1 9.9 %collective-permute-done.2.p1 = f32[448,128]{1,0:T(8,128)S(1)} collective-permute-done((f32[448,128]{1,0:T(8,128)S(1)}, f32[448,128]{1,0:T(8,128)S(1)}, u32[]{:S(2)}, u32[]{:S(2)}) %collective-permute-start.2) | collective-permute-done | bytes 229408 | tf_op jit(solution)/shard_map/ppermute | solution.py:394
  78.0 0.0 collective-permute-done.3.p2
  78.0 1.1 %collective-permute-done.4.p3 = f32[448,128]{1,0:T(8,128)S(1)} collective-permute-done((f32[448,128]{1,0:T(8,128)S(1)}, f32[448,128]{1,0:T(8,128)S(1)}, u32[]{:S(2)}, u32[]{:S(2)}) %collective-permute-start.4) | collective-permute-done | bytes 229408 | tf_op jit(solution)/shard_map/ppermute | solution.py:394
  79.1 1.9 %maxima.1 = f32[128,1,128]{2,1,0:T(1,128)} custom-call(s32[4]{0:T(128)S(1)} %pad_add_fusion.where_ref, s32[8,128]{1,0:T(8,128)S(1)} %get-tuple-element.96.meta_ref, f32[448,128]{1,0:T(8,128)S(1)} %get-tuple-element.99.p0, f32[448,128]{1,0:T(8,128)S(1)} %collective-permute-done.2.p1, f32[448,128]{1,0:T(8,128)S(1)} %collective-permute-done.3.p2, ...), custom_call_target="tpu_custom_call" | custom-call | tf_op jit(solution)/shard_map/maxima/pallas_call | solution.py:396
  81.0 6.2 %all-to-all-start.6 = ((f32[128,1,128]{2,1,0:T(1,128)}), f32[128,1,128]{2,1,0:T(1,128)S(1)}, u32[]{:S(2)}, u32[]{:S(2)}) async-start(f32[128,1,128]{2,1,0:T(1,128)} %maxima.1), calls=%async_computation.6 | async-start | bytes 131072 | tf_op jit(solution)/shard_map/all_to_all | solution.py:403
  87.2 0.5 slice.3
  88.4 8.3 %all-to-all-done.6 = f32[128,1,128]{2,1,0:T(1,128)S(1)} async-done(((f32[128,1,128]{2,1,0:T(1,128)}), f32[128,1,128]{2,1,0:T(1,128)S(1)}, u32[]{:S(2)}, u32[]{:S(2)}) %all-to-all-start.6) | async-done | bytes 65568 | tf_op jit(solution)/shard_map/all_to_all | solution.py:403
  96.7 0.9 pick.1
  97.6 0.0 copy-done
  97.6 0.0 copy-done.1
  97.6 0.0 copy-start.2
  97.6 0.5 copy-done.2
  (1 shorter events, 0.0 us)
Async XLA Ops:
  2.4 3.1 %collective-permute-start = (bf16[144,2048]{1,0:T(8,128)(2,1)S(1)}, bf16[144,2048]{1,0:T(8,128)(2,1)S(1)}, u32[]{:S(2)}, u32[]{:S(2)}) collective-permute-start(bf16[144,2048]{1,0:T(8,128)(2,1)S(1)} %get-tuple-element.94), channel_id=1, source_target_pairs={{0,1},{1,0},{2,3},{3,2},{4,5},{5,4},{6,7},{7,6},{8,9},{9,8},{10,11... | collective-permute-start | bytes 1769480 | tf_op jit(solution)/shard_map/ppermute | solution.py:362
  57.0 6.2 %collective-permute-start.1 = (bf16[1216,512]{1,0:T(8,128)(2,1)S(1)}, bf16[1216,512]{1,0:T(8,128)(2,1)S(1)}, u32[]{:S(2)}, u32[]{:S(2)}) collective-permute-start(bf16[1216,512]{1,0:T(8,128)(2,1)S(1)} %get-tuple-element.97.send_ref), channel_id=1, source_target_pairs={{0,1},{1,0},{2,3},{3,2},{4,5},{5,4},{6,7},{7,6},{8,9},{9,8},{10,11... | collective-permute-start | bytes 3735560 | tf_op jit(solution)/shard_map/ppermute | solution.py:377
  63.1 34.4 %copy-start = (s32[128]{0:T(128)S(1)}, s32[128]{0:T(128)}, u32[]{:S(2)}) copy-start(s32[128]{0:T(128)} %param.7) | copy-start | bytes 1540
  63.1 34.4 %copy-start.1 = (f32[128,4096]{1,0:T(8,128)S(1)}, f32[128,4096]{1,0:T(8,128)}, u32[]{:S(2)}) copy-start(f32[128,4096]{1,0:T(8,128)} %x_ref.1) | copy-start | bytes 6291460
  64.8 13.2 %collective-permute-start.2 = (f32[448,128]{1,0:T(8,128)S(1)}, f32[448,128]{1,0:T(8,128)S(1)}, u32[]{:S(2)}, u32[]{:S(2)}) collective-permute-start(f32[448,128]{1,0:T(8,128)S(1)} %get-tuple-element.100), channel_id=1, source_target_pairs={{0,2},{2,4},{4,6},{6,0},{1,3},{3,5},{5,7},{7,1},{8,10},{10,12},{12... | collective-permute-start | bytes 688136 | tf_op jit(solution)/shard_map/ppermute | solution.py:394
  65.3 12.7 %collective-permute-start.3 = (f32[448,128]{1,0:T(8,128)S(1)}, f32[448,128]{1,0:T(8,128)S(1)}, u32[]{:S(2)}, u32[]{:S(2)}) collective-permute-start(f32[448,128]{1,0:T(8,128)S(1)} %get-tuple-element.101), channel_id=1, source_target_pairs={{0,4},{2,6},{4,0},{6,2},{1,5},{3,7},{5,1},{7,3},{8,12},{10,14},{12... | collective-permute-start | bytes 688136 | tf_op jit(solution)/shard_map/ppermute | solution.py:394
  66.8 12.4 %collective-permute-start.4 = (f32[448,128]{1,0:T(8,128)S(1)}, f32[448,128]{1,0:T(8,128)S(1)}, u32[]{:S(2)}, u32[]{:S(2)}) collective-permute-start(f32[448,128]{1,0:T(8,128)S(1)} %get-tuple-element.102), channel_id=1, source_target_pairs={{0,6},{2,0},{4,2},{6,4},{1,7},{3,1},{5,3},{7,5},{8,14},{10,8},{12,... | collective-permute-start | bytes 688136 | tf_op jit(solution)/shard_map/ppermute | solution.py:394
  81.0 15.7 %all-to-all-start.6 = ((f32[128,1,128]{2,1,0:T(1,128)}), f32[128,1,128]{2,1,0:T(1,128)S(1)}, u32[]{:S(2)}, u32[]{:S(2)}) async-start(f32[128,1,128]{2,1,0:T(1,128)} %maxima.1), calls=%async_computation.6 | async-start | bytes 131072 | tf_op jit(solution)/shard_map/all_to_all | solution.py:403
  97.6 0.5 copy-start.2

commit v6 on v4

--- a/solution.py
+++ b/solution.py
@@ -11,8 +11,12 @@
 LABEL_ROWS = 16
 BINS = 16
 CHIPS = 64
-BLOCK = 40
+BLOCK = 24
 SLOTS = BLOCK - 1
+GROUP = 32
+GUESTS = 64
+ALL_GUESTS = 4 * GUESTS
+GUEST = 4096
 LANES = 128
 CAPS = (704, 512, 320, 192)
 STARTS = (0, 704, 1216, 1536)
@@ -75,29 +79,57 @@
         out_ref[ROWS:, :] = ids
 
 
-def pack_kernel(where_ref, keep_ref, got_ref, out_ref, code_ref, block_ref, sems):
-    first = where_ref[3] == 0
+def pack_kernel(where_ref, keep_ref, got_ref, out_ref, code_ref):
+    y, first = where_ref[2], where_ref[3] == 0
     kept = jnp.max(keep_ref[ROWS:, :ROWS].astype(f32), axis=0, keepdims=True)
     got = jnp.max(got_ref[ROWS:, :ROWS].astype(f32), axis=0, keepdims=True)
     labels = jnp.concatenate([jnp.where(first, kept, got), jnp.where(first, got, kept)], axis=0).astype(i32)
     bins = bin_of(labels)
-    member = jnp.concatenate([jnp.where(bins == b, 1.0, 0.0) for b in range(BINS)], axis=0)
-    member16 = member.astype(bf16)
-    along = dot(member16, as_bf16(iota((ROWS, ROWS), 0) < iota((ROWS, ROWS), 1)))
-    row, col = iota((2 * BINS, 2 * BINS), 0), iota((2 * BINS, 2 * BINS), 1)
-    earlier = dot(as_bf16(((row >> 1) == (col >> 1)) & (col < row)), member16)
-    ranks = member * (along + jnp.sum(earlier, axis=1, keepdims=True))
-    rank = sum(ranks[2 * b:2 * b + 2] for b in range(BINS)).astype(i32)
-    code = jnp.where(rank < SLOTS, bins * BLOCK + rank, -1)
-    code_ref[...] = jnp.concatenate([code] * 4, axis=0)
+    upper = as_bf16(iota((ROWS, ROWS), 0) < iota((ROWS, ROWS), 1))
+
+    def ranks_within(masks):
+        member = jnp.concatenate([jnp.where(mask, 1.0, 0.0) for mask in masks], axis=0)
+        row, col = iota((member.shape[0],) * 2, 0), iota((member.shape[0],) * 2, 1)
+        earlier = dot(as_bf16(((row >> 1) == (col >> 1)) & (col < row)), member.astype(bf16))
+        ranks = member * (dot(member.astype(bf16), upper) + jnp.sum(earlier, axis=1, keepdims=True))
+        rank = sum(ranks[2 * b:2 * b + 2] for b in range(len(masks)))
+        return rank.astype(i32), jnp.sum(member, axis=1, keepdims=True)
+
+    rank, sizes = ranks_within([bins == b for b in range(BINS)])
+    quad, line = bins >> 2, bins & 3
+    extra = rank >= SLOTS
+    turn, _ = ranks_within([extra & (quad == q) for q in range(4)])
+    room, used = [], []
+    for step in range(4):
+        taken = jnp.zeros(labels.shape, f32)
+        for at in range(4):
+            size = jnp.zeros(labels.shape, f32)
+            for q in range(4):
+                b = 4 * q + at
+                size = jnp.where(quad == q, sizes[2 * b:2 * b + 1] + sizes[2 * b + 1:2 * b + 2], size)
+            taken = jnp.where(((at - y) & 3) == step, size, taken)
+        taken = jnp.minimum(taken.astype(i32), SLOTS)
+        used.append(taken)
+        room.append(SLOTS - taken)
+    placed = jnp.logical_not(extra)
+    to_line, to_slot, start = line, rank, jnp.zeros(labels.shape, i32)
+    for step in range(4):
+        here = extra & (turn >= start) & (turn < start + room[step])
+        to_line = jnp.where(here, (y + step) & 3, to_line)
+        to_slot = jnp.where(here, used[step] + turn - start, to_slot)
+        placed = placed | here
+        start = start + room[step]
+    lane = jnp.where(placed, to_line * GROUP + to_slot, -1)
+    place = jnp.where(placed, (quad * 4 + to_line) * BLOCK + to_slot, -1)
+    code_ref[...] = jnp.concatenate([jnp.where(placed, bins * LANES + lane, -1)] * 4, axis=0)
     docs = 2 * ROWS
     flat = lambda v: jnp.concatenate([v[:1], v[1:]], axis=1)
-    rank_row, bin_row, label_row = flat(rank), flat(bins), flat(labels)
+    label_row = flat(labels)
     counts = dot_last(jnp.ones((8, docs), bf16), as_bf16(iota((LANES, docs), 0) == label_row))[:1]
-    named = jnp.where(iota((BINS, docs), 0) == bin_row, (label_row + 1).astype(f32), 0.0).astype(bf16)
-    names = dot_last(named, as_bf16((iota((LANES, docs), 0) == rank_row) & (rank_row < SLOTS)))
-    own = jnp.where(first, code[:1], code[1:])
-    other = jnp.where(first, code[1:], code[:1])
+    named = jnp.where(iota((8, docs), 0) == flat(quad), (label_row + 1).astype(f32), 0.0).astype(bf16)
+    names = dot_last(named, as_bf16(iota((LANES, docs), 0) == flat(lane)))
+    own = jnp.where(first, place[:1], place[1:])
+    other = jnp.where(first, place[1:], place[:1])
     onehot = as_bf16(iota((BINS * BLOCK, docs), 0) == jnp.concatenate([own, other], axis=1))
     is_last = iota((BLOCK, WIDTH), 0) == SLOTS
     for y in range(4):
@@ -105,44 +137,48 @@
         x = jnp.concatenate([keep_ref[:ROWS, columns], got_ref[:ROWS, columns]], axis=0)
         packed = dot(onehot, x)
         for b in range(BINS):
-            extra = jnp.concatenate([names[b:b + 1], counts, jnp.zeros((1, 2 * LANES), f32)], axis=1)
-            block_ref[y, b] = jnp.where(is_last, extra, packed[b * BLOCK:(b + 1) * BLOCK]).astype(bf16)
-        pltpu.make_async_copy(block_ref.at[y], out_ref.at[:, y], sems.at[y]).start()
-    for y in range(4):
-        pltpu.make_async_copy(block_ref.at[y], out_ref.at[:, y], sems.at[y]).wait()
-
-
-def sort_kernel(where_ref, x_ref, mine_ref, send_ref, pos_ref, meta_ref):
-    mine = where_ref[0] * 4 + where_ref[1]
+            extra = jnp.concatenate([names[b // 4:b // 4 + 1], counts, jnp.zeros((1, 2 * LANES), f32)], axis=1)
+            out_ref[4 * b + y] = jnp.where(is_last, extra, packed[b * BLOCK:(b + 1) * BLOCK]).astype(bf16)
+
+
+def labels_of(x_ref):
     tail = x_ref[:, BLOCK - 8:, :2 * LANES].astype(f32)
     tail = jnp.max(jnp.where(iota(tail.shape, 1) == 7, tail, 0.0), axis=1)
-    labels, chip_counts = tail[:, :LANES].astype(i32) - 1, tail[:, LANES:].astype(bf16)
+    return tail[:, :LANES].astype(i32) - 1, tail[:, LANES:].astype(bf16)
+
+
+def counts_of(chip_counts):
     row, col = iota((LANES, LANES), 0), iota((LANES, LANES), 1)
     in_bin = (bin_of(row) == col) & (row < 4 * BINS)
-    sizes, total = [], 0.0
-    for r in range(4):
-        counts = dot(chip_counts, as_bf16(in_bin & ((row & 3) == r)))
-        total = total + counts
-        sizes.append(jnp.sum(counts, axis=0, keepdims=True))
+    counts = [dot(chip_counts, as_bf16(in_bin & ((row & 3) == r))) for r in range(4)]
+    return counts, [jnp.sum(v, axis=0, keepdims=True) for v in counts]
+
+
+def in_order(sizes):
     a, b = jnp.maximum(sizes[0], sizes[1]), jnp.minimum(sizes[0], sizes[1])
     c, d = jnp.maximum(sizes[2], sizes[3]), jnp.minimum(sizes[2], sizes[3])
     first, e = jnp.maximum(a, c), jnp.minimum(a, c)
     g, fourth = jnp.maximum(b, d), jnp.minimum(b, d)
-    ordered = (first, jnp.maximum(e, g), jnp.minimum(e, g), fourth)
-    over = jnp.max(jnp.where(total > SLOTS, 1.0, 0.0), axis=0, keepdims=True)
-    for size, cap in zip(ordered, CAPS):
-        over = jnp.maximum(over, jnp.where(size > cap, 1.0, 0.0))
-    for share in SHARES:
-        length = sum(jnp.maximum(jnp.floor((ordered[q] + 63.0) * (1 / 64)) - first // HALF, 0.0) for q, first in share)
-        over = jnp.maximum(over, jnp.where(length > 4 * COUNT, 1.0, 0.0))
-    over = jnp.max(over, axis=1, keepdims=True)
+    return first, jnp.maximum(e, g), jnp.minimum(e, g), fourth
+
+
+def names_kernel(where_ref, x_ref, guest_ref, line_ref, key_ref, pos_ref, meta_ref):
+    mine, z = where_ref[0] * 4 + where_ref[1], where_ref[1]
+    labels, chip_counts = labels_of(x_ref)
+    _, sizes = counts_of(chip_counts)
     here = iota((1, LANES), 1) == mine
     own = lambda v: jnp.sum(jnp.where(here, v, 0.0), axis=1, keepdims=True)
     wide = lambda v: jnp.broadcast_to(v, (1, LANES))
-    meta_ref[...] = jnp.concatenate([wide(own(v)) for v in ordered] + [wide(over)] * 4, axis=0).astype(i32)
+    ordered = in_order(sizes)
+    meta_ref[...] = jnp.concatenate([wide(own(v)) for v in ordered] * 2, axis=0).astype(i32)
 
     n = [own(v) for v in sizes]
-    valid = (labels >= 0) & (iota(labels.shape, 1) < SLOTS)
+    row, col = iota((LANES, LANES), 0), iota((LANES, LANES), 1)
+    lane = iota(labels.shape, 1)
+    group = lane >> 5
+    valid = labels >= 0
+    home = bin_of(labels) & 3
+    at_home = valid & (home == z)
     upper = as_bf16(row < col)
     lower = as_bf16(iota((CHIPS, CHIPS), 1) < iota((CHIPS, CHIPS), 0))
     pos = jnp.full(labels.shape, -1.0, f32)
@@ -154,30 +190,104 @@
             place < 0.5, float(STARTS[0]),
             jnp.where(place < 1.5, float(STARTS[1]), jnp.where(place < 2.5, float(STARTS[2]), float(STARTS[3]))),
         )
-        member = valid & ((labels & 3) == r)
+        member = at_home & ((labels & 3) == r)
         member16 = as_bf16(member)
         rank = dot(member16, upper) + jnp.sum(dot(lower, member16), axis=1, keepdims=True)
         pos = jnp.where(member, start + rank, pos)
-    pos_ref[...] = pos.astype(i32)
+    pos = pos.astype(i32)
+    pos_ref[...] = pos
+    guest = valid & (home != group)
+    guest16 = as_bf16(guest)
+    same = (row >> 5) == (col >> 5)
+    turn = dot(guest16, as_bf16(same & (row < col))) + dot(dot(lower, guest16).astype(bf16), as_bf16(same))
+    turn = turn.astype(i32)
+    away = at_home & (group != z) & (turn < GUESTS)
+    key_ref[...] = jnp.where(away, (((z - group) & 3) - 1) * GUESTS + turn, -1)
     per, groups = 16, CHIPS // 16
-    plus = jnp.where(iota(pos.shape, 1) < BLOCK, pos + 1.0, 0.0)
+    value = jnp.where(group == z, jnp.where(guest, GUEST + turn, pos + 1), 0).astype(f32)
+    value = pltpu.roll(value, lax.rem(LANES - GROUP * z, LANES), 1)
+    value = jnp.where(lane < BLOCK, value, 0.0)
     lined = jnp.zeros((8, per * BLOCK), f32)
     for t in range(per):
-        rows = jnp.concatenate([plus[per * g + t:per * g + t + 1] for g in range(groups)] * 2, axis=0)
+        rows = jnp.concatenate([value[per * g + t:per * g + t + 1] for g in range(groups)] * 2, axis=0)
         rows = jnp.concatenate([rows, jnp.zeros((8, per * BLOCK - LANES), f32)], axis=1)
         lined = lined + (pltpu.roll(rows, t * BLOCK, 1) if t else rows)
-    pos_row = jnp.concatenate([lined[g:g + 1] for g in range(groups)], axis=1).astype(i32) - 1
+    slots = jnp.concatenate([lined[g:g + 1] for g in range(groups)], axis=1).astype(i32)
+    line_ref[...] = jnp.broadcast_to(slots, line_ref.shape)
+    onehot = as_bf16(iota((GUESTS, CHIPS * BLOCK), 0) + GUEST == slots)
+    guest_ref[...] = dot(onehot, x_ref[...].reshape(CHIPS * BLOCK, WIDTH)).astype(bf16)
+
+
+def sorted_rows(segment, slots, x):
+    onehot = as_bf16(iota((segment[1], x.shape[0]), 0) + (segment[0] + 1) == slots)
+    return dot(onehot, x).astype(bf16)
+
+
+def send_kernel(where_ref, x_ref, line_ref, send_ref):
     x = x_ref[...].reshape(CHIPS * BLOCK, WIDTH)
-    core = where_ref[3]
-    for first, rows, *offsets in SEGMENTS:
-        onehot = as_bf16(iota((rows, CHIPS * BLOCK), 0) + first == pos_row)
-        part = dot(onehot, x).astype(bf16)
-        for me in range(2):
-            @pl.when(core == me)
-            def _():
-                for share, at in enumerate(offsets):
-                    if at is not None:
-                        (mine_ref if share == me else send_ref)[at:at + rows, :] = part
+    slots = line_ref[:1, :]
+    for me in range(2):
+        @pl.when(where_ref[3] == me)
+        def _():
+            for segment in SEGMENTS:
+                at = segment[2 + 1 - me]
+                if at is not None:
+                    send_ref[at:at + segment[1], :] = sorted_rows(segment, slots, x)
+
+
+def mine_kernel(where_ref, x_ref, line_ref, send_ref, key_ref, pos_ref, mine_ref, far_ref, over_ref):
+    x = x_ref[...].reshape(CHIPS * BLOCK, WIDTH)
+    slots = line_ref[:1, :]
+    for core in range(2):
+        @pl.when(where_ref[3] == core)
+        def _():
+            for segment in SEGMENTS:
+                at, sent = segment[2 + core], segment[2 + 1 - core]
+                if at is not None:
+                    rows = segment[1]
+                    mine_ref[at:at + rows, :] = (
+                        send_ref[sent:sent + rows, :] if sent is not None else sorted_rows(segment, slots, x)
+                    )
+    total = jnp.zeros((8, ALL_GUESTS), f32)
+    step = 16
+    for first in range(0, CHIPS, step):
+        flat = lambda ref: jnp.concatenate([ref[s:s + 1, :] for s in range(first, first + step)], axis=1)
+        places = flat(pos_ref) + 1
+        parts = jnp.where(iota((8, step * LANES), 0) == 0, places >> 5, places & 31).astype(f32).astype(bf16)
+        total = total + dot_last(parts, as_bf16(iota((ALL_GUESTS, step * LANES), 0) == flat(key_ref)))
+    far_ref[...] = jnp.broadcast_to((32.0 * total[:1] + total[1:2]).astype(i32), far_ref.shape)
+    _, chip_counts = labels_of(x_ref)
+    counts, sizes = counts_of(chip_counts)
+    ordered = in_order(sizes)
+    over = jnp.zeros((1, LANES), f32)
+    for size, cap in zip(ordered, CAPS):
+        over = jnp.maximum(over, jnp.where(size > cap, 1.0, 0.0))
+    for share in SHARES:
+        length = sum(jnp.maximum(jnp.floor((ordered[q] + 63.0) * (1 / 64)) - first // HALF, 0.0) for q, first in share)
+        over = jnp.maximum(over, jnp.where(length > 4 * COUNT, 1.0, 0.0))
+    taken = counts[0] + counts[1] + counts[2] + counts[3]
+    extra, room = jnp.maximum(taken - SLOTS, 0.0), jnp.maximum(SLOTS - taken, 0.0)
+    row, col = iota((LANES, LANES), 0), iota((LANES, LANES), 1)
+    same = (row >> 2) == (col >> 2)
+    wanted = dot(extra.astype(bf16), as_bf16(same))
+    before = jnp.zeros(taken.shape, f32)
+    for turn in range(4):
+        earlier = same & (((row - turn) & 3) < ((col - turn) & 3))
+        before = jnp.where((iota(taken.shape, 0) & 3) == turn, dot(room.astype(bf16), as_bf16(earlier)), before)
+    held = jnp.sum(jnp.minimum(jnp.maximum(wanted - before, 0.0), room), axis=0, keepdims=True)
+    over = jnp.maximum(over, jnp.where(held > GUESTS, 1.0, 0.0))
+    full = jnp.where(wanted > dot(room.astype(bf16), as_bf16(same)), 1.0, 0.0)
+    over = jnp.maximum(over, jnp.max(full, axis=0, keepdims=True))
+    over_ref[...] = jnp.broadcast_to(jnp.max(over, axis=1, keepdims=True), over_ref.shape).astype(i32)
+
+
+def add_guests(core, base_ref, guests, far_ref, out_ref):
+    guests = jnp.concatenate([ref[...] for ref in guests] + [guests[0][...]], axis=0)
+    far = far_ref[:1, :]
+    for segment in SEGMENTS:
+        at, rows = segment[2 + core], segment[1]
+        if at is not None:
+            out_ref[at:at + rows, :] = base_ref[at:at + rows, :] + sorted_rows(segment, far, guests)
 
 
 def blocks_of(core):
@@ -189,14 +299,15 @@
 RAW_ROWS = max(sum(CAPS[q] - first for q, first in share) for share in SHARES)
 
 
-def own_kernel(where_ref, x_ref, raw_ref):
+def own_kernel(where_ref, x_ref, g1, g2, g3, far_ref, raw_ref, rows_ref):
     for core in range(2):
         @pl.when(where_ref[3] == core)
         def _():
+            add_guests(core, x_ref, (g1, g2, g3), far_ref, rows_ref)
             at = 0
             for q, first, left, right in blocks_of(core):
                 rows = CAPS[q] - first
-                raw_ref[at:at + rows, :] = dot_last(x_ref[left, :], x_ref[right, :])
+                raw_ref[at:at + rows, :] = dot_last(rows_ref[left, :], rows_ref[right, :])
                 at += rows
 
 
@@ -204,16 +315,17 @@
     return jnp.maximum(((size + HALF - 1) >> 6) - first // HALF, 0)
 
 
-def gram_kernel(where_ref, meta_ref, x_ref, raw_ref, out0, out1, out2, out3, part_ref):
+def gram_kernel(where_ref, meta_ref, x_ref, g1, g2, g3, far_ref, raw_ref, out0, out1, out2, out3, part_ref, rows_ref):
     y, c = where_ref[2], where_ref[3]
     part_ref[...] = jnp.full(part_ref.shape, -4.0, f32)
     for core in range(2):
         @pl.when(c == core)
         def _():
+            add_guests(core, x_ref, (g1, g2, g3), far_ref, rows_ref)
             at, to = 0, jnp.zeros((), i32)
             for q, first, left, right in blocks_of(core):
                 rows = CAPS[q] - first
-                score = raw_ref[at:at + rows, :] + dot_last(x_ref[left, :], x_ref[right, :])
+                score = raw_ref[at:at + rows, :] + dot_last(rows_ref[left, :], rows_ref[right, :])
                 at += rows
                 size = meta_ref[q, 0]
                 i, j = iota(score.shape, 0), iota(score.shape, 1)
@@ -263,19 +375,21 @@
         value = jnp.broadcast_to(best_ref[r:r + 1, :], pos.shape)
         value = jnp.take_along_axis(value, lane, axis=1, mode="promise_in_bounds")
         out = jnp.where(row == r, value, out)
-    out_ref[...] = out
+    out_ref[:CHIPS, :] = out
+    out_ref[CHIPS:, :] = out
 
 
 def pick_kernel(where_ref, v_ref, code_ref, out_ref):
     c = where_ref[3]
-    values = jnp.max(v_ref[...].reshape(BINS, 8, LANES), axis=1)
+    values = jnp.maximum(v_ref[:CHIPS, :], v_ref[CHIPS:, :])
+    values = jnp.max(values.reshape(BINS, 4, LANES), axis=1)
     eye = iota((LANES, LANES), 0) == iota((LANES, LANES), 1)
     code = jnp.max(jnp.where(iota((8, ROWS), 0) == c, code_ref[...], -1), axis=0, keepdims=True)
     code = jnp.max(jnp.where(eye, code.astype(f32), -1.0), axis=1, keepdims=True).astype(i32)
     slot = iota((ROWS, LANES), 1)
     best = jnp.full((ROWS, LANES), -1.0, f32)
     for b in range(BINS):
-        best = jnp.where((slot + b * BLOCK == code) & (slot < BLOCK), values[b:b + 1], best)
+        best = jnp.where(slot + b * LANES == code, values[b:b + 1], best)
     best = jnp.max(best, axis=1, keepdims=True)
     out_ref[...] = jnp.max(jnp.where(eye, best, -1.0), axis=0, keepdims=True)
 
@@ -335,52 +449,63 @@
     got = lax.ppermute(send, "c", [(0, 1), (1, 0)])
     packed, code = pl.pallas_call(
         pack_kernel,
-        out_shape=(shape((BINS, 4, BLOCK, WIDTH), bf16), shape((8, ROWS), i32)),
-        in_specs=[SCALARS, WHOLE, WHOLE], out_specs=(pl.BlockSpec(memory_space=pltpu.HBM), WHOLE),
-        scratch_shapes=[pltpu.VMEM((4, BINS, BLOCK, WIDTH), bf16), pltpu.SemaphoreType.DMA((4,))],
-        compiler_params=params(20), name="pack",
+        out_shape=(shape((CHIPS, BLOCK, WIDTH), bf16), shape((8, ROWS), i32)),
+        in_specs=[SCALARS, WHOLE, WHOLE], out_specs=(WHOLE, WHOLE), compiler_params=params(20), name="pack",
     )(where, keep, got)
-    packed = lax.all_to_all(packed.reshape(CHIPS, BLOCK, WIDTH), ("x", "z", "y"), 0, 0, tiled=True)
-    mine, send, pos, meta = pl.pallas_call(
-        sort_kernel,
-        out_shape=(
-            shape((SHARE_ROWS, WIDTH), bf16), shape((SHARE_ROWS, WIDTH), bf16),
-            shape((CHIPS, LANES), i32), shape((8, LANES), i32),
-        ),
-        in_specs=[SCALARS, WHOLE], out_specs=(WHOLE,) * 4, compiler_params=params(28), name="sort",
+    packed = lax.all_to_all(packed, ("x", "z", "y"), 0, 0, tiled=True)
+    table = shape((CHIPS, LANES), i32)
+    guests, line, key, pos, meta = pl.pallas_call(
+        names_kernel,
+        out_shape=(shape((GUESTS, WIDTH), bf16), shape((8, CHIPS * BLOCK), i32), table, table, shape((8, LANES), i32)),
+        in_specs=[SCALARS, WHOLE], out_specs=(WHOLE,) * 5, compiler_params=params(12), name="names",
     )(where, packed)
+    brought = [lax.ppermute(guests, "z", [(i, (i + s) % 4) for i in range(4)]) for s in (1, 2, 3)]
+    share = shape((SHARE_ROWS, WIDTH), bf16)
+    slots = CHIPS * BLOCK
+    send = pl.pallas_call(
+        send_kernel, out_shape=share,
+        in_specs=[SCALARS, WHOLE, WHOLE], out_specs=WHOLE, compiler_params=params(16), name="send",
+        cost_estimate=pl.CostEstimate(flops=2 * SHARE_ROWS * WIDTH * slots, bytes_accessed=4 << 20, transcendentals=0),
+    )(where, packed, line)
     other = lax.ppermute(send, "c", [(0, 1), (1, 0)])
+    mine, far, over = pl.pallas_call(
+        mine_kernel, out_shape=(share, shape((8, ALL_GUESTS), i32), shape((8, LANES), i32)),
+        in_specs=[SCALARS] + [WHOLE] * 5, out_specs=(WHOLE,) * 3, compiler_params=params(20), name="mine",
+        cost_estimate=pl.CostEstimate(flops=2 * SHARE_ROWS * WIDTH * slots, bytes_accessed=4 << 20, transcendentals=0),
+    )(where, packed, line, send, key, pos)
+    swapped = [lax.ppermute(v, "c", [(0, 1), (1, 0)]) for v in brought]
     raw = pl.pallas_call(
         own_kernel, out_shape=shape((RAW_ROWS, LANES), f32),
-        in_specs=[SCALARS, WHOLE], out_specs=WHOLE, compiler_params=params(12), name="own",
-        cost_estimate=pl.CostEstimate(flops=2 * RAW_ROWS * LANES * WIDTH, bytes_accessed=3 << 20, transcendentals=0),
-    )(where, mine)
+        in_specs=[SCALARS] + [WHOLE] * 5, out_specs=WHOLE,
+        scratch_shapes=[pltpu.VMEM((SHARE_ROWS, WIDTH), bf16)],
+        compiler_params=params(16), name="own",
+        cost_estimate=pl.CostEstimate(flops=2 * RAW_ROWS * LANES * WIDTH, bytes_accessed=4 << 20, transcendentals=0),
+    )(where, mine, *brought, far)
     partial = pl.pallas_call(
         gram_kernel,
         out_shape=[shape((CHUNK, LANES), f32)] * 4,
-        in_specs=[SCALARS, SCALARS, WHOLE, WHOLE], out_specs=[WHOLE] * 4,
-        scratch_shapes=[pltpu.VMEM((PARTIAL + CAPS[0], LANES), f32)],
+        in_specs=[SCALARS, SCALARS] + [WHOLE] * 6, out_specs=[WHOLE] * 4,
+        scratch_shapes=[pltpu.VMEM((PARTIAL + CAPS[0], LANES), f32), pltpu.VMEM((SHARE_ROWS, WIDTH), bf16)],
         compiler_params=params(16), name="gram",
-    )(where, meta, other, raw)
+    )(where, meta, other, *swapped, far, raw)
     arrived = [partial[0]] + [
         lax.ppermute(partial[s], "y", [(i, (i + s) % 4) for i in range(4)]) for s in (1, 2, 3)
     ]
     best = pl.pallas_call(
         max_kernel,
-        out_shape=shape((CHIPS, LANES), f32),
+        out_shape=shape((2 * CHIPS, LANES), f32),
         in_specs=[SCALARS] * 2 + [WHOLE] * 5, out_specs=WHOLE,
         scratch_shapes=[pltpu.VMEM((16, LANES), f32)],
         compiler_params=params(8), name="maxima",
     )(where, meta, *arrived, pos)
-    sent = jnp.broadcast_to(best[:, None, :], (CHIPS, 2, LANES)).reshape(2 * CHIPS, 1, LANES)
-    back = lax.all_to_all(sent, ("x", "z", "y", "c"), 0, 0, tiled=True)
+    back = lax.all_to_all(best.reshape(2 * CHIPS, 1, LANES), ("c", "x", "z", "y"), 0, 0, tiled=True)
     fitted = pl.pallas_call(
         pick_kernel,
         out_shape=shape((1, ROWS), f32),
         in_specs=[SCALARS, WHOLE, WHOLE], out_specs=WHOLE, compiler_params=params(8), name="pick",
     )(where, back.reshape(2 * CHIPS, LANES), code).reshape(ROWS)
     return lax.cond(
-        meta[4, 0] == 0,
+        over[0, 0] == 0,
         lambda fitted, embeddings, cluster_ids: fitted,
         lambda fitted, embeddings, cluster_ids: gather_groups(embeddings, cluster_ids),
         fitted, embeddings, cluster_ids,

time: 100 us -> 96.5 us (0.965)
  blocking collectives: 45.5 us -> 33.4 us
  starting transfers between devices: 14 us -> 18.2 us
  waiting for transfers between devices: 21.3 us -> 24.7 us
  Pallas kernels: 16.4 us -> 18.1 us
    all_to_all x1, blocking collectives: 45.5 us -> 33.4 us  [on_device(): packed = lax.all_to_all(packed, ('x', 'z', 'y'), 0, 0, tiled=True)]
    ppermute x0 -> x6, starting transfers between devices: none -> 4.13 us  [the longest x3 2.7 us: on_device(): lax.ppermute(guests, 'z', [(i, (i + s) % 4) for i in range(4)])]
    ppermute x0 -> x6, waiting for transfers between devices: none -> 3.59 us  [the longest x3 3.58 us: on_device(): lax.ppermute(guests, 'z', [(i, (i + s) % 4) for i in range(4)])]
    ppermute x1, waiting for transfers between devices: 1.09 us -> 0.01 us  [on_device(): other = lax.ppermute(send, 'c', [(0, 1), (1, 0)])]
    pallas_call x3 -> x5, Pallas kernels: 10.6 us -> 11.7 us  [the longest x1 3.69 us: on_device(): pl.pallas_call(mine_kernel, out_shape=(share, shape((8, ALL_GUESTS), i32)...]
  transfers between devices with their start and end apart: 6 -> 12, of which waited for: 5 -> 5; matrix products, arithmetic and copies ran while one was open for 1% -> 1% of each run, Pallas kernels for 1% -> 6%
where the time goes in v6:
time: 96.5 us; the launch traced here: 96.3 us
  blocking collectives  33.4 us (35%)
  waiting for transfers between devices  24.7 us (26%)
  starting transfers between devices  18.2 us (19%)
  Pallas kernels  18.1 us (19%)
  local copies, waits for them, and re-layouts  1.03 us (1%)
    all_to_all x1, blocking collectives, on_device(): packed = lax.all_to_all(packed, ('x', 'z', 'y'), 0, 0, tiled=True)  33.4 us
    ppermute x3, waiting for transfers between devices, on_device(): lax.ppermute(partial[s], 'y', [(i, (i + s) % 4) for i in range(4)])  11.2 us
    all_to_all x1, waiting for transfers between devices, on_device(): lax.all_to_all(best.reshape(2 * CHIPS, 1, LANES), ('c', 'x', 'z', 'y'), 0...  8.3 us
    all_to_all x1, starting transfers between devices, on_device(): lax.all_to_all(best.reshape(2 * CHIPS, 1, LANES), ('c', 'x', 'z', 'y'), 0...  6.32 us
    pallas_call x1, Pallas kernels, on_device(): pl.pallas_call(mine_kernel, out_shape=(share, shape((8, ALL_GUESTS), i32)...  3.69 us
    ppermute x3, waiting for transfers between devices, on_device(): lax.ppermute(guests, 'z', [(i, (i + s) % 4) for i in range(4)])  3.58 us
    ppermute x3, starting transfers between devices, on_device(): lax.ppermute(partial[s], 'y', [(i, (i + s) % 4) for i in range(4)])  3.22 us
    ppermute x1, starting transfers between devices, on_device(): other = lax.ppermute(send, 'c', [(0, 1), (1, 0)])  3 us
  transfers between devices with their start and end apart: 12, of which 5 were waited for; matrix products, arithmetic and copies ran while one was open for 1% of the time, Pallas kernels for 6%

profile of v6, /device:TPU:1, one launch (start us, length us, event | category | flops | bytes accessed | tf_op | source)
XLA Modules:
  0.0 96.3 jit_solution(5382301068048253893)
XLA Ops:
  0.0 0.1 pad_add_fusion.where_ref
  0.1 1.9 %unit.1 = (bf16[144,2048]{1,0:T(8,128)(2,1)S(1)}, bf16[144,2048]{1,0:T(8,128)(2,1)S(1)}) custom-call(s32[4]{0:T(128)S(1)} %pad_add_fusion.where_ref, f32[128,4096]{1,0:T(8,128)} %x_ref.1, s32[1,128]{1,0:T(1,128)} %bitcast.30), custom_call_target="tpu_custom_call" | custom-call | tf_op jit(solution)/shard_map/unit/pallas_call | solution.py:445
  2.0 1.5 %collective-permute-start = (bf16[144,2048]{1,0:T(8,128)(2,1)S(1)}, bf16[144,2048]{1,0:T(8,128)(2,1)S(1)}, u32[]{:S(2)}, u32[]{:S(2)}) collective-permute-start(bf16[144,2048]{1,0:T(8,128)(2,1)S(1)} %get-tuple-element.98), channel_id=1, source_target_pairs={{0,1},{1,0},{2,3},{3,2},{4,5},{5,4},{6,7},{7,6},{8,9},{9,8},{10,11... | collective-permute-start | bytes 1769480 | tf_op jit(solution)/shard_map/ppermute | solution.py:449
  3.5 1.6 %collective-permute-done.got_ref = bf16[144,2048]{1,0:T(8,128)(2,1)S(1)} collective-permute-done((bf16[144,2048]{1,0:T(8,128)(2,1)S(1)}, bf16[144,2048]{1,0:T(8,128)(2,1)S(1)}, u32[]{:S(2)}, u32[]{:S(2)}) %collective-permute-start) | collective-permute-done | bytes 589856 | tf_op jit(solution)/shard_map/ppermute | solution.py:449
  5.1 1.6 %pack.1 = (bf16[64,24,512]{2,1,0:T(8,128)(2,1)S(1)}, s32[8,128]{1,0:T(8,128)S(1)}) custom-call(s32[4]{0:T(128)S(1)} %pad_add_fusion.where_ref, bf16[144,2048]{1,0:T(8,128)(2,1)S(1)} %get-tuple-element.97.keep_ref, bf16[144,2048]{1,0:T(8,128)(2,1)S(1)} %collective-permute-done.got_ref), custom_call_target="tpu_custom_call" | custom-call | tf_op jit(solution)/shard_map/pack/pallas_call | solution.py:450
  6.7 33.4 %all_to_all.51.x_ref = bf16[64,24,512]{2,1,0:T(8,128)(2,1)S(1)} all-to-all(bf16[64,24,512]{2,1,0:T(8,128)(2,1)S(1)} %get-tuple-element.99), channel_id=1, replica_groups=mesh['x'=4,'z'=4,'y'=4,'c'=2] {'x','z','y'}, dimensions={0} | all-to-all | bytes 3145728 | tf_op jit(solution)/shard_map/all_to_all | solution.py:455
  40.1 2.1 %names.1 = (bf16[64,512]{1,0:T(8,128)(2,1)S(1)}, s32[8,1536]{1,0:T(8,128)S(1)}, s32[64,128]{1,0:T(8,128)S(1)}, s32[64,128]{1,0:T(8,128)S(1)}, s32[8,128]{1,0:T(8,128)S(1)}) custom-call(s32[4]{0:T(128)S(1)} %pad_add_fusion.where_ref, bf16[64,24,512]{2,1,0:T(8,128)(2,1)S(1)} %all_to_all.51.x_ref), custom_call_target="tpu_custom_call" | custom-call | tf_op jit(solution)/shard_map/names/pallas_call | solution.py:457
  42.2 2.4 %send.1.send_ref = bf16[1216,512]{1,0:T(8,128)(2,1)S(1)} custom-call(s32[4]{0:T(128)S(1)} %pad_add_fusion.where_ref, bf16[64,24,512]{2,1,0:T(8,128)(2,1)S(1)} %all_to_all.51.x_ref, s32[8,1536]{1,0:T(8,128)S(1)} %get-tuple-element.100.line_ref), custom_call_target="tpu_custom_call" | custom-call | flops 1912602624 | bytes 4194304 | tf_op jit(solution)/shard_map/send/pallas_call | solution.py:465
  44.7 3.0 %collective-permute-start.1 = (bf16[1216,512]{1,0:T(8,128)(2,1)S(1)}, bf16[1216,512]{1,0:T(8,128)(2,1)S(1)}, u32[]{:S(2)}, u32[]{:S(2)}) collective-permute-start(bf16[1216,512]{1,0:T(8,128)(2,1)S(1)} %send.1.send_ref), channel_id=1, source_target_pairs={{0,1},{1,0},{2,3},{3,2},{4,5},{5,4},{6,7},{7,6},{8,9},{9,8},{10,11... | collective-permute-start | bytes 3735560 | tf_op jit(solution)/shard_map/ppermute | solution.py:470
  47.7 0.3 collective-permute-start.2
  48.0 0.5 collective-permute-start.4
  48.5 1.9 %collective-permute-start.6 = (bf16[64,512]{1,0:T(8,128)(2,1)S(1)}, bf16[64,512]{1,0:T(8,128)(2,1)S(1)}, u32[]{:S(2)}, u32[]{:S(2)}) collective-permute-start(bf16[64,512]{1,0:T(8,128)(2,1)S(1)} %get-tuple-element.105), channel_id=1, source_target_pairs={{0,24},{8,0},{16,8},{24,16},{1,25},{9,1},{17,9},{25,17},{2,26},{10... | collective-permute-start | bytes 196616 | tf_op jit(solution)/shard_map/ppermute | solution.py:462
  50.4 3.6 %collective-permute-done.2.g1 = bf16[64,512]{1,0:T(8,128)(2,1)S(1)} collective-permute-done((bf16[64,512]{1,0:T(8,128)(2,1)S(1)}, bf16[64,512]{1,0:T(8,128)(2,1)S(1)}, u32[]{:S(2)}, u32[]{:S(2)}) %collective-permute-start.2) | collective-permute-done | bytes 65568 | tf_op jit(solution)/shard_map/ppermute | solution.py:462
  54.0 0.9 collective-permute-start.3
  54.8 0.0 collective-permute-done.4.g2
  54.8 0.0 collective-permute-start.5
  54.8 0.0 collective-permute-done.6.g3
  54.8 0.6 collective-permute-start.7
  55.4 3.7 %mine.1 = (bf16[1216,512]{1,0:T(8,128)(2,1)S(1)}, s32[8,256]{1,0:T(8,128)S(1)}, s32[8,128]{1,0:T(8,128)S(1)}) custom-call(s32[4]{0:T(128)S(1)} %pad_add_fusion.where_ref, bf16[64,24,512]{2,1,0:T(8,128)(2,1)S(1)} %all_to_all.51.x_ref, s32[8,1536]{1,0:T(8,128)S(1)} %get-tuple-element.100.line_ref, bf16[1216,512]{1,0:T(8,128)(2,1)S(1)} %send.1.send_ref, ...), custom_call_target="tpu_custom_call" | custom-call | flops 1912602624 | bytes 4194304 | tf_op jit(solution)/shard_map/mine/pallas_call | solution.py:471
  59.1 1.8 %own.1.raw_ref = f32[2560,128]{1,0:T(8,128)S(1)} custom-call(s32[4]{0:T(128)S(1)} %pad_add_fusion.where_ref, bf16[1216,512]{1,0:T(8,128)(2,1)S(1)} %get-tuple-element.107.x_ref, bf16[64,512]{1,0:T(8,128)(2,1)S(1)} %collective-permute-done.2.g1, bf16[64,512]{1,0:T(8,128)(2,1)S(1)} %collective-permute-done.4.g2, ...), custom_call_target="tpu_custom_call" | custom-call | flops 335544320 | bytes 4194304 | tf_op jit(solution)/shard_map/own/pallas_call | solution.py:477
  60.8 0.0 copy-start
  60.9 0.0 copy-start.1
  60.9 0.0 collective-permute-done.3.g1
  60.9 0.0 collective-permute-done.5.g2
  60.9 0.0 collective-permute-done.7.g3
  60.9 0.0 collective-permute-done.1.x_ref
  60.9 2.0 %gram.1 = (f32[448,128]{1,0:T(8,128)S(1)}, f32[448,128]{1,0:T(8,128)S(1)}, f32[448,128]{1,0:T(8,128)S(1)}, f32[448,128]{1,0:T(8,128)S(1)}) custom-call(s32[4]{0:T(128)S(1)} %pad_add_fusion.where_ref, s32[8,128]{1,0:T(8,128)S(1)} %get-tuple-element.104.meta_ref, bf16[1216,512]{1,0:T(8,128)(2,1)S(1)} %collective-permute-done.1.x_ref, ...), custom_call_target="tpu_custom_call" | custom-call | tf_op jit(solution)/shard_map/gram/pallas_call | solution.py:484
  62.9 0.4 collective-permute-start.8
  63.3 1.5 %collective-permute-start.9 = (f32[448,128]{1,0:T(8,128)S(1)}, f32[448,128]{1,0:T(8,128)S(1)}, u32[]{:S(2)}, u32[]{:S(2)}) collective-permute-start(f32[448,128]{1,0:T(8,128)S(1)} %get-tuple-element.110), channel_id=1, source_target_pairs={{0,4},{2,6},{4,0},{6,2},{1,5},{3,7},{5,1},{7,3},{8,12},{10,14},{12... | collective-permute-start | bytes 688136 | tf_op jit(solution)/shard_map/ppermute | solution.py:492
  64.8 1.4 %collective-permute-start.10 = (f32[448,128]{1,0:T(8,128)S(1)}, f32[448,128]{1,0:T(8,128)S(1)}, u32[]{:S(2)}, u32[]{:S(2)}) collective-permute-start(f32[448,128]{1,0:T(8,128)S(1)} %get-tuple-element.111), channel_id=1, source_target_pairs={{0,6},{2,0},{4,2},{6,4},{1,7},{3,1},{5,3},{7,5},{8,14},{10,8},{12,... | collective-permute-start | bytes 688136 | tf_op jit(solution)/shard_map/ppermute | solution.py:492
  66.1 10.0 %collective-permute-done.8.p1 = f32[448,128]{1,0:T(8,128)S(1)} collective-permute-done((f32[448,128]{1,0:T(8,128)S(1)}, f32[448,128]{1,0:T(8,128)S(1)}, u32[]{:S(2)}, u32[]{:S(2)}) %collective-permute-start.8) | collective-permute-done | bytes 229408 | tf_op jit(solution)/shard_map/ppermute | solution.py:492
  76.1 0.0 collective-permute-done.9.p2
  76.1 1.2 %collective-permute-done.10.p3 = f32[448,128]{1,0:T(8,128)S(1)} collective-permute-done((f32[448,128]{1,0:T(8,128)S(1)}, f32[448,128]{1,0:T(8,128)S(1)}, u32[]{:S(2)}, u32[]{:S(2)}) %collective-permute-start.10) | collective-permute-done | bytes 229408 | tf_op jit(solution)/shard_map/ppermute | solution.py:492
  77.3 1.9 %maxima.1 = f32[128,128]{1,0:T(8,128)} custom-call(s32[4]{0:T(128)S(1)} %pad_add_fusion.where_ref, s32[8,128]{1,0:T(8,128)S(1)} %get-tuple-element.104.meta_ref, f32[448,128]{1,0:T(8,128)S(1)} %get-tuple-element.108.p0, f32[448,128]{1,0:T(8,128)S(1)} %collective-permute-done.8.p1, f32[448,128]{1,0:T(8,128)S(1)} %collective-permute-done.9.p2, ...), custom_call_target="tpu_custom_call" | custom-call | tf_op jit(solution)/shard_map/maxima/pallas_call | solution.py:494
  79.2 6.3 %all-to-all-start.6 = ((f32[128,1,128]{2,1,0:T(1,128)}), f32[128,1,128]{2,1,0:T(1,128)S(1)}, u32[]{:S(2)}, u32[]{:S(2)}) async-start(f32[128,1,128]{2,1,0:T(1,128)} %bitcast.15), calls=%async_computation.6 | async-start | bytes 131072 | tf_op jit(solution)/shard_map/all_to_all | solution.py:501
  85.5 0.5 slice.3
  86.7 8.3 %all-to-all-done.6 = f32[128,1,128]{2,1,0:T(1,128)S(1)} async-done(((f32[128,1,128]{2,1,0:T(1,128)}), f32[128,1,128]{2,1,0:T(1,128)S(1)}, u32[]{:S(2)}, u32[]{:S(2)}) %all-to-all-start.6) | async-done | bytes 65568 | tf_op jit(solution)/shard_map/all_to_all | solution.py:501
  95.0 0.8 pick.1
  95.8 0.0 copy-done
  95.8 0.0 copy-done.1
  95.8 0.0 copy-start.2
  95.8 0.5 copy-done.2
  (1 shorter events, 0.0 us)
Async XLA Ops:
  2.0 3.1 %collective-permute-start = (bf16[144,2048]{1,0:T(8,128)(2,1)S(1)}, bf16[144,2048]{1,0:T(8,128)(2,1)S(1)}, u32[]{:S(2)}, u32[]{:S(2)}) collective-permute-start(bf16[144,2048]{1,0:T(8,128)(2,1)S(1)} %get-tuple-element.98), channel_id=1, source_target_pairs={{0,1},{1,0},{2,3},{3,2},{4,5},{5,4},{6,7},{7,6},{8,9},{9,8},{10,11... | collective-permute-start | bytes 1769480 | tf_op jit(solution)/shard_map/ppermute | solution.py:449
  44.7 16.2 %collective-permute-start.1 = (bf16[1216,512]{1,0:T(8,128)(2,1)S(1)}, bf16[1216,512]{1,0:T(8,128)(2,1)S(1)}, u32[]{:S(2)}, u32[]{:S(2)}) collective-permute-start(bf16[1216,512]{1,0:T(8,128)(2,1)S(1)} %send.1.send_ref), channel_id=1, source_target_pairs={{0,1},{1,0},{2,3},{3,2},{4,5},{5,4},{6,7},{7,6},{8,9},{9,8},{10,11... | collective-permute-start | bytes 3735560 | tf_op jit(solution)/shard_map/ppermute | solution.py:470
  47.7 6.3 %collective-permute-start.2 = (bf16[64,512]{1,0:T(8,128)(2,1)S(1)}, bf16[64,512]{1,0:T(8,128)(2,1)S(1)}, u32[]{:S(2)}, u32[]{:S(2)}) collective-permute-start(bf16[64,512]{1,0:T(8,128)(2,1)S(1)} %get-tuple-element.105), channel_id=1, source_target_pairs={{0,8},{8,16},{16,24},{24,0},{1,9},{9,17},{17,25},{25,1},{2,10},{10... | collective-permute-start | bytes 196616 | tf_op jit(solution)/shard_map/ppermute | solution.py:462
  48.0 6.8 %collective-permute-start.4 = (bf16[64,512]{1,0:T(8,128)(2,1)S(1)}, bf16[64,512]{1,0:T(8,128)(2,1)S(1)}, u32[]{:S(2)}, u32[]{:S(2)}) collective-permute-start(bf16[64,512]{1,0:T(8,128)(2,1)S(1)} %get-tuple-element.105), channel_id=1, source_target_pairs={{0,16},{8,24},{16,0},{24,8},{1,17},{9,25},{17,1},{25,9},{2,18},{10... | collective-permute-start | bytes 196616 | tf_op jit(solution)/shard_map/ppermute | solution.py:462
  48.5 6.3 %collective-permute-start.6 = (bf16[64,512]{1,0:T(8,128)(2,1)S(1)}, bf16[64,512]{1,0:T(8,128)(2,1)S(1)}, u32[]{:S(2)}, u32[]{:S(2)}) collective-permute-start(bf16[64,512]{1,0:T(8,128)(2,1)S(1)} %get-tuple-element.105), channel_id=1, source_target_pairs={{0,24},{8,0},{16,8},{24,16},{1,25},{9,1},{17,9},{25,17},{2,26},{10... | collective-permute-start | bytes 196616 | tf_op jit(solution)/shard_map/ppermute | solution.py:462
  54.0 6.9 %collective-permute-start.3 = (bf16[64,512]{1,0:T(8,128)(2,1)S(1)}, bf16[64,512]{1,0:T(8,128)(2,1)S(1)}, u32[]{:S(2)}, u32[]{:S(2)}) collective-permute-start(bf16[64,512]{1,0:T(8,128)(2,1)S(1)} %collective-permute-done.2.g1), channel_id=1, source_target_pairs={{0,1},{1,0},{2,3},{3,2},{4,5},{5,4},{6,7},{7,6},{8,9},{9,8},{10,11... | collective-permute-start | bytes 196616 | tf_op jit(solution)/shard_map/ppermute | solution.py:476
  54.8 6.1 %collective-permute-start.5 = (bf16[64,512]{1,0:T(8,128)(2,1)S(1)}, bf16[64,512]{1,0:T(8,128)(2,1)S(1)}, u32[]{:S(2)}, u32[]{:S(2)}) collective-permute-start(bf16[64,512]{1,0:T(8,128)(2,1)S(1)} %collective-permute-done.4.g2), channel_id=1, source_target_pairs={{0,1},{1,0},{2,3},{3,2},{4,5},{5,4},{6,7},{7,6},{8,9},{9,8},{10,11... | collective-permute-start | bytes 196616 | tf_op jit(solution)/shard_map/ppermute | solution.py:476
  54.8 6.1 %collective-permute-start.7 = (bf16[64,512]{1,0:T(8,128)(2,1)S(1)}, bf16[64,512]{1,0:T(8,128)(2,1)S(1)}, u32[]{:S(2)}, u32[]{:S(2)}) collective-permute-start(bf16[64,512]{1,0:T(8,128)(2,1)S(1)} %collective-permute-done.6.g3), channel_id=1, source_target_pairs={{0,1},{1,0},{2,3},{3,2},{4,5},{5,4},{6,7},{7,6},{8,9},{9,8},{10,11... | collective-permute-start | bytes 196616 | tf_op jit(solution)/shard_map/ppermute | solution.py:476
  60.8 34.9 %copy-start = (s32[128]{0:T(128)S(1)}, s32[128]{0:T(128)}, u32[]{:S(2)}) copy-start(s32[128]{0:T(128)} %param.7) | copy-start | bytes 1540
  60.9 34.9 %copy-start.1 = (f32[128,4096]{1,0:T(8,128)S(1)}, f32[128,4096]{1,0:T(8,128)}, u32[]{:S(2)}) copy-start(f32[128,4096]{1,0:T(8,128)} %x_ref.1) | copy-start | bytes 6291460
  62.9 13.2 %collective-permute-start.8 = (f32[448,128]{1,0:T(8,128)S(1)}, f32[448,128]{1,0:T(8,128)S(1)}, u32[]{:S(2)}, u32[]{:S(2)}) collective-permute-start(f32[448,128]{1,0:T(8,128)S(1)} %get-tuple-element.109), channel_id=1, source_target_pairs={{0,2},{2,4},{4,6},{6,0},{1,3},{3,5},{5,7},{7,1},{8,10},{10,12},{12... | collective-permute-start | bytes 688136 | tf_op jit(solution)/shard_map/ppermute | solution.py:492
  63.3 12.9 %collective-permute-start.9 = (f32[448,128]{1,0:T(8,128)S(1)}, f32[448,128]{1,0:T(8,128)S(1)}, u32[]{:S(2)}, u32[]{:S(2)}) collective-permute-start(f32[448,128]{1,0:T(8,128)S(1)} %get-tuple-element.110), channel_id=1, source_target_pairs={{0,4},{2,6},{4,0},{6,2},{1,5},{3,7},{5,1},{7,3},{8,12},{10,14},{12... | collective-permute-start | bytes 688136 | tf_op jit(solution)/shard_map/ppermute | solution.py:492
  64.8 12.6 %collective-permute-start.10 = (f32[448,128]{1,0:T(8,128)S(1)}, f32[448,128]{1,0:T(8,128)S(1)}, u32[]{:S(2)}, u32[]{:S(2)}) collective-permute-start(f32[448,128]{1,0:T(8,128)S(1)} %get-tuple-element.111), channel_id=1, source_target_pairs={{0,6},{2,0},{4,2},{6,4},{1,7},{3,1},{5,3},{7,5},{8,14},{10,8},{12,... | collective-permute-start | bytes 688136 | tf_op jit(solution)/shard_map/ppermute | solution.py:492
  79.2 15.8 %all-to-all-start.6 = ((f32[128,1,128]{2,1,0:T(1,128)}), f32[128,1,128]{2,1,0:T(1,128)S(1)}, u32[]{:S(2)}, u32[]{:S(2)}) async-start(f32[128,1,128]{2,1,0:T(1,128)} %bitcast.15), calls=%async_computation.6 | async-start | bytes 131072 | tf_op jit(solution)/shard_map/all_to_all | solution.py:501
  95.8 0.5 copy-start.2

commit v7 on v6

--- a/solution.py
+++ b/solution.py
@@ -473,6 +473,7 @@
         in_specs=[SCALARS] + [WHOLE] * 5, out_specs=(WHOLE,) * 3, compiler_params=params(20), name="mine",
         cost_estimate=pl.CostEstimate(flops=2 * SHARE_ROWS * WIDTH * slots, bytes_accessed=4 << 20, transcendentals=0),
     )(where, packed, line, send, key, pos)
+    brought, mine = lax.optimization_barrier((brought, mine))
     swapped = [lax.ppermute(v, "c", [(0, 1), (1, 0)]) for v in brought]
     raw = pl.pallas_call(
         own_kernel, out_shape=shape((RAW_ROWS, LANES), f32),
@@ -491,6 +492,7 @@
     arrived = [partial[0]] + [
         lax.ppermute(partial[s], "y", [(i, (i + s) % 4) for i in range(4)]) for s in (1, 2, 3)
     ]
+    arrived, fits = lax.optimization_barrier((arrived, over[0, 0] == 0))
     best = pl.pallas_call(
         max_kernel,
         out_shape=shape((2 * CHIPS, LANES), f32),
@@ -505,7 +507,7 @@
         in_specs=[SCALARS, WHOLE, WHOLE], out_specs=WHOLE, compiler_params=params(8), name="pick",
     )(where, back.reshape(2 * CHIPS, LANES), code).reshape(ROWS)
     return lax.cond(
-        over[0, 0] == 0,
+        fits,
         lambda fitted, embeddings, cluster_ids: fitted,
         lambda fitted, embeddings, cluster_ids: gather_groups(embeddings, cluster_ids),
         fitted, embeddings, cluster_ids,

time: 96.5 us -> 93.3 us (0.967)
  waiting for transfers between devices: 24.7 us -> 21.3 us
    ppermute x3, waiting for transfers between devices: 3.58 us -> 0.31 us  [on_device(): lax.ppermute(guests, 'z', [(i, (i + s) % 4) for i in range(4)])]
    ppermute x3, waiting for transfers between devices: 11.2 us -> 9.88 us  [on_device(): lax.ppermute(partial[s], 'y', [(i, (i + s) % 4) for i in range(4)])]
    all_to_all x1, waiting for transfers between devices: 8.3 us -> 9.47 us  [on_device(): lax.all_to_all(best.reshape(2 * CHIPS, 1, LANES), ('c', 'x', 'z', 'y'), 0...]
  transfers between devices with their start and end apart: 12 -> 12, of which waited for: 5 -> 6; matrix products, arithmetic and copies ran while one was open for 1% -> 1% of each run, Pallas kernels for 6% -> 6%
where the time goes in v7:
time: 93.3 us; the launch traced here: 93.1 us
  blocking collectives  33.4 us (36%)
  waiting for transfers between devices  21.3 us (23%)
  starting transfers between devices  18.6 us (20%)
  Pallas kernels  17.9 us (19%)
  local copies, waits for them, and re-layouts  1.03 us (1%)
    all_to_all x1, blocking collectives, on_device(): packed = lax.all_to_all(packed, ('x', 'z', 'y'), 0, 0, tiled=True)  33.4 us
    ppermute x3, waiting for transfers between devices, on_device(): lax.ppermute(partial[s], 'y', [(i, (i + s) % 4) for i in range(4)])  9.88 us
    all_to_all x1, waiting for transfers between devices, on_device(): lax.all_to_all(best.reshape(2 * CHIPS, 1, LANES), ('c', 'x', 'z', 'y'), 0...  9.47 us
    all_to_all x1, starting transfers between devices, on_device(): lax.all_to_all(best.reshape(2 * CHIPS, 1, LANES), ('c', 'x', 'z', 'y'), 0...  6.5 us
    pallas_call x1, Pallas kernels, on_device(): pl.pallas_call(mine_kernel, out_shape=(share, shape((8, ALL_GUESTS), i32)...  3.51 us
    ppermute x3, starting transfers between devices, on_device(): lax.ppermute(partial[s], 'y', [(i, (i + s) % 4) for i in range(4)])  3.22 us
    ppermute x1, starting transfers between devices, on_device(): other = lax.ppermute(send, 'c', [(0, 1), (1, 0)])  2.99 us
    ppermute x3, starting transfers between devices, on_device(): lax.ppermute(guests, 'z', [(i, (i + s) % 4) for i in range(4)])  2.71 us
  transfers between devices with their start and end apart: 12, of which 6 were waited for; matrix products, arithmetic and copies ran while one was open for 1% of the time, Pallas kernels for 6%

profile of v7, /device:TPU:1, one launch (start us, length us, event | category | flops | bytes accessed | tf_op | source)
XLA Modules:
  0.0 93.1 jit_solution(1258263999162707315)
XLA Ops:
  0.0 0.1 pad_add_fusion.where_ref
  0.1 1.9 %unit.1 = (bf16[144,2048]{1,0:T(8,128)(2,1)S(1)}, bf16[144,2048]{1,0:T(8,128)(2,1)S(1)}) custom-call(s32[4]{0:T(128)S(1)} %pad_add_fusion.where_ref, f32[128,4096]{1,0:T(8,128)} %x_ref.1, s32[1,128]{1,0:T(1,128)} %bitcast.30), custom_call_target="tpu_custom_call" | custom-call | tf_op jit(solution)/shard_map/unit/pallas_call | solution.py:445
  2.0 1.5 %collective-permute-start = (bf16[144,2048]{1,0:T(8,128)(2,1)S(1)}, bf16[144,2048]{1,0:T(8,128)(2,1)S(1)}, u32[]{:S(2)}, u32[]{:S(2)}) collective-permute-start(bf16[144,2048]{1,0:T(8,128)(2,1)S(1)} %get-tuple-element.107), channel_id=1, source_target_pairs={{0,1},{1,0},{2,3},{3,2},{4,5},{5,4},{6,7},{7,6},{8,9},{9,8},{10,11... | collective-permute-start | bytes 1769480 | tf_op jit(solution)/shard_map/ppermute | solution.py:449
  3.5 1.6 %collective-permute-done.got_ref = bf16[144,2048]{1,0:T(8,128)(2,1)S(1)} collective-permute-done((bf16[144,2048]{1,0:T(8,128)(2,1)S(1)}, bf16[144,2048]{1,0:T(8,128)(2,1)S(1)}, u32[]{:S(2)}, u32[]{:S(2)}) %collective-permute-start) | collective-permute-done | bytes 589856 | tf_op jit(solution)/shard_map/ppermute | solution.py:449
  5.1 1.6 %pack.1 = (bf16[64,24,512]{2,1,0:T(8,128)(2,1)S(1)}, s32[8,128]{1,0:T(8,128)S(1)}) custom-call(s32[4]{0:T(128)S(1)} %pad_add_fusion.where_ref, bf16[144,2048]{1,0:T(8,128)(2,1)S(1)} %get-tuple-element.106.keep_ref, bf16[144,2048]{1,0:T(8,128)(2,1)S(1)} %collective-permute-done.got_ref), custom_call_target="tpu_custom_call" | custom-call | tf_op jit(solution)/shard_map/pack/pallas_call | solution.py:450
  6.7 33.4 %all_to_all.51.x_ref = bf16[64,24,512]{2,1,0:T(8,128)(2,1)S(1)} all-to-all(bf16[64,24,512]{2,1,0:T(8,128)(2,1)S(1)} %get-tuple-element.108), channel_id=1, replica_groups=mesh['x'=4,'z'=4,'y'=4,'c'=2] {'x','z','y'}, dimensions={0} | all-to-all | bytes 3145728 | tf_op jit(solution)/shard_map/all_to_all | solution.py:455
  40.1 2.1 %names.1 = (bf16[64,512]{1,0:T(8,128)(2,1)S(1)}, s32[8,1536]{1,0:T(8,128)S(1)}, s32[64,128]{1,0:T(8,128)S(1)}, s32[64,128]{1,0:T(8,128)S(1)}, s32[8,128]{1,0:T(8,128)S(1)}) custom-call(s32[4]{0:T(128)S(1)} %pad_add_fusion.where_ref, bf16[64,24,512]{2,1,0:T(8,128)(2,1)S(1)} %all_to_all.51.x_ref), custom_call_target="tpu_custom_call" | custom-call | tf_op jit(solution)/shard_map/names/pallas_call | solution.py:457
  42.2 2.4 %send.1.send_ref = bf16[1216,512]{1,0:T(8,128)(2,1)S(1)} custom-call(s32[4]{0:T(128)S(1)} %pad_add_fusion.where_ref, bf16[64,24,512]{2,1,0:T(8,128)(2,1)S(1)} %all_to_all.51.x_ref, s32[8,1536]{1,0:T(8,128)S(1)} %get-tuple-element.110.line_ref), custom_call_target="tpu_custom_call" | custom-call | flops 1912602624 | bytes 4194304 | tf_op jit(solution)/shard_map/send/pallas_call | solution.py:465
  44.7 3.0 %collective-permute-start.1 = (bf16[1216,512]{1,0:T(8,128)(2,1)S(1)}, bf16[1216,512]{1,0:T(8,128)(2,1)S(1)}, u32[]{:S(2)}, u32[]{:S(2)}) collective-permute-start(bf16[1216,512]{1,0:T(8,128)(2,1)S(1)} %send.1.send_ref), channel_id=1, source_target_pairs={{0,1},{1,0},{2,3},{3,2},{4,5},{5,4},{6,7},{7,6},{8,9},{9,8},{10,11... | collective-permute-start | bytes 3735560 | tf_op jit(solution)/shard_map/ppermute | solution.py:470
  47.7 0.3 collective-permute-start.2
  48.0 0.5 collective-permute-start.3
  48.5 1.9 %collective-permute-start.4 = (bf16[64,512]{1,0:T(8,128)(2,1)S(1)}, bf16[64,512]{1,0:T(8,128)(2,1)S(1)}, u32[]{:S(2)}, u32[]{:S(2)}) collective-permute-start(bf16[64,512]{1,0:T(8,128)(2,1)S(1)} %get-tuple-element.111), channel_id=1, source_target_pairs={{0,24},{8,0},{16,8},{24,16},{1,25},{9,1},{17,9},{25,17},{2,26},{10... | collective-permute-start | bytes 196616 | tf_op jit(solution)/shard_map/ppermute | solution.py:462
  50.4 3.5 %mine.1 = (bf16[1216,512]{1,0:T(8,128)(2,1)S(1)}, s32[8,256]{1,0:T(8,128)S(1)}, s32[8,128]{1,0:T(8,128)S(1)}) custom-call(s32[4]{0:T(128)S(1)} %pad_add_fusion.where_ref, bf16[64,24,512]{2,1,0:T(8,128)(2,1)S(1)} %all_to_all.51.x_ref, s32[8,1536]{1,0:T(8,128)S(1)} %get-tuple-element.110.line_ref, bf16[1216,512]{1,0:T(8,128)(2,1)S(1)} %send.1.send_ref, ...), custom_call_target="tpu_custom_call" | custom-call | flops 1912602624 | bytes 4194304 | tf_op jit(solution)/shard_map/mine/pallas_call | solution.py:471
  53.9 0.1 collective-permute-done.2.g1
  54.0 0.0 collective-permute-done.3.g2
  54.0 0.3 collective-permute-done.4.g3
  54.2 1.2 %collective-permute-start.5 = (bf16[64,512]{1,0:T(8,128)(2,1)S(1)}, bf16[64,512]{1,0:T(8,128)(2,1)S(1)}, u32[]{:S(2)}, u32[]{:S(2)}) collective-permute-start(bf16[64,512]{1,0:T(8,128)(2,1)S(1)} %collective-permute-done.2.g1), channel_id=1, source_target_pairs={{0,1},{1,0},{2,3},{3,2},{4,5},{5,4},{6,7},{7,6},{8,9},{9,8},{10,11... | collective-permute-start | bytes 196616 | tf_op jit(solution)/shard_map/ppermute | solution.py:477
  55.4 0.0 collective-permute-start.6
  55.4 0.5 collective-permute-start.7
  55.9 1.7 %own.1.raw_ref = f32[2560,128]{1,0:T(8,128)S(1)} custom-call(s32[4]{0:T(128)S(1)} %pad_add_fusion.where_ref, bf16[1216,512]{1,0:T(8,128)(2,1)S(1)} %get-tuple-element.119.x_ref, bf16[64,512]{1,0:T(8,128)(2,1)S(1)} %collective-permute-done.2.g1, bf16[64,512]{1,0:T(8,128)(2,1)S(1)} %collective-permute-done.3.g2, ...), custom_call_target="tpu_custom_call" | custom-call | flops 335544320 | bytes 4194304 | tf_op jit(solution)/shard_map/own/pallas_call | solution.py:478
  57.7 0.0 copy-start
  57.7 0.0 copy-start.1
  57.7 0.0 collective-permute-done.5.g1
  57.7 0.0 collective-permute-done.6.g2
  57.7 0.0 collective-permute-done.7.g3
  57.7 0.0 collective-permute-done.1.x_ref
  57.7 2.0 %gram.1 = (f32[448,128]{1,0:T(8,128)S(1)}, f32[448,128]{1,0:T(8,128)S(1)}, f32[448,128]{1,0:T(8,128)S(1)}, f32[448,128]{1,0:T(8,128)S(1)}) custom-call(s32[4]{0:T(128)S(1)} %pad_add_fusion.where_ref, s32[8,128]{1,0:T(8,128)S(1)} %get-tuple-element.109.meta_ref, bf16[1216,512]{1,0:T(8,128)(2,1)S(1)} %collective-permute-done.1.x_ref, ...), custom_call_target="tpu_custom_call" | custom-call | tf_op jit(solution)/shard_map/gram/pallas_call | solution.py:485
  59.7 0.4 collective-permute-start.8
  60.1 1.5 %collective-permute-start.9 = (f32[448,128]{1,0:T(8,128)S(1)}, f32[448,128]{1,0:T(8,128)S(1)}, u32[]{:S(2)}, u32[]{:S(2)}) collective-permute-start(f32[448,128]{1,0:T(8,128)S(1)} %get-tuple-element.122), channel_id=1, source_target_pairs={{0,4},{2,6},{4,0},{6,2},{1,5},{3,7},{5,1},{7,3},{8,12},{10,14},{12... | collective-permute-start | bytes 688136 | tf_op jit(solution)/shard_map/ppermute | solution.py:493
  61.6 1.4 %collective-permute-start.10 = (f32[448,128]{1,0:T(8,128)S(1)}, f32[448,128]{1,0:T(8,128)S(1)}, u32[]{:S(2)}, u32[]{:S(2)}) collective-permute-start(f32[448,128]{1,0:T(8,128)S(1)} %get-tuple-element.123), channel_id=1, source_target_pairs={{0,6},{2,0},{4,2},{6,4},{1,7},{3,1},{5,3},{7,5},{8,14},{10,8},{12,... | collective-permute-start | bytes 688136 | tf_op jit(solution)/shard_map/ppermute | solution.py:493
  62.9 0.5 slice.3
  64.1 9.2 %collective-permute-done.8.p1 = f32[448,128]{1,0:T(8,128)S(1)} collective-permute-done((f32[448,128]{1,0:T(8,128)S(1)}, f32[448,128]{1,0:T(8,128)S(1)}, u32[]{:S(2)}, u32[]{:S(2)}) %collective-permute-start.8) | collective-permute-done | bytes 229408 | tf_op jit(solution)/shard_map/ppermute | solution.py:493
  73.3 0.0 collective-permute-done.9.p2
  73.3 0.7 collective-permute-done.10.p3
  74.0 1.9 %maxima.1 = f32[128,128]{1,0:T(8,128)} custom-call(s32[4]{0:T(128)S(1)} %pad_add_fusion.where_ref, s32[8,128]{1,0:T(8,128)S(1)} %get-tuple-element.109.meta_ref, f32[448,128]{1,0:T(8,128)S(1)} %get-tuple-element.126.p0, f32[448,128]{1,0:T(8,128)S(1)} %collective-permute-done.8.p1, f32[448,128]{1,0:T(8,128)S(1)} %collective-permute-done.9.p2, ...), custom_call_target="tpu_custom_call" | custom-call | tf_op jit(solution)/shard_map/maxima/pallas_call | solution.py:496
  75.8 6.5 %all-to-all-start.6 = ((f32[128,1,128]{2,1,0:T(1,128)}), f32[128,1,128]{2,1,0:T(1,128)S(1)}, u32[]{:S(2)}, u32[]{:S(2)}) async-start(f32[128,1,128]{2,1,0:T(1,128)} %bitcast.15), calls=%async_computation.6 | async-start | bytes 131072 | tf_op jit(solution)/shard_map/all_to_all | solution.py:503
  82.3 9.5 %all-to-all-done.6 = f32[128,1,128]{2,1,0:T(1,128)S(1)} async-done(((f32[128,1,128]{2,1,0:T(1,128)}), f32[128,1,128]{2,1,0:T(1,128)S(1)}, u32[]{:S(2)}, u32[]{:S(2)}) %all-to-all-start.6) | async-done | bytes 65568 | tf_op jit(solution)/shard_map/all_to_all | solution.py:503
  91.8 0.0 copy-done
  91.8 0.0 copy-done.1
  91.8 0.8 pick.1
  92.6 0.0 copy-start.2
  92.6 0.5 copy-done.2
  (1 shorter events, 0.0 us)
Async XLA Ops:
  2.0 3.1 %collective-permute-start = (bf16[144,2048]{1,0:T(8,128)(2,1)S(1)}, bf16[144,2048]{1,0:T(8,128)(2,1)S(1)}, u32[]{:S(2)}, u32[]{:S(2)}) collective-permute-start(bf16[144,2048]{1,0:T(8,128)(2,1)S(1)} %get-tuple-element.107), channel_id=1, source_target_pairs={{0,1},{1,0},{2,3},{3,2},{4,5},{5,4},{6,7},{7,6},{8,9},{9,8},{10,11... | collective-permute-start | bytes 1769480 | tf_op jit(solution)/shard_map/ppermute | solution.py:449
  44.7 13.0 %collective-permute-start.1 = (bf16[1216,512]{1,0:T(8,128)(2,1)S(1)}, bf16[1216,512]{1,0:T(8,128)(2,1)S(1)}, u32[]{:S(2)}, u32[]{:S(2)}) collective-permute-start(bf16[1216,512]{1,0:T(8,128)(2,1)S(1)} %send.1.send_ref), channel_id=1, source_target_pairs={{0,1},{1,0},{2,3},{3,2},{4,5},{5,4},{6,7},{7,6},{8,9},{9,8},{10,11... | collective-permute-start | bytes 3735560 | tf_op jit(solution)/shard_map/ppermute | solution.py:470
  47.7 6.3 %collective-permute-start.2 = (bf16[64,512]{1,0:T(8,128)(2,1)S(1)}, bf16[64,512]{1,0:T(8,128)(2,1)S(1)}, u32[]{:S(2)}, u32[]{:S(2)}) collective-permute-start(bf16[64,512]{1,0:T(8,128)(2,1)S(1)} %get-tuple-element.111), channel_id=1, source_target_pairs={{0,8},{8,16},{16,24},{24,0},{1,9},{9,17},{17,25},{25,1},{2,10},{10... | collective-permute-start | bytes 196616 | tf_op jit(solution)/shard_map/ppermute | solution.py:462
  48.0 6.0 %collective-permute-start.3 = (bf16[64,512]{1,0:T(8,128)(2,1)S(1)}, bf16[64,512]{1,0:T(8,128)(2,1)S(1)}, u32[]{:S(2)}, u32[]{:S(2)}) collective-permute-start(bf16[64,512]{1,0:T(8,128)(2,1)S(1)} %get-tuple-element.111), channel_id=1, source_target_pairs={{0,16},{8,24},{16,0},{24,8},{1,17},{9,25},{17,1},{25,9},{2,18},{10... | collective-permute-start | bytes 196616 | tf_op jit(solution)/shard_map/ppermute | solution.py:462
  48.5 5.7 %collective-permute-start.4 = (bf16[64,512]{1,0:T(8,128)(2,1)S(1)}, bf16[64,512]{1,0:T(8,128)(2,1)S(1)}, u32[]{:S(2)}, u32[]{:S(2)}) collective-permute-start(bf16[64,512]{1,0:T(8,128)(2,1)S(1)} %get-tuple-element.111), channel_id=1, source_target_pairs={{0,24},{8,0},{16,8},{24,16},{1,25},{9,1},{17,9},{25,17},{2,26},{10... | collective-permute-start | bytes 196616 | tf_op jit(solution)/shard_map/ppermute | solution.py:462
  54.2 3.5 %collective-permute-start.5 = (bf16[64,512]{1,0:T(8,128)(2,1)S(1)}, bf16[64,512]{1,0:T(8,128)(2,1)S(1)}, u32[]{:S(2)}, u32[]{:S(2)}) collective-permute-start(bf16[64,512]{1,0:T(8,128)(2,1)S(1)} %collective-permute-done.2.g1), channel_id=1, source_target_pairs={{0,1},{1,0},{2,3},{3,2},{4,5},{5,4},{6,7},{7,6},{8,9},{9,8},{10,11... | collective-permute-start | bytes 196616 | tf_op jit(solution)/shard_map/ppermute | solution.py:477
  55.4 2.3 %collective-permute-start.6 = (bf16[64,512]{1,0:T(8,128)(2,1)S(1)}, bf16[64,512]{1,0:T(8,128)(2,1)S(1)}, u32[]{:S(2)}, u32[]{:S(2)}) collective-permute-start(bf16[64,512]{1,0:T(8,128)(2,1)S(1)} %collective-permute-done.3.g2), channel_id=1, source_target_pairs={{0,1},{1,0},{2,3},{3,2},{4,5},{5,4},{6,7},{7,6},{8,9},{9,8},{10,11... | collective-permute-start | bytes 196616 | tf_op jit(solution)/shard_map/ppermute | solution.py:477
  55.4 2.3 %collective-permute-start.7 = (bf16[64,512]{1,0:T(8,128)(2,1)S(1)}, bf16[64,512]{1,0:T(8,128)(2,1)S(1)}, u32[]{:S(2)}, u32[]{:S(2)}) collective-permute-start(bf16[64,512]{1,0:T(8,128)(2,1)S(1)} %collective-permute-done.4.g3), channel_id=1, source_target_pairs={{0,1},{1,0},{2,3},{3,2},{4,5},{5,4},{6,7},{7,6},{8,9},{9,8},{10,11... | collective-permute-start | bytes 196616 | tf_op jit(solution)/shard_map/ppermute | solution.py:477
  57.7 34.1 %copy-start = (s32[128]{0:T(128)S(1)}, s32[128]{0:T(128)}, u32[]{:S(2)}) copy-start(s32[128]{0:T(128)} %param.7) | copy-start | bytes 1540
  57.7 34.1 %copy-start.1 = (f32[128,4096]{1,0:T(8,128)S(1)}, f32[128,4096]{1,0:T(8,128)}, u32[]{:S(2)}) copy-start(f32[128,4096]{1,0:T(8,128)} %x_ref.1) | copy-start | bytes 6291460
  59.7 13.6 %collective-permute-start.8 = (f32[448,128]{1,0:T(8,128)S(1)}, f32[448,128]{1,0:T(8,128)S(1)}, u32[]{:S(2)}, u32[]{:S(2)}) collective-permute-start(f32[448,128]{1,0:T(8,128)S(1)} %get-tuple-element.121), channel_id=1, source_target_pairs={{0,2},{2,4},{4,6},{6,0},{1,3},{3,5},{5,7},{7,1},{8,10},{10,12},{12... | collective-permute-start | bytes 688136 | tf_op jit(solution)/shard_map/ppermute | solution.py:493
  60.1 13.2 %collective-permute-start.9 = (f32[448,128]{1,0:T(8,128)S(1)}, f32[448,128]{1,0:T(8,128)S(1)}, u32[]{:S(2)}, u32[]{:S(2)}) collective-permute-start(f32[448,128]{1,0:T(8,128)S(1)} %get-tuple-element.122), channel_id=1, source_target_pairs={{0,4},{2,6},{4,0},{6,2},{1,5},{3,7},{5,1},{7,3},{8,12},{10,14},{12... | collective-permute-start | bytes 688136 | tf_op jit(solution)/shard_map/ppermute | solution.py:493
  61.6 12.4 %collective-permute-start.10 = (f32[448,128]{1,0:T(8,128)S(1)}, f32[448,128]{1,0:T(8,128)S(1)}, u32[]{:S(2)}, u32[]{:S(2)}) collective-permute-start(f32[448,128]{1,0:T(8,128)S(1)} %get-tuple-element.123), channel_id=1, source_target_pairs={{0,6},{2,0},{4,2},{6,4},{1,7},{3,1},{5,3},{7,5},{8,14},{10,8},{12,... | collective-permute-start | bytes 688136 | tf_op jit(solution)/shard_map/ppermute | solution.py:493
  75.8 16.0 %all-to-all-start.6 = ((f32[128,1,128]{2,1,0:T(1,128)}), f32[128,1,128]{2,1,0:T(1,128)S(1)}, u32[]{:S(2)}, u32[]{:S(2)}) async-start(f32[128,1,128]{2,1,0:T(1,128)} %bitcast.15), calls=%async_computation.6 | async-start | bytes 131072 | tf_op jit(solution)/shard_map/all_to_all | solution.py:503
  92.6 0.5 copy-start.2

commit v8 on v7

--- a/solution.py
+++ b/solution.py
@@ -44,6 +44,10 @@
     return pltpu.CompilerParams(vmem_limit_bytes=mib * 1024 * 1024)
 
 
+def index_on(axis):
+    return lax.axis_index(axis)
+
+
 def iota(shape, dim):
     return lax.broadcasted_iota(i32, shape, dim)
 
@@ -67,8 +71,8 @@
     return 4 * col + ((row - residue) & 3)
 
 
-def unit_kernel(where_ref, x_ref, ids_ref, keep_ref, send_ref):
-    c = where_ref[3]
+def unit_kernel(x_ref, ids_ref, keep_ref, send_ref):
+    c = index_on("c")
     x = x_ref[...]
     scale = lax.rsqrt(jnp.sum(x * x, axis=1, keepdims=True) + 1e-06)
     ids = jnp.concatenate([ids_ref[...].astype(f32), jnp.zeros((1, HALF_WIDTH - ROWS), f32)], axis=1)
@@ -79,8 +83,8 @@
         out_ref[ROWS:, :] = ids
 
 
-def pack_kernel(where_ref, keep_ref, got_ref, out_ref, code_ref):
-    y, first = where_ref[2], where_ref[3] == 0
+def pack_kernel(keep_ref, got_ref, out_ref, code_ref):
+    y, first = index_on("y"), index_on("c") == 0
     kept = jnp.max(keep_ref[ROWS:, :ROWS].astype(f32), axis=0, keepdims=True)
     got = jnp.max(got_ref[ROWS:, :ROWS].astype(f32), axis=0, keepdims=True)
     labels = jnp.concatenate([jnp.where(first, kept, got), jnp.where(first, got, kept)], axis=0).astype(i32)
@@ -162,8 +166,8 @@
     return first, jnp.maximum(e, g), jnp.minimum(e, g), fourth
 
 
-def names_kernel(where_ref, x_ref, guest_ref, line_ref, key_ref, pos_ref, meta_ref):
-    mine, z = where_ref[0] * 4 + where_ref[1], where_ref[1]
+def names_kernel(x_ref, guest_ref, line_ref, key_ref, pos_ref, meta_ref):
+    mine, z = index_on("x") * 4 + index_on("z"), index_on("z")
     labels, chip_counts = labels_of(x_ref)
     _, sizes = counts_of(chip_counts)
     here = iota((1, LANES), 1) == mine
@@ -223,11 +227,11 @@
     return dot(onehot, x).astype(bf16)
 
 
-def send_kernel(where_ref, x_ref, line_ref, send_ref):
+def send_kernel(x_ref, line_ref, send_ref):
     x = x_ref[...].reshape(CHIPS * BLOCK, WIDTH)
     slots = line_ref[:1, :]
     for me in range(2):
-        @pl.when(where_ref[3] == me)
+        @pl.when(index_on("c") == me)
         def _():
             for segment in SEGMENTS:
                 at = segment[2 + 1 - me]
@@ -235,11 +239,11 @@
                     send_ref[at:at + segment[1], :] = sorted_rows(segment, slots, x)
 
 
-def mine_kernel(where_ref, x_ref, line_ref, send_ref, key_ref, pos_ref, mine_ref, far_ref, over_ref):
+def mine_kernel(x_ref, line_ref, send_ref, key_ref, pos_ref, mine_ref, far_ref, over_ref):
     x = x_ref[...].reshape(CHIPS * BLOCK, WIDTH)
     slots = line_ref[:1, :]
     for core in range(2):
-        @pl.when(where_ref[3] == core)
+        @pl.when(index_on("c") == core)
         def _():
             for segment in SEGMENTS:
                 at, sent = segment[2 + core], segment[2 + 1 - core]
@@ -299,9 +303,9 @@
 RAW_ROWS = max(sum(CAPS[q] - first for q, first in share) for share in SHARES)
 
 
-def own_kernel(where_ref, x_ref, g1, g2, g3, far_ref, raw_ref, rows_ref):
+def own_kernel(x_ref, g1, g2, g3, far_ref, raw_ref, rows_ref):
     for core in range(2):
-        @pl.when(where_ref[3] == core)
+        @pl.when(index_on("c") == core)
         def _():
             add_guests(core, x_ref, (g1, g2, g3), far_ref, rows_ref)
             at = 0
@@ -315,8 +319,8 @@
     return jnp.maximum(((size + HALF - 1) >> 6) - first // HALF, 0)
 
 
-def gram_kernel(where_ref, meta_ref, x_ref, g1, g2, g3, far_ref, raw_ref, out0, out1, out2, out3, part_ref, rows_ref):
-    y, c = where_ref[2], where_ref[3]
+def gram_kernel(meta_ref, x_ref, g1, g2, g3, far_ref, raw_ref, out0, out1, out2, out3, part_ref, rows_ref):
+    y, c = index_on("y"), index_on("c")
     part_ref[...] = jnp.full(part_ref.shape, -4.0, f32)
     for core in range(2):
         @pl.when(c == core)
@@ -339,8 +343,8 @@
 FIRST_ROW = (0, 6, 10, 13)
 
 
-def max_kernel(where_ref, meta_ref, p0, p1, p2, p3, pos_ref, out_ref, best_ref):
-    y, c = where_ref[2], where_ref[3]
+def max_kernel(meta_ref, p0, p1, p2, p3, pos_ref, out_ref, best_ref):
+    y, c = index_on("y"), index_on("c")
     best_ref[...] = jnp.full(best_ref.shape, -1.0, f32)
     sub, lane = iota((HALF, LANES), 0), iota((HALF, LANES), 1)
     blocks = []
@@ -379,8 +383,8 @@
     out_ref[CHIPS:, :] = out
 
 
-def pick_kernel(where_ref, v_ref, code_ref, out_ref):
-    c = where_ref[3]
+def pick_kernel(v_ref, code_ref, out_ref):
+    c = index_on("c")
     values = jnp.maximum(v_ref[:CHIPS, :], v_ref[CHIPS:, :])
     values = jnp.max(values.reshape(BINS, 4, LANES), axis=1)
     eye = iota((LANES, LANES), 0) == iota((LANES, LANES), 1)
@@ -439,56 +443,55 @@
 
 
 def on_device(embeddings, cluster_ids):
-    where = jnp.stack([lax.axis_index(a) for a in ("x", "z", "y", "c")]).astype(i32)
     shape = jax.ShapeDtypeStruct
     half = shape((ROWS + LABEL_ROWS, HALF_WIDTH), bf16)
     keep, send = pl.pallas_call(
         unit_kernel, out_shape=(half, half),
-        in_specs=[SCALARS, WHOLE, WHOLE], out_specs=(WHOLE, WHOLE), compiler_params=params(12), name="unit",
-    )(where, embeddings, cluster_ids.reshape(1, ROWS))
+        in_specs=[WHOLE, WHOLE], out_specs=(WHOLE, WHOLE), compiler_params=params(12), name="unit",
+    )(embeddings, cluster_ids.reshape(1, ROWS))
     got = lax.ppermute(send, "c", [(0, 1), (1, 0)])
     packed, code = pl.pallas_call(
         pack_kernel,
         out_shape=(shape((CHIPS, BLOCK, WIDTH), bf16), shape((8, ROWS), i32)),
-        in_specs=[SCALARS, WHOLE, WHOLE], out_specs=(WHOLE, WHOLE), compiler_params=params(20), name="pack",
-    )(where, keep, got)
+        in_specs=[WHOLE, WHOLE], out_specs=(WHOLE, WHOLE), compiler_params=params(20), name="pack",
+    )(keep, got)
     packed = lax.all_to_all(packed, ("x", "z", "y"), 0, 0, tiled=True)
     table = shape((CHIPS, LANES), i32)
     guests, line, key, pos, meta = pl.pallas_call(
         names_kernel,
         out_shape=(shape((GUESTS, WIDTH), bf16), shape((8, CHIPS * BLOCK), i32), table, table, shape((8, LANES), i32)),
-        in_specs=[SCALARS, WHOLE], out_specs=(WHOLE,) * 5, compiler_params=params(12), name="names",
-    )(where, packed)
+        in_specs=[WHOLE], out_specs=(WHOLE,) * 5, compiler_params=params(12), name="names",
+    )(packed)
     brought = [lax.ppermute(guests, "z", [(i, (i + s) % 4) for i in range(4)]) for s in (1, 2, 3)]
     share = shape((SHARE_ROWS, WIDTH), bf16)
     slots = CHIPS * BLOCK
     send = pl.pallas_call(
         send_kernel, out_shape=share,
-        in_specs=[SCALARS, WHOLE, WHOLE], out_specs=WHOLE, compiler_params=params(16), name="send",
+        in_specs=[WHOLE, WHOLE], out_specs=WHOLE, compiler_params=params(16), name="send",
         cost_estimate=pl.CostEstimate(flops=2 * SHARE_ROWS * WIDTH * slots, bytes_accessed=4 << 20, transcendentals=0),
-    )(where, packed, line)
+    )(packed, line)
     other = lax.ppermute(send, "c", [(0, 1), (1, 0)])
     mine, far, over = pl.pallas_call(
         mine_kernel, out_shape=(share, shape((8, ALL_GUESTS), i32), shape((8, LANES), i32)),
-        in_specs=[SCALARS] + [WHOLE] * 5, out_specs=(WHOLE,) * 3, compiler_params=params(20), name="mine",
+        in_specs=[WHOLE] * 5, out_specs=(WHOLE,) * 3, compiler_params=params(20), name="mine",
         cost_estimate=pl.CostEstimate(flops=2 * SHARE_ROWS * WIDTH * slots, bytes_accessed=4 << 20, transcendentals=0),
-    )(where, packed, line, send, key, pos)
+    )(packed, line, send, key, pos)
     brought, mine = lax.optimization_barrier((brought, mine))
     swapped = [lax.ppermute(v, "c", [(0, 1), (1, 0)]) for v in brought]
     raw = pl.pallas_call(
         own_kernel, out_shape=shape((RAW_ROWS, LANES), f32),
-        in_specs=[SCALARS] + [WHOLE] * 5, out_specs=WHOLE,
+        in_specs=[WHOLE] * 5, out_specs=WHOLE,
         scratch_shapes=[pltpu.VMEM((SHARE_ROWS, WIDTH), bf16)],
         compiler_params=params(16), name="own",
         cost_estimate=pl.CostEstimate(flops=2 * RAW_ROWS * LANES * WIDTH, bytes_accessed=4 << 20, transcendentals=0),
-    )(where, mine, *brought, far)
+    )(mine, *brought, far)
     partial = pl.pallas_call(
         gram_kernel,
         out_shape=[shape((CHUNK, LANES), f32)] * 4,
-        in_specs=[SCALARS, SCALARS] + [WHOLE] * 6, out_specs=[WHOLE] * 4,
+        in_specs=[SCALARS] + [WHOLE] * 6, out_specs=[WHOLE] * 4,
         scratch_shapes=[pltpu.VMEM((PARTIAL + CAPS[0], LANES), f32), pltpu.VMEM((SHARE_ROWS, WIDTH), bf16)],
         compiler_params=params(16), name="gram",
-    )(where, meta, other, *swapped, far, raw)
+    )(meta, other, *swapped, far, raw)
     arrived = [partial[0]] + [
         lax.ppermute(partial[s], "y", [(i, (i + s) % 4) for i in range(4)]) for s in (1, 2, 3)
     ]
@@ -496,16 +499,16 @@
     best = pl.pallas_call(
         max_kernel,
         out_shape=shape((2 * CHIPS, LANES), f32),
-        in_specs=[SCALARS] * 2 + [WHOLE] * 5, out_specs=WHOLE,
+        in_specs=[SCALARS] + [WHOLE] * 5, out_specs=WHOLE,
         scratch_shapes=[pltpu.VMEM((16, LANES), f32)],
         compiler_params=params(8), name="maxima",
-    )(where, meta, *arrived, pos)
+    )(meta, *arrived, pos)
     back = lax.all_to_all(best.reshape(2 * CHIPS, 1, LANES), ("c", "x", "z", "y"), 0, 0, tiled=True)
     fitted = pl.pallas_call(
         pick_kernel,
         out_shape=shape((1, ROWS), f32),
-        in_specs=[SCALARS, WHOLE, WHOLE], out_specs=WHOLE, compiler_params=params(8), name="pick",
-    )(where, back.reshape(2 * CHIPS, LANES), code).reshape(ROWS)
+        in_specs=[WHOLE, WHOLE], out_specs=WHOLE, compiler_params=params(8), name="pick",
+    )(back.reshape(2 * CHIPS, LANES), code).reshape(ROWS)
     return lax.cond(
         fits,
         lambda fitted, embeddings, cluster_ids: fitted,

time: 93.3 us -> 90.6 us (0.971)
  Pallas kernels: 17.9 us -> 14.7 us
    pallas_call x3, Pallas kernels: 5.17 us -> 4.07 us  [the longest x1 1.91 us: on_device(): pl.pallas_call(unit_kernel, out_shape=(half, half), in_specs=[WHOLE, WHOL...]
  transfers between devices with their start and end apart: 12 -> 12, of which waited for: 6 -> 6; matrix products, arithmetic and copies ran while one was open for 1% -> 1% of each run, Pallas kernels for 6% -> 5%
where the time goes in v8:
time: 90.6 us; the launch traced here: 90.3 us
  blocking collectives  33.6 us (37%)
  waiting for transfers between devices  21.7 us (24%)
  starting transfers between devices  18.6 us (21%)
  Pallas kernels  14.7 us (16%)
  local copies, waits for them, and re-layouts  1.03 us (1%)
    all_to_all x1, blocking collectives, on_device(): packed = lax.all_to_all(packed, ('x', 'z', 'y'), 0, 0, tiled=True)  33.6 us
    ppermute x3, waiting for transfers between devices, on_device(): lax.ppermute(partial[s], 'y', [(i, (i + s) % 4) for i in range(4)])  9.72 us
    all_to_all x1, waiting for transfers between devices, on_device(): lax.all_to_all(best.reshape(2 * CHIPS, 1, LANES), ('c', 'x', 'z', 'y'), 0...  9.47 us
    all_to_all x1, starting transfers between devices, on_device(): lax.all_to_all(best.reshape(2 * CHIPS, 1, LANES), ('c', 'x', 'z', 'y'), 0...  6.67 us
    ppermute x3, starting transfers between devices, on_device(): lax.ppermute(partial[s], 'y', [(i, (i + s) % 4) for i in range(4)])  3.21 us
    pallas_call x1, Pallas kernels, on_device(): pl.pallas_call(mine_kernel, out_shape=(share, shape((8, ALL_GUESTS), i32)...  2.97 us
    ppermute x1, starting transfers between devices, on_device(): other = lax.ppermute(send, 'c', [(0, 1), (1, 0)])  2.86 us
    ppermute x3, starting transfers between devices, on_device(): lax.ppermute(guests, 'z', [(i, (i + s) % 4) for i in range(4)])  2.71 us
  transfers between devices with their start and end apart: 12, of which 6 were waited for; matrix products, arithmetic and copies ran while one was open for 1% of the time, Pallas kernels for 5%

profile of v8, /device:TPU:1, one launch (start us, length us, event | category | flops | bytes accessed | tf_op | source)
XLA Modules:
  0.0 90.3 jit_solution(16590121643781428963)
XLA Ops:
  0.0 1.9 %unit.1 = (bf16[144,2048]{1,0:T(8,128)(2,1)S(1)}, bf16[144,2048]{1,0:T(8,128)(2,1)S(1)}) custom-call(f32[128,4096]{1,0:T(8,128)} %x_ref.1, s32[1,128]{1,0:T(1,128)} %bitcast.26), custom_call_target="tpu_custom_call" | custom-call | tf_op jit(solution)/shard_map/unit/pallas_call | solution.py:448
  1.9 1.5 %collective-permute-start = (bf16[144,2048]{1,0:T(8,128)(2,1)S(1)}, bf16[144,2048]{1,0:T(8,128)(2,1)S(1)}, u32[]{:S(2)}, u32[]{:S(2)}) collective-permute-start(bf16[144,2048]{1,0:T(8,128)(2,1)S(1)} %get-tuple-element.107), channel_id=1, source_target_pairs={{0,1},{1,0},{2,3},{3,2},{4,5},{5,4},{6,7},{7,6},{8,9},{9,8},{10,11... | collective-permute-start | bytes 1769480 | tf_op jit(solution)/shard_map/ppermute | solution.py:452
  3.4 1.6 %collective-permute-done.got_ref = bf16[144,2048]{1,0:T(8,128)(2,1)S(1)} collective-permute-done((bf16[144,2048]{1,0:T(8,128)(2,1)S(1)}, bf16[144,2048]{1,0:T(8,128)(2,1)S(1)}, u32[]{:S(2)}, u32[]{:S(2)}) %collective-permute-start) | collective-permute-done | bytes 589856 | tf_op jit(solution)/shard_map/ppermute | solution.py:452
  5.0 1.1 %pack.1 = (bf16[64,24,512]{2,1,0:T(8,128)(2,1)S(1)}, s32[8,128]{1,0:T(8,128)S(1)}) custom-call(bf16[144,2048]{1,0:T(8,128)(2,1)S(1)} %get-tuple-element.106.keep_ref, bf16[144,2048]{1,0:T(8,128)(2,1)S(1)} %collective-permute-done.got_ref), custom_call_target="tpu_custom_call" | custom-call | tf_op jit(solution)/shard_map/pack/pallas_call | solution.py:453
  6.1 33.6 %all_to_all.51.x_ref = bf16[64,24,512]{2,1,0:T(8,128)(2,1)S(1)} all-to-all(bf16[64,24,512]{2,1,0:T(8,128)(2,1)S(1)} %get-tuple-element.108), channel_id=1, replica_groups=mesh['x'=4,'z'=4,'y'=4,'c'=2] {'x','z','y'}, dimensions={0} | all-to-all | bytes 3145728 | tf_op jit(solution)/shard_map/all_to_all | solution.py:458
  39.7 1.5 %names.1 = (bf16[64,512]{1,0:T(8,128)(2,1)S(1)}, s32[8,1536]{1,0:T(8,128)S(1)}, s32[64,128]{1,0:T(8,128)S(1)}, s32[64,128]{1,0:T(8,128)S(1)}, s32[8,128]{1,0:T(8,128)S(1)}) custom-call(bf16[64,24,512]{2,1,0:T(8,128)(2,1)S(1)} %all_to_all.51.x_ref), custom_call_target="tpu_custom_call" | custom-call | tf_op jit(solution)/shard_map/names/pallas_call | solution.py:460
  41.2 1.9 %send.1.send_ref = bf16[1216,512]{1,0:T(8,128)(2,1)S(1)} custom-call(bf16[64,24,512]{2,1,0:T(8,128)(2,1)S(1)} %all_to_all.51.x_ref, s32[8,1536]{1,0:T(8,128)S(1)} %get-tuple-element.110.line_ref), custom_call_target="tpu_custom_call" | custom-call | flops 1912602624 | bytes 4194304 | tf_op jit(solution)/shard_map/send/pallas_call | solution.py:468
  43.1 2.9 %collective-permute-start.1 = (bf16[1216,512]{1,0:T(8,128)(2,1)S(1)}, bf16[1216,512]{1,0:T(8,128)(2,1)S(1)}, u32[]{:S(2)}, u32[]{:S(2)}) collective-permute-start(bf16[1216,512]{1,0:T(8,128)(2,1)S(1)} %send.1.send_ref), channel_id=1, source_target_pairs={{0,1},{1,0},{2,3},{3,2},{4,5},{5,4},{6,7},{7,6},{8,9},{9,8},{10,11... | collective-permute-start | bytes 3735560 | tf_op jit(solution)/shard_map/ppermute | solution.py:473
  46.0 0.3 collective-permute-start.2
  46.3 0.5 collective-permute-start.3
  46.8 1.9 %collective-permute-start.4 = (bf16[64,512]{1,0:T(8,128)(2,1)S(1)}, bf16[64,512]{1,0:T(8,128)(2,1)S(1)}, u32[]{:S(2)}, u32[]{:S(2)}) collective-permute-start(bf16[64,512]{1,0:T(8,128)(2,1)S(1)} %get-tuple-element.111), channel_id=1, source_target_pairs={{0,24},{8,0},{16,8},{24,16},{1,25},{9,1},{17,9},{25,17},{2,26},{10... | collective-permute-start | bytes 196616 | tf_op jit(solution)/shard_map/ppermute | solution.py:465
  48.7 3.0 %mine.1 = (bf16[1216,512]{1,0:T(8,128)(2,1)S(1)}, s32[8,256]{1,0:T(8,128)S(1)}, s32[8,128]{1,0:T(8,128)S(1)}) custom-call(bf16[64,24,512]{2,1,0:T(8,128)(2,1)S(1)} %all_to_all.51.x_ref, s32[8,1536]{1,0:T(8,128)S(1)} %get-tuple-element.110.line_ref, bf16[1216,512]{1,0:T(8,128)(2,1)S(1)} %send.1.send_ref, s32[64,128]{1,0:T(8,128)S(1)} %get-tuple-element.112.key_ref, ...), custom_call_target="tpu_custom_call" | custom-call | flops 1912602624 | bytes 4194304 | tf_op jit(solution)/shard_map/mine/pallas_call | solution.py:474
  51.7 0.6 collective-permute-done.2.g1
  52.3 0.0 collective-permute-done.3.g2
  52.3 0.3 collective-permute-done.4.g3
  52.5 1.2 %collective-permute-start.5 = (bf16[64,512]{1,0:T(8,128)(2,1)S(1)}, bf16[64,512]{1,0:T(8,128)(2,1)S(1)}, u32[]{:S(2)}, u32[]{:S(2)}) collective-permute-start(bf16[64,512]{1,0:T(8,128)(2,1)S(1)} %collective-permute-done.2.g1), channel_id=1, source_target_pairs={{0,1},{1,0},{2,3},{3,2},{4,5},{5,4},{6,7},{7,6},{8,9},{9,8},{10,11... | collective-permute-start | bytes 196616 | tf_op jit(solution)/shard_map/ppermute | solution.py:480
  53.7 0.0 collective-permute-start.6
  53.7 0.5 collective-permute-start.7
  54.2 1.2 %own.1.raw_ref = f32[2560,128]{1,0:T(8,128)S(1)} custom-call(bf16[1216,512]{1,0:T(8,128)(2,1)S(1)} %get-tuple-element.119.x_ref, bf16[64,512]{1,0:T(8,128)(2,1)S(1)} %collective-permute-done.2.g1, bf16[64,512]{1,0:T(8,128)(2,1)S(1)} %collective-permute-done.3.g2, bf16[64,512]{1,0:T(8,128)(2,1)S(1)} %collective-permute-done.4.g3, ...), custom_call_target="tpu_custom_call" | custom-call | flops 335544320 | bytes 4194304 | tf_op jit(solution)/shard_map/own/pallas_call | solution.py:481
  55.4 0.0 copy-start
  55.4 0.0 copy-start.1
  55.4 0.0 collective-permute-done.5.g1
  55.4 0.0 collective-permute-done.6.g2
  55.5 0.0 collective-permute-done.7.g3
  55.5 0.0 collective-permute-done.1.x_ref
  55.5 2.0 %gram.1 = (f32[448,128]{1,0:T(8,128)S(1)}, f32[448,128]{1,0:T(8,128)S(1)}, f32[448,128]{1,0:T(8,128)S(1)}, f32[448,128]{1,0:T(8,128)S(1)}) custom-call(s32[8,128]{1,0:T(8,128)S(1)} %get-tuple-element.109.meta_ref, bf16[1216,512]{1,0:T(8,128)(2,1)S(1)} %collective-permute-done.1.x_ref, bf16[64,512]{1,0:T(8,128)(2,1)S(1)} %collective-permute-done.5.g1, ...), custom_call_target="tpu_custom_call" | custom-call | tf_op jit(solution)/shard_map/gram/pallas_call | solution.py:488
  57.4 0.4 collective-permute-start.8
  57.8 1.5 %collective-permute-start.9 = (f32[448,128]{1,0:T(8,128)S(1)}, f32[448,128]{1,0:T(8,128)S(1)}, u32[]{:S(2)}, u32[]{:S(2)}) collective-permute-start(f32[448,128]{1,0:T(8,128)S(1)} %get-tuple-element.122), channel_id=1, source_target_pairs={{0,4},{2,6},{4,0},{6,2},{1,5},{3,7},{5,1},{7,3},{8,12},{10,14},{12... | collective-permute-start | bytes 688136 | tf_op jit(solution)/shard_map/ppermute | solution.py:496
  59.3 1.3 %collective-permute-start.10 = (f32[448,128]{1,0:T(8,128)S(1)}, f32[448,128]{1,0:T(8,128)S(1)}, u32[]{:S(2)}, u32[]{:S(2)}) collective-permute-start(f32[448,128]{1,0:T(8,128)S(1)} %get-tuple-element.123), channel_id=1, source_target_pairs={{0,6},{2,0},{4,2},{6,4},{1,7},{3,1},{5,3},{7,5},{8,14},{10,8},{12,... | collective-permute-start | bytes 688136 | tf_op jit(solution)/shard_map/ppermute | solution.py:496
  60.7 0.5 slice.3
  61.8 9.3 %collective-permute-done.8.p1 = f32[448,128]{1,0:T(8,128)S(1)} collective-permute-done((f32[448,128]{1,0:T(8,128)S(1)}, f32[448,128]{1,0:T(8,128)S(1)}, u32[]{:S(2)}, u32[]{:S(2)}) %collective-permute-start.8) | collective-permute-done | bytes 229408 | tf_op jit(solution)/shard_map/ppermute | solution.py:496
  71.1 0.0 collective-permute-done.9.p2
  71.1 0.4 collective-permute-done.10.p3
  71.5 1.9 %maxima.1 = f32[128,128]{1,0:T(8,128)} custom-call(s32[8,128]{1,0:T(8,128)S(1)} %get-tuple-element.109.meta_ref, f32[448,128]{1,0:T(8,128)S(1)} %get-tuple-element.126.p0, f32[448,128]{1,0:T(8,128)S(1)} %collective-permute-done.8.p1, f32[448,128]{1,0:T(8,128)S(1)} %collective-permute-done.9.p2, f32[448,128]{1,0:T(8,128)S(1)} %collective-permute-done.10.p3, ...), custom_call_target="tpu_custom_call" | custom-call | tf_op jit(solution)/shard_map/maxima/pallas_call | solution.py:499
  73.4 6.7 %all-to-all-start.6 = ((f32[128,1,128]{2,1,0:T(1,128)}), f32[128,1,128]{2,1,0:T(1,128)S(1)}, u32[]{:S(2)}, u32[]{:S(2)}) async-start(f32[128,1,128]{2,1,0:T(1,128)} %bitcast.11), calls=%async_computation.6 | async-start | bytes 131072 | tf_op jit(solution)/shard_map/all_to_all | solution.py:506
  80.1 9.5 %all-to-all-done.6 = f32[128,1,128]{2,1,0:T(1,128)S(1)} async-done(((f32[128,1,128]{2,1,0:T(1,128)}), f32[128,1,128]{2,1,0:T(1,128)S(1)}, u32[]{:S(2)}, u32[]{:S(2)}) %all-to-all-start.6) | async-done | bytes 65568 | tf_op jit(solution)/shard_map/all_to_all | solution.py:506
  89.5 0.0 copy-done
  89.5 0.0 copy-done.1
  89.5 0.3 pick.1
  89.8 0.0 copy-start.2
  89.8 0.5 copy-done.2
  (1 shorter events, 0.0 us)
Async XLA Ops:
  1.9 3.1 %collective-permute-start = (bf16[144,2048]{1,0:T(8,128)(2,1)S(1)}, bf16[144,2048]{1,0:T(8,128)(2,1)S(1)}, u32[]{:S(2)}, u32[]{:S(2)}) collective-permute-start(bf16[144,2048]{1,0:T(8,128)(2,1)S(1)} %get-tuple-element.107), channel_id=1, source_target_pairs={{0,1},{1,0},{2,3},{3,2},{4,5},{5,4},{6,7},{7,6},{8,9},{9,8},{10,11... | collective-permute-start | bytes 1769480 | tf_op jit(solution)/shard_map/ppermute | solution.py:452
  43.1 12.3 %collective-permute-start.1 = (bf16[1216,512]{1,0:T(8,128)(2,1)S(1)}, bf16[1216,512]{1,0:T(8,128)(2,1)S(1)}, u32[]{:S(2)}, u32[]{:S(2)}) collective-permute-start(bf16[1216,512]{1,0:T(8,128)(2,1)S(1)} %send.1.send_ref), channel_id=1, source_target_pairs={{0,1},{1,0},{2,3},{3,2},{4,5},{5,4},{6,7},{7,6},{8,9},{9,8},{10,11... | collective-permute-start | bytes 3735560 | tf_op jit(solution)/shard_map/ppermute | solution.py:473
  46.0 6.3 %collective-permute-start.2 = (bf16[64,512]{1,0:T(8,128)(2,1)S(1)}, bf16[64,512]{1,0:T(8,128)(2,1)S(1)}, u32[]{:S(2)}, u32[]{:S(2)}) collective-permute-start(bf16[64,512]{1,0:T(8,128)(2,1)S(1)} %get-tuple-element.111), channel_id=1, source_target_pairs={{0,8},{8,16},{16,24},{24,0},{1,9},{9,17},{17,25},{25,1},{2,10},{10... | collective-permute-start | bytes 196616 | tf_op jit(solution)/shard_map/ppermute | solution.py:465
  46.3 6.0 %collective-permute-start.3 = (bf16[64,512]{1,0:T(8,128)(2,1)S(1)}, bf16[64,512]{1,0:T(8,128)(2,1)S(1)}, u32[]{:S(2)}, u32[]{:S(2)}) collective-permute-start(bf16[64,512]{1,0:T(8,128)(2,1)S(1)} %get-tuple-element.111), channel_id=1, source_target_pairs={{0,16},{8,24},{16,0},{24,8},{1,17},{9,25},{17,1},{25,9},{2,18},{10... | collective-permute-start | bytes 196616 | tf_op jit(solution)/shard_map/ppermute | solution.py:465
  46.8 5.7 %collective-permute-start.4 = (bf16[64,512]{1,0:T(8,128)(2,1)S(1)}, bf16[64,512]{1,0:T(8,128)(2,1)S(1)}, u32[]{:S(2)}, u32[]{:S(2)}) collective-permute-start(bf16[64,512]{1,0:T(8,128)(2,1)S(1)} %get-tuple-element.111), channel_id=1, source_target_pairs={{0,24},{8,0},{16,8},{24,16},{1,25},{9,1},{17,9},{25,17},{2,26},{10... | collective-permute-start | bytes 196616 | tf_op jit(solution)/shard_map/ppermute | solution.py:465
  52.5 2.9 %collective-permute-start.5 = (bf16[64,512]{1,0:T(8,128)(2,1)S(1)}, bf16[64,512]{1,0:T(8,128)(2,1)S(1)}, u32[]{:S(2)}, u32[]{:S(2)}) collective-permute-start(bf16[64,512]{1,0:T(8,128)(2,1)S(1)} %collective-permute-done.2.g1), channel_id=1, source_target_pairs={{0,1},{1,0},{2,3},{3,2},{4,5},{5,4},{6,7},{7,6},{8,9},{9,8},{10,11... | collective-permute-start | bytes 196616 | tf_op jit(solution)/shard_map/ppermute | solution.py:480
  53.7 1.8 %collective-permute-start.6 = (bf16[64,512]{1,0:T(8,128)(2,1)S(1)}, bf16[64,512]{1,0:T(8,128)(2,1)S(1)}, u32[]{:S(2)}, u32[]{:S(2)}) collective-permute-start(bf16[64,512]{1,0:T(8,128)(2,1)S(1)} %collective-permute-done.3.g2), channel_id=1, source_target_pairs={{0,1},{1,0},{2,3},{3,2},{4,5},{5,4},{6,7},{7,6},{8,9},{9,8},{10,11... | collective-permute-start | bytes 196616 | tf_op jit(solution)/shard_map/ppermute | solution.py:480
  53.7 1.8 %collective-permute-start.7 = (bf16[64,512]{1,0:T(8,128)(2,1)S(1)}, bf16[64,512]{1,0:T(8,128)(2,1)S(1)}, u32[]{:S(2)}, u32[]{:S(2)}) collective-permute-start(bf16[64,512]{1,0:T(8,128)(2,1)S(1)} %collective-permute-done.4.g3), channel_id=1, source_target_pairs={{0,1},{1,0},{2,3},{3,2},{4,5},{5,4},{6,7},{7,6},{8,9},{9,8},{10,11... | collective-permute-start | bytes 196616 | tf_op jit(solution)/shard_map/ppermute | solution.py:480
  55.4 34.1 %copy-start = (s32[128]{0:T(128)S(1)}, s32[128]{0:T(128)}, u32[]{:S(2)}) copy-start(s32[128]{0:T(128)} %param.7) | copy-start | bytes 1540
  55.4 34.1 %copy-start.1 = (f32[128,4096]{1,0:T(8,128)S(1)}, f32[128,4096]{1,0:T(8,128)}, u32[]{:S(2)}) copy-start(f32[128,4096]{1,0:T(8,128)} %x_ref.1) | copy-start | bytes 6291460
  57.4 13.7 %collective-permute-start.8 = (f32[448,128]{1,0:T(8,128)S(1)}, f32[448,128]{1,0:T(8,128)S(1)}, u32[]{:S(2)}, u32[]{:S(2)}) collective-permute-start(f32[448,128]{1,0:T(8,128)S(1)} %get-tuple-element.121), channel_id=1, source_target_pairs={{0,2},{2,4},{4,6},{6,0},{1,3},{3,5},{5,7},{7,1},{8,10},{10,12},{12... | collective-permute-start | bytes 688136 | tf_op jit(solution)/shard_map/ppermute | solution.py:496
  57.8 13.3 %collective-permute-start.9 = (f32[448,128]{1,0:T(8,128)S(1)}, f32[448,128]{1,0:T(8,128)S(1)}, u32[]{:S(2)}, u32[]{:S(2)}) collective-permute-start(f32[448,128]{1,0:T(8,128)S(1)} %get-tuple-element.122), channel_id=1, source_target_pairs={{0,4},{2,6},{4,0},{6,2},{1,5},{3,7},{5,1},{7,3},{8,12},{10,14},{12... | collective-permute-start | bytes 688136 | tf_op jit(solution)/shard_map/ppermute | solution.py:496
  59.3 12.2 %collective-permute-start.10 = (f32[448,128]{1,0:T(8,128)S(1)}, f32[448,128]{1,0:T(8,128)S(1)}, u32[]{:S(2)}, u32[]{:S(2)}) collective-permute-start(f32[448,128]{1,0:T(8,128)S(1)} %get-tuple-element.123), channel_id=1, source_target_pairs={{0,6},{2,0},{4,2},{6,4},{1,7},{3,1},{5,3},{7,5},{8,14},{10,8},{12,... | collective-permute-start | bytes 688136 | tf_op jit(solution)/shard_map/ppermute | solution.py:496
  73.4 16.1 %all-to-all-start.6 = ((f32[128,1,128]{2,1,0:T(1,128)}), f32[128,1,128]{2,1,0:T(1,128)S(1)}, u32[]{:S(2)}, u32[]{:S(2)}) async-start(f32[128,1,128]{2,1,0:T(1,128)} %bitcast.11), calls=%async_computation.6 | async-start | bytes 131072 | tf_op jit(solution)/shard_map/all_to_all | solution.py:506
  89.8 0.5 copy-start.2

commit v9 on v8

--- a/solution.py
+++ b/solution.py
@@ -1,3 +1,5 @@
+import functools
+
 import jax
 import jax.numpy as jnp
 from jax import lax
@@ -11,8 +13,7 @@
 LABEL_ROWS = 16
 BINS = 16
 CHIPS = 64
-BLOCK = 24
-SLOTS = BLOCK - 1
+BLOCKS = (24, 32)
 GROUP = 32
 GUESTS = 64
 ALL_GUESTS = 4 * GUESTS
@@ -37,7 +38,6 @@
 )
 f32, bf16, i32 = jnp.float32, jnp.bfloat16, jnp.int32
 WHOLE = pl.BlockSpec(memory_space=pltpu.VMEM)
-SCALARS = pl.BlockSpec(memory_space=pltpu.SMEM)
 
 
 def params(mib):
@@ -83,7 +83,7 @@
         out_ref[ROWS:, :] = ids
 
 
-def pack_kernel(keep_ref, got_ref, out_ref, code_ref):
+def pack_kernel(block, keep_ref, got_ref, out_ref, code_ref):
     y, first = index_on("y"), index_on("c") == 0
     kept = jnp.max(keep_ref[ROWS:, :ROWS].astype(f32), axis=0, keepdims=True)
     got = jnp.max(got_ref[ROWS:, :ROWS].astype(f32), axis=0, keepdims=True)
@@ -101,7 +101,7 @@
 
     rank, sizes = ranks_within([bins == b for b in range(BINS)])
     quad, line = bins >> 2, bins & 3
-    extra = rank >= SLOTS
+    extra = rank >= (block - 1)
     turn, _ = ranks_within([extra & (quad == q) for q in range(4)])
     room, used = [], []
     for step in range(4):
@@ -112,9 +112,9 @@
                 b = 4 * q + at
                 size = jnp.where(quad == q, sizes[2 * b:2 * b + 1] + sizes[2 * b + 1:2 * b + 2], size)
             taken = jnp.where(((at - y) & 3) == step, size, taken)
-        taken = jnp.minimum(taken.astype(i32), SLOTS)
+        taken = jnp.minimum(taken.astype(i32), (block - 1))
         used.append(taken)
-        room.append(SLOTS - taken)
+        room.append((block - 1) - taken)
     placed = jnp.logical_not(extra)
     to_line, to_slot, start = line, rank, jnp.zeros(labels.shape, i32)
     for step in range(4):
@@ -124,7 +124,7 @@
         placed = placed | here
         start = start + room[step]
     lane = jnp.where(placed, to_line * GROUP + to_slot, -1)
-    place = jnp.where(placed, (quad * 4 + to_line) * BLOCK + to_slot, -1)
+    place = jnp.where(placed, (quad * 4 + to_line) * block + to_slot, -1)
     code_ref[...] = jnp.concatenate([jnp.where(placed, bins * LANES + lane, -1)] * 4, axis=0)
     docs = 2 * ROWS
     flat = lambda v: jnp.concatenate([v[:1], v[1:]], axis=1)
@@ -134,19 +134,19 @@
     names = dot_last(named, as_bf16(iota((LANES, docs), 0) == flat(lane)))
     own = jnp.where(first, place[:1], place[1:])
     other = jnp.where(first, place[1:], place[:1])
-    onehot = as_bf16(iota((BINS * BLOCK, docs), 0) == jnp.concatenate([own, other], axis=1))
-    is_last = iota((BLOCK, WIDTH), 0) == SLOTS
+    onehot = as_bf16(iota((BINS * block, docs), 0) == jnp.concatenate([own, other], axis=1))
+    is_last = iota((block, WIDTH), 0) == (block - 1)
     for y in range(4):
         columns = slice(y * WIDTH, (y + 1) * WIDTH)
         x = jnp.concatenate([keep_ref[:ROWS, columns], got_ref[:ROWS, columns]], axis=0)
         packed = dot(onehot, x)
         for b in range(BINS):
             extra = jnp.concatenate([names[b // 4:b // 4 + 1], counts, jnp.zeros((1, 2 * LANES), f32)], axis=1)
-            out_ref[4 * b + y] = jnp.where(is_last, extra, packed[b * BLOCK:(b + 1) * BLOCK]).astype(bf16)
-
-
-def labels_of(x_ref):
-    tail = x_ref[:, BLOCK - 8:, :2 * LANES].astype(f32)
+            out_ref[4 * b + y] = jnp.where(is_last, extra, packed[b * block:(b + 1) * block]).astype(bf16)
+
+
+def labels_of(block, x_ref):
+    tail = x_ref[:, block - 8:, :2 * LANES].astype(f32)
     tail = jnp.max(jnp.where(iota(tail.shape, 1) == 7, tail, 0.0), axis=1)
     return tail[:, :LANES].astype(i32) - 1, tail[:, LANES:].astype(bf16)
 
@@ -166,9 +166,9 @@
     return first, jnp.maximum(e, g), jnp.minimum(e, g), fourth
 
 
-def names_kernel(x_ref, guest_ref, line_ref, key_ref, pos_ref, meta_ref):
+def names_kernel(block, x_ref, guest_ref, line_ref, key_ref, pos_ref, meta_ref):
     mine, z = index_on("x") * 4 + index_on("z"), index_on("z")
-    labels, chip_counts = labels_of(x_ref)
+    labels, chip_counts = labels_of(block, x_ref)
     _, sizes = counts_of(chip_counts)
     here = iota((1, LANES), 1) == mine
     own = lambda v: jnp.sum(jnp.where(here, v, 0.0), axis=1, keepdims=True)
@@ -210,16 +210,16 @@
     per, groups = 16, CHIPS // 16
     value = jnp.where(group == z, jnp.where(guest, GUEST + turn, pos + 1), 0).astype(f32)
     value = pltpu.roll(value, lax.rem(LANES - GROUP * z, LANES), 1)
-    value = jnp.where(lane < BLOCK, value, 0.0)
-    lined = jnp.zeros((8, per * BLOCK), f32)
+    value = jnp.where(lane < block, value, 0.0)
+    lined = jnp.zeros((8, per * block), f32)
     for t in range(per):
         rows = jnp.concatenate([value[per * g + t:per * g + t + 1] for g in range(groups)] * 2, axis=0)
-        rows = jnp.concatenate([rows, jnp.zeros((8, per * BLOCK - LANES), f32)], axis=1)
-        lined = lined + (pltpu.roll(rows, t * BLOCK, 1) if t else rows)
+        rows = jnp.concatenate([rows, jnp.zeros((8, per * block - LANES), f32)], axis=1)
+        lined = lined + (pltpu.roll(rows, t * block, 1) if t else rows)
     slots = jnp.concatenate([lined[g:g + 1] for g in range(groups)], axis=1).astype(i32)
     line_ref[...] = jnp.broadcast_to(slots, line_ref.shape)
-    onehot = as_bf16(iota((GUESTS, CHIPS * BLOCK), 0) + GUEST == slots)
-    guest_ref[...] = dot(onehot, x_ref[...].reshape(CHIPS * BLOCK, WIDTH)).astype(bf16)
+    onehot = as_bf16(iota((GUESTS, CHIPS * block), 0) + GUEST == slots)
+    guest_ref[...] = dot(onehot, x_ref[...].reshape(CHIPS * block, WIDTH)).astype(bf16)
 
 
 def sorted_rows(segment, slots, x):
@@ -227,8 +227,8 @@
     return dot(onehot, x).astype(bf16)
 
 
-def send_kernel(x_ref, line_ref, send_ref):
-    x = x_ref[...].reshape(CHIPS * BLOCK, WIDTH)
+def send_kernel(block, x_ref, line_ref, send_ref):
+    x = x_ref[...].reshape(CHIPS * block, WIDTH)
     slots = line_ref[:1, :]
     for me in range(2):
         @pl.when(index_on("c") == me)
@@ -239,8 +239,8 @@
                     send_ref[at:at + segment[1], :] = sorted_rows(segment, slots, x)
 
 
-def mine_kernel(x_ref, line_ref, send_ref, key_ref, pos_ref, mine_ref, far_ref, over_ref):
-    x = x_ref[...].reshape(CHIPS * BLOCK, WIDTH)
+def mine_kernel(block, x_ref, line_ref, send_ref, key_ref, pos_ref, mine_ref, far_ref):
+    x = x_ref[...].reshape(CHIPS * block, WIDTH)
     slots = line_ref[:1, :]
     for core in range(2):
         @pl.when(index_on("c") == core)
@@ -260,7 +260,10 @@
         parts = jnp.where(iota((8, step * LANES), 0) == 0, places >> 5, places & 31).astype(f32).astype(bf16)
         total = total + dot_last(parts, as_bf16(iota((ALL_GUESTS, step * LANES), 0) == flat(key_ref)))
     far_ref[...] = jnp.broadcast_to((32.0 * total[:1] + total[1:2]).astype(i32), far_ref.shape)
-    _, chip_counts = labels_of(x_ref)
+
+
+def fit_kernel(block, x_ref, over_ref):
+    _, chip_counts = labels_of(block, x_ref)
     counts, sizes = counts_of(chip_counts)
     ordered = in_order(sizes)
     over = jnp.zeros((1, LANES), f32)
@@ -270,7 +273,7 @@
         length = sum(jnp.maximum(jnp.floor((ordered[q] + 63.0) * (1 / 64)) - first // HALF, 0.0) for q, first in share)
         over = jnp.maximum(over, jnp.where(length > 4 * COUNT, 1.0, 0.0))
     taken = counts[0] + counts[1] + counts[2] + counts[3]
-    extra, room = jnp.maximum(taken - SLOTS, 0.0), jnp.maximum(SLOTS - taken, 0.0)
+    extra, room = jnp.maximum(taken - (block - 1), 0.0), jnp.maximum((block - 1) - taken, 0.0)
     row, col = iota((LANES, LANES), 0), iota((LANES, LANES), 1)
     same = (row >> 2) == (col >> 2)
     wanted = dot(extra.astype(bf16), as_bf16(same))
@@ -315,6 +318,10 @@
                 at += rows
 
 
+def size_of(meta_ref, q):
+    return jnp.max(meta_ref[q:q + 1, :].astype(f32)).astype(i32)
+
+
 def length_of(size, first):
     return jnp.maximum(((size + HALF - 1) >> 6) - first // HALF, 0)
 
@@ -331,7 +338,7 @@
                 rows = CAPS[q] - first
                 score = raw_ref[at:at + rows, :] + dot_last(rows_ref[left, :], rows_ref[right, :])
                 at += rows
-                size = meta_ref[q, 0]
+                size = size_of(meta_ref, q)
                 i, j = iota(score.shape, 0), iota(score.shape, 1)
                 keep = (i < size - first) & (j < size - first) & (i != j)
                 part_ref[pl.ds(pl.multiple_of(to, HALF), rows), :] = jnp.where(keep, score, -4.0)
@@ -347,11 +354,11 @@
     y, c = index_on("y"), index_on("c")
     best_ref[...] = jnp.full(best_ref.shape, -1.0, f32)
     sub, lane = iota((HALF, LANES), 0), iota((HALF, LANES), 1)
-    blocks = []
+    blocks, sizes = [], [size_of(meta_ref, q) for q in range(4)]
     for core, share in enumerate(SHARES):
         at = jnp.zeros((), i32)
         for q, first in share:
-            length = length_of(meta_ref[q, 0], first)
+            length = length_of(sizes[q], first)
             col = FIRST_ROW[q] + first // LANES
             blocks.append((jnp.where((c == core) & (length > 0), at, PARTIAL), col, 2 * col - at))
             at = at + length
@@ -442,7 +449,7 @@
     return returned[place]
 
 
-def on_device(embeddings, cluster_ids):
+def route(block, embeddings, cluster_ids):
     shape = jax.ShapeDtypeStruct
     half = shape((ROWS + LABEL_ROWS, HALF_WIDTH), bf16)
     keep, send = pl.pallas_call(
@@ -451,29 +458,29 @@
     )(embeddings, cluster_ids.reshape(1, ROWS))
     got = lax.ppermute(send, "c", [(0, 1), (1, 0)])
     packed, code = pl.pallas_call(
-        pack_kernel,
-        out_shape=(shape((CHIPS, BLOCK, WIDTH), bf16), shape((8, ROWS), i32)),
+        functools.partial(pack_kernel, block),
+        out_shape=(shape((CHIPS, block, WIDTH), bf16), shape((8, ROWS), i32)),
         in_specs=[WHOLE, WHOLE], out_specs=(WHOLE, WHOLE), compiler_params=params(20), name="pack",
     )(keep, got)
     packed = lax.all_to_all(packed, ("x", "z", "y"), 0, 0, tiled=True)
     table = shape((CHIPS, LANES), i32)
     guests, line, key, pos, meta = pl.pallas_call(
-        names_kernel,
-        out_shape=(shape((GUESTS, WIDTH), bf16), shape((8, CHIPS * BLOCK), i32), table, table, shape((8, LANES), i32)),
+        functools.partial(names_kernel, block),
+        out_shape=(shape((GUESTS, WIDTH), bf16), shape((8, CHIPS * block), i32), table, table, shape((8, LANES), i32)),
         in_specs=[WHOLE], out_specs=(WHOLE,) * 5, compiler_params=params(12), name="names",
     )(packed)
     brought = [lax.ppermute(guests, "z", [(i, (i + s) % 4) for i in range(4)]) for s in (1, 2, 3)]
     share = shape((SHARE_ROWS, WIDTH), bf16)
-    slots = CHIPS * BLOCK
+    slots = CHIPS * block
     send = pl.pallas_call(
-        send_kernel, out_shape=share,
+        functools.partial(send_kernel, block), out_shape=share,
         in_specs=[WHOLE, WHOLE], out_specs=WHOLE, compiler_params=params(16), name="send",
         cost_estimate=pl.CostEstimate(flops=2 * SHARE_ROWS * WIDTH * slots, bytes_accessed=4 << 20, transcendentals=0),
     )(packed, line)
     other = lax.ppermute(send, "c", [(0, 1), (1, 0)])
-    mine, far, over = pl.pallas_call(
-        mine_kernel, out_shape=(share, shape((8, ALL_GUESTS), i32), shape((8, LANES), i32)),
-        in_specs=[WHOLE] * 5, out_specs=(WHOLE,) * 3, compiler_params=params(20), name="mine",
+    mine, far = pl.pallas_call(
+        functools.partial(mine_kernel, block), out_shape=(share, shape((8, ALL_GUESTS), i32)),
+        in_specs=[WHOLE] * 5, out_specs=(WHOLE,) * 2, compiler_params=params(20), name="mine",
         cost_estimate=pl.CostEstimate(flops=2 * SHARE_ROWS * WIDTH * slots, bytes_accessed=4 << 20, transcendentals=0),
     )(packed, line, send, key, pos)
     brought, mine = lax.optimization_barrier((brought, mine))
@@ -488,32 +495,44 @@
     partial = pl.pallas_call(
         gram_kernel,
         out_shape=[shape((CHUNK, LANES), f32)] * 4,
-        in_specs=[SCALARS] + [WHOLE] * 6, out_specs=[WHOLE] * 4,
+        in_specs=[WHOLE] * 7, out_specs=[WHOLE] * 4,
         scratch_shapes=[pltpu.VMEM((PARTIAL + CAPS[0], LANES), f32), pltpu.VMEM((SHARE_ROWS, WIDTH), bf16)],
         compiler_params=params(16), name="gram",
     )(meta, other, *swapped, far, raw)
     arrived = [partial[0]] + [
         lax.ppermute(partial[s], "y", [(i, (i + s) % 4) for i in range(4)]) for s in (1, 2, 3)
     ]
+    over = pl.pallas_call(
+        functools.partial(fit_kernel, block), out_shape=shape((8, LANES), i32),
+        in_specs=[WHOLE], out_specs=WHOLE, compiler_params=params(8), name="fit",
+    )(packed)
     arrived, fits = lax.optimization_barrier((arrived, over[0, 0] == 0))
     best = pl.pallas_call(
         max_kernel,
         out_shape=shape((2 * CHIPS, LANES), f32),
-        in_specs=[SCALARS] + [WHOLE] * 5, out_specs=WHOLE,
+        in_specs=[WHOLE] * 6, out_specs=WHOLE,
         scratch_shapes=[pltpu.VMEM((16, LANES), f32)],
         compiler_params=params(8), name="maxima",
     )(meta, *arrived, pos)
     back = lax.all_to_all(best.reshape(2 * CHIPS, 1, LANES), ("c", "x", "z", "y"), 0, 0, tiled=True)
-    fitted = pl.pallas_call(
+    back, fits = lax.optimization_barrier((back, fits))
+    best = pl.pallas_call(
         pick_kernel,
         out_shape=shape((1, ROWS), f32),
         in_specs=[WHOLE, WHOLE], out_specs=WHOLE, compiler_params=params(8), name="pick",
     )(back.reshape(2 * CHIPS, LANES), code).reshape(ROWS)
+    return best, fits
+
+
+def on_device(embeddings, cluster_ids, blocks=BLOCKS):
+    if not blocks:
+        return gather_groups(embeddings, cluster_ids)
+    best, fits = route(blocks[0], embeddings, cluster_ids)
     return lax.cond(
         fits,
-        lambda fitted, embeddings, cluster_ids: fitted,
-        lambda fitted, embeddings, cluster_ids: gather_groups(embeddings, cluster_ids),
-        fitted, embeddings, cluster_ids,
+        lambda best, embeddings, cluster_ids: best,
+        lambda best, embeddings, cluster_ids: on_device(embeddings, cluster_ids, blocks[1:]),
+        best, embeddings, cluster_ids,
     )
 
 

time: 90.6 us -> 89.5 us (0.988)
    pallas_call x9 -> x10, Pallas kernels: 14.7 us -> 14.3 us  [the longest x1 2.59 us: route(): pl.pallas_call(functools.partial(mine_kernel, block), out_shape=(share, s...]
where the time goes in v9:
time: 89.5 us; the launch traced here: 89.3 us
  blocking collectives  33.4 us (37%)
  waiting for transfers between devices  21.5 us (24%)
  starting transfers between devices  18.8 us (21%)
  Pallas kernels  14.3 us (16%)
    all_to_all x1, blocking collectives, route(): packed = lax.all_to_all(packed, ('x', 'z', 'y'), 0, 0, tiled=True)  33.4 us
    all_to_all x1, waiting for transfers between devices, route(): lax.all_to_all(best.reshape(2 * CHIPS, 1, LANES), ('c', 'x', 'z', 'y'), 0...  9.46 us
    ppermute x3, waiting for transfers between devices, route(): lax.ppermute(partial[s], 'y', [(i, (i + s) % 4) for i in range(4)])  9.2 us
    all_to_all x1, starting transfers between devices, route(): lax.all_to_all(best.reshape(2 * CHIPS, 1, LANES), ('c', 'x', 'z', 'y'), 0...  6.66 us
    ppermute x3, starting transfers between devices, route(): lax.ppermute(partial[s], 'y', [(i, (i + s) % 4) for i in range(4)])  3.22 us
    ppermute x1, starting transfers between devices, route(): other = lax.ppermute(send, 'c', [(0, 1), (1, 0)])  3 us
    ppermute x3, starting transfers between devices, route(): lax.ppermute(guests, 'z', [(i, (i + s) % 4) for i in range(4)])  2.71 us
    pallas_call x1, Pallas kernels, route(): pl.pallas_call(functools.partial(mine_kernel, block), out_shape=(share, s...  2.59 us
  transfers between devices with their start and end apart: 12, of which 6 were waited for; matrix products, arithmetic and copies ran while one was open for 1% of the time, Pallas kernels for 5%

profile of v9, /device:TPU:1, one launch (start us, length us, event | category | flops | bytes accessed | tf_op | source)
XLA Modules:
  0.0 89.3 jit_solution(6165202125052684790)
XLA Ops:
  0.0 1.9 %unit.3 = (bf16[144,2048]{1,0:T(8,128)(2,1)S(1)}, bf16[144,2048]{1,0:T(8,128)(2,1)S(1)}) custom-call(f32[128,4096]{1,0:T(8,128)} %x_ref.1, s32[1,128]{1,0:T(1,128)} %bitcast.35), custom_call_target="tpu_custom_call" | custom-call | tf_op jit(solution)/shard_map/unit/pallas_call | solution.py:455
  1.9 1.5 %collective-permute-start.11 = (bf16[144,2048]{1,0:T(8,128)(2,1)S(1)}, bf16[144,2048]{1,0:T(8,128)(2,1)S(1)}, u32[]{:S(2)}, u32[]{:S(2)}) collective-permute-start(bf16[144,2048]{1,0:T(8,128)(2,1)S(1)} %get-tuple-element.146), channel_id=1, source_target_pairs={{0,1},{1,0},{2,3},{3,2},{4,5},{5,4},{6,7},{7,6},{8,9},{9,8},{10,11... | collective-permute-start | bytes 1769480 | tf_op jit(solution)/shard_map/ppermute | solution.py:459
  3.4 1.6 %collective-permute-done.11.got_ref = bf16[144,2048]{1,0:T(8,128)(2,1)S(1)} collective-permute-done((bf16[144,2048]{1,0:T(8,128)(2,1)S(1)}, bf16[144,2048]{1,0:T(8,128)(2,1)S(1)}, u32[]{:S(2)}, u32[]{:S(2)}) %collective-permute-start.11) | collective-permute-done | bytes 589856 | tf_op jit(solution)/shard_map/ppermute | solution.py:459
  5.0 1.0 %pack.3 = (bf16[64,24,512]{2,1,0:T(8,128)(2,1)S(1)}, s32[8,128]{1,0:T(8,128)S(1)}) custom-call(bf16[144,2048]{1,0:T(8,128)(2,1)S(1)} %get-tuple-element.145.keep_ref, bf16[144,2048]{1,0:T(8,128)(2,1)S(1)} %collective-permute-done.11.got_ref), custom_call_target="tpu_custom_call" | custom-call | tf_op jit(solution)/shard_map/pack/pallas_call | solution.py:460
  6.1 33.4 %all_to_all.61.x_ref = bf16[64,24,512]{2,1,0:T(8,128)(2,1)S(1)} all-to-all(bf16[64,24,512]{2,1,0:T(8,128)(2,1)S(1)} %get-tuple-element.147), channel_id=1, replica_groups=mesh['x'=4,'z'=4,'y'=4,'c'=2] {'x','z','y'}, dimensions={0} | all-to-all | bytes 3145728 | tf_op jit(solution)/shard_map/all_to_all | solution.py:465
  39.5 1.6 %names.3 = (bf16[64,512]{1,0:T(8,128)(2,1)S(1)}, s32[8,1536]{1,0:T(8,128)S(1)}, s32[64,128]{1,0:T(8,128)S(1)}, s32[64,128]{1,0:T(8,128)S(1)}, s32[8,128]{1,0:T(8,128)S(1)}) custom-call(bf16[64,24,512]{2,1,0:T(8,128)(2,1)S(1)} %all_to_all.61.x_ref), custom_call_target="tpu_custom_call" | custom-call | tf_op jit(solution)/shard_map/names/pallas_call | solution.py:467
  41.1 1.9 %send.3.send_ref = bf16[1216,512]{1,0:T(8,128)(2,1)S(1)} custom-call(bf16[64,24,512]{2,1,0:T(8,128)(2,1)S(1)} %all_to_all.61.x_ref, s32[8,1536]{1,0:T(8,128)S(1)} %get-tuple-element.149.line_ref), custom_call_target="tpu_custom_call" | custom-call | flops 1912602624 | bytes 4194304 | tf_op jit(solution)/shard_map/send/pallas_call | solution.py:475
  43.0 3.0 %collective-permute-start.12 = (bf16[1216,512]{1,0:T(8,128)(2,1)S(1)}, bf16[1216,512]{1,0:T(8,128)(2,1)S(1)}, u32[]{:S(2)}, u32[]{:S(2)}) collective-permute-start(bf16[1216,512]{1,0:T(8,128)(2,1)S(1)} %send.3.send_ref), channel_id=1, source_target_pairs={{0,1},{1,0},{2,3},{3,2},{4,5},{5,4},{6,7},{7,6},{8,9},{9,8},{10,11... | collective-permute-start | bytes 3735560 | tf_op jit(solution)/shard_map/ppermute | solution.py:480
  46.0 0.3 collective-permute-start.13
  46.3 0.5 collective-permute-start.14
  46.8 1.9 %collective-permute-start.15 = (bf16[64,512]{1,0:T(8,128)(2,1)S(1)}, bf16[64,512]{1,0:T(8,128)(2,1)S(1)}, u32[]{:S(2)}, u32[]{:S(2)}) collective-permute-start(bf16[64,512]{1,0:T(8,128)(2,1)S(1)} %get-tuple-element.150), channel_id=1, source_target_pairs={{0,24},{8,0},{16,8},{24,16},{1,25},{9,1},{17,9},{25,17},{2,26},{10... | collective-permute-start | bytes 196616 | tf_op jit(solution)/shard_map/ppermute | solution.py:472
  48.7 2.6 %mine.3 = (bf16[1216,512]{1,0:T(8,128)(2,1)S(1)}, s32[8,256]{1,0:T(8,128)S(1)}) custom-call(bf16[64,24,512]{2,1,0:T(8,128)(2,1)S(1)} %all_to_all.61.x_ref, s32[8,1536]{1,0:T(8,128)S(1)} %get-tuple-element.149.line_ref, bf16[1216,512]{1,0:T(8,128)(2,1)S(1)} %send.3.send_ref, s32[64,128]{1,0:T(8,128)S(1)} %get-tuple-element.151.key_ref, ...), custom_call_target="tpu_custom_call" | custom-call | flops 1912602624 | bytes 4194304 | tf_op jit(solution)/shard_map/mine/pallas_call | solution.py:481
  51.3 1.0 %collective-permute-done.13.g1 = bf16[64,512]{1,0:T(8,128)(2,1)S(1)} collective-permute-done((bf16[64,512]{1,0:T(8,128)(2,1)S(1)}, bf16[64,512]{1,0:T(8,128)(2,1)S(1)}, u32[]{:S(2)}, u32[]{:S(2)}) %collective-permute-start.13) | collective-permute-done | bytes 65568 | tf_op jit(solution)/shard_map/ppermute | solution.py:472
  52.3 0.0 collective-permute-done.14.g2
  52.3 0.3 collective-permute-done.15.g3
  52.5 1.2 %collective-permute-start.16 = (bf16[64,512]{1,0:T(8,128)(2,1)S(1)}, bf16[64,512]{1,0:T(8,128)(2,1)S(1)}, u32[]{:S(2)}, u32[]{:S(2)}) collective-permute-start(bf16[64,512]{1,0:T(8,128)(2,1)S(1)} %collective-permute-done.13.g1), channel_id=1, source_target_pairs={{0,1},{1,0},{2,3},{3,2},{4,5},{5,4},{6,7},{7,6},{8,9},{9,8},{10,11... | collective-permute-start | bytes 196616 | tf_op jit(solution)/shard_map/ppermute | solution.py:487
  53.7 0.0 collective-permute-start.17
  53.7 0.5 collective-permute-start.18
  54.2 1.2 %own.3.raw_ref = f32[2560,128]{1,0:T(8,128)S(1)} custom-call(bf16[1216,512]{1,0:T(8,128)(2,1)S(1)} %get-tuple-element.158.x_ref, bf16[64,512]{1,0:T(8,128)(2,1)S(1)} %collective-permute-done.13.g1, bf16[64,512]{1,0:T(8,128)(2,1)S(1)} %collective-permute-done.14.g2, bf16[64,512]{1,0:T(8,128)(2,1)S(1)} %collective-permute-done.15.g3, ...), custom_call_target="tpu_custom_call" | custom-call | flops 335544320 | bytes 4194304 | tf_op jit(solution)/shard_map/own/pallas_call | solution.py:488
  55.4 0.0 collective-permute-done.16.g1
  55.4 0.0 collective-permute-done.17.g2
  55.4 0.0 collective-permute-done.18.g3
  55.4 0.0 collective-permute-done.12.x_ref
  55.5 0.0 copy-start
  55.5 0.0 copy-start.1
  55.5 1.4 %gram.3 = (f32[448,128]{1,0:T(8,128)S(1)}, f32[448,128]{1,0:T(8,128)S(1)}, f32[448,128]{1,0:T(8,128)S(1)}, f32[448,128]{1,0:T(8,128)S(1)}) custom-call(s32[8,128]{1,0:T(8,128)S(1)} %get-tuple-element.148.meta_ref, bf16[1216,512]{1,0:T(8,128)(2,1)S(1)} %collective-permute-done.12.x_ref, bf16[64,512]{1,0:T(8,128)(2,1)S(1)} %collective-permute-done.16.g1, ...), custom_call_target="tpu_custom_call" | custom-call | tf_op jit(solution)/shard_map/gram/pallas_call | solution.py:495
  56.9 0.4 collective-permute-start.19
  57.3 1.5 %collective-permute-start.20 = (f32[448,128]{1,0:T(8,128)S(1)}, f32[448,128]{1,0:T(8,128)S(1)}, u32[]{:S(2)}, u32[]{:S(2)}) collective-permute-start(f32[448,128]{1,0:T(8,128)S(1)} %get-tuple-element.161), channel_id=1, source_target_pairs={{0,4},{2,6},{4,0},{6,2},{1,5},{3,7},{5,1},{7,3},{8,12},{10,14},{12... | collective-permute-start | bytes 688136 | tf_op jit(solution)/shard_map/ppermute | solution.py:503
  58.8 1.4 %collective-permute-start.21 = (f32[448,128]{1,0:T(8,128)S(1)}, f32[448,128]{1,0:T(8,128)S(1)}, u32[]{:S(2)}, u32[]{:S(2)}) collective-permute-start(f32[448,128]{1,0:T(8,128)S(1)} %get-tuple-element.162), channel_id=1, source_target_pairs={{0,6},{2,0},{4,2},{6,4},{1,7},{3,1},{5,3},{7,5},{8,14},{10,8},{12,... | collective-permute-start | bytes 688136 | tf_op jit(solution)/shard_map/ppermute | solution.py:503
  60.1 0.5 fit.3
  60.7 0.5 slice.6
  61.8 8.8 %collective-permute-done.19.p1 = f32[448,128]{1,0:T(8,128)S(1)} collective-permute-done((f32[448,128]{1,0:T(8,128)S(1)}, f32[448,128]{1,0:T(8,128)S(1)}, u32[]{:S(2)}, u32[]{:S(2)}) %collective-permute-start.19) | collective-permute-done | bytes 229408 | tf_op jit(solution)/shard_map/ppermute | solution.py:503
  70.6 0.0 collective-permute-done.20.p2
  70.6 0.4 collective-permute-done.21.p3
  71.0 1.4 %maxima.3 = f32[128,128]{1,0:T(8,128)} custom-call(s32[8,128]{1,0:T(8,128)S(1)} %get-tuple-element.148.meta_ref, f32[448,128]{1,0:T(8,128)S(1)} %get-tuple-element.163.p0, f32[448,128]{1,0:T(8,128)S(1)} %collective-permute-done.19.p1, f32[448,128]{1,0:T(8,128)S(1)} %collective-permute-done.20.p2, f32[448,128]{1,0:T(8,128)S(1)} %collective-permute-done.21.p3, ...), custom_call_target="tpu_custom_call" | custom-call | tf_op jit(solution)/shard_map/maxima/pallas_call | solution.py:510
  72.4 6.7 %all-to-all-start.8 = ((f32[128,1,128]{2,1,0:T(1,128)}), f32[128,1,128]{2,1,0:T(1,128)S(1)}, u32[]{:S(2)}, u32[]{:S(2)}) async-start(f32[128,1,128]{2,1,0:T(1,128)} %bitcast.17), calls=%async_computation.8 | async-start | bytes 131072 | tf_op jit(solution)/shard_map/all_to_all | solution.py:517
  79.1 9.5 %all-to-all-done.8 = f32[128,1,128]{2,1,0:T(1,128)S(1)} async-done(((f32[128,1,128]{2,1,0:T(1,128)}), f32[128,1,128]{2,1,0:T(1,128)S(1)}, u32[]{:S(2)}, u32[]{:S(2)}) %all-to-all-start.8) | async-done | bytes 65568 | tf_op jit(solution)/shard_map/all_to_all | solution.py:517
  88.5 0.0 copy-done
  88.5 0.0 copy-done.1
  88.5 0.8 pick.3
  (1 shorter events, 0.0 us)
Async XLA Ops:
  1.9 3.1 %collective-permute-start.11 = (bf16[144,2048]{1,0:T(8,128)(2,1)S(1)}, bf16[144,2048]{1,0:T(8,128)(2,1)S(1)}, u32[]{:S(2)}, u32[]{:S(2)}) collective-permute-start(bf16[144,2048]{1,0:T(8,128)(2,1)S(1)} %get-tuple-element.146), channel_id=1, source_target_pairs={{0,1},{1,0},{2,3},{3,2},{4,5},{5,4},{6,7},{7,6},{8,9},{9,8},{10,11... | collective-permute-start | bytes 1769480 | tf_op jit(solution)/shard_map/ppermute | solution.py:459
  43.0 12.5 %collective-permute-start.12 = (bf16[1216,512]{1,0:T(8,128)(2,1)S(1)}, bf16[1216,512]{1,0:T(8,128)(2,1)S(1)}, u32[]{:S(2)}, u32[]{:S(2)}) collective-permute-start(bf16[1216,512]{1,0:T(8,128)(2,1)S(1)} %send.3.send_ref), channel_id=1, source_target_pairs={{0,1},{1,0},{2,3},{3,2},{4,5},{5,4},{6,7},{7,6},{8,9},{9,8},{10,11... | collective-permute-start | bytes 3735560 | tf_op jit(solution)/shard_map/ppermute | solution.py:480
  46.0 6.3 %collective-permute-start.13 = (bf16[64,512]{1,0:T(8,128)(2,1)S(1)}, bf16[64,512]{1,0:T(8,128)(2,1)S(1)}, u32[]{:S(2)}, u32[]{:S(2)}) collective-permute-start(bf16[64,512]{1,0:T(8,128)(2,1)S(1)} %get-tuple-element.150), channel_id=1, source_target_pairs={{0,8},{8,16},{16,24},{24,0},{1,9},{9,17},{17,25},{25,1},{2,10},{10... | collective-permute-start | bytes 196616 | tf_op jit(solution)/shard_map/ppermute | solution.py:472
  46.3 6.0 %collective-permute-start.14 = (bf16[64,512]{1,0:T(8,128)(2,1)S(1)}, bf16[64,512]{1,0:T(8,128)(2,1)S(1)}, u32[]{:S(2)}, u32[]{:S(2)}) collective-permute-start(bf16[64,512]{1,0:T(8,128)(2,1)S(1)} %get-tuple-element.150), channel_id=1, source_target_pairs={{0,16},{8,24},{16,0},{24,8},{1,17},{9,25},{17,1},{25,9},{2,18},{10... | collective-permute-start | bytes 196616 | tf_op jit(solution)/shard_map/ppermute | solution.py:472
  46.8 5.7 %collective-permute-start.15 = (bf16[64,512]{1,0:T(8,128)(2,1)S(1)}, bf16[64,512]{1,0:T(8,128)(2,1)S(1)}, u32[]{:S(2)}, u32[]{:S(2)}) collective-permute-start(bf16[64,512]{1,0:T(8,128)(2,1)S(1)} %get-tuple-element.150), channel_id=1, source_target_pairs={{0,24},{8,0},{16,8},{24,16},{1,25},{9,1},{17,9},{25,17},{2,26},{10... | collective-permute-start | bytes 196616 | tf_op jit(solution)/shard_map/ppermute | solution.py:472
  52.5 2.9 %collective-permute-start.16 = (bf16[64,512]{1,0:T(8,128)(2,1)S(1)}, bf16[64,512]{1,0:T(8,128)(2,1)S(1)}, u32[]{:S(2)}, u32[]{:S(2)}) collective-permute-start(bf16[64,512]{1,0:T(8,128)(2,1)S(1)} %collective-permute-done.13.g1), channel_id=1, source_target_pairs={{0,1},{1,0},{2,3},{3,2},{4,5},{5,4},{6,7},{7,6},{8,9},{9,8},{10,11... | collective-permute-start | bytes 196616 | tf_op jit(solution)/shard_map/ppermute | solution.py:487
  53.7 1.7 %collective-permute-start.17 = (bf16[64,512]{1,0:T(8,128)(2,1)S(1)}, bf16[64,512]{1,0:T(8,128)(2,1)S(1)}, u32[]{:S(2)}, u32[]{:S(2)}) collective-permute-start(bf16[64,512]{1,0:T(8,128)(2,1)S(1)} %collective-permute-done.14.g2), channel_id=1, source_target_pairs={{0,1},{1,0},{2,3},{3,2},{4,5},{5,4},{6,7},{7,6},{8,9},{9,8},{10,11... | collective-permute-start | bytes 196616 | tf_op jit(solution)/shard_map/ppermute | solution.py:487
  53.7 1.7 %collective-permute-start.18 = (bf16[64,512]{1,0:T(8,128)(2,1)S(1)}, bf16[64,512]{1,0:T(8,128)(2,1)S(1)}, u32[]{:S(2)}, u32[]{:S(2)}) collective-permute-start(bf16[64,512]{1,0:T(8,128)(2,1)S(1)} %collective-permute-done.15.g3), channel_id=1, source_target_pairs={{0,1},{1,0},{2,3},{3,2},{4,5},{5,4},{6,7},{7,6},{8,9},{9,8},{10,11... | collective-permute-start | bytes 196616 | tf_op jit(solution)/shard_map/ppermute | solution.py:487
  55.5 33.1 %copy-start = (s32[128]{0:T(128)S(1)}, s32[128]{0:T(128)}, u32[]{:S(2)}) copy-start(s32[128]{0:T(128)} %param.9) | copy-start | bytes 1540
  55.5 33.1 %copy-start.1 = (f32[128,4096]{1,0:T(8,128)S(1)}, f32[128,4096]{1,0:T(8,128)}, u32[]{:S(2)}) copy-start(f32[128,4096]{1,0:T(8,128)} %x_ref.1) | copy-start | bytes 6291460
  56.9 13.7 %collective-permute-start.19 = (f32[448,128]{1,0:T(8,128)S(1)}, f32[448,128]{1,0:T(8,128)S(1)}, u32[]{:S(2)}, u32[]{:S(2)}) collective-permute-start(f32[448,128]{1,0:T(8,128)S(1)} %get-tuple-element.160), channel_id=1, source_target_pairs={{0,2},{2,4},{4,6},{6,0},{1,3},{3,5},{5,7},{7,1},{8,10},{10,12},{12... | collective-permute-start | bytes 688136 | tf_op jit(solution)/shard_map/ppermute | solution.py:503
  57.3 13.3 %collective-permute-start.20 = (f32[448,128]{1,0:T(8,128)S(1)}, f32[448,128]{1,0:T(8,128)S(1)}, u32[]{:S(2)}, u32[]{:S(2)}) collective-permute-start(f32[448,128]{1,0:T(8,128)S(1)} %get-tuple-element.161), channel_id=1, source_target_pairs={{0,4},{2,6},{4,0},{6,2},{1,5},{3,7},{5,1},{7,3},{8,12},{10,14},{12... | collective-permute-start | bytes 688136 | tf_op jit(solution)/shard_map/ppermute | solution.py:503
  58.8 12.2 %collective-permute-start.21 = (f32[448,128]{1,0:T(8,128)S(1)}, f32[448,128]{1,0:T(8,128)S(1)}, u32[]{:S(2)}, u32[]{:S(2)}) collective-permute-start(f32[448,128]{1,0:T(8,128)S(1)} %get-tuple-element.162), channel_id=1, source_target_pairs={{0,6},{2,0},{4,2},{6,4},{1,7},{3,1},{5,3},{7,5},{8,14},{10,8},{12,... | collective-permute-start | bytes 688136 | tf_op jit(solution)/shard_map/ppermute | solution.py:503
  72.4 16.1 %all-to-all-start.8 = ((f32[128,1,128]{2,1,0:T(1,128)}), f32[128,1,128]{2,1,0:T(1,128)S(1)}, u32[]{:S(2)}, u32[]{:S(2)}) async-start(f32[128,1,128]{2,1,0:T(1,128)} %bitcast.17), calls=%async_computation.8 | async-start | bytes 131072 | tf_op jit(solution)/shard_map/all_to_all | solution.py:517

commit v10 on v9

--- a/solution.py
+++ b/solution.py
@@ -13,7 +13,7 @@
 LABEL_ROWS = 16
 BINS = 16
 CHIPS = 64
-BLOCKS = (24, 32)
+TRIES = ((24, 11), (32, 16))
 GROUP = 32
 GUESTS = 64
 ALL_GUESTS = 4 * GUESTS
@@ -21,20 +21,16 @@
 LANES = 128
 CAPS = (704, 512, 320, 192)
 STARTS = (0, 704, 1216, 1536)
-HALF = 64
-COUNT = 7
-CHUNK = COUNT * HALF
-PARTIAL = 4 * CHUNK
+UNIT = 32
 SHARES = (
-    tuple((q, first) for q, first in ((0, 0), (0, 128), (2, 0), (2, 128), (2, 256))),
-    tuple((q, first) for q, first in (
-        (0, 256), (0, 384), (0, 512), (0, 640), (1, 0), (1, 128), (1, 256), (1, 384), (3, 0), (3, 128))),
+    ((0, 0), (0, 256), (2, 0), (2, 128), (2, 256), (3, 0)),
+    ((0, 128), (0, 384), (0, 512), (0, 640), (1, 0), (1, 128), (1, 256), (1, 384), (3, 128)),
 )
-BASES = ({0: 0, 2: 704}, {0: -256, 1: 448, 3: 960})
+BASES = ({0: 0, 2: 704, 3: 1024}, {0: -128, 1: 576, 3: 960})
 SHARE_ROWS = 1216
 SEGMENTS = (
-    (0, 256, 0, None), (256, 448, 256, 0), (704, 256, None, 448), (960, 256, None, 704),
-    (1216, 320, 704, None), (1536, 192, None, 960),
+    (0, 128, 0, None), (128, 576, 128, 0), (704, 256, None, 576), (960, 256, None, 832),
+    (1216, 320, 704, None), (1536, 128, 1024, None), (1664, 64, 1152, 1088),
 )
 f32, bf16, i32 = jnp.float32, jnp.bfloat16, jnp.int32
 WHOLE = pl.BlockSpec(memory_space=pltpu.VMEM)
@@ -262,7 +258,7 @@
     far_ref[...] = jnp.broadcast_to((32.0 * total[:1] + total[1:2]).astype(i32), far_ref.shape)
 
 
-def fit_kernel(block, x_ref, over_ref):
+def fit_kernel(block, units, x_ref, over_ref):
     _, chip_counts = labels_of(block, x_ref)
     counts, sizes = counts_of(chip_counts)
     ordered = in_order(sizes)
@@ -270,8 +266,11 @@
     for size, cap in zip(ordered, CAPS):
         over = jnp.maximum(over, jnp.where(size > cap, 1.0, 0.0))
     for share in SHARES:
-        length = sum(jnp.maximum(jnp.floor((ordered[q] + 63.0) * (1 / 64)) - first // HALF, 0.0) for q, first in share)
-        over = jnp.maximum(over, jnp.where(length > 4 * COUNT, 1.0, 0.0))
+        length = 0.0
+        for q, first in share:
+            rows = jnp.maximum(jnp.floor((ordered[q] + (UNIT - 1.0)) * (1 / UNIT)) - first // UNIT, 0.0)
+            length = length + jnp.where(rows >= 3.0, rows - 1.0, rows)
+        over = jnp.maximum(over, jnp.where(length > 4 * units, 1.0, 0.0))
     taken = counts[0] + counts[1] + counts[2] + counts[3]
     extra, room = jnp.maximum(taken - (block - 1), 0.0), jnp.maximum((block - 1) - taken, 0.0)
     row, col = iota((LANES, LANES), 0), iota((LANES, LANES), 1)
@@ -323,10 +322,18 @@
 
 
 def length_of(size, first):
-    return jnp.maximum(((size + HALF - 1) >> 6) - first // HALF, 0)
-
-
-def gram_kernel(meta_ref, x_ref, g1, g2, g3, far_ref, raw_ref, out0, out1, out2, out3, part_ref, rows_ref):
+    units = jnp.maximum(((size + UNIT - 1) >> 5) - first // UNIT, 0)
+    return jnp.where(units >= 3, units - 1, units)
+
+
+def folded(score):
+    away = jnp.full((UNIT, LANES), -4.0, f32) if score.shape[0] < LANES else score[2 * UNIT:3 * UNIT]
+    both = jnp.where(iota(away.shape, 1) < 3 * UNIT, away, pltpu.roll(score[:UNIT], 3 * UNIT, 1))
+    rest = [score[3 * UNIT:]] if score.shape[0] > 3 * UNIT else []
+    return jnp.concatenate([both, score[UNIT:2 * UNIT]] + rest, axis=0)
+
+
+def gram_kernel(units, meta_ref, x_ref, g1, g2, g3, far_ref, raw_ref, out0, out1, out2, out3, part_ref, rows_ref):
     y, c = index_on("y"), index_on("c")
     part_ref[...] = jnp.full(part_ref.shape, -4.0, f32)
     for core in range(2):
@@ -341,45 +348,53 @@
                 size = size_of(meta_ref, q)
                 i, j = iota(score.shape, 0), iota(score.shape, 1)
                 keep = (i < size - first) & (j < size - first) & (i != j)
-                part_ref[pl.ds(pl.multiple_of(to, HALF), rows), :] = jnp.where(keep, score, -4.0)
-                to = jnp.minimum(to + HALF * length_of(size, first), PARTIAL)
+                score = folded(jnp.where(keep, score, -4.0))
+                part_ref[pl.ds(pl.multiple_of(to, UNIT), score.shape[0]), :] = score
+                to = jnp.minimum(to + UNIT * length_of(size, first), 4 * units * UNIT)
+    chunk = units * UNIT
     for shift, out in enumerate((out0, out1, out2, out3)):
-        out[...] = part_ref[pl.ds(pl.multiple_of(lax.rem(y + shift, 4) * CHUNK, HALF), CHUNK), :]
+        out[...] = part_ref[pl.ds(pl.multiple_of(lax.rem(y + shift, 4) * chunk, UNIT), chunk), :]
 
 
 FIRST_ROW = (0, 6, 10, 13)
 
 
-def max_kernel(meta_ref, p0, p1, p2, p3, pos_ref, out_ref, best_ref):
+def max_kernel(units, meta_ref, p0, p1, p2, p3, pos_ref, out_ref, best_ref):
     y, c = index_on("y"), index_on("c")
     best_ref[...] = jnp.full(best_ref.shape, -1.0, f32)
-    sub, lane = iota((HALF, LANES), 0), iota((HALF, LANES), 1)
+    sub, lane = iota((UNIT, LANES), 0), iota((UNIT, LANES), 1)
     blocks, sizes = [], [size_of(meta_ref, q) for q in range(4)]
     for core, share in enumerate(SHARES):
         at = jnp.zeros((), i32)
         for q, first in share:
             length = length_of(sizes[q], first)
-            col = FIRST_ROW[q] + first // LANES
-            blocks.append((jnp.where((c == core) & (length > 0), at, PARTIAL), col, 2 * col - at))
+            blocks.append((jnp.where((c == core) & (length > 0), at, 4 * units), FIRST_ROW[q] + first // LANES, at))
             at = at + length
-    for t in range(COUNT):
-        at = slice(t * HALF, (t + 1) * HALF)
+    for t in range(units):
+        at = slice(t * UNIT, (t + 1) * UNIT)
         block = (p0[at, :] + p1[at, :]) + (p2[at, :] + p3[at, :])
-        index = y * COUNT + t
-        col, shift = jnp.asarray(15, i32), jnp.asarray(0, i32)
-        for start, block_col, block_shift in blocks:
-            inside = index >= start
-            col, shift = jnp.where(inside, block_col, col), jnp.where(inside, block_shift, shift)
-        row = jnp.minimum(jnp.maximum(index + shift, 0), 31)
-        along = jnp.max(block, axis=1, keepdims=True)
-        along = jnp.max(jnp.where(sub + (row & 1) * HALF == lane, along, -1.0), axis=0, keepdims=True)
-        row = row >> 1
+        index = y * units + t
+        col, start = jnp.asarray(15, i32), jnp.asarray(0, i32)
+        for block_start, block_col, block_at in blocks:
+            inside = index >= block_start
+            col, start = jnp.where(inside, block_col, col), jnp.where(inside, block_at, start)
+        turn = index - start
+        unit = 4 * col + jnp.where(turn == 0, 2, jnp.where(turn == 1, 1, turn + 1))
+        unit = jnp.minimum(jnp.maximum(unit, 0), 63)
+        beside = (lane >= 3 * UNIT) & (turn == 0)
+        one, two = jnp.where(beside, -4.0, block), jnp.where(beside, block, -4.0)
+        along = jnp.max(one, axis=1, keepdims=True)
+        along = jnp.max(jnp.where(sub + (unit & 3) * UNIT == lane, along, -1.0), axis=0, keepdims=True)
+        row = unit >> 2
         best_ref[pl.ds(row, 1), :] = jnp.maximum(best_ref[pl.ds(row, 1), :], along)
-        down = jnp.max(block, axis=0, keepdims=True)
+        down = jnp.max(one, axis=0, keepdims=True)
+        along = jnp.max(two, axis=1, keepdims=True)
+        two = jnp.maximum(jnp.where(sub == lane, along, -1.0), pltpu.roll(two, UNIT, 1))
+        down = jnp.maximum(down, jnp.max(two, axis=0, keepdims=True))
         best_ref[pl.ds(col, 1), :] = jnp.maximum(best_ref[pl.ds(col, 1), :], down)
     pos = pos_ref[...]
-    pos = jnp.where(pos >= STARTS[1], pos + HALF, pos)
-    pos = jnp.where(pos >= STARTS[3] + HALF, pos + HALF, pos)
+    pos = jnp.where(pos >= STARTS[1], pos + 64, pos)
+    pos = jnp.where(pos >= STARTS[3] + 64, pos + 64, pos)
     row, lane = pos >> 7, pos & (LANES - 1)
     out = jnp.full(pos.shape, -1.0, f32)
     for r in range(15):
@@ -449,7 +464,7 @@
     return returned[place]
 
 
-def route(block, embeddings, cluster_ids):
+def route(block, units, embeddings, cluster_ids):
     shape = jax.ShapeDtypeStruct
     half = shape((ROWS + LABEL_ROWS, HALF_WIDTH), bf16)
     keep, send = pl.pallas_call(
@@ -493,22 +508,22 @@
         cost_estimate=pl.CostEstimate(flops=2 * RAW_ROWS * LANES * WIDTH, bytes_accessed=4 << 20, transcendentals=0),
     )(mine, *brought, far)
     partial = pl.pallas_call(
-        gram_kernel,
-        out_shape=[shape((CHUNK, LANES), f32)] * 4,
+        functools.partial(gram_kernel, units),
+        out_shape=[shape((units * UNIT, LANES), f32)] * 4,
         in_specs=[WHOLE] * 7, out_specs=[WHOLE] * 4,
-        scratch_shapes=[pltpu.VMEM((PARTIAL + CAPS[0], LANES), f32), pltpu.VMEM((SHARE_ROWS, WIDTH), bf16)],
+        scratch_shapes=[pltpu.VMEM((4 * units * UNIT + CAPS[0], LANES), f32), pltpu.VMEM((SHARE_ROWS, WIDTH), bf16)],
         compiler_params=params(16), name="gram",
     )(meta, other, *swapped, far, raw)
     arrived = [partial[0]] + [
         lax.ppermute(partial[s], "y", [(i, (i + s) % 4) for i in range(4)]) for s in (1, 2, 3)
     ]
     over = pl.pallas_call(
-        functools.partial(fit_kernel, block), out_shape=shape((8, LANES), i32),
+        functools.partial(fit_kernel, block, units), out_shape=shape((8, LANES), i32),
         in_specs=[WHOLE], out_specs=WHOLE, compiler_params=params(8), name="fit",
     )(packed)
     arrived, fits = lax.optimization_barrier((arrived, over[0, 0] == 0))
     best = pl.pallas_call(
-        max_kernel,
+        functools.partial(max_kernel, units),
         out_shape=shape((2 * CHIPS, LANES), f32),
         in_specs=[WHOLE] * 6, out_specs=WHOLE,
         scratch_shapes=[pltpu.VMEM((16, LANES), f32)],
@@ -524,14 +539,14 @@
     return best, fits
 
 
-def on_device(embeddings, cluster_ids, blocks=BLOCKS):
-    if not blocks:
+def on_device(embeddings, cluster_ids, tries=TRIES):
+    if not tries:
         return gather_groups(embeddings, cluster_ids)
-    best, fits = route(blocks[0], embeddings, cluster_ids)
+    best, fits = route(*tries[0], embeddings, cluster_ids)
     return lax.cond(
         fits,
         lambda best, embeddings, cluster_ids: best,
-        lambda best, embeddings, cluster_ids: on_device(embeddings, cluster_ids, blocks[1:]),
+        lambda best, embeddings, cluster_ids: on_device(embeddings, cluster_ids, tries[1:]),
         best, embeddings, cluster_ids,
     )
 

time: 89.5 us -> 87.9 us (0.982)
  waiting for transfers between devices: 21.5 us -> 19.7 us
    ppermute x3, waiting for transfers between devices: 9.2 us -> 7.04 us  [route(): lax.ppermute(partial[s], 'y', [(i, (i + s) % 4) for i in range(4)])]
where the time goes in v10:
time: 87.9 us; the launch traced here: 87.7 us
  blocking collectives  33.4 us (38%)
  waiting for transfers between devices  19.7 us (22%)
  starting transfers between devices  18.5 us (21%)
  Pallas kernels  14.8 us (17%)
    all_to_all x1, blocking collectives, route(): packed = lax.all_to_all(packed, ('x', 'z', 'y'), 0, 0, tiled=True)  33.4 us
    all_to_all x1, waiting for transfers between devices, route(): lax.all_to_all(best.reshape(2 * CHIPS, 1, LANES), ('c', 'x', 'z', 'y'), 0...  9.46 us
    ppermute x3, waiting for transfers between devices, route(): lax.ppermute(partial[s], 'y', [(i, (i + s) % 4) for i in range(4)])  7.04 us
    all_to_all x1, starting transfers between devices, route(): lax.all_to_all(best.reshape(2 * CHIPS, 1, LANES), ('c', 'x', 'z', 'y'), 0...  6.73 us
    ppermute x3, starting transfers between devices, route(): lax.ppermute(partial[s], 'y', [(i, (i + s) % 4) for i in range(4)])  3.22 us
    ppermute x3, starting transfers between devices, route(): lax.ppermute(guests, 'z', [(i, (i + s) % 4) for i in range(4)])  2.71 us
    ppermute x1, starting transfers between devices, route(): other = lax.ppermute(send, 'c', [(0, 1), (1, 0)])  2.69 us
    pallas_call x1, Pallas kernels, route(): pl.pallas_call(functools.partial(send_kernel, block), out_shape=share, in...  2.34 us
  transfers between devices with their start and end apart: 12, of which 6 were waited for; matrix products, arithmetic and copies ran while one was open for 1% of the time, Pallas kernels for 5%

profile of v10, /device:TPU:1, one launch (start us, length us, event | category | flops | bytes accessed | tf_op | source)
XLA Modules:
  0.0 87.7 jit_solution(3872825258174403987)
XLA Ops:
  0.0 1.9 %unit.3 = (bf16[144,2048]{1,0:T(8,128)(2,1)S(1)}, bf16[144,2048]{1,0:T(8,128)(2,1)S(1)}) custom-call(f32[128,4096]{1,0:T(8,128)} %x_ref.1, s32[1,128]{1,0:T(1,128)} %bitcast.35), custom_call_target="tpu_custom_call" | custom-call | tf_op jit(solution)/shard_map/unit/pallas_call | solution.py:470
  1.9 1.5 %collective-permute-start.11 = (bf16[144,2048]{1,0:T(8,128)(2,1)S(1)}, bf16[144,2048]{1,0:T(8,128)(2,1)S(1)}, u32[]{:S(2)}, u32[]{:S(2)}) collective-permute-start(bf16[144,2048]{1,0:T(8,128)(2,1)S(1)} %get-tuple-element.146), channel_id=1, source_target_pairs={{0,1},{1,0},{2,3},{3,2},{4,5},{5,4},{6,7},{7,6},{8,9},{9,8},{10,11... | collective-permute-start | bytes 1769480 | tf_op jit(solution)/shard_map/ppermute | solution.py:474
  3.4 1.6 %collective-permute-done.11.got_ref = bf16[144,2048]{1,0:T(8,128)(2,1)S(1)} collective-permute-done((bf16[144,2048]{1,0:T(8,128)(2,1)S(1)}, bf16[144,2048]{1,0:T(8,128)(2,1)S(1)}, u32[]{:S(2)}, u32[]{:S(2)}) %collective-permute-start.11) | collective-permute-done | bytes 589856 | tf_op jit(solution)/shard_map/ppermute | solution.py:474
  5.0 1.0 %pack.3 = (bf16[64,24,512]{2,1,0:T(8,128)(2,1)S(1)}, s32[8,128]{1,0:T(8,128)S(1)}) custom-call(bf16[144,2048]{1,0:T(8,128)(2,1)S(1)} %get-tuple-element.145.keep_ref, bf16[144,2048]{1,0:T(8,128)(2,1)S(1)} %collective-permute-done.11.got_ref), custom_call_target="tpu_custom_call" | custom-call | tf_op jit(solution)/shard_map/pack/pallas_call | solution.py:475
  6.1 33.4 %all_to_all.61.x_ref = bf16[64,24,512]{2,1,0:T(8,128)(2,1)S(1)} all-to-all(bf16[64,24,512]{2,1,0:T(8,128)(2,1)S(1)} %get-tuple-element.147), channel_id=1, replica_groups=mesh['x'=4,'z'=4,'y'=4,'c'=2] {'x','z','y'}, dimensions={0} | all-to-all | bytes 3145728 | tf_op jit(solution)/shard_map/all_to_all | solution.py:480
  39.5 1.6 %names.3 = (bf16[64,512]{1,0:T(8,128)(2,1)S(1)}, s32[8,1536]{1,0:T(8,128)S(1)}, s32[64,128]{1,0:T(8,128)S(1)}, s32[64,128]{1,0:T(8,128)S(1)}, s32[8,128]{1,0:T(8,128)S(1)}) custom-call(bf16[64,24,512]{2,1,0:T(8,128)(2,1)S(1)} %all_to_all.61.x_ref), custom_call_target="tpu_custom_call" | custom-call | tf_op jit(solution)/shard_map/names/pallas_call | solution.py:482
  41.1 2.3 %send.3.send_ref = bf16[1216,512]{1,0:T(8,128)(2,1)S(1)} custom-call(bf16[64,24,512]{2,1,0:T(8,128)(2,1)S(1)} %all_to_all.61.x_ref, s32[8,1536]{1,0:T(8,128)S(1)} %get-tuple-element.149.line_ref), custom_call_target="tpu_custom_call" | custom-call | flops 1912602624 | bytes 4194304 | tf_op jit(solution)/shard_map/send/pallas_call | solution.py:490
  43.4 2.7 %collective-permute-start.12 = (bf16[1216,512]{1,0:T(8,128)(2,1)S(1)}, bf16[1216,512]{1,0:T(8,128)(2,1)S(1)}, u32[]{:S(2)}, u32[]{:S(2)}) collective-permute-start(bf16[1216,512]{1,0:T(8,128)(2,1)S(1)} %send.3.send_ref), channel_id=1, source_target_pairs={{0,1},{1,0},{2,3},{3,2},{4,5},{5,4},{6,7},{7,6},{8,9},{9,8},{10,11... | collective-permute-start | bytes 3735560 | tf_op jit(solution)/shard_map/ppermute | solution.py:495
  46.1 0.3 collective-permute-start.13
  46.4 0.5 collective-permute-start.14
  47.0 1.9 %collective-permute-start.15 = (bf16[64,512]{1,0:T(8,128)(2,1)S(1)}, bf16[64,512]{1,0:T(8,128)(2,1)S(1)}, u32[]{:S(2)}, u32[]{:S(2)}) collective-permute-start(bf16[64,512]{1,0:T(8,128)(2,1)S(1)} %get-tuple-element.150), channel_id=1, source_target_pairs={{0,24},{8,0},{16,8},{24,16},{1,25},{9,1},{17,9},{25,17},{2,26},{10... | collective-permute-start | bytes 196616 | tf_op jit(solution)/shard_map/ppermute | solution.py:487
  48.8 2.3 %mine.3 = (bf16[1216,512]{1,0:T(8,128)(2,1)S(1)}, s32[8,256]{1,0:T(8,128)S(1)}) custom-call(bf16[64,24,512]{2,1,0:T(8,128)(2,1)S(1)} %all_to_all.61.x_ref, s32[8,1536]{1,0:T(8,128)S(1)} %get-tuple-element.149.line_ref, bf16[1216,512]{1,0:T(8,128)(2,1)S(1)} %send.3.send_ref, s32[64,128]{1,0:T(8,128)S(1)} %get-tuple-element.151.key_ref, ...), custom_call_target="tpu_custom_call" | custom-call | flops 1912602624 | bytes 4194304 | tf_op jit(solution)/shard_map/mine/pallas_call | solution.py:496
  51.1 1.3 %collective-permute-done.13.g1 = bf16[64,512]{1,0:T(8,128)(2,1)S(1)} collective-permute-done((bf16[64,512]{1,0:T(8,128)(2,1)S(1)}, bf16[64,512]{1,0:T(8,128)(2,1)S(1)}, u32[]{:S(2)}, u32[]{:S(2)}) %collective-permute-start.13) | collective-permute-done | bytes 65568 | tf_op jit(solution)/shard_map/ppermute | solution.py:487
  52.4 0.0 collective-permute-done.14.g2
  52.4 0.3 collective-permute-done.15.g3
  52.7 1.2 %collective-permute-start.16 = (bf16[64,512]{1,0:T(8,128)(2,1)S(1)}, bf16[64,512]{1,0:T(8,128)(2,1)S(1)}, u32[]{:S(2)}, u32[]{:S(2)}) collective-permute-start(bf16[64,512]{1,0:T(8,128)(2,1)S(1)} %collective-permute-done.13.g1), channel_id=1, source_target_pairs={{0,1},{1,0},{2,3},{3,2},{4,5},{5,4},{6,7},{7,6},{8,9},{9,8},{10,11... | collective-permute-start | bytes 196616 | tf_op jit(solution)/shard_map/ppermute | solution.py:502
  53.8 0.0 collective-permute-start.17
  53.8 0.5 collective-permute-start.18
  54.3 1.2 %own.3.raw_ref = f32[2496,128]{1,0:T(8,128)S(1)} custom-call(bf16[1216,512]{1,0:T(8,128)(2,1)S(1)} %get-tuple-element.158.x_ref, bf16[64,512]{1,0:T(8,128)(2,1)S(1)} %collective-permute-done.13.g1, bf16[64,512]{1,0:T(8,128)(2,1)S(1)} %collective-permute-done.14.g2, bf16[64,512]{1,0:T(8,128)(2,1)S(1)} %collective-permute-done.15.g3, ...), custom_call_target="tpu_custom_call" | custom-call | flops 327155712 | bytes 4194304 | tf_op jit(solution)/shard_map/own/pallas_call | solution.py:503
  55.6 0.0 collective-permute-done.16.g1
  55.6 0.0 collective-permute-done.17.g2
  55.6 0.0 collective-permute-done.18.g3
  55.6 0.0 collective-permute-done.12.x_ref
  55.6 0.0 copy-start
  55.6 0.0 copy-start.1
  55.6 1.5 %gram.3 = (f32[352,128]{1,0:T(8,128)S(1)}, f32[352,128]{1,0:T(8,128)S(1)}, f32[352,128]{1,0:T(8,128)S(1)}, f32[352,128]{1,0:T(8,128)S(1)}) custom-call(s32[8,128]{1,0:T(8,128)S(1)} %get-tuple-element.148.meta_ref, bf16[1216,512]{1,0:T(8,128)(2,1)S(1)} %collective-permute-done.12.x_ref, bf16[64,512]{1,0:T(8,128)(2,1)S(1)} %collective-permute-done.16.g1, ...), custom_call_target="tpu_custom_call" | custom-call | tf_op jit(solution)/shard_map/gram/pallas_call | solution.py:510
  57.1 0.4 collective-permute-start.19
  57.5 1.5 %collective-permute-start.20 = (f32[352,128]{1,0:T(8,128)S(1)}, f32[352,128]{1,0:T(8,128)S(1)}, u32[]{:S(2)}, u32[]{:S(2)}) collective-permute-start(f32[352,128]{1,0:T(8,128)S(1)} %get-tuple-element.161), channel_id=1, source_target_pairs={{0,4},{2,6},{4,0},{6,2},{1,5},{3,7},{5,1},{7,3},{8,12},{10,14},{12... | collective-permute-start | bytes 540680 | tf_op jit(solution)/shard_map/ppermute | solution.py:518
  59.0 1.4 %collective-permute-start.21 = (f32[352,128]{1,0:T(8,128)S(1)}, f32[352,128]{1,0:T(8,128)S(1)}, u32[]{:S(2)}, u32[]{:S(2)}) collective-permute-start(f32[352,128]{1,0:T(8,128)S(1)} %get-tuple-element.162), channel_id=1, source_target_pairs={{0,6},{2,0},{4,2},{6,4},{1,7},{3,1},{5,3},{7,5},{8,14},{10,8},{12,... | collective-permute-start | bytes 540680 | tf_op jit(solution)/shard_map/ppermute | solution.py:518
  60.3 0.5 fit.3
  60.8 0.5 slice.6
  62.0 6.6 %collective-permute-done.19.p1 = f32[352,128]{1,0:T(8,128)S(1)} collective-permute-done((f32[352,128]{1,0:T(8,128)S(1)}, f32[352,128]{1,0:T(8,128)S(1)}, u32[]{:S(2)}, u32[]{:S(2)}) %collective-permute-start.19) | collective-permute-done | bytes 180256 | tf_op jit(solution)/shard_map/ppermute | solution.py:518
  68.6 0.0 collective-permute-done.20.p2
  68.6 0.4 collective-permute-done.21.p3
  69.1 1.7 %maxima.3 = f32[128,128]{1,0:T(8,128)} custom-call(s32[8,128]{1,0:T(8,128)S(1)} %get-tuple-element.148.meta_ref, f32[352,128]{1,0:T(8,128)S(1)} %get-tuple-element.163.p0, f32[352,128]{1,0:T(8,128)S(1)} %collective-permute-done.19.p1, f32[352,128]{1,0:T(8,128)S(1)} %collective-permute-done.20.p2, f32[352,128]{1,0:T(8,128)S(1)} %collective-permute-done.21.p3, ...), custom_call_target="tpu_custom_call" | custom-call | tf_op jit(solution)/shard_map/maxima/pallas_call | solution.py:525
  70.8 6.7 %all-to-all-start.8 = ((f32[128,1,128]{2,1,0:T(1,128)}), f32[128,1,128]{2,1,0:T(1,128)S(1)}, u32[]{:S(2)}, u32[]{:S(2)}) async-start(f32[128,1,128]{2,1,0:T(1,128)} %bitcast.17), calls=%async_computation.8 | async-start | bytes 131072 | tf_op jit(solution)/shard_map/all_to_all | solution.py:532
  77.5 9.5 %all-to-all-done.8 = f32[128,1,128]{2,1,0:T(1,128)S(1)} async-done(((f32[128,1,128]{2,1,0:T(1,128)}), f32[128,1,128]{2,1,0:T(1,128)S(1)}, u32[]{:S(2)}, u32[]{:S(2)}) %all-to-all-start.8) | async-done | bytes 65568 | tf_op jit(solution)/shard_map/all_to_all | solution.py:532
  86.9 0.0 copy-done
  87.0 0.0 copy-done.1
  87.0 0.8 pick.3
  (1 shorter events, 0.0 us)
Async XLA Ops:
  1.9 3.1 %collective-permute-start.11 = (bf16[144,2048]{1,0:T(8,128)(2,1)S(1)}, bf16[144,2048]{1,0:T(8,128)(2,1)S(1)}, u32[]{:S(2)}, u32[]{:S(2)}) collective-permute-start(bf16[144,2048]{1,0:T(8,128)(2,1)S(1)} %get-tuple-element.146), channel_id=1, source_target_pairs={{0,1},{1,0},{2,3},{3,2},{4,5},{5,4},{6,7},{7,6},{8,9},{9,8},{10,11... | collective-permute-start | bytes 1769480 | tf_op jit(solution)/shard_map/ppermute | solution.py:474
  43.4 12.2 %collective-permute-start.12 = (bf16[1216,512]{1,0:T(8,128)(2,1)S(1)}, bf16[1216,512]{1,0:T(8,128)(2,1)S(1)}, u32[]{:S(2)}, u32[]{:S(2)}) collective-permute-start(bf16[1216,512]{1,0:T(8,128)(2,1)S(1)} %send.3.send_ref), channel_id=1, source_target_pairs={{0,1},{1,0},{2,3},{3,2},{4,5},{5,4},{6,7},{7,6},{8,9},{9,8},{10,11... | collective-permute-start | bytes 3735560 | tf_op jit(solution)/shard_map/ppermute | solution.py:495
  46.1 6.3 %collective-permute-start.13 = (bf16[64,512]{1,0:T(8,128)(2,1)S(1)}, bf16[64,512]{1,0:T(8,128)(2,1)S(1)}, u32[]{:S(2)}, u32[]{:S(2)}) collective-permute-start(bf16[64,512]{1,0:T(8,128)(2,1)S(1)} %get-tuple-element.150), channel_id=1, source_target_pairs={{0,8},{8,16},{16,24},{24,0},{1,9},{9,17},{17,25},{25,1},{2,10},{10... | collective-permute-start | bytes 196616 | tf_op jit(solution)/shard_map/ppermute | solution.py:487
  46.4 6.0 %collective-permute-start.14 = (bf16[64,512]{1,0:T(8,128)(2,1)S(1)}, bf16[64,512]{1,0:T(8,128)(2,1)S(1)}, u32[]{:S(2)}, u32[]{:S(2)}) collective-permute-start(bf16[64,512]{1,0:T(8,128)(2,1)S(1)} %get-tuple-element.150), channel_id=1, source_target_pairs={{0,16},{8,24},{16,0},{24,8},{1,17},{9,25},{17,1},{25,9},{2,18},{10... | collective-permute-start | bytes 196616 | tf_op jit(solution)/shard_map/ppermute | solution.py:487
  47.0 5.7 %collective-permute-start.15 = (bf16[64,512]{1,0:T(8,128)(2,1)S(1)}, bf16[64,512]{1,0:T(8,128)(2,1)S(1)}, u32[]{:S(2)}, u32[]{:S(2)}) collective-permute-start(bf16[64,512]{1,0:T(8,128)(2,1)S(1)} %get-tuple-element.150), channel_id=1, source_target_pairs={{0,24},{8,0},{16,8},{24,16},{1,25},{9,1},{17,9},{25,17},{2,26},{10... | collective-permute-start | bytes 196616 | tf_op jit(solution)/shard_map/ppermute | solution.py:487
  52.7 2.9 %collective-permute-start.16 = (bf16[64,512]{1,0:T(8,128)(2,1)S(1)}, bf16[64,512]{1,0:T(8,128)(2,1)S(1)}, u32[]{:S(2)}, u32[]{:S(2)}) collective-permute-start(bf16[64,512]{1,0:T(8,128)(2,1)S(1)} %collective-permute-done.13.g1), channel_id=1, source_target_pairs={{0,1},{1,0},{2,3},{3,2},{4,5},{5,4},{6,7},{7,6},{8,9},{9,8},{10,11... | collective-permute-start | bytes 196616 | tf_op jit(solution)/shard_map/ppermute | solution.py:502
  53.8 1.8 %collective-permute-start.17 = (bf16[64,512]{1,0:T(8,128)(2,1)S(1)}, bf16[64,512]{1,0:T(8,128)(2,1)S(1)}, u32[]{:S(2)}, u32[]{:S(2)}) collective-permute-start(bf16[64,512]{1,0:T(8,128)(2,1)S(1)} %collective-permute-done.14.g2), channel_id=1, source_target_pairs={{0,1},{1,0},{2,3},{3,2},{4,5},{5,4},{6,7},{7,6},{8,9},{9,8},{10,11... | collective-permute-start | bytes 196616 | tf_op jit(solution)/shard_map/ppermute | solution.py:502
  53.8 1.8 %collective-permute-start.18 = (bf16[64,512]{1,0:T(8,128)(2,1)S(1)}, bf16[64,512]{1,0:T(8,128)(2,1)S(1)}, u32[]{:S(2)}, u32[]{:S(2)}) collective-permute-start(bf16[64,512]{1,0:T(8,128)(2,1)S(1)} %collective-permute-done.15.g3), channel_id=1, source_target_pairs={{0,1},{1,0},{2,3},{3,2},{4,5},{5,4},{6,7},{7,6},{8,9},{9,8},{10,11... | collective-permute-start | bytes 196616 | tf_op jit(solution)/shard_map/ppermute | solution.py:502
  55.6 31.3 %copy-start = (s32[128]{0:T(128)S(1)}, s32[128]{0:T(128)}, u32[]{:S(2)}) copy-start(s32[128]{0:T(128)} %param.9) | copy-start | bytes 1540
  55.6 31.3 %copy-start.1 = (f32[128,4096]{1,0:T(8,128)S(1)}, f32[128,4096]{1,0:T(8,128)}, u32[]{:S(2)}) copy-start(f32[128,4096]{1,0:T(8,128)} %x_ref.1) | copy-start | bytes 6291460
  57.1 11.5 %collective-permute-start.19 = (f32[352,128]{1,0:T(8,128)S(1)}, f32[352,128]{1,0:T(8,128)S(1)}, u32[]{:S(2)}, u32[]{:S(2)}) collective-permute-start(f32[352,128]{1,0:T(8,128)S(1)} %get-tuple-element.160), channel_id=1, source_target_pairs={{0,2},{2,4},{4,6},{6,0},{1,3},{3,5},{5,7},{7,1},{8,10},{10,12},{12... | collective-permute-start | bytes 540680 | tf_op jit(solution)/shard_map/ppermute | solution.py:518
  57.5 11.2 %collective-permute-start.20 = (f32[352,128]{1,0:T(8,128)S(1)}, f32[352,128]{1,0:T(8,128)S(1)}, u32[]{:S(2)}, u32[]{:S(2)}) collective-permute-start(f32[352,128]{1,0:T(8,128)S(1)} %get-tuple-element.161), channel_id=1, source_target_pairs={{0,4},{2,6},{4,0},{6,2},{1,5},{3,7},{5,1},{7,3},{8,12},{10,14},{12... | collective-permute-start | bytes 540680 | tf_op jit(solution)/shard_map/ppermute | solution.py:518
  59.0 10.1 %collective-permute-start.21 = (f32[352,128]{1,0:T(8,128)S(1)}, f32[352,128]{1,0:T(8,128)S(1)}, u32[]{:S(2)}, u32[]{:S(2)}) collective-permute-start(f32[352,128]{1,0:T(8,128)S(1)} %get-tuple-element.162), channel_id=1, source_target_pairs={{0,6},{2,0},{4,2},{6,4},{1,7},{3,1},{5,3},{7,5},{8,14},{10,8},{12,... | collective-permute-start | bytes 540680 | tf_op jit(solution)/shard_map/ppermute | solution.py:518
  70.8 16.2 %all-to-all-start.8 = ((f32[128,1,128]{2,1,0:T(1,128)}), f32[128,1,128]{2,1,0:T(1,128)S(1)}, u32[]{:S(2)}, u32[]{:S(2)}) async-start(f32[128,1,128]{2,1,0:T(1,128)} %bitcast.17), calls=%async_computation.8 | async-start | bytes 131072 | tf_op jit(solution)/shard_map/all_to_all | solution.py:532

commit v11 on v10

--- a/solution.py
+++ b/solution.py
@@ -16,7 +16,6 @@
 TRIES = ((24, 11), (32, 16))
 GROUP = 32
 GUESTS = 64
-ALL_GUESTS = 4 * GUESTS
 GUEST = 4096
 LANES = 128
 CAPS = (704, 512, 320, 192)
@@ -79,8 +78,14 @@
         out_ref[ROWS:, :] = ids
 
 
+def passed_on(over, before):
+    once = before(over, 1)
+    twice = before(over, 2)
+    return jnp.maximum(jnp.maximum(over, 0), jnp.maximum(over + once, over + once + twice))
+
+
 def pack_kernel(block, keep_ref, got_ref, out_ref, code_ref):
-    y, first = index_on("y"), index_on("c") == 0
+    first = index_on("c") == 0
     kept = jnp.max(keep_ref[ROWS:, :ROWS].astype(f32), axis=0, keepdims=True)
     got = jnp.max(got_ref[ROWS:, :ROWS].astype(f32), axis=0, keepdims=True)
     labels = jnp.concatenate([jnp.where(first, kept, got), jnp.where(first, got, kept)], axis=0).astype(i32)
@@ -97,28 +102,27 @@
 
     rank, sizes = ranks_within([bins == b for b in range(BINS)])
     quad, line = bins >> 2, bins & 3
-    extra = rank >= (block - 1)
-    turn, _ = ranks_within([extra & (quad == q) for q in range(4)])
-    room, used = [], []
-    for step in range(4):
-        taken = jnp.zeros(labels.shape, f32)
-        for at in range(4):
-            size = jnp.zeros(labels.shape, f32)
-            for q in range(4):
-                b = 4 * q + at
-                size = jnp.where(quad == q, sizes[2 * b:2 * b + 1] + sizes[2 * b + 1:2 * b + 2], size)
-            taken = jnp.where(((at - y) & 3) == step, size, taken)
-        taken = jnp.minimum(taken.astype(i32), (block - 1))
-        used.append(taken)
-        room.append((block - 1) - taken)
-    placed = jnp.logical_not(extra)
-    to_line, to_slot, start = line, rank, jnp.zeros(labels.shape, i32)
-    for step in range(4):
-        here = extra & (turn >= start) & (turn < start + room[step])
-        to_line = jnp.where(here, (y + step) & 3, to_line)
-        to_slot = jnp.where(here, used[step] + turn - start, to_slot)
-        placed = placed | here
-        start = start + room[step]
+    taken = []
+    for at in range(4):
+        size = jnp.zeros(labels.shape, f32)
+        for b in range(at, BINS, 4):
+            size = jnp.where(quad == b >> 2, sizes[2 * b:2 * b + 1] + sizes[2 * b + 1:2 * b + 2], size)
+        taken.append(size.astype(i32) - (block - 1))
+    stays = []
+    for at in range(4):
+        moved = passed_on(taken[at], lambda _, back: taken[(at - back) & 3])
+        stays.append(taken[at] + (block - 1) - moved)
+
+    def of_line(values, which):
+        out = values[0]
+        for at in range(1, 4):
+            out = jnp.where(which == at, values[at], out)
+        return out
+
+    stay = of_line(stays, line)
+    to_line = jnp.where(rank < stay, line, (line + 1) & 3)
+    to_slot = jnp.where(rank < stay, rank, of_line(stays, to_line) + rank - stay)
+    placed = to_slot < (block - 1)
     lane = jnp.where(placed, to_line * GROUP + to_slot, -1)
     place = jnp.where(placed, (quad * 4 + to_line) * block + to_slot, -1)
     code_ref[...] = jnp.concatenate([jnp.where(placed, bins * LANES + lane, -1)] * 4, axis=0)
@@ -163,16 +167,8 @@
 
 
 def names_kernel(block, x_ref, guest_ref, line_ref, key_ref, pos_ref, meta_ref):
-    mine, z = index_on("x") * 4 + index_on("z"), index_on("z")
-    labels, chip_counts = labels_of(block, x_ref)
-    _, sizes = counts_of(chip_counts)
-    here = iota((1, LANES), 1) == mine
-    own = lambda v: jnp.sum(jnp.where(here, v, 0.0), axis=1, keepdims=True)
-    wide = lambda v: jnp.broadcast_to(v, (1, LANES))
-    ordered = in_order(sizes)
-    meta_ref[...] = jnp.concatenate([wide(own(v)) for v in ordered] * 2, axis=0).astype(i32)
-
-    n = [own(v) for v in sizes]
+    z = index_on("z")
+    labels, _ = labels_of(block, x_ref)
     row, col = iota((LANES, LANES), 0), iota((LANES, LANES), 1)
     lane = iota(labels.shape, 1)
     group = lane >> 5
@@ -181,8 +177,14 @@
     at_home = valid & (home == z)
     upper = as_bf16(row < col)
     lower = as_bf16(iota((CHIPS, CHIPS), 1) < iota((CHIPS, CHIPS), 0))
+    members, n = [at_home & ((labels & 3) == r) for r in range(4)], []
+    for member in members:
+        size = jnp.sum(jnp.where(member, 1.0, 0.0), axis=0, keepdims=True)
+        n.append(jnp.sum(size, axis=1, keepdims=True))
+    wide = lambda v: jnp.broadcast_to(v, (1, LANES))
+    meta_ref[...] = jnp.concatenate([wide(v) for v in in_order(n)] * 2, axis=0).astype(i32)
     pos = jnp.full(labels.shape, -1.0, f32)
-    for r in range(4):
+    for r, member in enumerate(members):
         place = sum(
             jnp.where((n[q] > n[r]) | ((n[q] == n[r]) & (q < r)), 1.0, 0.0) for q in range(4) if q != r
         )
@@ -190,7 +192,6 @@
             place < 0.5, float(STARTS[0]),
             jnp.where(place < 1.5, float(STARTS[1]), jnp.where(place < 2.5, float(STARTS[2]), float(STARTS[3]))),
         )
-        member = at_home & ((labels & 3) == r)
         member16 = as_bf16(member)
         rank = dot(member16, upper) + jnp.sum(dot(lower, member16), axis=1, keepdims=True)
         pos = jnp.where(member, start + rank, pos)
@@ -202,7 +203,7 @@
     turn = dot(guest16, as_bf16(same & (row < col))) + dot(dot(lower, guest16).astype(bf16), as_bf16(same))
     turn = turn.astype(i32)
     away = at_home & (group != z) & (turn < GUESTS)
-    key_ref[...] = jnp.where(away, (((z - group) & 3) - 1) * GUESTS + turn, -1)
+    key_ref[...] = jnp.where(away, turn, -1)
     per, groups = 16, CHIPS // 16
     value = jnp.where(group == z, jnp.where(guest, GUEST + turn, pos + 1), 0).astype(f32)
     value = pltpu.roll(value, lax.rem(LANES - GROUP * z, LANES), 1)
@@ -248,13 +249,13 @@
                     mine_ref[at:at + rows, :] = (
                         send_ref[sent:sent + rows, :] if sent is not None else sorted_rows(segment, slots, x)
                     )
-    total = jnp.zeros((8, ALL_GUESTS), f32)
+    total = jnp.zeros((8, GUESTS), f32)
     step = 16
     for first in range(0, CHIPS, step):
         flat = lambda ref: jnp.concatenate([ref[s:s + 1, :] for s in range(first, first + step)], axis=1)
         places = flat(pos_ref) + 1
         parts = jnp.where(iota((8, step * LANES), 0) == 0, places >> 5, places & 31).astype(f32).astype(bf16)
-        total = total + dot_last(parts, as_bf16(iota((ALL_GUESTS, step * LANES), 0) == flat(key_ref)))
+        total = total + dot_last(parts, as_bf16(iota((GUESTS, step * LANES), 0) == flat(key_ref)))
     far_ref[...] = jnp.broadcast_to((32.0 * total[:1] + total[1:2]).astype(i32), far_ref.shape)
 
 
@@ -272,24 +273,20 @@
             length = length + jnp.where(rows >= 3.0, rows - 1.0, rows)
         over = jnp.maximum(over, jnp.where(length > 4 * units, 1.0, 0.0))
     taken = counts[0] + counts[1] + counts[2] + counts[3]
-    extra, room = jnp.maximum(taken - (block - 1), 0.0), jnp.maximum((block - 1) - taken, 0.0)
-    row, col = iota((LANES, LANES), 0), iota((LANES, LANES), 1)
-    same = (row >> 2) == (col >> 2)
-    wanted = dot(extra.astype(bf16), as_bf16(same))
-    before = jnp.zeros(taken.shape, f32)
-    for turn in range(4):
-        earlier = same & (((row - turn) & 3) < ((col - turn) & 3))
-        before = jnp.where((iota(taken.shape, 0) & 3) == turn, dot(room.astype(bf16), as_bf16(earlier)), before)
-    held = jnp.sum(jnp.minimum(jnp.maximum(wanted - before, 0.0), room), axis=0, keepdims=True)
+    lane = iota(taken.shape, 1) & 3
+    before = lambda v, back: jnp.where(lane >= back, pltpu.roll(v, back, 1), pltpu.roll(v, LANES - 4 + back, 1))
+    extra = taken - (block - 1)
+    moved = passed_on(extra, before)
+    held = jnp.sum(moved, axis=0, keepdims=True)
     over = jnp.maximum(over, jnp.where(held > GUESTS, 1.0, 0.0))
-    full = jnp.where(wanted > dot(room.astype(bf16), as_bf16(same)), 1.0, 0.0)
+    full = extra + before(extra, 1) + before(extra, 2) + before(extra, 3) > 0
+    full = jnp.where(full | (moved > block - 1), 1.0, 0.0)
     over = jnp.maximum(over, jnp.max(full, axis=0, keepdims=True))
     over_ref[...] = jnp.broadcast_to(jnp.max(over, axis=1, keepdims=True), over_ref.shape).astype(i32)
 
 
-def add_guests(core, base_ref, guests, far_ref, out_ref):
-    guests = jnp.concatenate([ref[...] for ref in guests] + [guests[0][...]], axis=0)
-    far = far_ref[:1, :]
+def add_guests(core, base_ref, guest_ref, far_ref, out_ref):
+    guests, far = guest_ref[...], far_ref[:1, :]
     for segment in SEGMENTS:
         at, rows = segment[2 + core], segment[1]
         if at is not None:
@@ -305,11 +302,11 @@
 RAW_ROWS = max(sum(CAPS[q] - first for q, first in share) for share in SHARES)
 
 
-def own_kernel(x_ref, g1, g2, g3, far_ref, raw_ref, rows_ref):
+def own_kernel(x_ref, guest_ref, far_ref, raw_ref, rows_ref):
     for core in range(2):
         @pl.when(index_on("c") == core)
         def _():
-            add_guests(core, x_ref, (g1, g2, g3), far_ref, rows_ref)
+            add_guests(core, x_ref, guest_ref, far_ref, rows_ref)
             at = 0
             for q, first, left, right in blocks_of(core):
                 rows = CAPS[q] - first
@@ -333,13 +330,13 @@
     return jnp.concatenate([both, score[UNIT:2 * UNIT]] + rest, axis=0)
 
 
-def gram_kernel(units, meta_ref, x_ref, g1, g2, g3, far_ref, raw_ref, out0, out1, out2, out3, part_ref, rows_ref):
+def gram_kernel(units, meta_ref, x_ref, guest_ref, far_ref, raw_ref, out0, out1, out2, out3, part_ref, rows_ref):
     y, c = index_on("y"), index_on("c")
     part_ref[...] = jnp.full(part_ref.shape, -4.0, f32)
     for core in range(2):
         @pl.when(c == core)
         def _():
-            add_guests(core, x_ref, (g1, g2, g3), far_ref, rows_ref)
+            add_guests(core, x_ref, guest_ref, far_ref, rows_ref)
             at, to = 0, jnp.zeros((), i32)
             for q, first, left, right in blocks_of(core):
                 rows = CAPS[q] - first
@@ -484,7 +481,7 @@
         out_shape=(shape((GUESTS, WIDTH), bf16), shape((8, CHIPS * block), i32), table, table, shape((8, LANES), i32)),
         in_specs=[WHOLE], out_specs=(WHOLE,) * 5, compiler_params=params(12), name="names",
     )(packed)
-    brought = [lax.ppermute(guests, "z", [(i, (i + s) % 4) for i in range(4)]) for s in (1, 2, 3)]
+    brought = lax.ppermute(guests, "z", [(i, (i + 3) % 4) for i in range(4)])
     share = shape((SHARE_ROWS, WIDTH), bf16)
     slots = CHIPS * block
     send = pl.pallas_call(
@@ -494,26 +491,26 @@
     )(packed, line)
     other = lax.ppermute(send, "c", [(0, 1), (1, 0)])
     mine, far = pl.pallas_call(
-        functools.partial(mine_kernel, block), out_shape=(share, shape((8, ALL_GUESTS), i32)),
+        functools.partial(mine_kernel, block), out_shape=(share, shape((8, GUESTS), i32)),
         in_specs=[WHOLE] * 5, out_specs=(WHOLE,) * 2, compiler_params=params(20), name="mine",
         cost_estimate=pl.CostEstimate(flops=2 * SHARE_ROWS * WIDTH * slots, bytes_accessed=4 << 20, transcendentals=0),
     )(packed, line, send, key, pos)
     brought, mine = lax.optimization_barrier((brought, mine))
-    swapped = [lax.ppermute(v, "c", [(0, 1), (1, 0)]) for v in brought]
+    swapped = lax.ppermute(brought, "c", [(0, 1), (1, 0)])
     raw = pl.pallas_call(
         own_kernel, out_shape=shape((RAW_ROWS, LANES), f32),
-        in_specs=[WHOLE] * 5, out_specs=WHOLE,
+        in_specs=[WHOLE] * 3, out_specs=WHOLE,
         scratch_shapes=[pltpu.VMEM((SHARE_ROWS, WIDTH), bf16)],
         compiler_params=params(16), name="own",
         cost_estimate=pl.CostEstimate(flops=2 * RAW_ROWS * LANES * WIDTH, bytes_accessed=4 << 20, transcendentals=0),
-    )(mine, *brought, far)
+    )(mine, brought, far)
     partial = pl.pallas_call(
         functools.partial(gram_kernel, units),
         out_shape=[shape((units * UNIT, LANES), f32)] * 4,
-        in_specs=[WHOLE] * 7, out_specs=[WHOLE] * 4,
+        in_specs=[WHOLE] * 5, out_specs=[WHOLE] * 4,
         scratch_shapes=[pltpu.VMEM((4 * units * UNIT + CAPS[0], LANES), f32), pltpu.VMEM((SHARE_ROWS, WIDTH), bf16)],
         compiler_params=params(16), name="gram",
-    )(meta, other, *swapped, far, raw)
+    )(meta, other, swapped, far, raw)
     arrived = [partial[0]] + [
         lax.ppermute(partial[s], "y", [(i, (i + s) % 4) for i in range(4)]) for s in (1, 2, 3)
     ]

time: 87.9 us -> 84 us (0.956)
  starting transfers between devices: 18.5 us -> 15.1 us
  Pallas kernels: 14.8 us -> 13.8 us
    ppermute x6 -> x2, starting transfers between devices: 4.4 us -> 0.86 us  [the longest x1 0.86 us: route(): swapped = lax.ppermute(brought, 'c', [(0, 1), (1, 0)])]
    ppermute x6 -> x2, waiting for transfers between devices: 1.54 us -> 2.17 us  [the longest x1 2.17 us: route(): brought = lax.ppermute(guests, 'z', [(i, (i + 3) % 4) for i in range(4)])]
  transfers between devices with their start and end apart: 12 -> 8, of which waited for: 6 -> 5; matrix products, arithmetic and copies ran while one was open for 1% -> 1% of each run, Pallas kernels for 5% -> 4%
where the time goes in v11:
time: 84 us; the launch traced here: 83.8 us
  blocking collectives  33.4 us (40%)
  waiting for transfers between devices  20.2 us (24%)
  starting transfers between devices  15.1 us (18%)
  Pallas kernels  13.8 us (16%)
    all_to_all x1, blocking collectives, route(): packed = lax.all_to_all(packed, ('x', 'z', 'y'), 0, 0, tiled=True)  33.4 us
    all_to_all x1, waiting for transfers between devices, route(): lax.all_to_all(best.reshape(2 * CHIPS, 1, LANES), ('c', 'x', 'z', 'y'), 0...  9.47 us
    ppermute x3, waiting for transfers between devices, route(): lax.ppermute(partial[s], 'y', [(i, (i + s) % 4) for i in range(4)])  6.93 us
    all_to_all x1, starting transfers between devices, route(): lax.all_to_all(best.reshape(2 * CHIPS, 1, LANES), ('c', 'x', 'z', 'y'), 0...  6.8 us
    ppermute x3, starting transfers between devices, route(): lax.ppermute(partial[s], 'y', [(i, (i + s) % 4) for i in range(4)])  3.23 us
    ppermute x1, starting transfers between devices, route(): other = lax.ppermute(send, 'c', [(0, 1), (1, 0)])  2.69 us
    pallas_call x1, Pallas kernels, route(): pl.pallas_call(functools.partial(send_kernel, block), out_shape=share, in...  2.34 us
    ppermute x1, waiting for transfers between devices, route(): brought = lax.ppermute(guests, 'z', [(i, (i + 3) % 4) for i in range(4)])  2.17 us
  transfers between devices with their start and end apart: 8, of which 5 were waited for; matrix products, arithmetic and copies ran while one was open for 1% of the time, Pallas kernels for 4%

profile of v11, /device:TPU:1, one launch (start us, length us, event | category | flops | bytes accessed | tf_op | source)
XLA Modules:
  0.0 83.8 jit_solution(6802148142614814801)
XLA Ops:
  0.0 1.9 %unit.3 = (bf16[144,2048]{1,0:T(8,128)(2,1)S(1)}, bf16[144,2048]{1,0:T(8,128)(2,1)S(1)}) custom-call(f32[128,4096]{1,0:T(8,128)} %x_ref.1, s32[1,128]{1,0:T(1,128)} %bitcast.35), custom_call_target="tpu_custom_call" | custom-call | tf_op jit(solution)/shard_map/unit/pallas_call | solution.py:467
  1.9 1.5 %collective-permute-start.7 = (bf16[144,2048]{1,0:T(8,128)(2,1)S(1)}, bf16[144,2048]{1,0:T(8,128)(2,1)S(1)}, u32[]{:S(2)}, u32[]{:S(2)}) collective-permute-start(bf16[144,2048]{1,0:T(8,128)(2,1)S(1)} %get-tuple-element.142), channel_id=1, source_target_pairs={{0,1},{1,0},{2,3},{3,2},{4,5},{5,4},{6,7},{7,6},{8,9},{9,8},{10,11... | collective-permute-start | bytes 1769480 | tf_op jit(solution)/shard_map/ppermute | solution.py:471
  3.4 1.6 %collective-permute-done.7.got_ref = bf16[144,2048]{1,0:T(8,128)(2,1)S(1)} collective-permute-done((bf16[144,2048]{1,0:T(8,128)(2,1)S(1)}, bf16[144,2048]{1,0:T(8,128)(2,1)S(1)}, u32[]{:S(2)}, u32[]{:S(2)}) %collective-permute-start.7) | collective-permute-done | bytes 589856 | tf_op jit(solution)/shard_map/ppermute | solution.py:471
  5.0 0.8 %pack.3 = (bf16[64,24,512]{2,1,0:T(8,128)(2,1)S(1)}, s32[8,128]{1,0:T(8,128)S(1)}) custom-call(bf16[144,2048]{1,0:T(8,128)(2,1)S(1)} %get-tuple-element.141.keep_ref, bf16[144,2048]{1,0:T(8,128)(2,1)S(1)} %collective-permute-done.7.got_ref), custom_call_target="tpu_custom_call" | custom-call | tf_op jit(solution)/shard_map/pack/pallas_call | solution.py:472
  5.9 33.4 %all_to_all.61.x_ref = bf16[64,24,512]{2,1,0:T(8,128)(2,1)S(1)} all-to-all(bf16[64,24,512]{2,1,0:T(8,128)(2,1)S(1)} %get-tuple-element.143), channel_id=1, replica_groups=mesh['x'=4,'z'=4,'y'=4,'c'=2] {'x','z','y'}, dimensions={0} | all-to-all | bytes 3145728 | tf_op jit(solution)/shard_map/all_to_all | solution.py:477
  39.3 1.5 %names.3 = (bf16[64,512]{1,0:T(8,128)(2,1)S(1)}, s32[8,1536]{1,0:T(8,128)S(1)}, s32[64,128]{1,0:T(8,128)S(1)}, s32[64,128]{1,0:T(8,128)S(1)}, s32[8,128]{1,0:T(8,128)S(1)}) custom-call(bf16[64,24,512]{2,1,0:T(8,128)(2,1)S(1)} %all_to_all.61.x_ref), custom_call_target="tpu_custom_call" | custom-call | tf_op jit(solution)/shard_map/names/pallas_call | solution.py:479
  40.8 2.3 %send.3.send_ref = bf16[1216,512]{1,0:T(8,128)(2,1)S(1)} custom-call(bf16[64,24,512]{2,1,0:T(8,128)(2,1)S(1)} %all_to_all.61.x_ref, s32[8,1536]{1,0:T(8,128)S(1)} %get-tuple-element.145.line_ref), custom_call_target="tpu_custom_call" | custom-call | flops 1912602624 | bytes 4194304 | tf_op jit(solution)/shard_map/send/pallas_call | solution.py:487
  43.2 2.7 %collective-permute-start.8 = (bf16[1216,512]{1,0:T(8,128)(2,1)S(1)}, bf16[1216,512]{1,0:T(8,128)(2,1)S(1)}, u32[]{:S(2)}, u32[]{:S(2)}) collective-permute-start(bf16[1216,512]{1,0:T(8,128)(2,1)S(1)} %send.3.send_ref), channel_id=1, source_target_pairs={{0,1},{1,0},{2,3},{3,2},{4,5},{5,4},{6,7},{7,6},{8,9},{9,8},{10,11... | collective-permute-start | bytes 3735560 | tf_op jit(solution)/shard_map/ppermute | solution.py:492
  45.9 0.0 collective-permute-start.9
  45.9 1.5 %mine.3 = (bf16[1216,512]{1,0:T(8,128)(2,1)S(1)}, s32[8,64]{1,0:T(8,128)S(1)}) custom-call(bf16[64,24,512]{2,1,0:T(8,128)(2,1)S(1)} %all_to_all.61.x_ref, s32[8,1536]{1,0:T(8,128)S(1)} %get-tuple-element.145.line_ref, bf16[1216,512]{1,0:T(8,128)(2,1)S(1)} %send.3.send_ref, s32[64,128]{1,0:T(8,128)S(1)} %get-tuple-element.147.key_ref, ...), custom_call_target="tpu_custom_call" | custom-call | flops 1912602624 | bytes 4194304 | tf_op jit(solution)/shard_map/mine/pallas_call | solution.py:493
  47.4 2.2 %collective-permute-done.9.guest_ref = bf16[64,512]{1,0:T(8,128)(2,1)S(1)} collective-permute-done((bf16[64,512]{1,0:T(8,128)(2,1)S(1)}, bf16[64,512]{1,0:T(8,128)(2,1)S(1)}, u32[]{:S(2)}, u32[]{:S(2)}) %collective-permute-start.9) | collective-permute-done | bytes 65568 | tf_op jit(solution)/shard_map/ppermute | solution.py:484
  49.5 0.9 %collective-permute-start.10 = (bf16[64,512]{1,0:T(8,128)(2,1)S(1)}, bf16[64,512]{1,0:T(8,128)(2,1)S(1)}, u32[]{:S(2)}, u32[]{:S(2)}) collective-permute-start(bf16[64,512]{1,0:T(8,128)(2,1)S(1)} %collective-permute-done.9.guest_ref), channel_id=1, source_target_pairs={{0,1},{1,0},{2,3},{3,2},{4,5},{5,4},{6,7},{7,6},{8,9},{9,8},{10,11... | collective-permute-start | bytes 196616 | tf_op jit(solution)/shard_map/ppermute | solution.py:499
  50.4 1.2 %own.3.raw_ref = f32[2496,128]{1,0:T(8,128)S(1)} custom-call(bf16[1216,512]{1,0:T(8,128)(2,1)S(1)} %get-tuple-element.152.x_ref, bf16[64,512]{1,0:T(8,128)(2,1)S(1)} %collective-permute-done.9.guest_ref, s32[8,64]{1,0:T(8,128)S(1)} %get-tuple-element.151.far_ref), custom_call_target="tpu_custom_call" | custom-call | flops 327155712 | bytes 4194304 | tf_op jit(solution)/shard_map/own/pallas_call | solution.py:500
  51.5 0.0 collective-permute-done.10.guest_ref
  51.6 0.0 collective-permute-done.8.x_ref
  51.6 0.0 copy-start
  51.6 0.0 copy-start.1
  51.6 1.6 %gram.3 = (f32[352,128]{1,0:T(8,128)S(1)}, f32[352,128]{1,0:T(8,128)S(1)}, f32[352,128]{1,0:T(8,128)S(1)}, f32[352,128]{1,0:T(8,128)S(1)}) custom-call(s32[8,128]{1,0:T(8,128)S(1)} %get-tuple-element.144.meta_ref, bf16[1216,512]{1,0:T(8,128)(2,1)S(1)} %collective-permute-done.8.x_ref, bf16[64,512]{1,0:T(8,128)(2,1)S(1)} %collective-permute-done.10.guest_ref, ...), custom_call_target="tpu_custom_call" | custom-call | tf_op jit(solution)/shard_map/gram/pallas_call | solution.py:507
  53.2 0.4 collective-permute-start.11
  53.6 1.5 %collective-permute-start.12 = (f32[352,128]{1,0:T(8,128)S(1)}, f32[352,128]{1,0:T(8,128)S(1)}, u32[]{:S(2)}, u32[]{:S(2)}) collective-permute-start(f32[352,128]{1,0:T(8,128)S(1)} %get-tuple-element.155), channel_id=1, source_target_pairs={{0,4},{2,6},{4,0},{6,2},{1,5},{3,7},{5,1},{7,3},{8,12},{10,14},{12... | collective-permute-start | bytes 540680 | tf_op jit(solution)/shard_map/ppermute | solution.py:515
  55.1 1.4 %collective-permute-start.13 = (f32[352,128]{1,0:T(8,128)S(1)}, f32[352,128]{1,0:T(8,128)S(1)}, u32[]{:S(2)}, u32[]{:S(2)}) collective-permute-start(f32[352,128]{1,0:T(8,128)S(1)} %get-tuple-element.156), channel_id=1, source_target_pairs={{0,6},{2,0},{4,2},{6,4},{1,7},{3,1},{5,3},{7,5},{8,14},{10,8},{12,... | collective-permute-start | bytes 540680 | tf_op jit(solution)/shard_map/ppermute | solution.py:515
  56.5 0.4 fit.3
  56.9 0.5 slice.6
  58.1 6.6 %collective-permute-done.11.p1 = f32[352,128]{1,0:T(8,128)S(1)} collective-permute-done((f32[352,128]{1,0:T(8,128)S(1)}, f32[352,128]{1,0:T(8,128)S(1)}, u32[]{:S(2)}, u32[]{:S(2)}) %collective-permute-start.11) | collective-permute-done | bytes 180256 | tf_op jit(solution)/shard_map/ppermute | solution.py:515
  64.6 0.0 collective-permute-done.12.p2
  64.6 0.4 collective-permute-done.13.p3
  65.0 1.7 %maxima.3 = f32[128,128]{1,0:T(8,128)} custom-call(s32[8,128]{1,0:T(8,128)S(1)} %get-tuple-element.144.meta_ref, f32[352,128]{1,0:T(8,128)S(1)} %get-tuple-element.157.p0, f32[352,128]{1,0:T(8,128)S(1)} %collective-permute-done.11.p1, f32[352,128]{1,0:T(8,128)S(1)} %collective-permute-done.12.p2, f32[352,128]{1,0:T(8,128)S(1)} %collective-permute-done.13.p3, ...), custom_call_target="tpu_custom_call" | custom-call | tf_op jit(solution)/shard_map/maxima/pallas_call | solution.py:522
  66.7 6.8 %all-to-all-start.8 = ((f32[128,1,128]{2,1,0:T(1,128)}), f32[128,1,128]{2,1,0:T(1,128)S(1)}, u32[]{:S(2)}, u32[]{:S(2)}) async-start(f32[128,1,128]{2,1,0:T(1,128)} %bitcast.17), calls=%async_computation.8 | async-start | bytes 131072 | tf_op jit(solution)/shard_map/all_to_all | solution.py:529
  73.5 9.5 %all-to-all-done.8 = f32[128,1,128]{2,1,0:T(1,128)S(1)} async-done(((f32[128,1,128]{2,1,0:T(1,128)}), f32[128,1,128]{2,1,0:T(1,128)S(1)}, u32[]{:S(2)}, u32[]{:S(2)}) %all-to-all-start.8) | async-done | bytes 65568 | tf_op jit(solution)/shard_map/all_to_all | solution.py:529
  83.0 0.0 copy-done
  83.0 0.0 copy-done.1
  83.0 0.8 pick.3
  (1 shorter events, 0.0 us)
Async XLA Ops:
  1.9 3.1 %collective-permute-start.7 = (bf16[144,2048]{1,0:T(8,128)(2,1)S(1)}, bf16[144,2048]{1,0:T(8,128)(2,1)S(1)}, u32[]{:S(2)}, u32[]{:S(2)}) collective-permute-start(bf16[144,2048]{1,0:T(8,128)(2,1)S(1)} %get-tuple-element.142), channel_id=1, source_target_pairs={{0,1},{1,0},{2,3},{3,2},{4,5},{5,4},{6,7},{7,6},{8,9},{9,8},{10,11... | collective-permute-start | bytes 1769480 | tf_op jit(solution)/shard_map/ppermute | solution.py:471
  43.2 8.4 %collective-permute-start.8 = (bf16[1216,512]{1,0:T(8,128)(2,1)S(1)}, bf16[1216,512]{1,0:T(8,128)(2,1)S(1)}, u32[]{:S(2)}, u32[]{:S(2)}) collective-permute-start(bf16[1216,512]{1,0:T(8,128)(2,1)S(1)} %send.3.send_ref), channel_id=1, source_target_pairs={{0,1},{1,0},{2,3},{3,2},{4,5},{5,4},{6,7},{7,6},{8,9},{9,8},{10,11... | collective-permute-start | bytes 3735560 | tf_op jit(solution)/shard_map/ppermute | solution.py:492
  45.9 3.7 %collective-permute-start.9 = (bf16[64,512]{1,0:T(8,128)(2,1)S(1)}, bf16[64,512]{1,0:T(8,128)(2,1)S(1)}, u32[]{:S(2)}, u32[]{:S(2)}) collective-permute-start(bf16[64,512]{1,0:T(8,128)(2,1)S(1)} %get-tuple-element.146), channel_id=1, source_target_pairs={{0,24},{8,0},{16,8},{24,16},{1,25},{9,1},{17,9},{25,17},{2,26},{10... | collective-permute-start | bytes 196616 | tf_op jit(solution)/shard_map/ppermute | solution.py:484
  49.5 2.0 %collective-permute-start.10 = (bf16[64,512]{1,0:T(8,128)(2,1)S(1)}, bf16[64,512]{1,0:T(8,128)(2,1)S(1)}, u32[]{:S(2)}, u32[]{:S(2)}) collective-permute-start(bf16[64,512]{1,0:T(8,128)(2,1)S(1)} %collective-permute-done.9.guest_ref), channel_id=1, source_target_pairs={{0,1},{1,0},{2,3},{3,2},{4,5},{5,4},{6,7},{7,6},{8,9},{9,8},{10,11... | collective-permute-start | bytes 196616 | tf_op jit(solution)/shard_map/ppermute | solution.py:499
  51.6 31.4 %copy-start = (s32[128]{0:T(128)S(1)}, s32[128]{0:T(128)}, u32[]{:S(2)}) copy-start(s32[128]{0:T(128)} %param.9) | copy-start | bytes 1540
  51.6 31.4 %copy-start.1 = (f32[128,4096]{1,0:T(8,128)S(1)}, f32[128,4096]{1,0:T(8,128)}, u32[]{:S(2)}) copy-start(f32[128,4096]{1,0:T(8,128)} %x_ref.1) | copy-start | bytes 6291460
  53.2 11.4 %collective-permute-start.11 = (f32[352,128]{1,0:T(8,128)S(1)}, f32[352,128]{1,0:T(8,128)S(1)}, u32[]{:S(2)}, u32[]{:S(2)}) collective-permute-start(f32[352,128]{1,0:T(8,128)S(1)} %get-tuple-element.154), channel_id=1, source_target_pairs={{0,2},{2,4},{4,6},{6,0},{1,3},{3,5},{5,7},{7,1},{8,10},{10,12},{12... | collective-permute-start | bytes 540680 | tf_op jit(solution)/shard_map/ppermute | solution.py:515
  53.6 11.1 %collective-permute-start.12 = (f32[352,128]{1,0:T(8,128)S(1)}, f32[352,128]{1,0:T(8,128)S(1)}, u32[]{:S(2)}, u32[]{:S(2)}) collective-permute-start(f32[352,128]{1,0:T(8,128)S(1)} %get-tuple-element.155), channel_id=1, source_target_pairs={{0,4},{2,6},{4,0},{6,2},{1,5},{3,7},{5,1},{7,3},{8,12},{10,14},{12... | collective-permute-start | bytes 540680 | tf_op jit(solution)/shard_map/ppermute | solution.py:515
  55.1 9.9 %collective-permute-start.13 = (f32[352,128]{1,0:T(8,128)S(1)}, f32[352,128]{1,0:T(8,128)S(1)}, u32[]{:S(2)}, u32[]{:S(2)}) collective-permute-start(f32[352,128]{1,0:T(8,128)S(1)} %get-tuple-element.156), channel_id=1, source_target_pairs={{0,6},{2,0},{4,2},{6,4},{1,7},{3,1},{5,3},{7,5},{8,14},{10,8},{12,... | collective-permute-start | bytes 540680 | tf_op jit(solution)/shard_map/ppermute | solution.py:515
  66.7 16.3 %all-to-all-start.8 = ((f32[128,1,128]{2,1,0:T(1,128)}), f32[128,1,128]{2,1,0:T(1,128)S(1)}, u32[]{:S(2)}, u32[]{:S(2)}) async-start(f32[128,1,128]{2,1,0:T(1,128)} %bitcast.17), calls=%async_computation.8 | async-start | bytes 131072 | tf_op jit(solution)/shard_map/all_to_all | solution.py:529

commit v12 on v11

--- a/solution.py
+++ b/solution.py
@@ -224,31 +224,17 @@
     return dot(onehot, x).astype(bf16)
 
 
-def send_kernel(block, x_ref, line_ref, send_ref):
-    x = x_ref[...].reshape(CHIPS * block, WIDTH)
-    slots = line_ref[:1, :]
-    for me in range(2):
-        @pl.when(index_on("c") == me)
-        def _():
-            for segment in SEGMENTS:
-                at = segment[2 + 1 - me]
-                if at is not None:
-                    send_ref[at:at + segment[1], :] = sorted_rows(segment, slots, x)
-
-
-def mine_kernel(block, x_ref, line_ref, send_ref, key_ref, pos_ref, mine_ref, far_ref):
+def sort_kernel(block, x_ref, line_ref, key_ref, pos_ref, send_ref, mine_ref, far_ref):
     x = x_ref[...].reshape(CHIPS * block, WIDTH)
     slots = line_ref[:1, :]
     for core in range(2):
         @pl.when(index_on("c") == core)
         def _():
             for segment in SEGMENTS:
-                at, sent = segment[2 + core], segment[2 + 1 - core]
-                if at is not None:
-                    rows = segment[1]
-                    mine_ref[at:at + rows, :] = (
-                        send_ref[sent:sent + rows, :] if sent is not None else sorted_rows(segment, slots, x)
-                    )
+                rows = sorted_rows(segment, slots, x)
+                for out_ref, at in ((mine_ref, segment[2 + core]), (send_ref, segment[2 + 1 - core])):
+                    if at is not None:
+                        out_ref[at:at + segment[1], :] = rows
     total = jnp.zeros((8, GUESTS), f32)
     step = 16
     for first in range(0, CHIPS, step):
@@ -483,18 +469,11 @@
     )(packed)
     brought = lax.ppermute(guests, "z", [(i, (i + 3) % 4) for i in range(4)])
     share = shape((SHARE_ROWS, WIDTH), bf16)
-    slots = CHIPS * block
-    send = pl.pallas_call(
-        functools.partial(send_kernel, block), out_shape=share,
-        in_specs=[WHOLE, WHOLE], out_specs=WHOLE, compiler_params=params(16), name="send",
-        cost_estimate=pl.CostEstimate(flops=2 * SHARE_ROWS * WIDTH * slots, bytes_accessed=4 << 20, transcendentals=0),
-    )(packed, line)
+    send, mine, far = pl.pallas_call(
+        functools.partial(sort_kernel, block), out_shape=(share, share, shape((8, GUESTS), i32)),
+        in_specs=[WHOLE] * 4, out_specs=(WHOLE,) * 3, compiler_params=params(24), name="sort",
+    )(packed, line, key, pos)
     other = lax.ppermute(send, "c", [(0, 1), (1, 0)])
-    mine, far = pl.pallas_call(
-        functools.partial(mine_kernel, block), out_shape=(share, shape((8, GUESTS), i32)),
-        in_specs=[WHOLE] * 5, out_specs=(WHOLE,) * 2, compiler_params=params(20), name="mine",
-        cost_estimate=pl.CostEstimate(flops=2 * SHARE_ROWS * WIDTH * slots, bytes_accessed=4 << 20, transcendentals=0),
-    )(packed, line, send, key, pos)
     brought, mine = lax.optimization_barrier((brought, mine))
     swapped = lax.ppermute(brought, "c", [(0, 1), (1, 0)])
     raw = pl.pallas_call(

time: 84 us -> 85.3 us (1.015)
  waiting for transfers between devices: 20.2 us -> 21.8 us
    ppermute x1, waiting for transfers between devices: 2.17 us -> 3.67 us  [route(): brought = lax.ppermute(guests, 'z', [(i, (i + 3) % 4) for i in range(4)])]
    pallas_call x2 -> x1, Pallas kernels: 3.83 us -> 3.53 us  [route(): pl.pallas_call(functools.partial(sort_kernel, block), out_shape=(share, s...]
  transfers between devices with their start and end apart: 8 -> 8, of which waited for: 5 -> 5; matrix products, arithmetic and copies ran while one was open for 1% -> 1% of each run, Pallas kernels for 4% -> 2%
where the time goes in v12:
time: 85.3 us; the launch traced here: 85.1 us
  blocking collectives  33.4 us (39%)
  waiting for transfers between devices  21.8 us (26%)
  starting transfers between devices  15 us (18%)
  Pallas kernels  13.6 us (16%)
    all_to_all x1, blocking collectives, route(): packed = lax.all_to_all(packed, ('x', 'z', 'y'), 0, 0, tiled=True)  33.4 us
    all_to_all x1, waiting for transfers between devices, route(): lax.all_to_all(best.reshape(2 * CHIPS, 1, LANES), ('c', 'x', 'z', 'y'), 0...  9.47 us
    ppermute x3, waiting for transfers between devices, route(): lax.ppermute(partial[s], 'y', [(i, (i + s) % 4) for i in range(4)])  7.05 us
    all_to_all x1, starting transfers between devices, route(): lax.all_to_all(best.reshape(2 * CHIPS, 1, LANES), ('c', 'x', 'z', 'y'), 0...  6.69 us
    ppermute x1, waiting for transfers between devices, route(): brought = lax.ppermute(guests, 'z', [(i, (i + 3) % 4) for i in range(4)])  3.67 us
    pallas_call x1, Pallas kernels, route(): pl.pallas_call(functools.partial(sort_kernel, block), out_shape=(share, s...  3.53 us
    ppermute x3, starting transfers between devices, route(): lax.ppermute(partial[s], 'y', [(i, (i + s) % 4) for i in range(4)])  3.22 us
    ppermute x1, starting transfers between devices, route(): other = lax.ppermute(send, 'c', [(0, 1), (1, 0)])  2.73 us
  transfers between devices with their start and end apart: 8, of which 5 were waited for; matrix products, arithmetic and copies ran while one was open for 1% of the time, Pallas kernels for 2%

profile of v12, /device:TPU:1, one launch (start us, length us, event | category | flops | bytes accessed | tf_op | source)
XLA Modules:
  0.0 85.1 jit_solution(4179792292488359018)
XLA Ops:
  0.0 1.9 %unit.3 = (bf16[144,2048]{1,0:T(8,128)(2,1)S(1)}, bf16[144,2048]{1,0:T(8,128)(2,1)S(1)}) custom-call(f32[128,4096]{1,0:T(8,128)} %x_ref.1, s32[1,128]{1,0:T(1,128)} %bitcast.35), custom_call_target="tpu_custom_call" | custom-call | tf_op jit(solution)/shard_map/unit/pallas_call | solution.py:453
  1.9 1.5 %collective-permute-start.7 = (bf16[144,2048]{1,0:T(8,128)(2,1)S(1)}, bf16[144,2048]{1,0:T(8,128)(2,1)S(1)}, u32[]{:S(2)}, u32[]{:S(2)}) collective-permute-start(bf16[144,2048]{1,0:T(8,128)(2,1)S(1)} %get-tuple-element.144), channel_id=1, source_target_pairs={{0,1},{1,0},{2,3},{3,2},{4,5},{5,4},{6,7},{7,6},{8,9},{9,8},{10,11... | collective-permute-start | bytes 1769480 | tf_op jit(solution)/shard_map/ppermute | solution.py:457
  3.4 1.6 %collective-permute-done.7.got_ref = bf16[144,2048]{1,0:T(8,128)(2,1)S(1)} collective-permute-done((bf16[144,2048]{1,0:T(8,128)(2,1)S(1)}, bf16[144,2048]{1,0:T(8,128)(2,1)S(1)}, u32[]{:S(2)}, u32[]{:S(2)}) %collective-permute-start.7) | collective-permute-done | bytes 589856 | tf_op jit(solution)/shard_map/ppermute | solution.py:457
  5.0 0.8 pack.3
  5.9 33.4 %all_to_all.61.x_ref = bf16[64,24,512]{2,1,0:T(8,128)(2,1)S(1)} all-to-all(bf16[64,24,512]{2,1,0:T(8,128)(2,1)S(1)} %get-tuple-element.145), channel_id=1, replica_groups=mesh['x'=4,'z'=4,'y'=4,'c'=2] {'x','z','y'}, dimensions={0} | all-to-all | bytes 3145728 | tf_op jit(solution)/shard_map/all_to_all | solution.py:463
  39.3 1.5 %names.3 = (bf16[64,512]{1,0:T(8,128)(2,1)S(1)}, s32[8,1536]{1,0:T(8,128)S(1)}, s32[64,128]{1,0:T(8,128)S(1)}, s32[64,128]{1,0:T(8,128)S(1)}, s32[8,128]{1,0:T(8,128)S(1)}) custom-call(bf16[64,24,512]{2,1,0:T(8,128)(2,1)S(1)} %all_to_all.61.x_ref), custom_call_target="tpu_custom_call" | custom-call | tf_op jit(solution)/shard_map/names/pallas_call | solution.py:465
  40.8 3.5 %sort.3 = (bf16[1216,512]{1,0:T(8,128)(2,1)S(1)}, bf16[1216,512]{1,0:T(8,128)(2,1)S(1)}, s32[8,64]{1,0:T(8,128)S(1)}) custom-call(bf16[64,24,512]{2,1,0:T(8,128)(2,1)S(1)} %all_to_all.61.x_ref, s32[8,1536]{1,0:T(8,128)S(1)} %get-tuple-element.147.line_ref, s32[64,128]{1,0:T(8,128)S(1)} %get-tuple-element.148.key_ref, s32[64,128]{1,0:T(8,128)S(1)} %get-tuple-element.149.pos_ref), custom_call_target="tpu_custom_call" | custom-call | tf_op jit(solution)/shard_map/sort/pallas_call | solution.py:472
  44.4 2.7 %collective-permute-start.8 = (bf16[1216,512]{1,0:T(8,128)(2,1)S(1)}, bf16[1216,512]{1,0:T(8,128)(2,1)S(1)}, u32[]{:S(2)}, u32[]{:S(2)}) collective-permute-start(bf16[1216,512]{1,0:T(8,128)(2,1)S(1)} %get-tuple-element.150), channel_id=1, source_target_pairs={{0,1},{1,0},{2,3},{3,2},{4,5},{5,4},{6,7},{7,6},{8,9},{9,8},{10,11... | collective-permute-start | bytes 3735560 | tf_op jit(solution)/shard_map/ppermute | solution.py:476
  47.1 0.0 collective-permute-start.9
  47.1 3.7 %collective-permute-done.9.guest_ref = bf16[64,512]{1,0:T(8,128)(2,1)S(1)} collective-permute-done((bf16[64,512]{1,0:T(8,128)(2,1)S(1)}, bf16[64,512]{1,0:T(8,128)(2,1)S(1)}, u32[]{:S(2)}, u32[]{:S(2)}) %collective-permute-start.9) | collective-permute-done | bytes 65568 | tf_op jit(solution)/shard_map/ppermute | solution.py:470
  50.8 0.8 collective-permute-start.10
  51.6 1.2 %own.3.raw_ref = f32[2496,128]{1,0:T(8,128)S(1)} custom-call(bf16[1216,512]{1,0:T(8,128)(2,1)S(1)} %get-tuple-element.155.x_ref, bf16[64,512]{1,0:T(8,128)(2,1)S(1)} %collective-permute-done.9.guest_ref, s32[8,64]{1,0:T(8,128)S(1)} %get-tuple-element.154.far_ref), custom_call_target="tpu_custom_call" | custom-call | flops 327155712 | bytes 4194304 | tf_op jit(solution)/shard_map/own/pallas_call | solution.py:479
  52.8 0.0 collective-permute-done.10.guest_ref
  52.8 0.0 collective-permute-done.8.x_ref
  52.8 0.0 copy-start
  52.8 0.0 copy-start.1
  52.8 1.7 %gram.3 = (f32[352,128]{1,0:T(8,128)S(1)}, f32[352,128]{1,0:T(8,128)S(1)}, f32[352,128]{1,0:T(8,128)S(1)}, f32[352,128]{1,0:T(8,128)S(1)}) custom-call(s32[8,128]{1,0:T(8,128)S(1)} %get-tuple-element.146.meta_ref, bf16[1216,512]{1,0:T(8,128)(2,1)S(1)} %collective-permute-done.8.x_ref, bf16[64,512]{1,0:T(8,128)(2,1)S(1)} %collective-permute-done.10.guest_ref, ...), custom_call_target="tpu_custom_call" | custom-call | tf_op jit(solution)/shard_map/gram/pallas_call | solution.py:486
  54.5 0.4 collective-permute-start.11
  54.9 1.5 %collective-permute-start.12 = (f32[352,128]{1,0:T(8,128)S(1)}, f32[352,128]{1,0:T(8,128)S(1)}, u32[]{:S(2)}, u32[]{:S(2)}) collective-permute-start(f32[352,128]{1,0:T(8,128)S(1)} %get-tuple-element.158), channel_id=1, source_target_pairs={{0,4},{2,6},{4,0},{6,2},{1,5},{3,7},{5,1},{7,3},{8,12},{10,14},{12... | collective-permute-start | bytes 540680 | tf_op jit(solution)/shard_map/ppermute | solution.py:494
  56.4 1.3 %collective-permute-start.13 = (f32[352,128]{1,0:T(8,128)S(1)}, f32[352,128]{1,0:T(8,128)S(1)}, u32[]{:S(2)}, u32[]{:S(2)}) collective-permute-start(f32[352,128]{1,0:T(8,128)S(1)} %get-tuple-element.159), channel_id=1, source_target_pairs={{0,6},{2,0},{4,2},{6,4},{1,7},{3,1},{5,3},{7,5},{8,14},{10,8},{12,... | collective-permute-start | bytes 540680 | tf_op jit(solution)/shard_map/ppermute | solution.py:494
  57.8 0.4 fit.3
  58.2 0.5 slice.6
  59.4 6.6 %collective-permute-done.11.p1 = f32[352,128]{1,0:T(8,128)S(1)} collective-permute-done((f32[352,128]{1,0:T(8,128)S(1)}, f32[352,128]{1,0:T(8,128)S(1)}, u32[]{:S(2)}, u32[]{:S(2)}) %collective-permute-start.11) | collective-permute-done | bytes 180256 | tf_op jit(solution)/shard_map/ppermute | solution.py:494
  66.0 0.0 collective-permute-done.12.p2
  66.0 0.5 collective-permute-done.13.p3
  66.4 1.7 %maxima.3 = f32[128,128]{1,0:T(8,128)} custom-call(s32[8,128]{1,0:T(8,128)S(1)} %get-tuple-element.146.meta_ref, f32[352,128]{1,0:T(8,128)S(1)} %get-tuple-element.160.p0, f32[352,128]{1,0:T(8,128)S(1)} %collective-permute-done.11.p1, f32[352,128]{1,0:T(8,128)S(1)} %collective-permute-done.12.p2, f32[352,128]{1,0:T(8,128)S(1)} %collective-permute-done.13.p3, ...), custom_call_target="tpu_custom_call" | custom-call | tf_op jit(solution)/shard_map/maxima/pallas_call | solution.py:501
  68.1 6.7 %all-to-all-start.8 = ((f32[128,1,128]{2,1,0:T(1,128)}), f32[128,1,128]{2,1,0:T(1,128)S(1)}, u32[]{:S(2)}, u32[]{:S(2)}) async-start(f32[128,1,128]{2,1,0:T(1,128)} %bitcast.17), calls=%async_computation.8 | async-start | bytes 131072 | tf_op jit(solution)/shard_map/all_to_all | solution.py:508
  74.8 9.5 %all-to-all-done.8 = f32[128,1,128]{2,1,0:T(1,128)S(1)} async-done(((f32[128,1,128]{2,1,0:T(1,128)}), f32[128,1,128]{2,1,0:T(1,128)S(1)}, u32[]{:S(2)}, u32[]{:S(2)}) %all-to-all-start.8) | async-done | bytes 65568 | tf_op jit(solution)/shard_map/all_to_all | solution.py:508
  84.3 0.0 copy-done
  84.3 0.0 copy-done.1
  84.3 0.8 pick.3
  (1 shorter events, 0.0 us)
Async XLA Ops:
  1.9 3.1 %collective-permute-start.7 = (bf16[144,2048]{1,0:T(8,128)(2,1)S(1)}, bf16[144,2048]{1,0:T(8,128)(2,1)S(1)}, u32[]{:S(2)}, u32[]{:S(2)}) collective-permute-start(bf16[144,2048]{1,0:T(8,128)(2,1)S(1)} %get-tuple-element.144), channel_id=1, source_target_pairs={{0,1},{1,0},{2,3},{3,2},{4,5},{5,4},{6,7},{7,6},{8,9},{9,8},{10,11... | collective-permute-start | bytes 1769480 | tf_op jit(solution)/shard_map/ppermute | solution.py:457
  44.4 8.4 %collective-permute-start.8 = (bf16[1216,512]{1,0:T(8,128)(2,1)S(1)}, bf16[1216,512]{1,0:T(8,128)(2,1)S(1)}, u32[]{:S(2)}, u32[]{:S(2)}) collective-permute-start(bf16[1216,512]{1,0:T(8,128)(2,1)S(1)} %get-tuple-element.150), channel_id=1, source_target_pairs={{0,1},{1,0},{2,3},{3,2},{4,5},{5,4},{6,7},{7,6},{8,9},{9,8},{10,11... | collective-permute-start | bytes 3735560 | tf_op jit(solution)/shard_map/ppermute | solution.py:476
  47.1 3.7 %collective-permute-start.9 = (bf16[64,512]{1,0:T(8,128)(2,1)S(1)}, bf16[64,512]{1,0:T(8,128)(2,1)S(1)}, u32[]{:S(2)}, u32[]{:S(2)}) collective-permute-start(bf16[64,512]{1,0:T(8,128)(2,1)S(1)} %get-tuple-element.151), channel_id=1, source_target_pairs={{0,24},{8,0},{16,8},{24,16},{1,25},{9,1},{17,9},{25,17},{2,26},{10... | collective-permute-start | bytes 196616 | tf_op jit(solution)/shard_map/ppermute | solution.py:470
  50.8 2.0 %collective-permute-start.10 = (bf16[64,512]{1,0:T(8,128)(2,1)S(1)}, bf16[64,512]{1,0:T(8,128)(2,1)S(1)}, u32[]{:S(2)}, u32[]{:S(2)}) collective-permute-start(bf16[64,512]{1,0:T(8,128)(2,1)S(1)} %collective-permute-done.9.guest_ref), channel_id=1, source_target_pairs={{0,1},{1,0},{2,3},{3,2},{4,5},{5,4},{6,7},{7,6},{8,9},{9,8},{10,11... | collective-permute-start | bytes 196616 | tf_op jit(solution)/shard_map/ppermute | solution.py:478
  52.8 31.5 %copy-start = (s32[128]{0:T(128)S(1)}, s32[128]{0:T(128)}, u32[]{:S(2)}) copy-start(s32[128]{0:T(128)} %param.9) | copy-start | bytes 1540
  52.8 31.5 %copy-start.1 = (f32[128,4096]{1,0:T(8,128)S(1)}, f32[128,4096]{1,0:T(8,128)}, u32[]{:S(2)}) copy-start(f32[128,4096]{1,0:T(8,128)} %x_ref.1) | copy-start | bytes 6291460
  54.5 11.4 %collective-permute-start.11 = (f32[352,128]{1,0:T(8,128)S(1)}, f32[352,128]{1,0:T(8,128)S(1)}, u32[]{:S(2)}, u32[]{:S(2)}) collective-permute-start(f32[352,128]{1,0:T(8,128)S(1)} %get-tuple-element.157), channel_id=1, source_target_pairs={{0,2},{2,4},{4,6},{6,0},{1,3},{3,5},{5,7},{7,1},{8,10},{10,12},{12... | collective-permute-start | bytes 540680 | tf_op jit(solution)/shard_map/ppermute | solution.py:494
  54.9 11.1 %collective-permute-start.12 = (f32[352,128]{1,0:T(8,128)S(1)}, f32[352,128]{1,0:T(8,128)S(1)}, u32[]{:S(2)}, u32[]{:S(2)}) collective-permute-start(f32[352,128]{1,0:T(8,128)S(1)} %get-tuple-element.158), channel_id=1, source_target_pairs={{0,4},{2,6},{4,0},{6,2},{1,5},{3,7},{5,1},{7,3},{8,12},{10,14},{12... | collective-permute-start | bytes 540680 | tf_op jit(solution)/shard_map/ppermute | solution.py:494
  56.4 10.0 %collective-permute-start.13 = (f32[352,128]{1,0:T(8,128)S(1)}, f32[352,128]{1,0:T(8,128)S(1)}, u32[]{:S(2)}, u32[]{:S(2)}) collective-permute-start(f32[352,128]{1,0:T(8,128)S(1)} %get-tuple-element.159), channel_id=1, source_target_pairs={{0,6},{2,0},{4,2},{6,4},{1,7},{3,1},{5,3},{7,5},{8,14},{10,8},{12,... | collective-permute-start | bytes 540680 | tf_op jit(solution)/shard_map/ppermute | solution.py:494
  68.1 16.2 %all-to-all-start.8 = ((f32[128,1,128]{2,1,0:T(1,128)}), f32[128,1,128]{2,1,0:T(1,128)S(1)}, u32[]{:S(2)}, u32[]{:S(2)}) async-start(f32[128,1,128]{2,1,0:T(1,128)} %bitcast.17), calls=%async_computation.8 | async-start | bytes 131072 | tf_op jit(solution)/shard_map/all_to_all | solution.py:508
